TPU v7x, 256 devices: a whole 4x4x8 slice. The times are simulated.
256 devices in a mesh: space: 32 (over z, x_lo, core), lib: 8 (over y, x_hi).
Axes of the slice: x: 4 (x_hi: 2, x_lo: 2; x = x_hi * 2 + x_lo), y: 4, z: 8, core: 2. Of those that a mesh axis runs over, the one named last changes fastest.
Arguments:
- targets: bfloat16 [8, 64, 131072], P(None, 'lib', 'space'), may hold values from -6 to 6
- library: bfloat16 [2560, 131072], P('lib', 'space'), may hold values from -6 to 6
- anchors: int32 [2048], P('lib'), may hold values from 7 to 295, as said below
- leads: int32 [4], replicated, may hold values from 1 to 24, as said below
- spread: float32 [64], replicated, may hold values from 0.3 to 1
Outputs:
- forecast: bfloat16 [64, 4, 131072], P('lib', None, 'space')
Inputs may be any that keep to these rules, and one draw needn't show every extreme that they name: `anchors`: within each aligned block of 256 entries the positions are distinct. `leads`: Distinct.
All inputs are finite; a program needn't handle non-finite values.
Results may differ from a plain program's by a relative error of at most 0.017.
Values may be sent and summed in bfloat16 or wider, within the bound.
No kernel may reach another device: no remote copies, remote signals or barrier semaphores. Data moves between devices by JAX's collectives and lax.ppermute only.
A program may use at most 192 MiB of HBM per device.

v0:
```python
import math

import jax
import jax.numpy as jnp
from jax import lax
from jax.sharding import PartitionSpec as P


def stacked_lags(block, spots, lags):
    rows = jnp.stack([jnp.take(block, spots - lag, axis=0) for lag in range(lags)], axis=0)
    lnorm = jnp.zeros((spots.shape[0],), jnp.float32)
    for lag in range(lags):
        lnorm = lnorm + jnp.sum(jnp.square(rows[lag].astype(jnp.float32)), axis=1)
    return (rows, lnorm)


def history_norms(history):
    tnorm = jnp.zeros((history.shape[1],), jnp.float32)
    for lag in range(history.shape[0]):
        tnorm = tnorm + jnp.sum(jnp.square(history[lag].astype(jnp.float32)), axis=1)
    return tnorm


def per_device(targets, library, anchors, leads, spread):
    lags = targets.shape[0]
    spaces = lax.axis_size("space")
    scale = math.sqrt(lags * targets.shape[2] * spaces)
    lagged, lnorm = stacked_lags(library, anchors, lags)
    piece = lax.all_gather(targets, "lib", axis=1, tiled=True)
    cross = jnp.einsum("lts,ljs->tj", piece, lagged, preferred_element_type=jnp.float32)
    partial_value = history_norms(piece)[:, None] + lnorm[None, :] - 2.0 * cross
    dist = lax.psum(partial_value, "space")
    scores = -dist / (spread[:, None] * scale)
    top = lax.pmax(jnp.max(scores, axis=1), "lib")
    weights = jnp.exp(scores - top[:, None]).astype(jnp.bfloat16)
    total = lax.psum(jnp.sum(weights.astype(jnp.float32), axis=1), "lib")
    ahead = jnp.take(library, anchors[None, :] + leads[:, None], axis=0)
    composite = jnp.einsum("tj,kjs->tks", weights, ahead, preferred_element_type=jnp.float32)
    summed = lax.psum_scatter(
        composite.astype(jnp.bfloat16), "lib", scatter_dimension=0, tiled=True
    ).astype(jnp.float32)
    count = summed.shape[0]
    mine = lax.dynamic_slice_in_dim(total, lax.axis_index("lib") * count, count)
    return (summed / mine[:, None, None]).astype(jnp.bfloat16)


def solution(mesh):
    placed = (P(None, "lib", "space"), P("lib", "space"), P("lib"), P(), P())
    return jax.shard_map(
        per_device, mesh=mesh, in_specs=placed, out_specs=P("lib", None, "space"), check_vma=False
    )
```

profile of v0, /device:TPU:32, one launch (start us, length us, event | category | flops | bytes accessed | tf_op | source)
XLA Modules:
  0.0 411.8 jit_solution(14615562505758429796)
XLA Ops:
  8.7 3.2 gather_fusion.1
  11.9 3.7 bitcast_dynamic-update-slice_fusion.7
  16.3 3.2 gather_fusion.2
  19.5 3.2 gather_fusion.3
  22.7 3.1 gather_fusion.4
  25.9 3.2 gather_fusion.5
  29.1 3.2 gather_fusion.6
  32.3 3.2 gather_fusion.7
  35.4 3.2 gather_fusion.8
  38.7 2.6 multiply_reduce_fusion
  48.2 1.9 bitcast_dynamic-update-slice_fusion.5
  50.1 1.9 bitcast_dynamic-update-slice_fusion.4
  52.1 2.0 bitcast_dynamic-update-slice_fusion.3
  55.9 1.9 bitcast_dynamic-update-slice_fusion.1
  57.9 1.9 bitcast_dynamic-update-slice_fusion
  59.8 29.3 %all-gather.2.cloned.1.call-done = bf16[8,64,4096]{2,1,0:T(8,128)(2,1)} async-done(((bf16[8,8,4096]{2,1,0:T(8,128)(2,1)}), bf16[8,64,4096]{2,1,0:T(8,128)(2,1)}) %all-gather.2.cloned.1.call-update) | async-done | bytes 4194320 | tf_op jit(solution)/shard_map/all_gather | solution.py:29
  89.1 3.6 multiply_reduce_fusion.14
  92.7 11.8 %fusion.12 = f32[64,256]{1,0:T(8,128)} fusion(bf16[8,256,4096]{2,1,0:T(8,128)(2,1)} %bitcast_dynamic-update-slice_fusion, bf16[8,64,4096]{2,1,0:T(8,128)(2,1)S(1)} %copy-done.9, f32[256]{0:T(256)S(1)} %add_add_fusion, f32[64]{0:T(128)S(1)} %add_add_fusion.1), kind=kOutput, calls=%fused_computation.42 | convolution fusion | flops 1073790976 | bytes 21038336 | tf_op jit(solution)/shard_map/lts,ljs->tj/dot_general | solution.py:30
  104.6 7.7 %gather_fusion = bf16[1024,4096]{1,0:T(8,128)(2,1)} fusion(bf16[320,4096]{1,0:T(8,128)(2,1)S(1)} %copy-done, s32[1024]{0:T(1024)S(1)} %broadcast_clamp_fusion), kind=kCustom, calls=%fused_computation.8 | custom fusion | bytes 16781312 | tf_op jit(solution)/shard_map/jit(_take)/gather | solution.py:37
  112.3 181.9 %all-reduce.2.cloned.1.call-done = f32[64,256]{1,0:T(8,128)} async-done(((f32[64,256]{1,0:T(8,128)}), f32[64,256]{1,0:T(8,128)}) %all-reduce.2.cloned.1.call-update) | async-done | bytes 65552 | tf_op jit(solution)/shard_map/psum | solution.py:32
  295.3 23.9 %pmax.7 = f32[64]{0:T(128)S(1)} all-reduce(f32[64]{0:T(128)S(1)} %fusion.14), channel_id=1, replica_groups=mesh['space'=32,'lib'=8] {'lib'}, use_global_device_ids=true, to_apply=%region_18.20 | all-reduce | flops 64 | bytes 512 | tf_op jit(solution)/shard_map/pmax | solution.py:34
  320.2 5.5 %fusion.6 = bf16[4,8,8,4096]{3,2,1,0:T(8,128)(2,1)S(1)} fusion(bf16[4,256,4096]{2,1,0:T(8,128)(2,1)} %bitcast.43, pred[4,256]{1,0:T(4,128)(4,1)S(1)} %fusion.18, bf16[64,256]{1,0:T(8,128)(2,1)S(1)} %get-tuple-element.15), kind=kOutput, calls=%fused_computation.13 | convolution fusion | flops 542113792 | bytes 10519552 | tf_op jit(solution)/shard_map/tj,kjs->tks/dot_general | solution.py:38
  327.3 19.1 %psum.15 = f32[64]{0:T(128)S(1)} all-reduce(f32[64]{0:T(128)S(1)} %get-tuple-element.14), channel_id=1, replica_groups=mesh['space'=32,'lib'=8] {'lib'}, use_global_device_ids=true, to_apply=%region_21.23 | all-reduce | flops 64 | bytes 512 | tf_op jit(solution)/shard_map/psum | solution.py:36
  346.5 56.8 %reduce-scatter.4.cloned.1.call-done = bf16[8,16384]{1,0:T(8,128)(2,1)} async-done(((bf16[64,16384]{1,0:T(8,128)(2,1)}), bf16[8,16384]{1,0:T(8,128)(2,1)}) %reduce-scatter.4.cloned.1.call-update) | async-done | bytes 262160
  (60 shorter events, 17.4 us)
Async XLA Ops:
  6.5 2.2 copy-start
  6.5 82.5 %all-gather.2.cloned.1.call-start = ((), (), s32[]{:S(2)}) async-start(), calls=%async_computation.1 | async-start | bytes 4718592 | tf_op jit(solution)/shard_map/all_gather | solution.py:29
  7.3 287.0 %all-reduce.2.cloned.1.call-start = ((), (), s32[]{:S(2)}) async-start(), calls=%async_computation.2 | async-start | bytes 131072 | tf_op jit(solution)/shard_map/psum | solution.py:32
  11.9 3.7 copy-start.8
  35.4 3.2 copy-start.10
  35.4 3.2 copy-start.11
  38.6 2.7 copy-start.7
  38.7 3.4 copy-start.4
  41.4 1.6 copy-start.5
  42.1 1.8 copy-start.2
  43.0 1.7 copy-start.3
  43.8 1.7 copy-start.1
  55.9 1.9 copy-start.6
  89.1 3.6 copy-start.9
  92.7 11.9 %copy-start.12 = (f32[64]{0:T(128)S(1)}, f32[64]{0:T(128)}, u32[]{:S(2)}) copy-start(f32[64]{0:T(128)} %param.11) | copy-start | bytes 772
  104.5 298.8 %reduce-scatter.4.cloned.1.call-start = ((), (), s32[]{:S(2)}) async-start(), calls=%async_computation.3 | async-start | bytes 2359296
Sparse Core Ops, SparseCore 0:
  10.0 79.0 all-gather.1
  104.7 189.5 all-reduce.1
  327.4 75.8 reduce-scatter.3
where the time goes:
time: 412 us
  waiting for transfers between devices  269 us (65%)
  blocking collectives  43.1 us (10%)
  local copies, waits for them, and re-layouts  36.4 us (9%)
  other arithmetic  32.9 us (8%)
  matrix products  17.3 us (4%)
  between operations  13.2 us (3%)
    psum x1, waiting for transfers between devices, per_device(): dist = lax.psum(partial_value, 'space')  182 us
    unnamed x4, waiting for transfers between devices  57.6 us
    all_gather x1, waiting for transfers between devices, per_device(): piece = lax.all_gather(targets, 'lib', axis=1, tiled=True)  29.3 us
    gather x8, local copies, waits for them, and re-layouts, stacked_lags(): jnp.take(block, spots - lag, axis=0)  25.5 us
    pmax x1, blocking collectives, per_device(): top = lax.pmax(jnp.max(scores, axis=1), 'lib')  23.9 us
    psum x1, blocking collectives, per_device(): total = lax.psum(jnp.sum(weights.astype(jnp.float32), axis=1), 'lib')  19.1 us
    unnamed x8, other arithmetic  15.2 us
    dot_general x1, matrix products, per_device(): jnp.einsum('lts,ljs->tj', piece, lagged, preferred_element_type=jnp.float32)  11.8 us
  transfers between devices with their start and end apart: 3, of which 3 were waited for; matrix products, arithmetic and copies ran while one was open for 14% of the time, Pallas kernels for 0%

commit v1 on v0

v1 whole, which is shorter than its diff:
```python
import functools
import math

import jax
import jax.numpy as jnp
from jax import lax
from jax.experimental import pallas as pl
from jax.experimental.pallas import tpu as pltpu
from jax.sharding import Mesh, PartitionSpec as P

F32 = jnp.float32
BF16 = jnp.bfloat16
LIB = ("y", "xh")
SPACE = ("z", "xl", "co")
NEG = -3.0e38
VM = pl.BlockSpec(memory_space=pltpu.VMEM)
SM = pl.BlockSpec(memory_space=pltpu.SMEM)
PARAMS = pltpu.CompilerParams(vmem_limit_bytes=40 * 1024 * 1024)


def flip(n, bit):
    return [(i, i ^ bit) for i in range(n)]


def turn(n, by):
    return [(i, (i + by) % n) for i in range(n)]


def gather_targets(own):
    half = own.shape[0] // 2
    across = lax.ppermute(own, "xh", flip(2, 1))
    below = lax.ppermute(own, "y", turn(4, 1))
    above = lax.ppermute(own, "y", turn(4, -1))
    far_a = lax.ppermute(below[:half], "y", turn(4, 1))
    far_b = lax.ppermute(above[half:], "y", turn(4, -1))
    below_x = lax.ppermute(across, "y", turn(4, 1))
    above_x = lax.ppermute(across, "y", turn(4, -1))
    far_xa = lax.ppermute(far_a, "xh", flip(2, 1))
    far_xb = lax.ppermute(far_b, "xh", flip(2, 1))
    return (own, across, below, above, below_x, above_x, far_a, far_b, far_xa, far_xb)


def cross_kernel(lags, place, *refs):
    pieces, (block, lnorm, out, acc) = refs[:10], refs[10:]
    rows, width = block.shape
    step = 512
    acc[...] = jnp.zeros_like(acc)

    def body(i, norms):
        cols = pl.ds(pl.multiple_of(i * step, step), step)
        lhs = jnp.concatenate([p[:, cols] for p in pieces], axis=0)
        acc[:, :rows] += lax.dot_general(
            lhs, block[:, cols], (((1,), (1,)), ((), ())), preferred_element_type=F32
        )
        wide = lhs.astype(F32)
        wide = wide * wide
        part = wide[:, :128]
        for c in range(128, step, 128):
            part = part + wide[:, c : c + 128]
        return norms + part

    norms = lax.fori_loop(0, width // step, body, jnp.zeros((acc.shape[0], 128), F32))
    norms = jnp.sum(norms, axis=1, keepdims=True)
    count = acc.shape[0] // 8 // lags
    for r in range(8):
        cross = jnp.zeros((count, acc.shape[1]), F32)
        tnorm = jnp.zeros((count, 1), F32)
        for lag in range(lags):
            at = (r * lags + lag) * count
            here = acc[at : at + count, :]
            cross = cross + (pltpu.roll(here, lag, 1) if lag else here)
            tnorm = tnorm + norms[at : at + count]
        value = tnorm + lnorm[:1, :] - 2.0 * cross
        out[pl.ds(pl.multiple_of(place[r] * count, count), count), :] = value


def compose_kernel(leads, dist, mask, scale, perm, block, out):
    rows, width = block.shape
    targets = dist.shape[0]
    wide = dist.shape[1]
    scores = jnp.where(mask[:1, :] > 0.0, -dist[...] / scale[:, :1], NEG)
    top = jnp.max(scores, axis=1, keepdims=True)
    top_hi = top.astype(BF16)
    top_lo = (top - top_hi.astype(F32)).astype(BF16)
    shift = top_hi.astype(F32) + top_lo.astype(F32)
    weights = jnp.where(mask[:1, :] > 0.0, jnp.exp(scores - shift), 0.0).astype(BF16).astype(F32)
    total = jnp.sum(weights, axis=1, keepdims=True)
    tot_hi = total.astype(BF16)
    tot_lo = (total - tot_hi.astype(F32)).astype(BF16)
    count = leads.shape[0]
    stack = jnp.concatenate([pltpu.roll(weights, leads[k], 1) for k in range(count)], axis=0).astype(BF16)
    mixed = jnp.dot(perm[...], stack, preferred_element_type=F32).astype(BF16)[:, :rows]
    lane = lax.broadcasted_iota(jnp.int32, (targets, 128), 1)
    facts = jnp.where(
        lane == 0,
        top_hi.astype(F32),
        jnp.where(lane == 1, top_lo.astype(F32), jnp.where(lane == 2, tot_hi.astype(F32), tot_lo.astype(F32))),
    ).astype(BF16)
    facts = jnp.concatenate([facts] * count, axis=0)
    facts = jnp.dot(perm[...], facts, preferred_element_type=F32).astype(BF16)
    out[:, width : width + 128] = facts
    step = 512
    for c in range(0, width, step):
        out[:, c : c + step] = jnp.dot(mixed, block[:, c : c + step], preferred_element_type=F32).astype(BF16)


def combine_kernel(parts, out):
    n, rows, wide = parts.shape
    width = wide - 128
    facts = [parts[b, :, width:].astype(F32) for b in range(n)]
    tops = [f[:, 0:1] + f[:, 1:2] for f in facts]
    top = functools.reduce(jnp.maximum, tops)
    factors = [jnp.exp(t - top) for t in tops]
    total = sum(f * (x[:, 2:3] + x[:, 3:4]) for f, x in zip(factors, facts))
    factors = [f / total for f in factors]
    step = 512
    for c in range(0, width, step):
        summed = factors[0] * parts[0, :, c : c + step].astype(F32)
        for b in range(1, n):
            summed = summed + factors[b] * parts[b, :, c : c + step].astype(F32)
        out[:, c : c + step] = summed.astype(BF16)


def total_over_space(value):
    for axis, n, bit in (("co", 2, 1), ("xl", 2, 1), ("z", 8, 1), ("z", 8, 2), ("z", 8, 4)):
        value = value + lax.ppermute(value, axis, flip(n, bit))
    return value


def per_device(targets, library, anchors, leads, spread):
    lags, count, width = targets.shape
    rows = library.shape[0]
    lead_n = leads.shape[0]
    n_lib = lax.axis_size(LIB)
    n_target = count * n_lib
    wide = -(-rows // 128) * 128
    scale = math.sqrt(lags * width * lax.axis_size(SPACE))

    pieces = gather_targets(targets.reshape(lags * count, width))

    y, xh = lax.axis_index("y"), lax.axis_index("xh")
    hops = ((0, 0), (0, 1), (3, 0), (1, 0), (3, 1), (1, 1), (2, 0), (2, 1))
    place = jnp.stack([((y + dy) % 4) * 2 + (xh ^ dx) for dy, dx in hops]).astype(jnp.int32)

    norm = jnp.sum(jnp.square(library.astype(F32)), axis=1)
    norm = jnp.pad(norm, (0, wide - rows))
    lnorm = functools.reduce(jnp.add, [jnp.roll(norm, lag) for lag in range(lags)])
    lnorm = jnp.broadcast_to(lnorm[None, :], (8, wide))
    spots = lax.broadcasted_iota(jnp.int32, (wide, 1), 0)
    mask = jnp.any(spots == anchors[None, :], axis=1).astype(F32)
    mask = jnp.broadcast_to(mask[None, :], (8, wide))
    scales = jnp.broadcast_to((spread * scale)[:, None], (n_target, 128))
    row = lax.broadcasted_iota(jnp.int32, (lead_n * n_target, lead_n * n_target), 0)
    col = lax.broadcasted_iota(jnp.int32, (lead_n * n_target, lead_n * n_target), 1)
    perm = ((row % lead_n) * n_target + row // lead_n == col).astype(BF16)

    partial_dist = pl.pallas_call(
        functools.partial(cross_kernel, lags),
        out_shape=jax.ShapeDtypeStruct((n_target, wide), F32),
        in_specs=[SM] + [VM] * 12,
        out_specs=VM,
        scratch_shapes=[pltpu.VMEM((lags * n_target, wide), F32)],
        compiler_params=PARAMS,
        cost_estimate=pl.CostEstimate(flops=2 * lags * n_target * wide * width, bytes_accessed=7 << 20, transcendentals=0),
        name="cross",
    )(place, *pieces, library, lnorm)

    dist = total_over_space(partial_dist)

    parts = pl.pallas_call(
        compose_kernel,
        out_shape=jax.ShapeDtypeStruct((lead_n * n_target, width + 128), BF16),
        in_specs=[SM] + [VM] * 5,
        out_specs=VM,
        compiler_params=PARAMS,
        cost_estimate=pl.CostEstimate(flops=2 * lead_n * n_target * rows * width, bytes_accessed=5 << 20, transcendentals=n_target * wide),
        name="compose",
    )(leads, dist, mask, scales, perm, library)

    parts = parts.reshape(n_lib, lead_n * count, width + 128)
    parts = lax.all_to_all(parts, LIB, 0, 0, tiled=True)

    out = pl.pallas_call(
        combine_kernel,
        out_shape=jax.ShapeDtypeStruct((lead_n * count, width), BF16),
        in_specs=[VM],
        out_specs=VM,
        compiler_params=PARAMS,
        cost_estimate=pl.CostEstimate(flops=2 * n_target * lead_n * width, bytes_accessed=3 << 20, transcendentals=0),
        name="combine",
    )(parts)
    return out.reshape(count, lead_n, width)


def solution(mesh):
    fine = Mesh(mesh.devices.reshape(8, 2, 2, 4, 2), SPACE + LIB)
    placed = (P(None, LIB, SPACE), P(LIB, SPACE), P(LIB), P(), P())
    return jax.shard_map(per_device, mesh=fine, in_specs=placed, out_specs=P(LIB, None, SPACE), check_vma=False)
```

time: 412 us -> 108 us (0.26)
  waiting for transfers between devices: 269 us -> 30.5 us
  local copies, waits for them, and re-layouts: 36.4 us -> 3.93 us
  other arithmetic: 32.9 us -> 2.93 us
  starting transfers between devices: 0.08 us -> 30 us
  matrix products: 17.3 us -> 0 us
  between operations: 13.2 us -> 0.13 us
  blocking collectives: 43.1 us -> 30.9 us
  Pallas kernels: 0 us -> 8.67 us
    psum x1 -> x0, waiting for transfers between devices: 182 us -> none  [per_device(): dist = lax.psum(partial_value, 'space')]
    unnamed x4 -> x0, waiting for transfers between devices: 57.6 us -> none
    gather x9 -> x0, local copies, waits for them, and re-layouts: 33.2 us -> none  [the longest x8 25.5 us: stacked_lags(): jnp.take(block, spots - lag, axis=0)]
    all_to_all x0 -> x1, blocking collectives: none -> 30.9 us  [per_device(): parts = lax.all_to_all(parts, LIB, 0, 0, tiled=True)]
    ppermute x0 -> x14, waiting for transfers between devices: none -> 30.5 us  [the longest x5 14.3 us: total_over_space(): value = value + lax.ppermute(value, axis, flip(n, bit))]
    ppermute x0 -> x14, starting transfers between devices: none -> 30 us  [the longest x5 11.1 us: total_over_space(): value = value + lax.ppermute(value, axis, flip(n, bit))]
    all_gather x1 -> x0, waiting for transfers between devices: 29.3 us -> none  [per_device(): piece = lax.all_gather(targets, 'lib', axis=1, tiled=True)]
    pmax x1 -> x0, blocking collectives: 23.9 us -> none  [per_device(): top = lax.pmax(jnp.max(scores, axis=1), 'lib')]
  transfers between devices with their start and end apart: 3 -> 14, of which waited for: 3 -> 11; matrix products, arithmetic and copies ran while one was open for 14% -> 3% of each run, Pallas kernels for 0% -> 0%
where the time goes in v1:
time: 108 us; the launch traced here: 107 us
  blocking collectives  30.9 us (29%)
  waiting for transfers between devices  30.5 us (28%)
  starting transfers between devices  30 us (28%)
  Pallas kernels  8.67 us (8%)
  local copies, waits for them, and re-layouts  3.93 us (4%)
  other arithmetic  2.93 us (3%)
    all_to_all x1, blocking collectives, per_device(): parts = lax.all_to_all(parts, LIB, 0, 0, tiled=True)  30.9 us
    ppermute x5, waiting for transfers between devices, total_over_space(): value = value + lax.ppermute(value, axis, flip(n, bit))  14.3 us
    ppermute x5, starting transfers between devices, total_over_space(): value = value + lax.ppermute(value, axis, flip(n, bit))  11.1 us
    ppermute x1, waiting for transfers between devices, gather_targets(): above = lax.ppermute(own, 'y', turn(4, -1))  6.09 us
    pallas_call x1, Pallas kernels, per_device(): pl.pallas_call(functools.partial(cross_kernel, lags), out_shape=jax.Shape...  5.81 us
    ppermute x1, starting transfers between devices, gather_targets(): far_b = lax.ppermute(above[half:], 'y', turn(4, -1))  3.66 us
    ppermute x1, starting transfers between devices, gather_targets(): above_x = lax.ppermute(across, 'y', turn(4, -1))  3.23 us
    ppermute x1, starting transfers between devices, gather_targets(): across = lax.ppermute(own, 'xh', flip(2, 1))  3.02 us
  transfers between devices with their start and end apart: 14, of which 11 were waited for; matrix products, arithmetic and copies ran while one was open for 3% of the time, Pallas kernels for 0%

profile of v1, /device:TPU:32, one launch (start us, length us, event | category | flops | bytes accessed | tf_op | source)
XLA Modules:
  0.0 107.1 jit_solution(7151867823983671343)
XLA Ops:
  0.0 3.0 %collective-permute-start.2 = (bf16[64,4096]{1,0:T(8,128)(2,1)}, bf16[64,4096]{1,0:T(8,128)(2,1)S(1)}, u32[]{:S(2)}, u32[]{:S(2)}) collective-permute-start(bf16[64,4096]{1,0:T(8,128)(2,1)} %bitcast.11), channel_id=1, source_target_pairs={{0,6},{2,0},{4,2},{6,4},{1,7},{3,1},{5,3},{7,5},{8,14},{10,8},{12,... | collective-permute-start | bytes 1572872 | tf_op jit(solution)/shard_map/ppermute | solution.py:33
  3.0 3.0 %collective-permute-start = (bf16[64,4096]{1,0:T(8,128)(2,1)}, bf16[64,4096]{1,0:T(8,128)(2,1)}, u32[]{:S(2)}, u32[]{:S(2)}) collective-permute-start(bf16[64,4096]{1,0:T(8,128)(2,1)} %bitcast.13), channel_id=1, source_target_pairs={{0,1},{1,0},{2,3},{3,2},{4,5},{5,4},{6,7},{7,6},{8,9},{9,8},{10,11... | collective-permute-start | bytes 1572872 | tf_op jit(solution)/shard_map/ppermute | solution.py:31
  6.0 2.3 %multiply_reduce_fusion = f32[320]{0:T(512)S(1)} fusion(bf16[320,4096]{1,0:T(8,128)(2,1)} %block.1), kind=kLoop, calls=%fused_computation | loop fusion | flops 3931840 | bytes 2622720 | tf_op jit(solution)/shard_map/reduce_sum | solution.py:145
  8.4 6.1 %collective-permute-done.2.refs_3_ = bf16[64,4096]{1,0:T(8,128)(2,1)S(1)} collective-permute-done((bf16[64,4096]{1,0:T(8,128)(2,1)}, bf16[64,4096]{1,0:T(8,128)(2,1)S(1)}, u32[]{:S(2)}, u32[]{:S(2)}) %collective-permute-start.2) | collective-permute-done | bytes 524320 | tf_op jit(solution)/shard_map/ppermute | solution.py:33
  14.5 3.7 %collective-permute-start.6 = (bf16[32,4096]{1,0:T(8,128)(2,1)S(1)}, bf16[32,4096]{1,0:T(8,128)(2,1)S(1)}, u32[]{:S(2)}, u32[]{:S(2)}) collective-permute-start(bf16[32,4096]{1,0:T(8,128)(2,1)S(1)} %slice.58), channel_id=1, source_target_pairs={{0,6},{2,0},{4,2},{6,4},{1,7},{3,1},{5,3},{7,5},{8,14},{10,8},{12,... | collective-permute-start | bytes 786440 | tf_op jit(solution)/shard_map/ppermute | solution.py:35
  19.1 3.2 %collective-permute-start.4 = (bf16[64,4096]{1,0:T(8,128)(2,1)}, bf16[64,4096]{1,0:T(8,128)(2,1)}, u32[]{:S(2)}, u32[]{:S(2)}) collective-permute-start(bf16[64,4096]{1,0:T(8,128)(2,1)} %collective-permute-done.refs_1_), channel_id=1, source_target_pairs={{0,6},{2,0},{4,2},{6,4},{1,7},{3,1},{5,3},{7,5},{8,14},{10,8},{12,... | collective-permute-start | bytes 1572872 | tf_op jit(solution)/shard_map/ppermute | solution.py:37
  22.3 2.5 %collective-permute-done.6.refs_7_ = bf16[32,4096]{1,0:T(8,128)(2,1)S(1)} collective-permute-done((bf16[32,4096]{1,0:T(8,128)(2,1)S(1)}, bf16[32,4096]{1,0:T(8,128)(2,1)S(1)}, u32[]{:S(2)}, u32[]{:S(2)}) %collective-permute-start.6) | collective-permute-done | bytes 262176 | tf_op jit(solution)/shard_map/ppermute | solution.py:35
  24.8 2.9 %collective-permute-start.8 = (bf16[32,4096]{1,0:T(8,128)(2,1)S(1)}, bf16[32,4096]{1,0:T(8,128)(2,1)}, u32[]{:S(2)}, u32[]{:S(2)}) collective-permute-start(bf16[32,4096]{1,0:T(8,128)(2,1)S(1)} %collective-permute-done.6.refs_7_), channel_id=1, source_target_pairs={{0,1},{1,0},{2,3},{3,2},{4,5},{5,4},{6,7},{7,6},{8,9},{9,8},{10,11... | collective-permute-start | bytes 786440 | tf_op jit(solution)/shard_map/ppermute | solution.py:39
  27.7 1.9 %collective-permute-done.5.refs_6_ = bf16[32,4096]{1,0:T(8,128)(2,1)} collective-permute-done((bf16[32,4096]{1,0:T(8,128)(2,1)S(1)}, bf16[32,4096]{1,0:T(8,128)(2,1)}, u32[]{:S(2)}, u32[]{:S(2)}) %collective-permute-start.5) | collective-permute-done | bytes 262176 | tf_op jit(solution)/shard_map/ppermute | solution.py:34
  29.6 3.0 %collective-permute-start.7 = (bf16[32,4096]{1,0:T(8,128)(2,1)}, bf16[32,4096]{1,0:T(8,128)(2,1)}, u32[]{:S(2)}, u32[]{:S(2)}) collective-permute-start(bf16[32,4096]{1,0:T(8,128)(2,1)} %collective-permute-done.5.refs_6_), channel_id=1, source_target_pairs={{0,1},{1,0},{2,3},{3,2},{4,5},{5,4},{6,7},{7,6},{8,9},{9,8},{10,11... | collective-permute-start | bytes 786440 | tf_op jit(solution)/shard_map/ppermute | solution.py:38
  32.8 2.5 %collective-permute-done.8.refs_9_ = bf16[32,4096]{1,0:T(8,128)(2,1)} collective-permute-done((bf16[32,4096]{1,0:T(8,128)(2,1)S(1)}, bf16[32,4096]{1,0:T(8,128)(2,1)}, u32[]{:S(2)}, u32[]{:S(2)}) %collective-permute-start.8) | collective-permute-done | bytes 262176 | tf_op jit(solution)/shard_map/ppermute | solution.py:39
  35.3 2.8 %collective-permute-done.7.refs_8_ = bf16[32,4096]{1,0:T(8,128)(2,1)} collective-permute-done((bf16[32,4096]{1,0:T(8,128)(2,1)}, bf16[32,4096]{1,0:T(8,128)(2,1)}, u32[]{:S(2)}, u32[]{:S(2)}) %collective-permute-start.7) | collective-permute-done | bytes 262176 | tf_op jit(solution)/shard_map/ppermute | solution.py:38
  38.6 1.0 copy-done.2
  40.7 5.8 %cross.1 = f32[64,384]{1,0:T(8,128)S(1)} custom-call(s32[8]{0:T(128)S(1)} %stack.35.place, bf16[64,4096]{1,0:T(8,128)(2,1)S(1)} %bitcast.14, bf16[64,4096]{1,0:T(8,128)(2,1)} %collective-permute-done.refs_1_, bf16[64,4096]{1,0:T(8,128)(2,1)S(1)} %copy-done.2, bf16[64,4096]{1,0:T(8,128)(2,1)S(1)} %collective-permute-done.2.refs_3_, ...), custom_call_target="tpu_custom_call" | custom-call | flops 1610612736 | bytes 7340032 | tf_op jit(solution)/shard_map/cross/pallas_call | solution.py:157
  46.6 1.3 %collective-permute-done.9 = f32[64,384]{1,0:T(8,128)S(1)} collective-permute-done((f32[64,384]{1,0:T(8,128)S(1)}, f32[64,384]{1,0:T(8,128)S(1)}, u32[]{:S(2)}, u32[]{:S(2)}) %collective-permute-start.9) | collective-permute-done | bytes 98336 | tf_op jit(solution)/shard_map/ppermute | solution.py:126
  47.9 1.5 %collective-permute-start.10 = (f32[64,384]{1,0:T(8,128)S(1)}, f32[64,384]{1,0:T(8,128)S(1)}, u32[]{:S(2)}, u32[]{:S(2)}) collective-permute-start(f32[64,384]{1,0:T(8,128)S(1)} %add.139), channel_id=1, source_target_pairs={{0,16},{16,0},{1,17},{17,1},{2,18},{18,2},{3,19},{19,3},{4,20},{20... | collective-permute-start | bytes 294920 | tf_op jit(solution)/shard_map/ppermute | solution.py:126
  49.4 3.5 %collective-permute-done.10 = f32[64,384]{1,0:T(8,128)S(1)} collective-permute-done((f32[64,384]{1,0:T(8,128)S(1)}, f32[64,384]{1,0:T(8,128)S(1)}, u32[]{:S(2)}, u32[]{:S(2)}) %collective-permute-start.10) | collective-permute-done | bytes 98336 | tf_op jit(solution)/shard_map/ppermute | solution.py:126
  53.3 4.2 %collective-permute-done.11 = f32[64,384]{1,0:T(8,128)S(1)} collective-permute-done((f32[64,384]{1,0:T(8,128)S(1)}, f32[64,384]{1,0:T(8,128)S(1)}, u32[]{:S(2)}, u32[]{:S(2)}) %collective-permute-start.11) | collective-permute-done | bytes 98336 | tf_op jit(solution)/shard_map/ppermute | solution.py:126
  57.6 3.4 %collective-permute-start.12 = (f32[64,384]{1,0:T(8,128)S(1)}, f32[64,384]{1,0:T(8,128)S(1)}, u32[]{:S(2)}, u32[]{:S(2)}) collective-permute-start(f32[64,384]{1,0:T(8,128)S(1)} %add.141), channel_id=1, source_target_pairs={{0,64},{32,96},{64,0},{96,32},{128,192},{160,224},{192,128},{224,1... | collective-permute-start | bytes 294920 | tf_op jit(solution)/shard_map/ppermute | solution.py:126
  60.9 2.7 %collective-permute-done.12 = f32[64,384]{1,0:T(8,128)S(1)} collective-permute-done((f32[64,384]{1,0:T(8,128)S(1)}, f32[64,384]{1,0:T(8,128)S(1)}, u32[]{:S(2)}, u32[]{:S(2)}) %collective-permute-start.12) | collective-permute-done | bytes 98336 | tf_op jit(solution)/shard_map/ppermute | solution.py:126
  63.7 6.0 %collective-permute-start.13 = (f32[64,384]{1,0:T(8,128)S(1)}, f32[64,384]{1,0:T(8,128)S(1)}, u32[]{:S(2)}, u32[]{:S(2)}) collective-permute-start(f32[64,384]{1,0:T(8,128)S(1)} %add.142), channel_id=1, source_target_pairs={{0,128},{32,160},{64,192},{96,224},{128,0},{160,32},{192,64},{224,... | collective-permute-start | bytes 294920 | tf_op jit(solution)/shard_map/ppermute | solution.py:126
  69.8 2.6 %collective-permute-done.13 = f32[64,384]{1,0:T(8,128)S(1)} collective-permute-done((f32[64,384]{1,0:T(8,128)S(1)}, f32[64,384]{1,0:T(8,128)S(1)}, u32[]{:S(2)}, u32[]{:S(2)}) %collective-permute-start.13) | collective-permute-done | bytes 98336 | tf_op jit(solution)/shard_map/ppermute | solution.py:126
  72.5 2.2 %compose.1 = bf16[256,4224]{1,0:T(8,128)(2,1)S(1)} custom-call(s32[4]{0:T(128)S(1)} %copy-done.4, f32[64,384]{1,0:T(8,128)S(1)} %add.143.dist, f32[8,384]{1,0:T(8,128)S(1)} %broadcast_in_dim.7.mask, f32[64,128]{1,0:T(8,128)S(1)} %broadcast_in_dim.8.scale, bf16[256,256]{1,0:T(8,128)(2,1)S(1)} %fusion.1.perm, bf16[320,4096]{1,0:T(8,128)(2,1)S(1)} %copy-done), custom_call_target="tpu_custom_call" | custom-call | flops 671088640 | bytes 5242880 | tf_op jit(solution)/shard_map/compose/pallas_call | solution.py:170
  74.7 30.9 %all_to_all.5.parts = bf16[8,32,4224]{2,1,0:T(8,128)(2,1)S(1)} all-to-all(bf16[8,32,4224]{2,1,0:T(8,128)(2,1)S(1)} %bitcast.10), channel_id=1, replica_groups=mesh['z'=8,'xl'=2,'co'=2,'y'=4,'xh'=2] {'y','xh'}, dimensions={0} | all-to-all | bytes 4325376 | tf_op jit(solution)/shard_map/all_to_all | solution.py:181
  (50 shorter events, 4.9 us)
Async XLA Ops:
  0.0 38.6 %copy-start = (bf16[320,4096]{1,0:T(8,128)(2,1)S(1)}, bf16[320,4096]{1,0:T(8,128)(2,1)}, u32[]{:S(2)}) copy-start(bf16[320,4096]{1,0:T(8,128)(2,1)} %block.1) | copy-start | bytes 7864324
  0.0 14.5 %collective-permute-start.2 = (bf16[64,4096]{1,0:T(8,128)(2,1)}, bf16[64,4096]{1,0:T(8,128)(2,1)S(1)}, u32[]{:S(2)}, u32[]{:S(2)}) collective-permute-start(bf16[64,4096]{1,0:T(8,128)(2,1)} %bitcast.11), channel_id=1, source_target_pairs={{0,6},{2,0},{4,2},{6,4},{1,7},{3,1},{5,3},{7,5},{8,14},{10,8},{12,... | collective-permute-start | bytes 1572872 | tf_op jit(solution)/shard_map/ppermute | solution.py:33
  3.0 15.2 %collective-permute-start.1 = (bf16[64,4096]{1,0:T(8,128)(2,1)}, bf16[64,4096]{1,0:T(8,128)(2,1)S(1)}, u32[]{:S(2)}, u32[]{:S(2)}) collective-permute-start(bf16[64,4096]{1,0:T(8,128)(2,1)} %bitcast.12), channel_id=1, source_target_pairs={{0,2},{2,4},{4,6},{6,0},{1,3},{3,5},{5,7},{7,1},{8,10},{10,12},{12... | collective-permute-start | bytes 1572872 | tf_op jit(solution)/shard_map/ppermute | solution.py:32
  3.0 16.0 %collective-permute-start = (bf16[64,4096]{1,0:T(8,128)(2,1)}, bf16[64,4096]{1,0:T(8,128)(2,1)}, u32[]{:S(2)}, u32[]{:S(2)}) collective-permute-start(bf16[64,4096]{1,0:T(8,128)(2,1)} %bitcast.13), channel_id=1, source_target_pairs={{0,1},{1,0},{2,3},{3,2},{4,5},{5,4},{6,7},{7,6},{8,9},{9,8},{10,11... | collective-permute-start | bytes 1572872 | tf_op jit(solution)/shard_map/ppermute | solution.py:31
  14.5 10.3 %collective-permute-start.6 = (bf16[32,4096]{1,0:T(8,128)(2,1)S(1)}, bf16[32,4096]{1,0:T(8,128)(2,1)S(1)}, u32[]{:S(2)}, u32[]{:S(2)}) collective-permute-start(bf16[32,4096]{1,0:T(8,128)(2,1)S(1)} %slice.58), channel_id=1, source_target_pairs={{0,6},{2,0},{4,2},{6,4},{1,7},{3,1},{5,3},{7,5},{8,14},{10,8},{12,... | collective-permute-start | bytes 786440 | tf_op jit(solution)/shard_map/ppermute | solution.py:35
  18.2 0.8 copy-start.1
  19.0 10.6 %collective-permute-start.5 = (bf16[32,4096]{1,0:T(8,128)(2,1)S(1)}, bf16[32,4096]{1,0:T(8,128)(2,1)}, u32[]{:S(2)}, u32[]{:S(2)}) collective-permute-start(bf16[32,4096]{1,0:T(8,128)(2,1)S(1)} %slice.57), channel_id=1, source_target_pairs={{0,2},{2,4},{4,6},{6,0},{1,3},{3,5},{5,7},{7,1},{8,10},{10,12},{12... | collective-permute-start | bytes 786440 | tf_op jit(solution)/shard_map/ppermute | solution.py:34
  19.1 19.0 %collective-permute-start.4 = (bf16[64,4096]{1,0:T(8,128)(2,1)}, bf16[64,4096]{1,0:T(8,128)(2,1)}, u32[]{:S(2)}, u32[]{:S(2)}) collective-permute-start(bf16[64,4096]{1,0:T(8,128)(2,1)} %collective-permute-done.refs_1_), channel_id=1, source_target_pairs={{0,6},{2,0},{4,2},{6,4},{1,7},{3,1},{5,3},{7,5},{8,14},{10,8},{12,... | collective-permute-start | bytes 1572872 | tf_op jit(solution)/shard_map/ppermute | solution.py:37
  22.3 16.3 %collective-permute-start.3 = (bf16[64,4096]{1,0:T(8,128)(2,1)}, bf16[64,4096]{1,0:T(8,128)(2,1)}, u32[]{:S(2)}, u32[]{:S(2)}) collective-permute-start(bf16[64,4096]{1,0:T(8,128)(2,1)} %collective-permute-done.refs_1_), channel_id=1, source_target_pairs={{0,2},{2,4},{4,6},{6,0},{1,3},{3,5},{5,7},{7,1},{8,10},{10,12},{12... | collective-permute-start | bytes 1572872 | tf_op jit(solution)/shard_map/ppermute | solution.py:36
  24.8 10.5 %collective-permute-start.8 = (bf16[32,4096]{1,0:T(8,128)(2,1)S(1)}, bf16[32,4096]{1,0:T(8,128)(2,1)}, u32[]{:S(2)}, u32[]{:S(2)}) collective-permute-start(bf16[32,4096]{1,0:T(8,128)(2,1)S(1)} %collective-permute-done.6.refs_7_), channel_id=1, source_target_pairs={{0,1},{1,0},{2,3},{3,2},{4,5},{5,4},{6,7},{7,6},{8,9},{9,8},{10,11... | collective-permute-start | bytes 786440 | tf_op jit(solution)/shard_map/ppermute | solution.py:39
  29.6 8.5 %collective-permute-start.7 = (bf16[32,4096]{1,0:T(8,128)(2,1)}, bf16[32,4096]{1,0:T(8,128)(2,1)}, u32[]{:S(2)}, u32[]{:S(2)}) collective-permute-start(bf16[32,4096]{1,0:T(8,128)(2,1)} %collective-permute-done.5.refs_6_), channel_id=1, source_target_pairs={{0,1},{1,0},{2,3},{3,2},{4,5},{5,4},{6,7},{7,6},{8,9},{9,8},{10,11... | collective-permute-start | bytes 786440 | tf_op jit(solution)/shard_map/ppermute | solution.py:38
  38.6 1.0 copy-start.2
  39.6 1.0 copy-start.3
  40.7 20.3 %copy-start.6 = (f32[64]{0:T(128)S(1)}, f32[64]{0:T(128)}, u32[]{:S(2)}) copy-start(f32[64]{0:T(128)} %param.9) | copy-start | bytes 772
  40.7 29.0 %copy-start.5 = (s32[256]{0:T(256)S(1)}, s32[256]{0:T(256)}, u32[]{:S(2)}) copy-start(s32[256]{0:T(256)} %param.7) | copy-start | bytes 3076
  40.7 31.8 %copy-start.4 = (s32[4]{0:T(128)S(1)}, s32[4]{0:T(128)}, u32[]{:S(2)}) copy-start(s32[4]{0:T(128)} %leads.1) | copy-start | bytes 52
  46.5 1.4 %collective-permute-start.9 = (f32[64,384]{1,0:T(8,128)S(1)}, f32[64,384]{1,0:T(8,128)S(1)}, u32[]{:S(2)}, u32[]{:S(2)}) collective-permute-start(f32[64,384]{1,0:T(8,128)S(1)} %cross.1), channel_id=1, source_target_pairs={{0,8},{8,0},{1,9},{9,1},{2,10},{10,2},{3,11},{11,3},{4,12},{12,4},... | collective-permute-start | bytes 294920 | tf_op jit(solution)/shard_map/ppermute | solution.py:126
  47.9 4.9 %collective-permute-start.10 = (f32[64,384]{1,0:T(8,128)S(1)}, f32[64,384]{1,0:T(8,128)S(1)}, u32[]{:S(2)}, u32[]{:S(2)}) collective-permute-start(f32[64,384]{1,0:T(8,128)S(1)} %add.139), channel_id=1, source_target_pairs={{0,16},{16,0},{1,17},{17,1},{2,18},{18,2},{3,19},{19,3},{4,20},{20... | collective-permute-start | bytes 294920 | tf_op jit(solution)/shard_map/ppermute | solution.py:126
  52.9 4.7 %collective-permute-start.11 = (f32[64,384]{1,0:T(8,128)S(1)}, f32[64,384]{1,0:T(8,128)S(1)}, u32[]{:S(2)}, u32[]{:S(2)}) collective-permute-start(f32[64,384]{1,0:T(8,128)S(1)} %add.140), channel_id=1, source_target_pairs={{0,32},{32,0},{64,96},{96,64},{128,160},{160,128},{192,224},{224,1... | collective-permute-start | bytes 294920 | tf_op jit(solution)/shard_map/ppermute | solution.py:126
  57.6 6.1 %collective-permute-start.12 = (f32[64,384]{1,0:T(8,128)S(1)}, f32[64,384]{1,0:T(8,128)S(1)}, u32[]{:S(2)}, u32[]{:S(2)}) collective-permute-start(f32[64,384]{1,0:T(8,128)S(1)} %add.141), channel_id=1, source_target_pairs={{0,64},{32,96},{64,0},{96,32},{128,192},{160,224},{192,128},{224,1... | collective-permute-start | bytes 294920 | tf_op jit(solution)/shard_map/ppermute | solution.py:126
  63.7 8.7 %collective-permute-start.13 = (f32[64,384]{1,0:T(8,128)S(1)}, f32[64,384]{1,0:T(8,128)S(1)}, u32[]{:S(2)}, u32[]{:S(2)}) collective-permute-start(f32[64,384]{1,0:T(8,128)S(1)} %add.142), channel_id=1, source_target_pairs={{0,128},{32,160},{64,192},{96,224},{128,0},{160,32},{192,64},{224,... | collective-permute-start | bytes 294920 | tf_op jit(solution)/shard_map/ppermute | solution.py:126

commit v2 on v1

v2 whole, which is shorter than its diff:
```python
import functools
import math

import jax
import jax.numpy as jnp
from jax import lax
from jax.experimental import pallas as pl
from jax.experimental.pallas import tpu as pltpu
from jax.sharding import Mesh, PartitionSpec as P

F32 = jnp.float32
BF16 = jnp.bfloat16
LIB = ("y", "xh")
SPACE = ("z", "xl", "co")
FAR = 3.0e38
VM = pl.BlockSpec(memory_space=pltpu.VMEM)
SM = pl.BlockSpec(memory_space=pltpu.SMEM)
PARAMS = pltpu.CompilerParams(vmem_limit_bytes=16 * 1024 * 1024)
NEAR = ((0, 0), (0, 1), (3, 0), (1, 0))
AWAY = ((3, 1), (1, 1), (2, 0), (2, 1))


def flip(n, bit):
    return [(i, i ^ bit) for i in range(n)]


def turn(n, by):
    return [(i, (i + by) % n) for i in range(n)]


def gather_targets(own):
    half = own.shape[0] // 2
    across = lax.ppermute(own, "xh", flip(2, 1))
    below = lax.ppermute(own, "y", turn(4, 1))
    above = lax.ppermute(own, "y", turn(4, -1))
    far_a = lax.ppermute(below[:half], "y", turn(4, 1))
    far_b = lax.ppermute(above[half:], "y", turn(4, -1))
    below_x = lax.ppermute(across, "y", turn(4, 1))
    above_x = lax.ppermute(across, "y", turn(4, -1))
    far_xa = lax.ppermute(far_a, "xh", flip(2, 1))
    far_xb = lax.ppermute(far_b, "xh", flip(2, 1))
    return (own, across, below, above), (below_x, above_x, far_a, far_b, far_xa, far_xb)


def cross_rows(lags, pieces, block, lnorm, acc):
    rows, width = block.shape
    step = 512
    acc[...] = jnp.zeros_like(acc)

    def body(i, norms):
        cols = pl.ds(pl.multiple_of(i * step, step), step)
        lhs = jnp.concatenate([p[:, cols] for p in pieces], axis=0)
        acc[:, :rows] += lax.dot_general(
            lhs, block[:, cols], (((1,), (1,)), ((), ())), preferred_element_type=F32
        )
        wide = lhs.astype(F32)
        wide = wide * wide
        part = wide[:, :128]
        for c in range(128, step, 128):
            part = part + wide[:, c : c + 128]
        return norms + part

    norms = lax.fori_loop(0, width // step, body, jnp.zeros((acc.shape[0], 128), F32))
    norms = jnp.sum(norms, axis=1, keepdims=True)
    count = acc.shape[0] // 4 // lags
    values = []
    for r in range(4):
        cross = jnp.zeros((count, acc.shape[1]), F32)
        tnorm = jnp.zeros((count, 1), F32)
        for lag in range(lags):
            at = (r * lags + lag) * count
            here = acc[at : at + count, :]
            cross = cross + (pltpu.roll(here, lag, 1) if lag else here)
            tnorm = tnorm + norms[at : at + count]
        values.append(tnorm + lnorm[:1, :] - 2.0 * cross)
    return values


def near_kernel(lags, *refs):
    pieces, (block, lnorm, out, acc) = refs[:4], refs[4:]
    out[...] = jnp.concatenate(cross_rows(lags, pieces, block, lnorm, acc), axis=0)


def away_kernel(lags, place, *refs):
    pieces, (block, lnorm, near, out, acc) = refs[:6], refs[6:]
    values = cross_rows(lags, pieces, block, lnorm, acc)
    count = values[0].shape[0]
    for r, (dy, dx) in enumerate(NEAR + AWAY):
        owner = lax.rem(place[0] + dy, 4) * 2 + lax.rem(place[1] + dx, 2)
        value = near[r * count : (r + 1) * count, :] if r < 4 else values[r - 4]
        out[pl.ds(pl.multiple_of(owner * count, count), count), :] = value


def compose_kernel(leads, dist, dist_other, scale, perm, block, block_other, out):
    rows, width = block.shape
    targets = dist.shape[0]
    both = [-d[...] / scale[:, :1] for d in (dist, dist_other)]
    top = functools.reduce(jnp.maximum, [jnp.max(s, axis=1, keepdims=True) for s in both])
    top_hi = top.astype(BF16)
    top_lo = (top - top_hi.astype(F32)).astype(BF16)
    shift = top_hi.astype(F32) + top_lo.astype(F32)
    both = [jnp.exp(s - shift).astype(BF16).astype(F32) for s in both]
    total = sum(jnp.sum(w, axis=1, keepdims=True) for w in both)
    tot_hi = total.astype(BF16)
    tot_lo = (total - tot_hi.astype(F32)).astype(BF16)
    count = leads.shape[0]
    mixed = []
    for weights in both:
        stack = jnp.concatenate([pltpu.roll(weights, leads[k], 1) for k in range(count)], axis=0).astype(BF16)
        mixed.append(jnp.dot(perm[...], stack, preferred_element_type=F32).astype(BF16)[:, :rows])
    lane = lax.broadcasted_iota(jnp.int32, (targets, 128), 1)
    facts = jnp.where(
        lane == 0,
        top_hi.astype(F32),
        jnp.where(lane == 1, top_lo.astype(F32), jnp.where(lane == 2, tot_hi.astype(F32), tot_lo.astype(F32))),
    ).astype(BF16)
    facts = jnp.concatenate([facts] * count, axis=0)
    facts = jnp.dot(perm[...], facts, preferred_element_type=F32).astype(BF16)
    out[:, width : width + 128] = facts
    step = 512
    for c in range(0, width, step):
        value = jnp.dot(mixed[0], block[:, c : c + step], preferred_element_type=F32)
        value = value + jnp.dot(mixed[1], block_other[:, c : c + step], preferred_element_type=F32)
        out[:, c : c + step] = value.astype(BF16)


def combine_kernel(parts, out):
    n, rows, wide = parts.shape
    width = wide - 128
    count, lead_n, _ = out.shape
    facts = [parts[b, :, width:].astype(F32) for b in range(n)]
    tops = [f[:, 0:1] + f[:, 1:2] for f in facts]
    top = functools.reduce(jnp.maximum, tops)
    factors = [jnp.exp(t - top) for t in tops]
    total = 0.5 * sum(f * (x[:, 2:3] + x[:, 3:4]) for f, x in zip(factors, facts))
    factors = [f / total for f in factors]
    step = 512
    for h in range(2):
        mine = [b for b in range(n) if (b // 2) % 2 == h]
        for c in range(0, width, step):
            summed = sum(factors[b] * parts[b, :, c : c + step].astype(F32) for b in mine)
            summed = summed.reshape(count, lead_n, step).astype(BF16)
            out[:, :, h * width + c : h * width + c + step] = summed


def total_over_space(value):
    value = value + lax.ppermute(value, "co", flip(2, 1))
    value = value + lax.ppermute(value, "xl", flip(2, 1))
    down = lax.ppermute(value, "z", turn(8, 1))
    up = lax.ppermute(value, "z", turn(8, -1))
    three, two = value + down + up, value + up
    high = lax.ppermute(three, "z", turn(8, -3))
    low = lax.ppermute(two, "z", turn(8, 3))
    return three + high + low


def per_device(targets, library, anchors, leads, spread):
    lags, count, width = targets.shape
    rows = library.shape[0]
    lead_n = leads.shape[0]
    n_lib = lax.axis_size(LIB)
    n_target = count * n_lib
    wide = -(-rows // 128) * 128
    scale = math.sqrt(lags * width * lax.axis_size(SPACE))
    half = width // 2

    near, away = gather_targets(targets.reshape(lags * count, width))

    y, xh = lax.axis_index("y"), lax.axis_index("xh")
    place = jnp.stack([y, xh]).astype(jnp.int32)
    norm = jnp.sum(jnp.square(library.astype(F32)), axis=1)
    norm = jnp.pad(norm, (0, wide - rows))
    lnorm = functools.reduce(jnp.add, [jnp.roll(norm, lag) for lag in range(lags)])
    lnorm = jnp.broadcast_to(lnorm[None, :], (8, wide))
    spots = lax.broadcasted_iota(jnp.int32, (wide, 1), 0)
    chosen = jnp.any(spots == anchors[None, :], axis=1)
    scales = jnp.broadcast_to((spread * scale)[:, None], (n_target, 128))
    row = lax.broadcasted_iota(jnp.int32, (lead_n * n_target, lead_n * n_target), 0)
    col = lax.broadcasted_iota(jnp.int32, (lead_n * n_target, lead_n * n_target), 1)
    perm = ((row % lead_n) * n_target + row // lead_n == col).astype(BF16)

    flops = lags * n_target * wide * width
    near_dist = pl.pallas_call(
        functools.partial(near_kernel, lags),
        out_shape=jax.ShapeDtypeStruct((n_target // 2, wide), F32),
        in_specs=[VM] * 6,
        out_specs=VM,
        scratch_shapes=[pltpu.VMEM((lags * n_target // 2, wide), F32)],
        compiler_params=PARAMS,
        cost_estimate=pl.CostEstimate(flops=flops, bytes_accessed=5 << 20, transcendentals=0),
        name="near",
    )(*near, library, lnorm)
    partial_dist = pl.pallas_call(
        functools.partial(away_kernel, lags),
        out_shape=jax.ShapeDtypeStruct((n_target, wide), F32),
        in_specs=[SM] + [VM] * 9,
        out_specs=VM,
        scratch_shapes=[pltpu.VMEM((lags * n_target // 2, wide), F32)],
        compiler_params=PARAMS,
        cost_estimate=pl.CostEstimate(flops=flops, bytes_accessed=5 << 20, transcendentals=0),
        name="away",
    )(place, *away, library, lnorm, near_dist)

    mine = lax.rem(y, 2) * half
    kept = lax.dynamic_slice_in_dim(library, mine, half, axis=1)
    given = lax.dynamic_slice_in_dim(library, half - mine, half, axis=1)
    given, partial_dist = lax.optimization_barrier((given, partial_dist))
    other = lax.ppermute(given, "y", flip(4, 1))

    dist = total_over_space(partial_dist)
    dist = jnp.where(chosen[None, :], dist, FAR)
    dist_other = lax.ppermute(dist, "y", flip(4, 1))

    parts = pl.pallas_call(
        compose_kernel,
        out_shape=jax.ShapeDtypeStruct((lead_n * n_target, half + 128), BF16),
        in_specs=[SM] + [VM] * 6,
        out_specs=VM,
        compiler_params=PARAMS,
        cost_estimate=pl.CostEstimate(flops=2 * lead_n * n_target * rows * width, bytes_accessed=5 << 20, transcendentals=n_target * wide),
        name="compose",
    )(leads, dist, dist_other, scales, perm, kept, other)

    parts = parts.reshape(n_lib, lead_n * count, half + 128)
    parts = lax.all_to_all(parts, LIB, 0, 0, tiled=True)

    return pl.pallas_call(
        combine_kernel,
        out_shape=jax.ShapeDtypeStruct((count, lead_n, width), BF16),
        in_specs=[VM],
        out_specs=VM,
        compiler_params=PARAMS,
        cost_estimate=pl.CostEstimate(flops=2 * n_target * lead_n * width, bytes_accessed=3 << 20, transcendentals=0),
        name="combine",
    )(parts)


def solution(mesh):
    fine = Mesh(mesh.devices.reshape(8, 2, 2, 4, 2), SPACE + LIB)
    placed = (P(None, LIB, SPACE), P(LIB, SPACE), P(LIB), P(), P())
    return jax.shard_map(per_device, mesh=fine, in_specs=placed, out_specs=P(LIB, None, SPACE), check_vma=False)
```

time: 108 us -> 101 us (0.935)
  blocking collectives: 30.9 us -> 21.7 us
  waiting for transfers between devices: 30.5 us -> 37 us
  starting transfers between devices: 30 us -> 26.4 us
  local copies, waits for them, and re-layouts: 3.93 us -> 1.43 us
  Pallas kernels: 8.67 us -> 10.8 us
    ppermute x1, waiting for transfers between devices: 0.01 us -> 9.22 us  [gather_targets(): below = lax.ppermute(own, 'y', turn(4, 1))]
    all_to_all x1, blocking collectives: 30.9 us -> 21.7 us  [per_device(): parts = lax.all_to_all(parts, LIB, 0, 0, tiled=True)]
    ppermute x5 -> x8, waiting for transfers between devices: 14.3 us -> 21.3 us  [the longest x1 6.11 us: total_over_space(): low = lax.ppermute(two, 'z', turn(8, 3))]
    ppermute x1, waiting for transfers between devices: 6.09 us -> 0.01 us  [gather_targets(): above = lax.ppermute(own, 'y', turn(4, -1))]
    unnamed x14 -> x10, local copies, waits for them, and re-layouts: 2.91 us -> 0.03 us
    ppermute x1, starting transfers between devices: 3.02 us -> 0.51 us  [gather_targets(): far_xa = lax.ppermute(far_a, 'xh', flip(2, 1))]
    pallas_call x2 -> x3, Pallas kernels: 6.46 us -> 8.58 us  [the longest x1 4.01 us: per_device(): pl.pallas_call(functools.partial(near_kernel, lags), out_shape=jax.ShapeD...]
    ppermute x1, waiting for transfers between devices: 2.81 us -> 1.02 us  [gather_targets(): far_xa = lax.ppermute(far_a, 'xh', flip(2, 1))]
  transfers between devices with their start and end apart: 14 -> 17, of which waited for: 11 -> 12; matrix products, arithmetic and copies ran while one was open for 3% -> 4% of each run, Pallas kernels for 0% -> 4%
where the time goes in v2:
time: 101 us
  waiting for transfers between devices  37 us (37%)
  starting transfers between devices  26.4 us (26%)
  blocking collectives  21.7 us (21%)
  Pallas kernels  10.8 us (11%)
  other arithmetic  3 us (3%)
  local copies, waits for them, and re-layouts  1.43 us (1%)
    all_to_all x1, blocking collectives, per_device(): parts = lax.all_to_all(parts, LIB, 0, 0, tiled=True)  21.7 us
    ppermute x1, waiting for transfers between devices, gather_targets(): below = lax.ppermute(own, 'y', turn(4, 1))  9.22 us
    ppermute x1, waiting for transfers between devices, total_over_space(): low = lax.ppermute(two, 'z', turn(8, 3))  6.11 us
    ppermute x1, starting transfers between devices, total_over_space(): high = lax.ppermute(three, 'z', turn(8, -3))  5.2 us
    ppermute x1, waiting for transfers between devices, total_over_space(): value = value + lax.ppermute(value, 'xl', flip(2, 1))  4.25 us
    pallas_call x1, Pallas kernels, per_device(): pl.pallas_call(functools.partial(near_kernel, lags), out_shape=jax.ShapeD...  4.01 us
    pallas_call x1, Pallas kernels, per_device(): pl.pallas_call(functools.partial(away_kernel, lags), out_shape=jax.ShapeD...  3.35 us
    ppermute x1, starting transfers between devices, gather_targets(): above_x = lax.ppermute(across, 'y', turn(4, -1))  3.23 us
  transfers between devices with their start and end apart: 17, of which 12 were waited for; matrix products, arithmetic and copies ran while one was open for 4% of the time, Pallas kernels for 4%

profile of v2, /device:TPU:32, one launch (start us, length us, event | category | flops | bytes accessed | tf_op | source)
XLA Modules:
  0.0 100.6 jit_solution(15847469740023917813)
XLA Ops:
  0.0 3.0 %collective-permute-start = (bf16[64,4096]{1,0:T(8,128)(2,1)}, bf16[64,4096]{1,0:T(8,128)(2,1)}, u32[]{:S(2)}, u32[]{:S(2)}) collective-permute-start(bf16[64,4096]{1,0:T(8,128)(2,1)} %bitcast.5), channel_id=1, source_target_pairs={{0,1},{1,0},{2,3},{3,2},{4,5},{5,4},{6,7},{7,6},{8,9},{9,8},{10,11... | collective-permute-start | bytes 1572872 | tf_op jit(solution)/shard_map/ppermute | solution.py:33
  3.0 1.6 %collective-permute-start.3 = (bf16[64,4096]{1,0:T(8,128)(2,1)}, bf16[64,4096]{1,0:T(8,128)(2,1)S(1)}, u32[]{:S(2)}, u32[]{:S(2)}) collective-permute-start(bf16[64,4096]{1,0:T(8,128)(2,1)} %bitcast.6), channel_id=1, source_target_pairs={{0,2},{2,4},{4,6},{6,0},{1,3},{3,5},{5,7},{7,1},{8,10},{10,12},{12... | collective-permute-start | bytes 1572872 | tf_op jit(solution)/shard_map/ppermute | solution.py:34
  4.6 1.7 %collective-permute-start.5 = (bf16[64,4096]{1,0:T(8,128)(2,1)}, bf16[64,4096]{1,0:T(8,128)(2,1)}, u32[]{:S(2)}, u32[]{:S(2)}) collective-permute-start(bf16[64,4096]{1,0:T(8,128)(2,1)} %bitcast.7), channel_id=1, source_target_pairs={{0,6},{2,0},{4,2},{6,4},{1,7},{3,1},{5,3},{7,5},{8,14},{10,8},{12,... | collective-permute-start | bytes 1572872 | tf_op jit(solution)/shard_map/ppermute | solution.py:35
  6.3 2.3 %multiply_reduce_fusion = f32[320]{0:T(512)S(1)} fusion(bf16[320,4096]{1,0:T(8,128)(2,1)} %refs_6_.1), kind=kLoop, calls=%fused_computation | loop fusion | flops 3931840 | bytes 2622720 | tf_op jit(solution)/shard_map/reduce_sum | solution.py:171
  8.7 9.2 %collective-permute-done.3.refs_2_ = bf16[64,4096]{1,0:T(8,128)(2,1)S(1)} collective-permute-done((bf16[64,4096]{1,0:T(8,128)(2,1)}, bf16[64,4096]{1,0:T(8,128)(2,1)S(1)}, u32[]{:S(2)}, u32[]{:S(2)}) %collective-permute-start.3) | collective-permute-done | bytes 524320 | tf_op jit(solution)/shard_map/ppermute | solution.py:34
  19.3 3.0 %collective-permute-start.6 = (bf16[32,4096]{1,0:T(8,128)(2,1)S(1)}, bf16[32,4096]{1,0:T(8,128)(2,1)S(1)}, u32[]{:S(2)}, u32[]{:S(2)}) collective-permute-start(bf16[32,4096]{1,0:T(8,128)(2,1)S(1)} %slice.58), channel_id=1, source_target_pairs={{0,6},{2,0},{4,2},{6,4},{1,7},{3,1},{5,3},{7,5},{8,14},{10,8},{12,... | collective-permute-start | bytes 786440 | tf_op jit(solution)/shard_map/ppermute | solution.py:37
  22.3 3.2 %collective-permute-start.2 = (bf16[64,4096]{1,0:T(8,128)(2,1)}, bf16[64,4096]{1,0:T(8,128)(2,1)S(1)}, u32[]{:S(2)}, u32[]{:S(2)}) collective-permute-start(bf16[64,4096]{1,0:T(8,128)(2,1)} %collective-permute-done.refs_1_), channel_id=1, source_target_pairs={{0,6},{2,0},{4,2},{6,4},{1,7},{3,1},{5,3},{7,5},{8,14},{10,8},{12,... | collective-permute-start | bytes 1572872 | tf_op jit(solution)/shard_map/ppermute | solution.py:39
  25.9 1.9 %collective-permute-done.4.refs_2_ = bf16[32,4096]{1,0:T(8,128)(2,1)S(1)} collective-permute-done((bf16[32,4096]{1,0:T(8,128)(2,1)S(1)}, bf16[32,4096]{1,0:T(8,128)(2,1)S(1)}, u32[]{:S(2)}, u32[]{:S(2)}) %collective-permute-start.4) | collective-permute-done | bytes 262176 | tf_op jit(solution)/shard_map/ppermute | solution.py:36
  29.1 2.2 %collective-permute-start.8 = (bf16[32,4096]{1,0:T(8,128)(2,1)S(1)}, bf16[32,4096]{1,0:T(8,128)(2,1)S(1)}, u32[]{:S(2)}, u32[]{:S(2)}) collective-permute-start(bf16[32,4096]{1,0:T(8,128)(2,1)S(1)} %collective-permute-done.6.refs_3_), channel_id=1, source_target_pairs={{0,1},{1,0},{2,3},{3,2},{4,5},{5,4},{6,7},{7,6},{8,9},{9,8},{10,11... | collective-permute-start | bytes 786440 | tf_op jit(solution)/shard_map/ppermute | solution.py:41
  31.5 4.0 %near.1.refs_8_ = f32[32,384]{1,0:T(8,128)S(1)} custom-call(bf16[64,4096]{1,0:T(8,128)(2,1)S(1)} %bitcast.8, bf16[64,4096]{1,0:T(8,128)(2,1)} %collective-permute-done.refs_1_, bf16[64,4096]{1,0:T(8,128)(2,1)S(1)} %collective-permute-done.3.refs_2_, bf16[64,4096]{1,0:T(8,128)(2,1)} %collective-permute-done.5.refs_3_, bf16[320,4096]{1,0:T(8,128)(2,1)S(1)} %copy-done, ...), custom_call_target="tpu_custom_call" | custom-call | flops 805306368 | bytes 5242880 | tf_op jit(solution)/shard_map/near/pallas_call | solution.py:183
  36.5 2.8 %collective-permute-done.8.refs_5_ = bf16[32,4096]{1,0:T(8,128)(2,1)S(1)} collective-permute-done((bf16[32,4096]{1,0:T(8,128)(2,1)S(1)}, bf16[32,4096]{1,0:T(8,128)(2,1)S(1)}, u32[]{:S(2)}, u32[]{:S(2)}) %collective-permute-start.8) | collective-permute-done | bytes 262176 | tf_op jit(solution)/shard_map/ppermute | solution.py:41
  39.4 3.4 %away.1 = f32[64,384]{1,0:T(8,128)S(1)} custom-call(s32[2]{0:T(128)S(1)} %pad_add_fusion.1.place, bf16[64,4096]{1,0:T(8,128)(2,1)S(1)} %collective-permute-done.1.refs_0_, bf16[64,4096]{1,0:T(8,128)(2,1)S(1)} %collective-permute-done.2.refs_1_, bf16[32,4096]{1,0:T(8,128)(2,1)S(1)} %collective-permute-done.4.refs_2_, ...), custom_call_target="tpu_custom_call" | custom-call | flops 805306368 | bytes 5242880 | tf_op jit(solution)/shard_map/away/pallas_call | solution.py:193
  43.0 1.3 %collective-permute-done.9 = f32[64,384]{1,0:T(8,128)S(1)} collective-permute-done((f32[64,384]{1,0:T(8,128)S(1)}, f32[64,384]{1,0:T(8,128)S(1)}, u32[]{:S(2)}, u32[]{:S(2)}) %collective-permute-start.9) | collective-permute-done | bytes 98336 | tf_op jit(solution)/shard_map/ppermute | solution.py:147
  44.9 4.3 %collective-permute-done.10 = f32[64,384]{1,0:T(8,128)S(1)} collective-permute-done((f32[64,384]{1,0:T(8,128)S(1)}, f32[64,384]{1,0:T(8,128)S(1)}, u32[]{:S(2)}, u32[]{:S(2)}) %collective-permute-start.10) | collective-permute-done | bytes 98336 | tf_op jit(solution)/shard_map/ppermute | solution.py:148
  49.2 2.0 %collective-permute-start.11 = (f32[64,384]{1,0:T(8,128)S(1)}, f32[64,384]{1,0:T(8,128)S(1)}, u32[]{:S(2)}, u32[]{:S(2)}) collective-permute-start(f32[64,384]{1,0:T(8,128)S(1)} %add.86), channel_id=1, source_target_pairs={{0,32},{32,64},{64,96},{96,128},{128,160},{160,192},{192,224},{224... | collective-permute-start | bytes 294920 | tf_op jit(solution)/shard_map/ppermute | solution.py:149
  51.6 2.3 %collective-permute-done.11 = f32[64,384]{1,0:T(8,128)S(1)} collective-permute-done((f32[64,384]{1,0:T(8,128)S(1)}, f32[64,384]{1,0:T(8,128)S(1)}, u32[]{:S(2)}, u32[]{:S(2)}) %collective-permute-start.11) | collective-permute-done | bytes 98336 | tf_op jit(solution)/shard_map/ppermute | solution.py:149
  53.9 1.9 %collective-permute-done.12 = f32[64,384]{1,0:T(8,128)S(1)} collective-permute-done((f32[64,384]{1,0:T(8,128)S(1)}, f32[64,384]{1,0:T(8,128)S(1)}, u32[]{:S(2)}, u32[]{:S(2)}) %collective-permute-start.12) | collective-permute-done | bytes 98336 | tf_op jit(solution)/shard_map/ppermute | solution.py:150
  55.9 5.2 %collective-permute-start.13 = (f32[64,384]{1,0:T(8,128)S(1)}, f32[64,384]{1,0:T(8,128)S(1)}, u32[]{:S(2)}, u32[]{:S(2)}) collective-permute-start(f32[64,384]{1,0:T(8,128)S(1)} %get-tuple-element.11), channel_id=1, source_target_pairs={{0,160},{32,192},{64,224},{96,0},{128,32},{160,64},{192,96},{224,1... | collective-permute-start | bytes 294920 | tf_op jit(solution)/shard_map/ppermute | solution.py:152
  61.8 2.7 %collective-permute-done.13 = f32[64,384]{1,0:T(8,128)S(1)} collective-permute-done((f32[64,384]{1,0:T(8,128)S(1)}, f32[64,384]{1,0:T(8,128)S(1)}, u32[]{:S(2)}, u32[]{:S(2)}) %collective-permute-start.13) | collective-permute-done | bytes 98336 | tf_op jit(solution)/shard_map/ppermute | solution.py:152
  64.5 6.1 %collective-permute-done.14 = f32[64,384]{1,0:T(8,128)S(1)} collective-permute-done((f32[64,384]{1,0:T(8,128)S(1)}, f32[64,384]{1,0:T(8,128)S(1)}, u32[]{:S(2)}, u32[]{:S(2)}) %collective-permute-start.14) | collective-permute-done | bytes 98336 | tf_op jit(solution)/shard_map/ppermute | solution.py:153
  70.7 2.0 %collective-permute-start.15 = (f32[64,384]{1,0:T(8,128)S(1)}, f32[64,384]{1,0:T(8,128)S(1)}, u32[]{:S(2)}, u32[]{:S(2)}) collective-permute-start(f32[64,384]{1,0:T(8,128)S(1)} %add_select_fusion.dist), channel_id=1, source_target_pairs={{0,2},{2,0},{4,6},{6,4},{1,3},{3,1},{5,7},{7,5},{8,10},{10,8},{12,... | collective-permute-start | bytes 294920 | tf_op jit(solution)/shard_map/ppermute | solution.py:212
  72.7 2.7 %collective-permute-done.15.dist_other = f32[64,384]{1,0:T(8,128)S(1)} collective-permute-done((f32[64,384]{1,0:T(8,128)S(1)}, f32[64,384]{1,0:T(8,128)S(1)}, u32[]{:S(2)}, u32[]{:S(2)}) %collective-permute-start.15) | collective-permute-done | bytes 98336 | tf_op jit(solution)/shard_map/ppermute | solution.py:212
  75.4 2.3 %compose.1 = bf16[256,2176]{1,0:T(8,128)(2,1)S(1)} custom-call(s32[4]{0:T(128)S(1)} %copy-done.2, f32[64,384]{1,0:T(8,128)S(1)} %add_select_fusion.dist, f32[64,384]{1,0:T(8,128)S(1)} %collective-permute-done.15.dist_other, f32[64,128]{1,0:T(8,128)S(1)} %broadcast_in_dim.29.scale, bf16[256,256]{1,0:T(8,128)(2,1)S(1)} %fusion.1.perm, ...), custom_call_target="tpu_custom_call" | custom-call | flops 671088640 | bytes 5242880 | tf_op jit(solution)/shard_map/compose/pallas_call | solution.py:214
  77.7 21.7 %all_to_all.5.parts = bf16[8,32,2176]{2,1,0:T(8,128)(2,1)S(1)} all-to-all(bf16[8,32,2176]{2,1,0:T(8,128)(2,1)S(1)} %bitcast.4), channel_id=1, replica_groups=mesh['z'=8,'xl'=2,'co'=2,'y'=4,'xh'=2] {'y','xh'}, dimensions={0} | all-to-all | bytes 2228224 | tf_op jit(solution)/shard_map/all_to_all | solution.py:225
  (50 shorter events, 7.6 us)
Async XLA Ops:
  0.0 25.6 %copy-start = (bf16[320,4096]{1,0:T(8,128)(2,1)S(1)}, bf16[320,4096]{1,0:T(8,128)(2,1)}, u32[]{:S(2)}) copy-start(bf16[320,4096]{1,0:T(8,128)(2,1)} %refs_6_.1) | copy-start | bytes 7864324
  0.0 22.3 %collective-permute-start = (bf16[64,4096]{1,0:T(8,128)(2,1)}, bf16[64,4096]{1,0:T(8,128)(2,1)}, u32[]{:S(2)}, u32[]{:S(2)}) collective-permute-start(bf16[64,4096]{1,0:T(8,128)(2,1)} %bitcast.5), channel_id=1, source_target_pairs={{0,1},{1,0},{2,3},{3,2},{4,5},{5,4},{6,7},{7,6},{8,9},{9,8},{10,11... | collective-permute-start | bytes 1572872 | tf_op jit(solution)/shard_map/ppermute | solution.py:33
  3.0 14.9 %collective-permute-start.3 = (bf16[64,4096]{1,0:T(8,128)(2,1)}, bf16[64,4096]{1,0:T(8,128)(2,1)S(1)}, u32[]{:S(2)}, u32[]{:S(2)}) collective-permute-start(bf16[64,4096]{1,0:T(8,128)(2,1)} %bitcast.6), channel_id=1, source_target_pairs={{0,2},{2,4},{4,6},{6,0},{1,3},{3,5},{5,7},{7,1},{8,10},{10,12},{12... | collective-permute-start | bytes 1572872 | tf_op jit(solution)/shard_map/ppermute | solution.py:34
  4.6 13.7 %collective-permute-start.5 = (bf16[64,4096]{1,0:T(8,128)(2,1)}, bf16[64,4096]{1,0:T(8,128)(2,1)}, u32[]{:S(2)}, u32[]{:S(2)}) collective-permute-start(bf16[64,4096]{1,0:T(8,128)(2,1)} %bitcast.7), channel_id=1, source_target_pairs={{0,6},{2,0},{4,2},{6,4},{1,7},{3,1},{5,3},{7,5},{8,14},{10,8},{12,... | collective-permute-start | bytes 1572872 | tf_op jit(solution)/shard_map/ppermute | solution.py:35
  17.9 9.8 %collective-permute-start.4 = (bf16[32,4096]{1,0:T(8,128)(2,1)S(1)}, bf16[32,4096]{1,0:T(8,128)(2,1)S(1)}, u32[]{:S(2)}, u32[]{:S(2)}) collective-permute-start(bf16[32,4096]{1,0:T(8,128)(2,1)S(1)} %slice.57), channel_id=1, source_target_pairs={{0,2},{2,4},{4,6},{6,0},{1,3},{3,5},{5,7},{7,1},{8,10},{10,12},{12... | collective-permute-start | bytes 786440 | tf_op jit(solution)/shard_map/ppermute | solution.py:36
  19.3 12.2 %copy-start.1 = (bf16[8,8,4096]{2,1,0:T(8,128)(2,1)S(1)}, bf16[8,8,4096]{2,1,0:T(8,128)(2,1)}, u32[]{:S(2)}) copy-start(bf16[8,8,4096]{2,1,0:T(8,128)(2,1)} %param.5) | copy-start | bytes 1572868
  19.3 9.8 %collective-permute-start.6 = (bf16[32,4096]{1,0:T(8,128)(2,1)S(1)}, bf16[32,4096]{1,0:T(8,128)(2,1)S(1)}, u32[]{:S(2)}, u32[]{:S(2)}) collective-permute-start(bf16[32,4096]{1,0:T(8,128)(2,1)S(1)} %slice.58), channel_id=1, source_target_pairs={{0,6},{2,0},{4,2},{6,4},{1,7},{3,1},{5,3},{7,5},{8,14},{10,8},{12,... | collective-permute-start | bytes 786440 | tf_op jit(solution)/shard_map/ppermute | solution.py:37
  22.3 17.0 %collective-permute-start.1 = (bf16[64,4096]{1,0:T(8,128)(2,1)}, bf16[64,4096]{1,0:T(8,128)(2,1)S(1)}, u32[]{:S(2)}, u32[]{:S(2)}) collective-permute-start(bf16[64,4096]{1,0:T(8,128)(2,1)} %collective-permute-done.refs_1_), channel_id=1, source_target_pairs={{0,2},{2,4},{4,6},{6,0},{1,3},{3,5},{5,7},{7,1},{8,10},{10,12},{12... | collective-permute-start | bytes 1572872 | tf_op jit(solution)/shard_map/ppermute | solution.py:38
  22.3 17.0 %collective-permute-start.2 = (bf16[64,4096]{1,0:T(8,128)(2,1)}, bf16[64,4096]{1,0:T(8,128)(2,1)S(1)}, u32[]{:S(2)}, u32[]{:S(2)}) collective-permute-start(bf16[64,4096]{1,0:T(8,128)(2,1)} %collective-permute-done.refs_1_), channel_id=1, source_target_pairs={{0,6},{2,0},{4,2},{6,4},{1,7},{3,1},{5,3},{7,5},{8,14},{10,8},{12,... | collective-permute-start | bytes 1572872 | tf_op jit(solution)/shard_map/ppermute | solution.py:39
  27.8 8.8 %collective-permute-start.7 = (bf16[32,4096]{1,0:T(8,128)(2,1)S(1)}, bf16[32,4096]{1,0:T(8,128)(2,1)S(1)}, u32[]{:S(2)}, u32[]{:S(2)}) collective-permute-start(bf16[32,4096]{1,0:T(8,128)(2,1)S(1)} %collective-permute-done.4.refs_2_), channel_id=1, source_target_pairs={{0,1},{1,0},{2,3},{3,2},{4,5},{5,4},{6,7},{7,6},{8,9},{9,8},{10,11... | collective-permute-start | bytes 786440 | tf_op jit(solution)/shard_map/ppermute | solution.py:40
  29.1 10.3 %collective-permute-start.8 = (bf16[32,4096]{1,0:T(8,128)(2,1)S(1)}, bf16[32,4096]{1,0:T(8,128)(2,1)S(1)}, u32[]{:S(2)}, u32[]{:S(2)}) collective-permute-start(bf16[32,4096]{1,0:T(8,128)(2,1)S(1)} %collective-permute-done.6.refs_3_), channel_id=1, source_target_pairs={{0,1},{1,0},{2,3},{3,2},{4,5},{5,4},{6,7},{7,6},{8,9},{9,8},{10,11... | collective-permute-start | bytes 786440 | tf_op jit(solution)/shard_map/ppermute | solution.py:41
  35.5 26.1 %copy-start.3 = (s32[256]{0:T(256)S(1)}, s32[256]{0:T(256)}, u32[]{:S(2)}) copy-start(s32[256]{0:T(256)} %param.7) | copy-start | bytes 3076
  42.7 30.0 %copy-start.4 = (f32[64]{0:T(128)S(1)}, f32[64]{0:T(128)}, u32[]{:S(2)}) copy-start(f32[64]{0:T(128)} %param.9) | copy-start | bytes 772
  42.7 32.7 %copy-start.2 = (s32[4]{0:T(128)S(1)}, s32[4]{0:T(128)}, u32[]{:S(2)}) copy-start(s32[4]{0:T(128)} %leads.1) | copy-start | bytes 52
  42.7 32.6 %collective-permute-start.16 = (bf16[320,2048]{1,0:T(8,128)(2,1)S(1)}, bf16[320,2048]{1,0:T(8,128)(2,1)S(1)}, u32[]{:S(2)}, u32[]{:S(2)}) collective-permute-start(bf16[320,2048]{1,0:T(8,128)(2,1)S(1)} %get-tuple-element.8), channel_id=1, source_target_pairs={{0,2},{2,0},{4,6},{6,4},{1,3},{3,1},{5,7},{7,5},{8,10},{10,8},{12,... | collective-permute-start | bytes 3932168 | tf_op jit(solution)/shard_map/ppermute | solution.py:208
  42.9 1.4 %collective-permute-start.9 = (f32[64,384]{1,0:T(8,128)S(1)}, f32[64,384]{1,0:T(8,128)S(1)}, u32[]{:S(2)}, u32[]{:S(2)}) collective-permute-start(f32[64,384]{1,0:T(8,128)S(1)} %away.1), channel_id=1, source_target_pairs={{0,8},{8,0},{1,9},{9,1},{2,10},{10,2},{3,11},{11,3},{4,12},{12,4},... | collective-permute-start | bytes 294920 | tf_op jit(solution)/shard_map/ppermute | solution.py:147
  44.3 4.9 %collective-permute-start.10 = (f32[64,384]{1,0:T(8,128)S(1)}, f32[64,384]{1,0:T(8,128)S(1)}, u32[]{:S(2)}, u32[]{:S(2)}) collective-permute-start(f32[64,384]{1,0:T(8,128)S(1)} %add.85), channel_id=1, source_target_pairs={{0,16},{16,0},{1,17},{17,1},{2,18},{18,2},{3,19},{19,3},{4,20},{20... | collective-permute-start | bytes 294920 | tf_op jit(solution)/shard_map/ppermute | solution.py:148
  49.2 4.7 %collective-permute-start.11 = (f32[64,384]{1,0:T(8,128)S(1)}, f32[64,384]{1,0:T(8,128)S(1)}, u32[]{:S(2)}, u32[]{:S(2)}) collective-permute-start(f32[64,384]{1,0:T(8,128)S(1)} %add.86), channel_id=1, source_target_pairs={{0,32},{32,64},{64,96},{96,128},{128,160},{160,192},{192,224},{224... | collective-permute-start | bytes 294920 | tf_op jit(solution)/shard_map/ppermute | solution.py:149
  51.2 4.6 %collective-permute-start.12 = (f32[64,384]{1,0:T(8,128)S(1)}, f32[64,384]{1,0:T(8,128)S(1)}, u32[]{:S(2)}, u32[]{:S(2)}) collective-permute-start(f32[64,384]{1,0:T(8,128)S(1)} %add.86), channel_id=1, source_target_pairs={{0,224},{32,0},{64,32},{96,64},{128,96},{160,128},{192,160},{224,1... | collective-permute-start | bytes 294920 | tf_op jit(solution)/shard_map/ppermute | solution.py:150
  55.9 8.7 %collective-permute-start.13 = (f32[64,384]{1,0:T(8,128)S(1)}, f32[64,384]{1,0:T(8,128)S(1)}, u32[]{:S(2)}, u32[]{:S(2)}) collective-permute-start(f32[64,384]{1,0:T(8,128)S(1)} %get-tuple-element.11), channel_id=1, source_target_pairs={{0,160},{32,192},{64,224},{96,0},{128,32},{160,64},{192,96},{224,1... | collective-permute-start | bytes 294920 | tf_op jit(solution)/shard_map/ppermute | solution.py:152
  61.1 9.6 %collective-permute-start.14 = (f32[64,384]{1,0:T(8,128)S(1)}, f32[64,384]{1,0:T(8,128)S(1)}, u32[]{:S(2)}, u32[]{:S(2)}) collective-permute-start(f32[64,384]{1,0:T(8,128)S(1)} %get-tuple-element.12), channel_id=1, source_target_pairs={{0,96},{32,128},{64,160},{96,192},{128,224},{160,0},{192,32},{224,... | collective-permute-start | bytes 294920 | tf_op jit(solution)/shard_map/ppermute | solution.py:153
  70.7 4.7 %collective-permute-start.15 = (f32[64,384]{1,0:T(8,128)S(1)}, f32[64,384]{1,0:T(8,128)S(1)}, u32[]{:S(2)}, u32[]{:S(2)}) collective-permute-start(f32[64,384]{1,0:T(8,128)S(1)} %add_select_fusion.dist), channel_id=1, source_target_pairs={{0,2},{2,0},{4,6},{6,4},{1,3},{3,1},{5,7},{7,5},{8,10},{10,8},{12,... | collective-permute-start | bytes 294920 | tf_op jit(solution)/shard_map/ppermute | solution.py:212

commit v3 on v2

v3 whole, which is shorter than its diff:
```python
import functools
import math

import jax
import jax.numpy as jnp
from jax import lax
from jax.experimental import pallas as pl
from jax.experimental.pallas import tpu as pltpu
from jax.sharding import Mesh, PartitionSpec as P

F32 = jnp.float32
BF16 = jnp.bfloat16
Y = ("yh", "yl")
LIB = ("yh", "yl", "xh")
SPACE = ("z", "xl", "co")
CHIPS = ("xl", "co")
VM = pl.BlockSpec(memory_space=pltpu.VMEM)
SM = pl.BlockSpec(memory_space=pltpu.SMEM)
PARAMS = pltpu.CompilerParams(vmem_limit_bytes=16 * 1024 * 1024)
NEAR = ((0, 0), (0, 1), (3, 0), (1, 0))
AWAY = ((3, 1), (1, 1), (2, 0), (2, 1))


def flip(n, bit):
    return [(i, i ^ bit) for i in range(n)]


def turn(n, by):
    return [(i, (i + by) % n) for i in range(n)]


def gather_targets(own):
    half = own.shape[0] // 2
    across = lax.ppermute(own, "xh", flip(2, 1))
    below = lax.ppermute(own, Y, turn(4, 1))
    above = lax.ppermute(own, Y, turn(4, -1))
    far_a = lax.ppermute(below[:half], Y, turn(4, 1))
    far_b = lax.ppermute(above[half:], Y, turn(4, -1))
    below_x = lax.ppermute(across, Y, turn(4, 1))
    above_x = lax.ppermute(across, Y, turn(4, -1))
    far_xa = lax.ppermute(far_a, "xh", flip(2, 1))
    far_xb = lax.ppermute(far_b, "xh", flip(2, 1))
    return (own, across, below, above), (below_x, above_x, far_a, far_b, far_xa, far_xb)


def cross_rows(lags, pieces, block, lnorm, acc):
    rows, width = block.shape
    acc[...] = jnp.zeros_like(acc)
    lhs = jnp.concatenate([p[...] for p in pieces], axis=0)
    acc[:, :rows] = lax.dot_general(lhs, block[...], (((1,), (1,)), ((), ())), preferred_element_type=F32)
    norms = jnp.zeros((acc.shape[0], 128), F32)
    for c in range(0, width, 128):
        part = lhs[:, c : c + 128].astype(F32)
        norms = norms + part * part
    norms = jnp.sum(norms, axis=1, keepdims=True)
    count = acc.shape[0] // 4 // lags
    values = []
    for r in range(4):
        cross = jnp.zeros((count, acc.shape[1]), F32)
        tnorm = jnp.zeros((count, 1), F32)
        for lag in range(lags):
            at = (r * lags + lag) * count
            here = acc[at : at + count, :]
            cross = cross + (pltpu.roll(here, lag, 1) if lag else here)
            tnorm = tnorm + norms[at : at + count]
        values.append(tnorm + lnorm[:1, :] - 2.0 * cross)
    return values


def near_kernel(lags, *refs):
    pieces, (block, lnorm, out, acc) = refs[:4], refs[4:]
    out[...] = jnp.concatenate(cross_rows(lags, pieces, block, lnorm, acc), axis=0)


def away_kernel(lags, place, *refs):
    pieces, (block, lnorm, near, picks, out, acc) = refs[:6], refs[6:]
    values = cross_rows(lags, pieces, block, lnorm, acc)
    count = values[0].shape[0]
    value = jnp.concatenate([near[...]] + values, axis=0)
    first = value.astype(BF16)
    rest = value - first.astype(F32)
    second = rest.astype(BF16)
    third = (rest - second.astype(F32)).astype(BF16)
    picked = [jnp.dot(part, picks[...], preferred_element_type=F32) for part in (first, second, third)]
    value = picked[0] + picked[1] + picked[2]
    for r, (dy, dx) in enumerate(NEAR + AWAY):
        owner = lax.rem(place[0] + dy, 4) * 2 + lax.rem(place[1] + dx, 2)
        out[pl.ds(pl.multiple_of(owner * count, count), count), :] = value[r * count : (r + 1) * count, :]


def weights_kernel(dist, scale, spots, out):
    summed = dist[0]
    for i in range(1, dist.shape[0]):
        summed = summed + dist[i]
    scores = -summed / scale[:, :1]
    top = jnp.max(scores, axis=1, keepdims=True)
    top_hi = top.astype(BF16)
    top_lo = (top - top_hi.astype(F32)).astype(BF16)
    shift = top_hi.astype(F32) + top_lo.astype(F32)
    weights = jnp.exp(scores - shift).astype(BF16)
    weights = jnp.dot(weights, spots[...], preferred_element_type=F32).astype(BF16)
    lane = lax.broadcasted_iota(jnp.int32, (weights.shape[0], 128), 1)
    facts = jnp.where(lane == 0, top_hi.astype(F32), top_lo.astype(F32)).astype(BF16)
    weights = jnp.concatenate([weights, facts], axis=1)
    for i in range(out.shape[0]):
        out[i] = weights


def compose_kernel(leads, place, given, perm, block, block_other, out):
    rows, width = block.shape
    sides = given.shape[0] // 2
    mine = lax.rem(place[0], 2)
    both = [
        jnp.concatenate([given[2 * i + at].astype(F32) for i in range(sides)], axis=0) for at in (mine, 1 - mine)
    ]
    wide = both[0].shape[1] - 128
    tops = [w[:, wide : wide + 1] + w[:, wide + 1 : wide + 2] for w in both]
    larger = tops[0] >= tops[1]
    top = jnp.where(larger, tops[0], tops[1])
    top_hi = jnp.where(larger, both[0][:, wide : wide + 1], both[1][:, wide : wide + 1])
    top_lo = jnp.where(larger, both[0][:, wide + 1 : wide + 2], both[1][:, wide + 1 : wide + 2])
    both = [(w[:, :wide] * jnp.exp(t - top)).astype(BF16).astype(F32) for w, t in zip(both, tops)]
    total = jnp.sum(both[0] + both[1], axis=1, keepdims=True)
    tot_hi = total.astype(BF16).astype(F32)
    tot_lo = total - tot_hi
    count = leads.shape[0]
    mixed = []
    for weights in both:
        stack = jnp.concatenate([pltpu.roll(weights, leads[k], 1) for k in range(count)], axis=0).astype(BF16)
        mixed.append(jnp.dot(perm[...], stack, preferred_element_type=F32).astype(BF16)[:, :rows])
    lane = lax.broadcasted_iota(jnp.int32, (total.shape[0], 128), 1)
    facts = jnp.where(lane == 0, top_hi, jnp.where(lane == 1, top_lo, jnp.where(lane == 2, tot_hi, tot_lo)))
    facts = jnp.concatenate([facts.astype(BF16)] * count, axis=0)
    facts = jnp.dot(perm[...], facts, preferred_element_type=F32).astype(BF16)
    out[:, width : width + 128] = facts
    step = 512
    for c in range(0, width, step):
        value = jnp.dot(mixed[0], block[:, c : c + step], preferred_element_type=F32)
        value = value + jnp.dot(mixed[1], block_other[:, c : c + step], preferred_element_type=F32)
        out[:, c : c + step] = value.astype(BF16)


def combine_kernel(parts, out):
    n, rows, wide = parts.shape
    width = wide - 128
    count, lead_n, _ = out.shape
    facts = [parts[b, :, width:].astype(F32) for b in range(n)]
    tops = [f[:, 0:1] + f[:, 1:2] for f in facts]
    top = functools.reduce(jnp.maximum, tops)
    factors = [jnp.exp(t - top) for t in tops]
    total = 0.5 * sum(f * (x[:, 2:3] + x[:, 3:4]) for f, x in zip(factors, facts))
    factors = [f / total for f in factors]
    step = 512
    for h in range(2):
        mine = [b for b in range(n) if (b // 2) % 2 == h]
        for c in range(0, width, step):
            summed = sum(factors[b] * parts[b, :, c : c + step].astype(F32) for b in mine)
            summed = summed.reshape(count, lead_n, step).astype(BF16)
            out[:, :, h * width + c : h * width + c + step] = summed


def per_device(targets, library, anchors, leads, spread):
    lags, count, width = targets.shape
    rows = library.shape[0]
    lead_n = leads.shape[0]
    n_lib = lax.axis_size(LIB)
    n_target = count * n_lib
    wide = -(-rows // 128) * 128
    scale = math.sqrt(lags * width * lax.axis_size(SPACE))
    half = width // 2

    near, away = gather_targets(targets.reshape(lags * count, width))

    y, xh = lax.axis_index(Y), lax.axis_index("xh")
    place = jnp.stack([y, xh]).astype(jnp.int32)
    norm = jnp.sum(jnp.square(library.astype(F32)), axis=1)
    norm = jnp.pad(norm, (0, wide - rows))
    lnorm = functools.reduce(jnp.add, [jnp.roll(norm, lag) for lag in range(lags)])
    lnorm = jnp.broadcast_to(lnorm[None, :], (8, wide))
    spots = lax.broadcasted_iota(jnp.int32, (anchors.shape[0], wide), 1)
    spots = (spots == anchors[:, None]).astype(BF16)
    picks = lax.broadcasted_iota(jnp.int32, (wide, anchors.shape[0]), 0)
    picks = (picks == anchors[None, :]).astype(BF16)
    group = lax.axis_size(CHIPS)
    few = n_target // group
    scales = lax.dynamic_slice_in_dim(spread, lax.axis_index(CHIPS) * few, few) * scale
    scales = jnp.broadcast_to(scales[:, None], (few, 128))
    row = lax.broadcasted_iota(jnp.int32, (lead_n * n_target, lead_n * n_target), 0)
    col = lax.broadcasted_iota(jnp.int32, (lead_n * n_target, lead_n * n_target), 1)
    perm = ((row % lead_n) * n_target + row // lead_n == col).astype(BF16)

    flops = lags * n_target * wide * width
    near_dist = pl.pallas_call(
        functools.partial(near_kernel, lags),
        out_shape=jax.ShapeDtypeStruct((n_target // 2, wide), F32),
        in_specs=[VM] * 6,
        out_specs=VM,
        scratch_shapes=[pltpu.VMEM((lags * n_target // 2, wide), F32)],
        compiler_params=PARAMS,
        cost_estimate=pl.CostEstimate(flops=flops, bytes_accessed=5 << 20, transcendentals=0),
        name="near",
    )(*near, library, lnorm)
    partial_dist = pl.pallas_call(
        functools.partial(away_kernel, lags),
        out_shape=jax.ShapeDtypeStruct((n_target, anchors.shape[0]), F32),
        in_specs=[SM] + [VM] * 10,
        out_specs=VM,
        scratch_shapes=[pltpu.VMEM((lags * n_target // 2, wide), F32)],
        compiler_params=PARAMS,
        cost_estimate=pl.CostEstimate(flops=flops, bytes_accessed=5 << 20, transcendentals=0),
        name="away",
    )(place, *away, library, lnorm, near_dist, picks)

    mine = lax.rem(y, 2) * half
    kept = lax.dynamic_slice_in_dim(library, mine, half, axis=1)
    given = lax.dynamic_slice_in_dim(library, half - mine, half, axis=1)
    given, partial_dist = lax.optimization_barrier((given, partial_dist))
    other = lax.ppermute(given, Y, flip(4, 1))

    dist = partial_dist.reshape(group, few, anchors.shape[0])
    dist = jnp.sum(lax.all_to_all(dist, CHIPS, 0, 0, tiled=True), axis=0)
    dist = jnp.broadcast_to(dist[None], (lax.axis_size("z"),) + dist.shape)
    dist = lax.all_to_all(dist, "z", 0, 0, tiled=True)

    weights = pl.pallas_call(
        weights_kernel,
        out_shape=jax.ShapeDtypeStruct((2 * group, few, wide + 128), BF16),
        in_specs=[VM] * 3,
        out_specs=VM,
        compiler_params=PARAMS,
        cost_estimate=pl.CostEstimate(flops=2 * few * wide * 256, bytes_accessed=1 << 20, transcendentals=few * 256),
        name="weights",
    )(dist, scales, spots)
    weights = lax.all_to_all(weights, CHIPS + ("yl",), 0, 0, tiled=True)

    parts = pl.pallas_call(
        compose_kernel,
        out_shape=jax.ShapeDtypeStruct((lead_n * n_target, half + 128), BF16),
        in_specs=[SM] * 2 + [VM] * 4,
        out_specs=VM,
        compiler_params=PARAMS,
        cost_estimate=pl.CostEstimate(flops=2 * lead_n * n_target * rows * width, bytes_accessed=5 << 20, transcendentals=n_target * wide),
        name="compose",
    )(leads, place, weights, perm, kept, other)

    parts = parts.reshape(n_lib, lead_n * count, half + 128)
    parts = lax.all_to_all(parts, LIB, 0, 0, tiled=True)

    return pl.pallas_call(
        combine_kernel,
        out_shape=jax.ShapeDtypeStruct((count, lead_n, width), BF16),
        in_specs=[VM],
        out_specs=VM,
        compiler_params=PARAMS,
        cost_estimate=pl.CostEstimate(flops=2 * n_target * lead_n * width, bytes_accessed=3 << 20, transcendentals=0),
        name="combine",
    )(parts)


def solution(mesh):
    fine = Mesh(mesh.devices.reshape(8, 2, 2, 2, 2, 2), SPACE + LIB)
    placed = (P(None, LIB, SPACE), P(LIB, SPACE), P(LIB), P(), P())
    return jax.shard_map(per_device, mesh=fine, in_specs=placed, out_specs=P(LIB, None, SPACE), check_vma=False)
```

time: 101 us -> 104 us (1.030); the launches traced: 101 us -> 103 us
  starting transfers between devices: 26.4 us -> 31 us
  waiting for transfers between devices: 37 us -> 32.8 us
  local copies, waits for them, and re-layouts: 1.43 us -> 3.45 us
    ppermute x14 -> x7, waiting for transfers between devices: 33.2 us -> 10.4 us  [the longest x1 9.08 us: gather_targets(): below = lax.ppermute(own, Y, turn(4, 1))]
    all_to_all x0 -> x3, waiting for transfers between devices: none -> 16.2 us  [the longest x1 7.53 us: per_device(): dist = lax.all_to_all(dist, 'z', 0, 0, tiled=True)]
    all_to_all x0 -> x3, starting transfers between devices: none -> 15.4 us  [the longest x1 8.57 us: per_device(): dist = lax.all_to_all(dist, 'z', 0, 0, tiled=True)]
    ppermute x14 -> x7, starting transfers between devices: 20.6 us -> 9.87 us  [the longest x1 3.23 us: gather_targets(): above_x = lax.ppermute(across, Y, turn(4, -1))]
    ppermute x1, waiting for transfers between devices: 1.02 us -> 3.42 us  [gather_targets(): far_xa = lax.ppermute(far_a, 'xh', flip(2, 1))]
    pallas_call x1, Pallas kernels: 4.01 us -> 2.59 us  [per_device(): pl.pallas_call(functools.partial(near_kernel, lags), out_shape=jax.ShapeD...]
    dynamic_slice x1, local copies, waits for them, and re-layouts: 0.31 us -> 1.67 us  [per_device(): kept = lax.dynamic_slice_in_dim(library, mine, half, axis=1)]
  transfers between devices with their start and end apart: 17 -> 13, of which waited for: 12 -> 8; matrix products, arithmetic and copies ran while one was open for 4% -> 6% of each run, Pallas kernels for 4% -> 3%
where the time goes in v3:
time: 104 us; the launch traced here: 103 us
  waiting for transfers between devices  32.8 us (32%)
  starting transfers between devices  31 us (30%)
  blocking collectives  22.2 us (21%)
  Pallas kernels  9.84 us (9%)
  local copies, waits for them, and re-layouts  3.45 us (3%)
  other arithmetic  3.02 us (3%)
    all_to_all x1, blocking collectives, per_device(): parts = lax.all_to_all(parts, LIB, 0, 0, tiled=True)  22.2 us
    ppermute x1, waiting for transfers between devices, gather_targets(): below = lax.ppermute(own, Y, turn(4, 1))  9.08 us
    all_to_all x1, starting transfers between devices, per_device(): dist = lax.all_to_all(dist, 'z', 0, 0, tiled=True)  8.57 us
    all_to_all x1, waiting for transfers between devices, per_device(): dist = lax.all_to_all(dist, 'z', 0, 0, tiled=True)  7.53 us
    all_to_all x1, waiting for transfers between devices, per_device(): weights = lax.all_to_all(weights, CHIPS + ('yl',), 0, 0, tiled=True)  4.59 us
    all_to_all x1, waiting for transfers between devices, per_device(): dist = jnp.sum(lax.all_to_all(dist, CHIPS, 0, 0, tiled=True), axis=0)  4.07 us
    all_to_all x1, starting transfers between devices, per_device(): dist = jnp.sum(lax.all_to_all(dist, CHIPS, 0, 0, tiled=True), axis=0)  3.43 us
    ppermute x1, waiting for transfers between devices, gather_targets(): far_xa = lax.ppermute(far_a, 'xh', flip(2, 1))  3.42 us
  transfers between devices with their start and end apart: 13, of which 8 were waited for; matrix products, arithmetic and copies ran while one was open for 6% of the time, Pallas kernels for 3%

profile of v3, /device:TPU:32, one launch (start us, length us, event | category | flops | bytes accessed | tf_op | source)
XLA Modules:
  0.0 102.5 jit_solution(17975055064588747047)
XLA Ops:
  0.0 3.0 %collective-permute-start = (bf16[64,4096]{1,0:T(8,128)(2,1)}, bf16[64,4096]{1,0:T(8,128)(2,1)}, u32[]{:S(2)}, u32[]{:S(2)}) collective-permute-start(bf16[64,4096]{1,0:T(8,128)(2,1)} %bitcast.6), channel_id=1, source_target_pairs={{0,1},{1,0},{2,3},{3,2},{4,5},{5,4},{6,7},{7,6},{8,9},{9,8},{10,11... | collective-permute-start | bytes 1572872 | tf_op jit(solution)/shard_map/ppermute | solution.py:34
  3.0 1.6 %collective-permute-start.3 = (bf16[64,4096]{1,0:T(8,128)(2,1)}, bf16[64,4096]{1,0:T(8,128)(2,1)S(1)}, u32[]{:S(2)}, u32[]{:S(2)}) collective-permute-start(bf16[64,4096]{1,0:T(8,128)(2,1)} %bitcast.7), channel_id=1, source_target_pairs={{0,2},{2,4},{4,6},{6,0},{1,3},{3,5},{5,7},{7,1},{8,10},{10,12},{12... | collective-permute-start | bytes 1572872 | tf_op jit(solution)/shard_map/ppermute | solution.py:35
  4.6 1.7 %collective-permute-start.5 = (bf16[64,4096]{1,0:T(8,128)(2,1)}, bf16[64,4096]{1,0:T(8,128)(2,1)}, u32[]{:S(2)}, u32[]{:S(2)}) collective-permute-start(bf16[64,4096]{1,0:T(8,128)(2,1)} %bitcast.8), channel_id=1, source_target_pairs={{0,6},{2,0},{4,2},{6,4},{1,7},{3,1},{5,3},{7,5},{8,14},{10,8},{12,... | collective-permute-start | bytes 1572872 | tf_op jit(solution)/shard_map/ppermute | solution.py:36
  6.3 2.3 %multiply_reduce_fusion = f32[320]{0:T(512)S(1)} fusion(bf16[320,4096]{1,0:T(8,128)(2,1)} %refs_6_.1), kind=kLoop, calls=%fused_computation | loop fusion | flops 3931840 | bytes 2622720 | tf_op jit(solution)/shard_map/reduce_sum | solution.py:176
  8.8 9.1 %collective-permute-done.3.refs_2_ = bf16[64,4096]{1,0:T(8,128)(2,1)S(1)} collective-permute-done((bf16[64,4096]{1,0:T(8,128)(2,1)}, bf16[64,4096]{1,0:T(8,128)(2,1)S(1)}, u32[]{:S(2)}, u32[]{:S(2)}) %collective-permute-start.3) | collective-permute-done | bytes 524320 | tf_op jit(solution)/shard_map/ppermute | solution.py:35
  18.3 1.0 slice.58
  19.3 3.0 %collective-permute-start.6 = (bf16[32,4096]{1,0:T(8,128)(2,1)S(1)}, bf16[32,4096]{1,0:T(8,128)(2,1)S(1)}, u32[]{:S(2)}, u32[]{:S(2)}) collective-permute-start(bf16[32,4096]{1,0:T(8,128)(2,1)S(1)} %slice.58), channel_id=1, source_target_pairs={{0,6},{2,0},{4,2},{6,4},{1,7},{3,1},{5,3},{7,5},{8,14},{10,8},{12,... | collective-permute-start | bytes 786440 | tf_op jit(solution)/shard_map/ppermute | solution.py:38
  22.3 3.2 %collective-permute-start.2 = (bf16[64,4096]{1,0:T(8,128)(2,1)}, bf16[64,4096]{1,0:T(8,128)(2,1)S(1)}, u32[]{:S(2)}, u32[]{:S(2)}) collective-permute-start(bf16[64,4096]{1,0:T(8,128)(2,1)} %collective-permute-done.refs_1_), channel_id=1, source_target_pairs={{0,6},{2,0},{4,2},{6,4},{1,7},{3,1},{5,3},{7,5},{8,14},{10,8},{12,... | collective-permute-start | bytes 1572872 | tf_op jit(solution)/shard_map/ppermute | solution.py:40
  25.6 1.7 %constant_dynamic-slice_fusion = (bf16[320,2048]{1,0:T(8,128)(2,1)}, bf16[320,2048]{1,0:T(8,128)(2,1)}) fusion(bf16[320,4096]{1,0:T(8,128)(2,1)S(1)} %copy-done, s32[]{:T(128)S(6)} %select_n.25, s32[]{:T(128)S(6)} %select_n.21), kind=kLoop, calls=%fused_computation.18 | loop fusion | bytes 5242888 | tf_op jit(solution)/shard_map/dynamic_slice | solution.py:215
  29.1 2.2 %collective-permute-start.8 = (bf16[32,4096]{1,0:T(8,128)(2,1)S(1)}, bf16[32,4096]{1,0:T(8,128)(2,1)S(1)}, u32[]{:S(2)}, u32[]{:S(2)}) collective-permute-start(bf16[32,4096]{1,0:T(8,128)(2,1)S(1)} %collective-permute-done.6.refs_3_), channel_id=1, source_target_pairs={{0,1},{1,0},{2,3},{3,2},{4,5},{5,4},{6,7},{7,6},{8,9},{9,8},{10,11... | collective-permute-start | bytes 786440 | tf_op jit(solution)/shard_map/ppermute | solution.py:42
  31.4 2.6 %near.1.refs_8_ = f32[32,384]{1,0:T(8,128)S(1)} custom-call(bf16[64,4096]{1,0:T(8,128)(2,1)S(1)} %bitcast.9, bf16[64,4096]{1,0:T(8,128)(2,1)} %collective-permute-done.refs_1_, bf16[64,4096]{1,0:T(8,128)(2,1)S(1)} %collective-permute-done.3.refs_2_, bf16[64,4096]{1,0:T(8,128)(2,1)} %collective-permute-done.5.refs_3_, bf16[320,4096]{1,0:T(8,128)(2,1)S(1)} %copy-done, ...), custom_call_target="tpu_custom_call" | custom-call | flops 805306368 | bytes 5242880 | tf_op jit(solution)/shard_map/near/pallas_call | solution.py:193
  34.0 3.4 %collective-permute-done.7.refs_4_ = bf16[32,4096]{1,0:T(8,128)(2,1)S(1)} collective-permute-done((bf16[32,4096]{1,0:T(8,128)(2,1)S(1)}, bf16[32,4096]{1,0:T(8,128)(2,1)S(1)}, u32[]{:S(2)}, u32[]{:S(2)}) %collective-permute-start.7) | collective-permute-done | bytes 262176 | tf_op jit(solution)/shard_map/ppermute | solution.py:41
  37.4 2.8 %collective-permute-done.8.refs_5_ = bf16[32,4096]{1,0:T(8,128)(2,1)S(1)} collective-permute-done((bf16[32,4096]{1,0:T(8,128)(2,1)S(1)}, bf16[32,4096]{1,0:T(8,128)(2,1)S(1)}, u32[]{:S(2)}, u32[]{:S(2)}) %collective-permute-start.8) | collective-permute-done | bytes 262176 | tf_op jit(solution)/shard_map/ppermute | solution.py:42
  40.2 2.8 %away.1 = f32[64,256]{1,0:T(8,128)} custom-call(s32[2]{0:T(128)S(1)} %pad_add_fusion.1.place, bf16[64,4096]{1,0:T(8,128)(2,1)S(1)} %collective-permute-done.1.refs_0_, bf16[64,4096]{1,0:T(8,128)(2,1)S(1)} %collective-permute-done.2.refs_1_, bf16[32,4096]{1,0:T(8,128)(2,1)S(1)} %collective-permute-done.4.refs_2_, ...), custom_call_target="tpu_custom_call" | custom-call | flops 805306368 | bytes 5242880 | tf_op jit(solution)/shard_map/away/pallas_call | solution.py:203
  43.1 3.4 %all-to-all-start = ((f32[4,16,256]{2,1,0:T(8,128)}), f32[4,16,256]{2,1,0:T(8,128)S(1)}, u32[]{:S(2)}, u32[]{:S(2)}) async-start(f32[4,16,256]{2,1,0:T(8,128)} %bitcast.3), calls=%async_computation | async-start | bytes 131072 | tf_op jit(solution)/shard_map/all_to_all | solution.py:221
  46.6 4.1 %all-to-all-done = f32[4,16,256]{2,1,0:T(8,128)S(1)} async-done(((f32[4,16,256]{2,1,0:T(8,128)}), f32[4,16,256]{2,1,0:T(8,128)S(1)}, u32[]{:S(2)}, u32[]{:S(2)}) %all-to-all-start) | async-done | bytes 65568 | tf_op jit(solution)/shard_map/all_to_all | solution.py:221
  51.3 8.6 %all-to-all-start.1 = ((f32[8,16,256]{2,1,0:T(8,128)}), f32[8,16,256]{2,1,0:T(8,128)S(1)}, u32[]{:S(2)}, u32[]{:S(2)}) async-start(f32[8,16,256]{2,1,0:T(8,128)} %broadcast_in_dim.7), calls=%async_computation.1 | async-start | bytes 262144 | tf_op jit(solution)/shard_map/all_to_all | solution.py:223
  60.1 7.5 %all-to-all-done.1.dist = f32[8,16,256]{2,1,0:T(8,128)S(1)} async-done(((f32[8,16,256]{2,1,0:T(8,128)}), f32[8,16,256]{2,1,0:T(8,128)S(1)}, u32[]{:S(2)}, u32[]{:S(2)}) %all-to-all-start.1) | async-done | bytes 131104 | tf_op jit(solution)/shard_map/all_to_all | solution.py:223
  67.7 1.0 weights.1
  68.6 3.4 %all-to-all-start.2 = ((bf16[8,16,512]{2,1,0:T(8,128)(2,1)}), bf16[8,16,512]{2,1,0:T(8,128)(2,1)S(1)}, u32[]{:S(2)}, u32[]{:S(2)}) async-start(bf16[8,16,512]{2,1,0:T(8,128)(2,1)} %weights.1), calls=%async_computation.2 | async-start | bytes 262144 | tf_op jit(solution)/shard_map/all_to_all | solution.py:234
  72.3 4.6 %all-to-all-done.2.given = bf16[8,16,512]{2,1,0:T(8,128)(2,1)S(1)} async-done(((bf16[8,16,512]{2,1,0:T(8,128)(2,1)}), bf16[8,16,512]{2,1,0:T(8,128)(2,1)S(1)}, u32[]{:S(2)}, u32[]{:S(2)}) %all-to-all-start.2) | async-done | bytes 131104 | tf_op jit(solution)/shard_map/all_to_all | solution.py:234
  76.9 2.2 %compose.1 = bf16[256,2176]{1,0:T(8,128)(2,1)S(1)} custom-call(s32[4]{0:T(128)S(1)} %copy-done.3, s32[2]{0:T(128)S(1)} %pad_add_fusion.1.place, bf16[8,16,512]{2,1,0:T(8,128)(2,1)S(1)} %all-to-all-done.2.given, bf16[256,256]{1,0:T(8,128)(2,1)S(1)} %fusion.2.perm, bf16[320,2048]{1,0:T(8,128)(2,1)S(1)} %copy-done.1, ...), custom_call_target="tpu_custom_call" | custom-call | flops 671088640 | bytes 5242880 | tf_op jit(solution)/shard_map/compose/pallas_call | solution.py:236
  79.1 22.2 %all_to_all.20.parts = bf16[8,32,2176]{2,1,0:T(8,128)(2,1)S(1)} all-to-all(bf16[8,32,2176]{2,1,0:T(8,128)(2,1)S(1)} %bitcast.5), channel_id=1, replica_groups=mesh['z'=8,'xl'=2,'co'=2,'yh'=2,'yl'=2,'xh'=2] {'yh','yl','xh'}, dimensions={0} | all-to-all | bytes 2228224 | tf_op jit(solution)/shard_map/all_to_all | solution.py:247
  101.3 1.2 %combine.1 = bf16[8,4,4096]{2,1,0:T(4,128)(2,1)} custom-call(bf16[8,32,2176]{2,1,0:T(8,128)(2,1)S(1)} %all_to_all.20.parts), custom_call_target="tpu_custom_call" | custom-call | flops 2097152 | bytes 3145728 | tf_op jit(solution)/shard_map/combine/pallas_call | solution.py:249
  (44 shorter events, 3.7 us)
Async XLA Ops:
  0.0 25.6 %copy-start = (bf16[320,4096]{1,0:T(8,128)(2,1)S(1)}, bf16[320,4096]{1,0:T(8,128)(2,1)}, u32[]{:S(2)}) copy-start(bf16[320,4096]{1,0:T(8,128)(2,1)} %refs_6_.1) | copy-start | bytes 7864324
  0.0 22.3 %collective-permute-start = (bf16[64,4096]{1,0:T(8,128)(2,1)}, bf16[64,4096]{1,0:T(8,128)(2,1)}, u32[]{:S(2)}, u32[]{:S(2)}) collective-permute-start(bf16[64,4096]{1,0:T(8,128)(2,1)} %bitcast.6), channel_id=1, source_target_pairs={{0,1},{1,0},{2,3},{3,2},{4,5},{5,4},{6,7},{7,6},{8,9},{9,8},{10,11... | collective-permute-start | bytes 1572872 | tf_op jit(solution)/shard_map/ppermute | solution.py:34
  3.0 14.9 %collective-permute-start.3 = (bf16[64,4096]{1,0:T(8,128)(2,1)}, bf16[64,4096]{1,0:T(8,128)(2,1)S(1)}, u32[]{:S(2)}, u32[]{:S(2)}) collective-permute-start(bf16[64,4096]{1,0:T(8,128)(2,1)} %bitcast.7), channel_id=1, source_target_pairs={{0,2},{2,4},{4,6},{6,0},{1,3},{3,5},{5,7},{7,1},{8,10},{10,12},{12... | collective-permute-start | bytes 1572872 | tf_op jit(solution)/shard_map/ppermute | solution.py:35
  4.6 13.7 %collective-permute-start.5 = (bf16[64,4096]{1,0:T(8,128)(2,1)}, bf16[64,4096]{1,0:T(8,128)(2,1)}, u32[]{:S(2)}, u32[]{:S(2)}) collective-permute-start(bf16[64,4096]{1,0:T(8,128)(2,1)} %bitcast.8), channel_id=1, source_target_pairs={{0,6},{2,0},{4,2},{6,4},{1,7},{3,1},{5,3},{7,5},{8,14},{10,8},{12,... | collective-permute-start | bytes 1572872 | tf_op jit(solution)/shard_map/ppermute | solution.py:36
  17.9 9.8 %collective-permute-start.4 = (bf16[32,4096]{1,0:T(8,128)(2,1)S(1)}, bf16[32,4096]{1,0:T(8,128)(2,1)S(1)}, u32[]{:S(2)}, u32[]{:S(2)}) collective-permute-start(bf16[32,4096]{1,0:T(8,128)(2,1)S(1)} %slice.57), channel_id=1, source_target_pairs={{0,2},{2,4},{4,6},{6,0},{1,3},{3,5},{5,7},{7,1},{8,10},{10,12},{12... | collective-permute-start | bytes 786440 | tf_op jit(solution)/shard_map/ppermute | solution.py:37
  19.3 12.0 %copy-start.4 = (s32[256]{0:T(256)S(1)}, s32[256]{0:T(256)}, u32[]{:S(2)}) copy-start(s32[256]{0:T(256)} %param.7) | copy-start | bytes 3076
  19.3 12.1 %copy-start.2 = (bf16[8,8,4096]{2,1,0:T(8,128)(2,1)S(1)}, bf16[8,8,4096]{2,1,0:T(8,128)(2,1)}, u32[]{:S(2)}) copy-start(bf16[8,8,4096]{2,1,0:T(8,128)(2,1)} %param.5) | copy-start | bytes 1572868
  19.3 9.8 %collective-permute-start.6 = (bf16[32,4096]{1,0:T(8,128)(2,1)S(1)}, bf16[32,4096]{1,0:T(8,128)(2,1)S(1)}, u32[]{:S(2)}, u32[]{:S(2)}) collective-permute-start(bf16[32,4096]{1,0:T(8,128)(2,1)S(1)} %slice.58), channel_id=1, source_target_pairs={{0,6},{2,0},{4,2},{6,4},{1,7},{3,1},{5,3},{7,5},{8,14},{10,8},{12,... | collective-permute-start | bytes 786440 | tf_op jit(solution)/shard_map/ppermute | solution.py:38
  22.3 17.9 %collective-permute-start.1 = (bf16[64,4096]{1,0:T(8,128)(2,1)}, bf16[64,4096]{1,0:T(8,128)(2,1)S(1)}, u32[]{:S(2)}, u32[]{:S(2)}) collective-permute-start(bf16[64,4096]{1,0:T(8,128)(2,1)} %collective-permute-done.refs_1_), channel_id=1, source_target_pairs={{0,2},{2,4},{4,6},{6,0},{1,3},{3,5},{5,7},{7,1},{8,10},{10,12},{12... | collective-permute-start | bytes 1572872 | tf_op jit(solution)/shard_map/ppermute | solution.py:39
  22.3 17.9 %collective-permute-start.2 = (bf16[64,4096]{1,0:T(8,128)(2,1)}, bf16[64,4096]{1,0:T(8,128)(2,1)S(1)}, u32[]{:S(2)}, u32[]{:S(2)}) collective-permute-start(bf16[64,4096]{1,0:T(8,128)(2,1)} %collective-permute-done.refs_1_), channel_id=1, source_target_pairs={{0,6},{2,0},{4,2},{6,4},{1,7},{3,1},{5,3},{7,5},{8,14},{10,8},{12,... | collective-permute-start | bytes 1572872 | tf_op jit(solution)/shard_map/ppermute | solution.py:40
  27.8 9.6 %collective-permute-start.7 = (bf16[32,4096]{1,0:T(8,128)(2,1)S(1)}, bf16[32,4096]{1,0:T(8,128)(2,1)S(1)}, u32[]{:S(2)}, u32[]{:S(2)}) collective-permute-start(bf16[32,4096]{1,0:T(8,128)(2,1)S(1)} %collective-permute-done.4.refs_2_), channel_id=1, source_target_pairs={{0,1},{1,0},{2,3},{3,2},{4,5},{5,4},{6,7},{7,6},{8,9},{9,8},{10,11... | collective-permute-start | bytes 786440 | tf_op jit(solution)/shard_map/ppermute | solution.py:41
  29.1 11.1 %collective-permute-start.8 = (bf16[32,4096]{1,0:T(8,128)(2,1)S(1)}, bf16[32,4096]{1,0:T(8,128)(2,1)S(1)}, u32[]{:S(2)}, u32[]{:S(2)}) collective-permute-start(bf16[32,4096]{1,0:T(8,128)(2,1)S(1)} %collective-permute-done.6.refs_3_), channel_id=1, source_target_pairs={{0,1},{1,0},{2,3},{3,2},{4,5},{5,4},{6,7},{7,6},{8,9},{9,8},{10,11... | collective-permute-start | bytes 786440 | tf_op jit(solution)/shard_map/ppermute | solution.py:42
  34.0 25.9 %copy-start.5 = (f32[64]{0:T(128)S(1)}, f32[64]{0:T(128)}, u32[]{:S(2)}) copy-start(f32[64]{0:T(128)} %param.9) | copy-start | bytes 772
  43.1 33.8 %copy-start.1 = (bf16[320,2048]{1,0:T(8,128)(2,1)S(1)}, bf16[320,2048]{1,0:T(8,128)(2,1)}, u32[]{:S(2)}) copy-start(bf16[320,2048]{1,0:T(8,128)(2,1)} %get-tuple-element.9.block) | copy-start | bytes 3932164
  43.1 33.8 %copy-start.3 = (s32[4]{0:T(128)S(1)}, s32[4]{0:T(128)}, u32[]{:S(2)}) copy-start(s32[4]{0:T(128)} %leads.1) | copy-start | bytes 52
  43.1 33.8 %collective-permute-start.9 = (bf16[320,2048]{1,0:T(8,128)(2,1)}, bf16[320,2048]{1,0:T(8,128)(2,1)S(1)}, u32[]{:S(2)}, u32[]{:S(2)}) collective-permute-start(bf16[320,2048]{1,0:T(8,128)(2,1)} %get-tuple-element.8), channel_id=1, source_target_pairs={{0,2},{2,0},{4,6},{6,4},{1,3},{3,1},{5,7},{7,5},{8,10},{10,8},{12,... | collective-permute-start | bytes 3932168 | tf_op jit(solution)/shard_map/ppermute | solution.py:218
  43.1 7.5 %all-to-all-start = ((f32[4,16,256]{2,1,0:T(8,128)}), f32[4,16,256]{2,1,0:T(8,128)S(1)}, u32[]{:S(2)}, u32[]{:S(2)}) async-start(f32[4,16,256]{2,1,0:T(8,128)} %bitcast.3), calls=%async_computation | async-start | bytes 131072 | tf_op jit(solution)/shard_map/all_to_all | solution.py:221
  51.3 16.3 %all-to-all-start.1 = ((f32[8,16,256]{2,1,0:T(8,128)}), f32[8,16,256]{2,1,0:T(8,128)S(1)}, u32[]{:S(2)}, u32[]{:S(2)}) async-start(f32[8,16,256]{2,1,0:T(8,128)} %broadcast_in_dim.7), calls=%async_computation.1 | async-start | bytes 262144 | tf_op jit(solution)/shard_map/all_to_all | solution.py:223
  68.6 8.3 %all-to-all-start.2 = ((bf16[8,16,512]{2,1,0:T(8,128)(2,1)}), bf16[8,16,512]{2,1,0:T(8,128)(2,1)S(1)}, u32[]{:S(2)}, u32[]{:S(2)}) async-start(bf16[8,16,512]{2,1,0:T(8,128)(2,1)} %weights.1), calls=%async_computation.2 | async-start | bytes 262144 | tf_op jit(solution)/shard_map/all_to_all | solution.py:234

commit v4 on v3

--- a/solution.py
+++ b/solution.py
@@ -13,7 +13,6 @@
 Y = ("yh", "yl")
 LIB = ("yh", "yl", "xh")
 SPACE = ("z", "xl", "co")
-CHIPS = ("xl", "co")
 VM = pl.BlockSpec(memory_space=pltpu.VMEM)
 SM = pl.BlockSpec(memory_space=pltpu.SMEM)
 PARAMS = pltpu.CompilerParams(vmem_limit_bytes=16 * 1024 * 1024)
@@ -89,74 +88,91 @@
 
 
 def weights_kernel(dist, scale, spots, out):
-    summed = dist[0]
-    for i in range(1, dist.shape[0]):
-        summed = summed + dist[i]
-    scores = -summed / scale[:, :1]
+    scores = -dist[...] / scale[:, :1]
     top = jnp.max(scores, axis=1, keepdims=True)
-    top_hi = top.astype(BF16)
-    top_lo = (top - top_hi.astype(F32)).astype(BF16)
-    shift = top_hi.astype(F32) + top_lo.astype(F32)
-    weights = jnp.exp(scores - shift).astype(BF16)
-    weights = jnp.dot(weights, spots[...], preferred_element_type=F32).astype(BF16)
-    lane = lax.broadcasted_iota(jnp.int32, (weights.shape[0], 128), 1)
-    facts = jnp.where(lane == 0, top_hi.astype(F32), top_lo.astype(F32)).astype(BF16)
-    weights = jnp.concatenate([weights, facts], axis=1)
-    for i in range(out.shape[0]):
-        out[i] = weights
-
-
-def compose_kernel(leads, place, given, perm, block, block_other, out):
-    rows, width = block.shape
-    sides = given.shape[0] // 2
-    mine = lax.rem(place[0], 2)
-    both = [
-        jnp.concatenate([given[2 * i + at].astype(F32) for i in range(sides)], axis=0) for at in (mine, 1 - mine)
-    ]
-    wide = both[0].shape[1] - 128
-    tops = [w[:, wide : wide + 1] + w[:, wide + 1 : wide + 2] for w in both]
-    larger = tops[0] >= tops[1]
-    top = jnp.where(larger, tops[0], tops[1])
-    top_hi = jnp.where(larger, both[0][:, wide : wide + 1], both[1][:, wide : wide + 1])
-    top_lo = jnp.where(larger, both[0][:, wide + 1 : wide + 2], both[1][:, wide + 1 : wide + 2])
-    both = [(w[:, :wide] * jnp.exp(t - top)).astype(BF16).astype(F32) for w, t in zip(both, tops)]
-    total = jnp.sum(both[0] + both[1], axis=1, keepdims=True)
-    tot_hi = total.astype(BF16).astype(F32)
-    tot_lo = total - tot_hi
+    top_hi, top_lo = halves(top)
+    weights = jnp.exp(scores - (top_hi + top_lo)).astype(BF16)
+    tot_hi, tot_lo = halves(jnp.sum(weights.astype(F32), axis=1, keepdims=True))
+    wide = spots.shape[1]
+    out[:, :wide] = jnp.dot(weights, spots[...], preferred_element_type=F32).astype(BF16)
+    out[:, wide:] = in_lanes((top_hi, top_lo, tot_hi, tot_lo)).astype(BF16)
+
+
+def halves(value):
+    first = value.astype(BF16).astype(F32)
+    return first, (value - first).astype(BF16).astype(F32)
+
+
+def in_lanes(columns):
+    lane = lax.broadcasted_iota(jnp.int32, (columns[0].shape[0], 128), 1)
+    value = columns[-1]
+    for i in range(len(columns) - 2, -1, -1):
+        value = jnp.where(lane == i, columns[i], value)
+    return value
+
+
+def compose_kernel(leads, place, own, up, down, perm, block, block_up, block_down, out):
+    rows, quarter = block_up.shape
+    targets, wide = own.shape[0], own.shape[1] - 128
     count = leads.shape[0]
-    mixed = []
-    for weights in both:
+    odd = lax.rem(place[0], 2)
+    mixed, facts = [], []
+    for w in (own, up, down):
+        weights = w[:, :wide].astype(F32)
         stack = jnp.concatenate([pltpu.roll(weights, leads[k], 1) for k in range(count)], axis=0).astype(BF16)
         mixed.append(jnp.dot(perm[...], stack, preferred_element_type=F32).astype(BF16)[:, :rows])
-    lane = lax.broadcasted_iota(jnp.int32, (total.shape[0], 128), 1)
-    facts = jnp.where(lane == 0, top_hi, jnp.where(lane == 1, top_lo, jnp.where(lane == 2, tot_hi, tot_lo)))
-    facts = jnp.concatenate([facts.astype(BF16)] * count, axis=0)
-    facts = jnp.dot(perm[...], facts, preferred_element_type=F32).astype(BF16)
-    out[:, width : width + 128] = facts
+        fact = jnp.concatenate([w[:, wide:]] * count, axis=0)
+        facts.append(jnp.dot(perm[...], fact, preferred_element_type=F32))
+    tops = [f[:, 0:1] + f[:, 1:2] for f in facts]
+    totals = [f[:, 2:3] + f[:, 3:4] for f in facts]
     step = 512
-    for c in range(0, width, step):
-        value = jnp.dot(mixed[0], block[:, c : c + step], preferred_element_type=F32)
-        value = value + jnp.dot(mixed[1], block_other[:, c : c + step], preferred_element_type=F32)
-        out[:, c : c + step] = value.astype(BF16)
+    columns = []
+    for side, (other, start) in enumerate(((block_up, 2 * odd), (block_down, 3 - 2 * odd))):
+        i = side + 1
+        larger = tops[0] >= tops[i]
+        top = jnp.where(larger, tops[0], tops[i])
+        first, second = jnp.exp(tops[0] - top), jnp.exp(tops[i] - top)
+        columns += [jnp.where(larger, facts[0][:, j : j + 1], facts[i][:, j : j + 1]) for j in range(2)]
+        columns += halves(first * totals[0] + second * totals[i])
+        for c in range(0, quarter, step):
+            mine = block[:, pl.ds(pl.multiple_of(start * quarter + c, step), step)]
+            value = first * jnp.dot(mixed[0], mine, preferred_element_type=F32)
+            value = value + second * jnp.dot(mixed[i], other[:, c : c + step], preferred_element_type=F32)
+            out[:, side * quarter + c : side * quarter + c + step] = value.astype(BF16)
+    out[:, 2 * quarter :] = in_lanes(columns).astype(BF16)
 
 
 def combine_kernel(parts, out):
     n, rows, wide = parts.shape
-    width = wide - 128
-    count, lead_n, _ = out.shape
-    facts = [parts[b, :, width:].astype(F32) for b in range(n)]
-    tops = [f[:, 0:1] + f[:, 1:2] for f in facts]
-    top = functools.reduce(jnp.maximum, tops)
-    factors = [jnp.exp(t - top) for t in tops]
-    total = 0.5 * sum(f * (x[:, 2:3] + x[:, 3:4]) for f, x in zip(factors, facts))
-    factors = [f / total for f in factors]
+    count, lead_n, width = out.shape
+    quarter = width // 4
+    facts = [parts[b, :, wide - 128 :].astype(F32) for b in range(n)]
     step = 512
-    for h in range(2):
-        mine = [b for b in range(n) if (b // 2) % 2 == h]
-        for c in range(0, width, step):
-            summed = sum(factors[b] * parts[b, :, c : c + step].astype(F32) for b in mine)
+    for q in range(4):
+        odd, side = ((0, 0), (1, 1), (1, 0), (0, 1))[q]
+        sources = [b for b in range(n) if (b // 2) % 2 == odd]
+        at = 4 * side
+        tops = [facts[b][:, at : at + 1] + facts[b][:, at + 1 : at + 2] for b in sources]
+        top = functools.reduce(jnp.maximum, tops)
+        factors = [jnp.exp(t - top) for t in tops]
+        total = sum(f * (facts[b][:, at + 2 : at + 3] + facts[b][:, at + 3 : at + 4]) for f, b in zip(factors, sources))
+        factors = [f / total for f in factors]
+        for c in range(0, quarter, step):
+            from_c = side * quarter + c
+            summed = sum(f * parts[b, :, from_c : from_c + step].astype(F32) for f, b in zip(factors, sources))
             summed = summed.reshape(count, lead_n, step).astype(BF16)
-            out[:, :, h * width + c : h * width + c + step] = summed
+            out[:, :, q * quarter + c : q * quarter + c + step] = summed
+
+
+def total_over_space(value):
+    value = value + lax.ppermute(value, "co", flip(2, 1))
+    value = value + lax.ppermute(value, "xl", flip(2, 1))
+    down = lax.ppermute(value, "z", turn(8, 1))
+    up = lax.ppermute(value, "z", turn(8, -1))
+    three, two = value + down + up, value + up
+    high = lax.ppermute(three, "z", turn(8, -3))
+    low = lax.ppermute(two, "z", turn(8, 3))
+    return three + high + low
 
 
 def per_device(targets, library, anchors, leads, spread):
@@ -167,7 +183,7 @@
     n_target = count * n_lib
     wide = -(-rows // 128) * 128
     scale = math.sqrt(lags * width * lax.axis_size(SPACE))
-    half = width // 2
+    quarter = width // 4
 
     near, away = gather_targets(targets.reshape(lags * count, width))
 
@@ -181,10 +197,7 @@
     spots = (spots == anchors[:, None]).astype(BF16)
     picks = lax.broadcasted_iota(jnp.int32, (wide, anchors.shape[0]), 0)
     picks = (picks == anchors[None, :]).astype(BF16)
-    group = lax.axis_size(CHIPS)
-    few = n_target // group
-    scales = lax.dynamic_slice_in_dim(spread, lax.axis_index(CHIPS) * few, few) * scale
-    scales = jnp.broadcast_to(scales[:, None], (few, 128))
+    scales = jnp.broadcast_to((spread * scale)[:, None], (n_target, 128))
     row = lax.broadcasted_iota(jnp.int32, (lead_n * n_target, lead_n * n_target), 0)
     col = lax.broadcasted_iota(jnp.int32, (lead_n * n_target, lead_n * n_target), 1)
     perm = ((row % lead_n) * n_target + row // lead_n == col).astype(BF16)
@@ -211,39 +224,37 @@
         name="away",
     )(place, *away, library, lnorm, near_dist, picks)
 
-    mine = lax.rem(y, 2) * half
-    kept = lax.dynamic_slice_in_dim(library, mine, half, axis=1)
-    given = lax.dynamic_slice_in_dim(library, half - mine, half, axis=1)
-    given, partial_dist = lax.optimization_barrier((given, partial_dist))
-    other = lax.ppermute(given, Y, flip(4, 1))
-
-    dist = partial_dist.reshape(group, few, anchors.shape[0])
-    dist = jnp.sum(lax.all_to_all(dist, CHIPS, 0, 0, tiled=True), axis=0)
-    dist = jnp.broadcast_to(dist[None], (lax.axis_size("z"),) + dist.shape)
-    dist = lax.all_to_all(dist, "z", 0, 0, tiled=True)
-
-    weights = pl.pallas_call(
+    odd = lax.rem(y, 2)
+    for_up = lax.dynamic_slice_in_dim(library, (1 + 2 * odd) * quarter, quarter, axis=1)
+    for_down = lax.dynamic_slice_in_dim(library, (2 - 2 * odd) * quarter, quarter, axis=1)
+    for_up, for_down, partial_dist = lax.optimization_barrier((for_up, for_down, partial_dist))
+    block_down = lax.ppermute(for_up, Y, turn(4, 1))
+    block_up = lax.ppermute(for_down, Y, turn(4, -1))
+
+    dist = total_over_space(partial_dist)
+    own = pl.pallas_call(
         weights_kernel,
-        out_shape=jax.ShapeDtypeStruct((2 * group, few, wide + 128), BF16),
+        out_shape=jax.ShapeDtypeStruct((n_target, wide + 128), BF16),
         in_specs=[VM] * 3,
         out_specs=VM,
         compiler_params=PARAMS,
-        cost_estimate=pl.CostEstimate(flops=2 * few * wide * 256, bytes_accessed=1 << 20, transcendentals=few * 256),
+        cost_estimate=pl.CostEstimate(flops=2 * n_target * wide * 256, bytes_accessed=1 << 20, transcendentals=n_target * 256),
         name="weights",
     )(dist, scales, spots)
-    weights = lax.all_to_all(weights, CHIPS + ("yl",), 0, 0, tiled=True)
+    down = lax.ppermute(own, Y, turn(4, 1))
+    up = lax.ppermute(own, Y, turn(4, -1))
 
     parts = pl.pallas_call(
         compose_kernel,
-        out_shape=jax.ShapeDtypeStruct((lead_n * n_target, half + 128), BF16),
-        in_specs=[SM] * 2 + [VM] * 4,
+        out_shape=jax.ShapeDtypeStruct((lead_n * n_target, 2 * quarter + 128), BF16),
+        in_specs=[SM] * 2 + [VM] * 7,
         out_specs=VM,
         compiler_params=PARAMS,
         cost_estimate=pl.CostEstimate(flops=2 * lead_n * n_target * rows * width, bytes_accessed=5 << 20, transcendentals=n_target * wide),
         name="compose",
-    )(leads, place, weights, perm, kept, other)
-
-    parts = parts.reshape(n_lib, lead_n * count, half + 128)
+    )(leads, place, own, up, down, perm, library, block_up, block_down)
+
+    parts = parts.reshape(n_lib, lead_n * count, 2 * quarter + 128)
     parts = lax.all_to_all(parts, LIB, 0, 0, tiled=True)
 
     return pl.pallas_call(

time: 104 us -> 97.8 us (0.940)
  blocking collectives: 22.2 us -> 16.9 us
  waiting for transfers between devices: 32.8 us -> 36.4 us
  starting transfers between devices: 31 us -> 27.7 us
    ppermute x1 -> x10, waiting for transfers between devices: 0.01 us -> 19.1 us  [the longest x1 4.99 us: total_over_space(): low = lax.ppermute(two, 'z', turn(8, 3))]
    all_to_all x3 -> x0, waiting for transfers between devices: 16.2 us -> none  [the longest x1 7.53 us: per_device(): dist = lax.all_to_all(dist, 'z', 0, 0, tiled=True)]
    all_to_all x3 -> x0, starting transfers between devices: 15.4 us -> none  [the longest x1 8.57 us: per_device(): dist = lax.all_to_all(dist, 'z', 0, 0, tiled=True)]
    ppermute x1 -> x10, starting transfers between devices: 0.01 us -> 13 us  [the longest x1 5.02 us: total_over_space(): high = lax.ppermute(three, 'z', turn(8, -3))]
    all_to_all x1, blocking collectives: 22.2 us -> 16.9 us  [per_device(): parts = lax.all_to_all(parts, LIB, 0, 0, tiled=True)]
    unnamed x12 -> x14, local copies, waits for them, and re-layouts: 0.03 us -> 1.88 us
    dynamic_slice x1, local copies, waits for them, and re-layouts: 1.67 us -> 0.11 us  [per_device(): lax.dynamic_slice_in_dim(library, (2 - 2 * odd) * quarter, quarter, axis=1)]
    ppermute x1, waiting for transfers between devices: 3.42 us -> 2.22 us  [gather_targets(): far_xa = lax.ppermute(far_a, 'xh', flip(2, 1))]
  transfers between devices with their start and end apart: 13 -> 19, of which waited for: 8 -> 12; matrix products, arithmetic and copies ran while one was open for 6% -> 5% of each run, Pallas kernels for 3% -> 3%
where the time goes in v4:
time: 97.8 us; the launch traced here: 97.2 us
  waiting for transfers between devices  36.4 us (37%)
  starting transfers between devices  27.7 us (28%)
  blocking collectives  16.9 us (17%)
  Pallas kernels  9.41 us (10%)
  local copies, waits for them, and re-layouts  3.54 us (4%)
  other arithmetic  2.98 us (3%)
    all_to_all x1, blocking collectives, per_device(): parts = lax.all_to_all(parts, LIB, 0, 0, tiled=True)  16.9 us
    ppermute x1, waiting for transfers between devices, gather_targets(): below = lax.ppermute(own, Y, turn(4, 1))  9.17 us
    ppermute x1, starting transfers between devices, total_over_space(): high = lax.ppermute(three, 'z', turn(8, -3))  5.02 us
    ppermute x1, waiting for transfers between devices, total_over_space(): low = lax.ppermute(two, 'z', turn(8, 3))  4.99 us
    ppermute x1, waiting for transfers between devices, total_over_space(): value = value + lax.ppermute(value, 'xl', flip(2, 1))  3.67 us
    ppermute x1, waiting for transfers between devices, per_device(): down = lax.ppermute(own, Y, turn(4, 1))  3.57 us
    ppermute x1, starting transfers between devices, gather_targets(): above_x = lax.ppermute(across, Y, turn(4, -1))  3.22 us
    pallas_call x1, Pallas kernels, per_device(): pl.pallas_call(functools.partial(away_kernel, lags), out_shape=jax.ShapeD...  3.17 us
  transfers between devices with their start and end apart: 19, of which 12 were waited for; matrix products, arithmetic and copies ran while one was open for 5% of the time, Pallas kernels for 3%

profile of v4, /device:TPU:32, one launch (start us, length us, event | category | flops | bytes accessed | tf_op | source)
XLA Modules:
  0.0 97.2 jit_solution(10611983408433036846)
XLA Ops:
  0.0 3.0 %collective-permute-start = (bf16[64,4096]{1,0:T(8,128)(2,1)}, bf16[64,4096]{1,0:T(8,128)(2,1)}, u32[]{:S(2)}, u32[]{:S(2)}) collective-permute-start(bf16[64,4096]{1,0:T(8,128)(2,1)} %bitcast.5), channel_id=1, source_target_pairs={{0,1},{1,0},{2,3},{3,2},{4,5},{5,4},{6,7},{7,6},{8,9},{9,8},{10,11... | collective-permute-start | bytes 1572872 | tf_op jit(solution)/shard_map/ppermute | solution.py:33
  3.0 1.6 %collective-permute-start.3 = (bf16[64,4096]{1,0:T(8,128)(2,1)}, bf16[64,4096]{1,0:T(8,128)(2,1)S(1)}, u32[]{:S(2)}, u32[]{:S(2)}) collective-permute-start(bf16[64,4096]{1,0:T(8,128)(2,1)} %bitcast.6), channel_id=1, source_target_pairs={{0,2},{2,4},{4,6},{6,0},{1,3},{3,5},{5,7},{7,1},{8,10},{10,12},{12... | collective-permute-start | bytes 1572872 | tf_op jit(solution)/shard_map/ppermute | solution.py:34
  4.6 1.7 %collective-permute-start.5 = (bf16[64,4096]{1,0:T(8,128)(2,1)}, bf16[64,4096]{1,0:T(8,128)(2,1)S(1)}, u32[]{:S(2)}, u32[]{:S(2)}) collective-permute-start(bf16[64,4096]{1,0:T(8,128)(2,1)} %bitcast.7), channel_id=1, source_target_pairs={{0,6},{2,0},{4,2},{6,4},{1,7},{3,1},{5,3},{7,5},{8,14},{10,8},{12,... | collective-permute-start | bytes 1572872 | tf_op jit(solution)/shard_map/ppermute | solution.py:35
  6.3 2.3 %multiply_reduce_fusion = f32[320]{0:T(512)S(1)} fusion(bf16[320,4096]{1,0:T(8,128)(2,1)} %block.1), kind=kLoop, calls=%fused_computation | loop fusion | flops 3931840 | bytes 2622720 | tf_op jit(solution)/shard_map/reduce_sum | solution.py:192
  8.8 9.2 %collective-permute-done.3.refs_2_ = bf16[64,4096]{1,0:T(8,128)(2,1)S(1)} collective-permute-done((bf16[64,4096]{1,0:T(8,128)(2,1)}, bf16[64,4096]{1,0:T(8,128)(2,1)S(1)}, u32[]{:S(2)}, u32[]{:S(2)}) %collective-permute-start.3) | collective-permute-done | bytes 524320 | tf_op jit(solution)/shard_map/ppermute | solution.py:34
  20.4 3.0 %collective-permute-start.6 = (bf16[32,4096]{1,0:T(8,128)(2,1)}, bf16[32,4096]{1,0:T(8,128)(2,1)}, u32[]{:S(2)}, u32[]{:S(2)}) collective-permute-start(bf16[32,4096]{1,0:T(8,128)(2,1)} %slice.58), channel_id=1, source_target_pairs={{0,6},{2,0},{4,2},{6,4},{1,7},{3,1},{5,3},{7,5},{8,14},{10,8},{12,... | collective-permute-start | bytes 786440 | tf_op jit(solution)/shard_map/ppermute | solution.py:37
  23.6 3.2 %collective-permute-start.2 = (bf16[64,4096]{1,0:T(8,128)(2,1)}, bf16[64,4096]{1,0:T(8,128)(2,1)}, u32[]{:S(2)}, u32[]{:S(2)}) collective-permute-start(bf16[64,4096]{1,0:T(8,128)(2,1)} %collective-permute-done.refs_1_), channel_id=1, source_target_pairs={{0,6},{2,0},{4,2},{6,4},{1,7},{3,1},{5,3},{7,5},{8,14},{10,8},{12,... | collective-permute-start | bytes 1572872 | tf_op jit(solution)/shard_map/ppermute | solution.py:39
  28.8 1.6 %collective-permute-done.6.refs_3_ = bf16[32,4096]{1,0:T(8,128)(2,1)} collective-permute-done((bf16[32,4096]{1,0:T(8,128)(2,1)}, bf16[32,4096]{1,0:T(8,128)(2,1)}, u32[]{:S(2)}, u32[]{:S(2)}) %collective-permute-start.6) | collective-permute-done | bytes 262176 | tf_op jit(solution)/shard_map/ppermute | solution.py:37
  33.1 2.4 %near.1.refs_8_ = f32[32,384]{1,0:T(8,128)S(1)} custom-call(bf16[64,4096]{1,0:T(8,128)(2,1)S(1)} %bitcast.8, bf16[64,4096]{1,0:T(8,128)(2,1)} %collective-permute-done.refs_1_, bf16[64,4096]{1,0:T(8,128)(2,1)S(1)} %collective-permute-done.3.refs_2_, bf16[64,4096]{1,0:T(8,128)(2,1)S(1)} %copy-done.2, bf16[320,4096]{1,0:T(8,128)(2,1)S(1)} %copy-done, ...), custom_call_target="tpu_custom_call" | custom-call | flops 805306368 | bytes 5242880 | tf_op jit(solution)/shard_map/near/pallas_call | solution.py:206
  35.6 2.2 %collective-permute-done.7.refs_4_ = bf16[32,4096]{1,0:T(8,128)(2,1)} collective-permute-done((bf16[32,4096]{1,0:T(8,128)(2,1)}, bf16[32,4096]{1,0:T(8,128)(2,1)}, u32[]{:S(2)}, u32[]{:S(2)}) %collective-permute-start.7) | collective-permute-done | bytes 262176 | tf_op jit(solution)/shard_map/ppermute | solution.py:40
  37.8 2.8 %collective-permute-done.8.refs_5_ = bf16[32,4096]{1,0:T(8,128)(2,1)} collective-permute-done((bf16[32,4096]{1,0:T(8,128)(2,1)}, bf16[32,4096]{1,0:T(8,128)(2,1)}, u32[]{:S(2)}, u32[]{:S(2)}) %collective-permute-start.8) | collective-permute-done | bytes 262176 | tf_op jit(solution)/shard_map/ppermute | solution.py:41
  40.6 3.2 %away.1 = f32[64,256]{1,0:T(8,128)S(1)} custom-call(s32[2]{0:T(128)S(1)} %pad_add_fusion.1.place, bf16[64,4096]{1,0:T(8,128)(2,1)} %collective-permute-done.1.refs_0_, bf16[64,4096]{1,0:T(8,128)(2,1)} %collective-permute-done.2.refs_1_, bf16[32,4096]{1,0:T(8,128)(2,1)} %collective-permute-done.4.refs_2_, bf16[32,4096]{1,0:T(8,128)(2,1)} %collective-permute-done.6.refs_3_, ...), custom_call_target="tpu_custom_call" | custom-call | flops 805306368 | bytes 5242880 | tf_op jit(solution)/shard_map/away/pallas_call | solution.py:216
  45.8 3.7 %collective-permute-done.10 = f32[64,256]{1,0:T(8,128)S(1)} collective-permute-done((f32[64,256]{1,0:T(8,128)S(1)}, f32[64,256]{1,0:T(8,128)S(1)}, u32[]{:S(2)}, u32[]{:S(2)}) %collective-permute-start.10) | collective-permute-done | bytes 65568 | tf_op jit(solution)/shard_map/ppermute | solution.py:169
  49.5 2.0 %collective-permute-start.11 = (f32[64,256]{1,0:T(8,128)S(1)}, f32[64,256]{1,0:T(8,128)S(1)}, u32[]{:S(2)}, u32[]{:S(2)}) collective-permute-start(f32[64,256]{1,0:T(8,128)S(1)} %add.94), channel_id=1, source_target_pairs={{0,32},{32,64},{64,96},{96,128},{128,160},{160,192},{192,224},{224... | collective-permute-start | bytes 196616 | tf_op jit(solution)/shard_map/ppermute | solution.py:170
  51.6 2.2 %collective-permute-start.17 = (bf16[320,1024]{1,0:T(8,128)(2,1)S(1)}, bf16[320,1024]{1,0:T(8,128)(2,1)S(1)}, u32[]{:S(2)}, u32[]{:S(2)}) collective-permute-start(bf16[320,1024]{1,0:T(8,128)(2,1)S(1)} %get-tuple-element.9), channel_id=1, source_target_pairs={{0,6},{2,0},{4,2},{6,4},{1,7},{3,1},{5,3},{7,5},{8,14},{10,8},{12,... | collective-permute-start | bytes 1966088 | tf_op jit(solution)/shard_map/ppermute | solution.py:232
  53.9 1.9 %collective-permute-done.12 = f32[64,256]{1,0:T(8,128)S(1)} collective-permute-done((f32[64,256]{1,0:T(8,128)S(1)}, f32[64,256]{1,0:T(8,128)S(1)}, u32[]{:S(2)}, u32[]{:S(2)}) %collective-permute-start.12) | collective-permute-done | bytes 65568 | tf_op jit(solution)/shard_map/ppermute | solution.py:171
  55.8 5.0 %collective-permute-start.13 = (f32[64,256]{1,0:T(8,128)S(1)}, f32[64,256]{1,0:T(8,128)S(1)}, u32[]{:S(2)}, u32[]{:S(2)}) collective-permute-start(f32[64,256]{1,0:T(8,128)S(1)} %get-tuple-element.13), channel_id=1, source_target_pairs={{0,160},{32,192},{64,224},{96,0},{128,32},{160,64},{192,96},{224,1... | collective-permute-start | bytes 196616 | tf_op jit(solution)/shard_map/ppermute | solution.py:173
  61.2 2.1 %collective-permute-done.13 = f32[64,256]{1,0:T(8,128)S(1)} collective-permute-done((f32[64,256]{1,0:T(8,128)S(1)}, f32[64,256]{1,0:T(8,128)S(1)}, u32[]{:S(2)}, u32[]{:S(2)}) %collective-permute-start.13) | collective-permute-done | bytes 65568 | tf_op jit(solution)/shard_map/ppermute | solution.py:173
  63.3 5.0 %collective-permute-done.14 = f32[64,256]{1,0:T(8,128)S(1)} collective-permute-done((f32[64,256]{1,0:T(8,128)S(1)}, f32[64,256]{1,0:T(8,128)S(1)}, u32[]{:S(2)}, u32[]{:S(2)}) %collective-permute-start.14) | collective-permute-done | bytes 65568 | tf_op jit(solution)/shard_map/ppermute | solution.py:174
  68.7 2.5 %collective-permute-start.15 = (bf16[64,512]{1,0:T(8,128)(2,1)S(1)}, bf16[64,512]{1,0:T(8,128)(2,1)S(1)}, u32[]{:S(2)}, u32[]{:S(2)}) collective-permute-start(bf16[64,512]{1,0:T(8,128)(2,1)S(1)} %weights.1.own), channel_id=1, source_target_pairs={{0,6},{2,0},{4,2},{6,4},{1,7},{3,1},{5,3},{7,5},{8,14},{10,8},{12,... | collective-permute-start | bytes 196616 | tf_op jit(solution)/shard_map/ppermute | solution.py:245
  71.5 1.6 %collective-permute-done.15.up = bf16[64,512]{1,0:T(8,128)(2,1)S(1)} collective-permute-done((bf16[64,512]{1,0:T(8,128)(2,1)S(1)}, bf16[64,512]{1,0:T(8,128)(2,1)S(1)}, u32[]{:S(2)}, u32[]{:S(2)}) %collective-permute-start.15) | collective-permute-done | bytes 65568 | tf_op jit(solution)/shard_map/ppermute | solution.py:245
  73.1 3.6 %collective-permute-done.16.down = bf16[64,512]{1,0:T(8,128)(2,1)S(1)} collective-permute-done((bf16[64,512]{1,0:T(8,128)(2,1)S(1)}, bf16[64,512]{1,0:T(8,128)(2,1)S(1)}, u32[]{:S(2)}, u32[]{:S(2)}) %collective-permute-start.16) | collective-permute-done | bytes 65568 | tf_op jit(solution)/shard_map/ppermute | solution.py:244
  76.7 2.3 %compose.1 = bf16[256,2176]{1,0:T(8,128)(2,1)S(1)} custom-call(s32[4]{0:T(128)S(1)} %copy-done.4, s32[2]{0:T(128)S(1)} %pad_add_fusion.1.place, bf16[64,512]{1,0:T(8,128)(2,1)S(1)} %weights.1.own, bf16[64,512]{1,0:T(8,128)(2,1)S(1)} %collective-permute-done.15.up, bf16[64,512]{1,0:T(8,128)(2,1)S(1)} %collective-permute-done.16.down, ...), custom_call_target="tpu_custom_call" | custom-call | flops 671088640 | bytes 5242880 | tf_op jit(solution)/shard_map/compose/pallas_call | solution.py:247
  79.0 16.9 %all_to_all.5.parts = bf16[8,32,2176]{2,1,0:T(8,128)(2,1)S(1)} all-to-all(bf16[8,32,2176]{2,1,0:T(8,128)(2,1)S(1)} %bitcast.4), channel_id=1, replica_groups=mesh['z'=8,'xl'=2,'co'=2,'yh'=2,'yl'=2,'xh'=2] {'yh','yl','xh'}, dimensions={0} | all-to-all | bytes 2228224 | tf_op jit(solution)/shard_map/all_to_all | solution.py:258
  (60 shorter events, 11.8 us)
Async XLA Ops:
  0.0 31.9 %copy-start = (bf16[320,4096]{1,0:T(8,128)(2,1)S(1)}, bf16[320,4096]{1,0:T(8,128)(2,1)}, u32[]{:S(2)}) copy-start(bf16[320,4096]{1,0:T(8,128)(2,1)} %block.1) | copy-start | bytes 7864324
  0.0 8.7 %copy-start.5 = (s32[256]{0:T(256)S(1)}, s32[256]{0:T(256)}, u32[]{:S(2)}) copy-start(s32[256]{0:T(256)} %param.7) | copy-start | bytes 3076
  0.0 23.5 %collective-permute-start = (bf16[64,4096]{1,0:T(8,128)(2,1)}, bf16[64,4096]{1,0:T(8,128)(2,1)}, u32[]{:S(2)}, u32[]{:S(2)}) collective-permute-start(bf16[64,4096]{1,0:T(8,128)(2,1)} %bitcast.5), channel_id=1, source_target_pairs={{0,1},{1,0},{2,3},{3,2},{4,5},{5,4},{6,7},{7,6},{8,9},{9,8},{10,11... | collective-permute-start | bytes 1572872 | tf_op jit(solution)/shard_map/ppermute | solution.py:33
  3.0 14.9 %collective-permute-start.3 = (bf16[64,4096]{1,0:T(8,128)(2,1)}, bf16[64,4096]{1,0:T(8,128)(2,1)S(1)}, u32[]{:S(2)}, u32[]{:S(2)}) collective-permute-start(bf16[64,4096]{1,0:T(8,128)(2,1)} %bitcast.6), channel_id=1, source_target_pairs={{0,2},{2,4},{4,6},{6,0},{1,3},{3,5},{5,7},{7,1},{8,10},{10,12},{12... | collective-permute-start | bytes 1572872 | tf_op jit(solution)/shard_map/ppermute | solution.py:34
  4.6 14.3 %collective-permute-start.5 = (bf16[64,4096]{1,0:T(8,128)(2,1)}, bf16[64,4096]{1,0:T(8,128)(2,1)S(1)}, u32[]{:S(2)}, u32[]{:S(2)}) collective-permute-start(bf16[64,4096]{1,0:T(8,128)(2,1)} %bitcast.7), channel_id=1, source_target_pairs={{0,6},{2,0},{4,2},{6,4},{1,7},{3,1},{5,3},{7,5},{8,14},{10,8},{12,... | collective-permute-start | bytes 1572872 | tf_op jit(solution)/shard_map/ppermute | solution.py:35
  18.6 9.7 %collective-permute-start.4 = (bf16[32,4096]{1,0:T(8,128)(2,1)}, bf16[32,4096]{1,0:T(8,128)(2,1)}, u32[]{:S(2)}, u32[]{:S(2)}) collective-permute-start(bf16[32,4096]{1,0:T(8,128)(2,1)} %slice.57), channel_id=1, source_target_pairs={{0,2},{2,4},{4,6},{6,0},{1,3},{3,5},{5,7},{7,1},{8,10},{10,12},{12... | collective-permute-start | bytes 786440 | tf_op jit(solution)/shard_map/ppermute | solution.py:36
  20.4 10.0 %collective-permute-start.6 = (bf16[32,4096]{1,0:T(8,128)(2,1)}, bf16[32,4096]{1,0:T(8,128)(2,1)}, u32[]{:S(2)}, u32[]{:S(2)}) collective-permute-start(bf16[32,4096]{1,0:T(8,128)(2,1)} %slice.58), channel_id=1, source_target_pairs={{0,6},{2,0},{4,2},{6,4},{1,7},{3,1},{5,3},{7,5},{8,14},{10,8},{12,... | collective-permute-start | bytes 786440 | tf_op jit(solution)/shard_map/ppermute | solution.py:37
  23.5 17.1 %collective-permute-start.1 = (bf16[64,4096]{1,0:T(8,128)(2,1)}, bf16[64,4096]{1,0:T(8,128)(2,1)}, u32[]{:S(2)}, u32[]{:S(2)}) collective-permute-start(bf16[64,4096]{1,0:T(8,128)(2,1)} %collective-permute-done.refs_1_), channel_id=1, source_target_pairs={{0,2},{2,4},{4,6},{6,0},{1,3},{3,5},{5,7},{7,1},{8,10},{10,12},{12... | collective-permute-start | bytes 1572872 | tf_op jit(solution)/shard_map/ppermute | solution.py:38
  23.6 17.0 %collective-permute-start.2 = (bf16[64,4096]{1,0:T(8,128)(2,1)}, bf16[64,4096]{1,0:T(8,128)(2,1)}, u32[]{:S(2)}, u32[]{:S(2)}) collective-permute-start(bf16[64,4096]{1,0:T(8,128)(2,1)} %collective-permute-done.refs_1_), channel_id=1, source_target_pairs={{0,6},{2,0},{4,2},{6,4},{1,7},{3,1},{5,3},{7,5},{8,14},{10,8},{12,... | collective-permute-start | bytes 1572872 | tf_op jit(solution)/shard_map/ppermute | solution.py:39
  28.3 9.5 %collective-permute-start.7 = (bf16[32,4096]{1,0:T(8,128)(2,1)}, bf16[32,4096]{1,0:T(8,128)(2,1)}, u32[]{:S(2)}, u32[]{:S(2)}) collective-permute-start(bf16[32,4096]{1,0:T(8,128)(2,1)} %collective-permute-done.4.refs_2_), channel_id=1, source_target_pairs={{0,1},{1,0},{2,3},{3,2},{4,5},{5,4},{6,7},{7,6},{8,9},{9,8},{10,11... | collective-permute-start | bytes 786440 | tf_op jit(solution)/shard_map/ppermute | solution.py:40
  30.5 10.1 %collective-permute-start.8 = (bf16[32,4096]{1,0:T(8,128)(2,1)}, bf16[32,4096]{1,0:T(8,128)(2,1)}, u32[]{:S(2)}, u32[]{:S(2)}) collective-permute-start(bf16[32,4096]{1,0:T(8,128)(2,1)} %collective-permute-done.6.refs_3_), channel_id=1, source_target_pairs={{0,1},{1,0},{2,3},{3,2},{4,5},{5,4},{6,7},{7,6},{8,9},{9,8},{10,11... | collective-permute-start | bytes 786440 | tf_op jit(solution)/shard_map/ppermute | solution.py:41
  31.9 1.2 %copy-start.3 = (bf16[8,8,4096]{2,1,0:T(8,128)(2,1)S(1)}, bf16[8,8,4096]{2,1,0:T(8,128)(2,1)}, u32[]{:S(2)}) copy-start(bf16[8,8,4096]{2,1,0:T(8,128)(2,1)} %param.5) | copy-start | bytes 1572868
  35.6 8.3 %copy-start.6 = (f32[64]{0:T(128)S(1)}, f32[64]{0:T(128)}, u32[]{:S(2)}) copy-start(f32[64]{0:T(128)} %param.9) | copy-start | bytes 772
  35.6 41.1 %copy-start.4 = (s32[4]{0:T(128)S(1)}, s32[4]{0:T(128)}, u32[]{:S(2)}) copy-start(s32[4]{0:T(128)} %leads.1) | copy-start | bytes 52
  43.8 1.3 %collective-permute-start.9 = (f32[64,256]{1,0:T(8,128)S(1)}, f32[64,256]{1,0:T(8,128)S(1)}, u32[]{:S(2)}, u32[]{:S(2)}) collective-permute-start(f32[64,256]{1,0:T(8,128)S(1)} %away.1), channel_id=1, source_target_pairs={{0,8},{8,0},{1,9},{9,1},{2,10},{10,2},{3,11},{11,3},{4,12},{12,4},... | collective-permute-start | bytes 196616 | tf_op jit(solution)/shard_map/ppermute | solution.py:168
  45.1 4.4 %collective-permute-start.10 = (f32[64,256]{1,0:T(8,128)S(1)}, f32[64,256]{1,0:T(8,128)S(1)}, u32[]{:S(2)}, u32[]{:S(2)}) collective-permute-start(f32[64,256]{1,0:T(8,128)S(1)} %add.93), channel_id=1, source_target_pairs={{0,16},{16,0},{1,17},{17,1},{2,18},{18,2},{3,19},{19,3},{4,20},{20... | collective-permute-start | bytes 196616 | tf_op jit(solution)/shard_map/ppermute | solution.py:169
  49.5 4.3 %collective-permute-start.11 = (f32[64,256]{1,0:T(8,128)S(1)}, f32[64,256]{1,0:T(8,128)S(1)}, u32[]{:S(2)}, u32[]{:S(2)}) collective-permute-start(f32[64,256]{1,0:T(8,128)S(1)} %add.94), channel_id=1, source_target_pairs={{0,32},{32,64},{64,96},{96,128},{128,160},{160,192},{192,224},{224... | collective-permute-start | bytes 196616 | tf_op jit(solution)/shard_map/ppermute | solution.py:170
  51.5 4.3 %collective-permute-start.12 = (f32[64,256]{1,0:T(8,128)S(1)}, f32[64,256]{1,0:T(8,128)S(1)}, u32[]{:S(2)}, u32[]{:S(2)}) collective-permute-start(f32[64,256]{1,0:T(8,128)S(1)} %add.94), channel_id=1, source_target_pairs={{0,224},{32,0},{64,32},{96,64},{128,96},{160,128},{192,160},{224,1... | collective-permute-start | bytes 196616 | tf_op jit(solution)/shard_map/ppermute | solution.py:171
  51.6 25.1 %collective-permute-start.17 = (bf16[320,1024]{1,0:T(8,128)(2,1)S(1)}, bf16[320,1024]{1,0:T(8,128)(2,1)S(1)}, u32[]{:S(2)}, u32[]{:S(2)}) collective-permute-start(bf16[320,1024]{1,0:T(8,128)(2,1)S(1)} %get-tuple-element.9), channel_id=1, source_target_pairs={{0,6},{2,0},{4,2},{6,4},{1,7},{3,1},{5,3},{7,5},{8,14},{10,8},{12,... | collective-permute-start | bytes 1966088 | tf_op jit(solution)/shard_map/ppermute | solution.py:232
  53.8 22.9 %collective-permute-start.18 = (bf16[320,1024]{1,0:T(8,128)(2,1)S(1)}, bf16[320,1024]{1,0:T(8,128)(2,1)S(1)}, u32[]{:S(2)}, u32[]{:S(2)}) collective-permute-start(bf16[320,1024]{1,0:T(8,128)(2,1)S(1)} %get-tuple-element.10), channel_id=1, source_target_pairs={{0,2},{2,4},{4,6},{6,0},{1,3},{3,5},{5,7},{7,1},{8,10},{10,12},{12... | collective-permute-start | bytes 1966088 | tf_op jit(solution)/shard_map/ppermute | solution.py:231
  55.8 7.5 %collective-permute-start.13 = (f32[64,256]{1,0:T(8,128)S(1)}, f32[64,256]{1,0:T(8,128)S(1)}, u32[]{:S(2)}, u32[]{:S(2)}) collective-permute-start(f32[64,256]{1,0:T(8,128)S(1)} %get-tuple-element.13), channel_id=1, source_target_pairs={{0,160},{32,192},{64,224},{96,0},{128,32},{160,64},{192,96},{224,1... | collective-permute-start | bytes 196616 | tf_op jit(solution)/shard_map/ppermute | solution.py:173
  60.8 7.5 %collective-permute-start.14 = (f32[64,256]{1,0:T(8,128)S(1)}, f32[64,256]{1,0:T(8,128)S(1)}, u32[]{:S(2)}, u32[]{:S(2)}) collective-permute-start(f32[64,256]{1,0:T(8,128)S(1)} %get-tuple-element.14), channel_id=1, source_target_pairs={{0,96},{32,128},{64,160},{96,192},{128,224},{160,0},{192,32},{224,... | collective-permute-start | bytes 196616 | tf_op jit(solution)/shard_map/ppermute | solution.py:174
  68.7 4.4 %collective-permute-start.15 = (bf16[64,512]{1,0:T(8,128)(2,1)S(1)}, bf16[64,512]{1,0:T(8,128)(2,1)S(1)}, u32[]{:S(2)}, u32[]{:S(2)}) collective-permute-start(bf16[64,512]{1,0:T(8,128)(2,1)S(1)} %weights.1.own), channel_id=1, source_target_pairs={{0,6},{2,0},{4,2},{6,4},{1,7},{3,1},{5,3},{7,5},{8,14},{10,8},{12,... | collective-permute-start | bytes 196616 | tf_op jit(solution)/shard_map/ppermute | solution.py:245
  71.2 5.5 %collective-permute-start.16 = (bf16[64,512]{1,0:T(8,128)(2,1)S(1)}, bf16[64,512]{1,0:T(8,128)(2,1)S(1)}, u32[]{:S(2)}, u32[]{:S(2)}) collective-permute-start(bf16[64,512]{1,0:T(8,128)(2,1)S(1)} %weights.1.own), channel_id=1, source_target_pairs={{0,2},{2,4},{4,6},{6,0},{1,3},{3,5},{5,7},{7,1},{8,10},{10,12},{12... | collective-permute-start | bytes 196616 | tf_op jit(solution)/shard_map/ppermute | solution.py:244
  (2 other events, 1.8 us)

commit v5 on v4

--- a/solution.py
+++ b/solution.py
@@ -28,18 +28,53 @@
     return [(i, (i + by) % n) for i in range(n)]
 
 
-def gather_targets(own):
-    half = own.shape[0] // 2
+def gather_targets(targets):
+    lags, count, width = targets.shape
+    own = targets.reshape(lags * count, width)
+    half = lags * count // 2
+    early, late = own[:half], own[half:]
     across = lax.ppermute(own, "xh", flip(2, 1))
-    below = lax.ppermute(own, Y, turn(4, 1))
-    above = lax.ppermute(own, Y, turn(4, -1))
-    far_a = lax.ppermute(below[:half], Y, turn(4, 1))
-    far_b = lax.ppermute(above[half:], Y, turn(4, -1))
+    below_a = lax.ppermute(early, Y, turn(4, 1))
+    above_b = lax.ppermute(late, Y, turn(4, -1))
+    below_b = lax.ppermute(late, Y, turn(4, 1))
+    above_a = lax.ppermute(early, Y, turn(4, -1))
+    far_a = lax.ppermute(below_a, Y, turn(4, 1))
+    far_b = lax.ppermute(above_b, Y, turn(4, -1))
+    across, below_b, above_a = lax.optimization_barrier((across, below_b, above_a))
     below_x = lax.ppermute(across, Y, turn(4, 1))
     above_x = lax.ppermute(across, Y, turn(4, -1))
     far_xa = lax.ppermute(far_a, "xh", flip(2, 1))
     far_xb = lax.ppermute(far_b, "xh", flip(2, 1))
-    return (own, across, below, above), (below_x, above_x, far_a, far_b, far_xa, far_xb)
+    return (own, across, below_a, below_b, above_a, above_b), (below_x, above_x, far_a, far_b, far_xa, far_xb)
+
+
+def place_on_y():
+    return lax.axis_index("yh") * 2 + lax.axis_index("yl")
+
+
+def prepare_kernel(lags, factor, library, anchors, spread, lnorm, picks, scale, for_up, for_down):
+    rows, width = library.shape
+    wide = picks.shape[0]
+    squares = jnp.zeros((rows, 128), F32)
+    for c in range(0, width, 128):
+        part = library[:, c : c + 128].astype(F32)
+        squares = squares + part * part
+    squares = jnp.concatenate([squares, jnp.zeros((wide - rows, 128), F32)], axis=0)
+    norm = jnp.sum(squares.T, axis=0, keepdims=True)
+    norm = jnp.broadcast_to(norm, lnorm.shape)
+    total = norm
+    for lag in range(1, lags):
+        total = total + pltpu.roll(norm, lag, 1)
+    lnorm[...] = total
+    spots = lax.broadcasted_iota(jnp.int32, picks.shape, 0)
+    picks[...] = jnp.where(spots == anchors[...], 1.0, 0.0).astype(BF16)
+    count = scale.shape[0]
+    wider = jnp.concatenate([spread[...] * factor, jnp.ones((1, 128 - count), F32)], axis=1)
+    scale[...] = jnp.broadcast_to(wider, (128, 128)).T[:count, :]
+    quarter = for_up.shape[1]
+    odd = lax.axis_index("yl")
+    for_up[...] = library[:, pl.ds(pl.multiple_of((1 + 2 * odd) * quarter, quarter), quarter)]
+    for_down[...] = library[:, pl.ds(pl.multiple_of((2 - 2 * odd) * quarter, quarter), quarter)]
 
 
 def cross_rows(lags, pieces, block, lnorm, acc):
@@ -66,35 +101,44 @@
     return values
 
 
-def near_kernel(lags, *refs):
-    pieces, (block, lnorm, out, acc) = refs[:4], refs[4:]
-    out[...] = jnp.concatenate(cross_rows(lags, pieces, block, lnorm, acc), axis=0)
-
-
-def away_kernel(lags, place, *refs):
-    pieces, (block, lnorm, near, picks, out, acc) = refs[:6], refs[6:]
-    values = cross_rows(lags, pieces, block, lnorm, acc)
-    count = values[0].shape[0]
-    value = jnp.concatenate([near[...]] + values, axis=0)
+def at_anchors(value, picks):
     first = value.astype(BF16)
     rest = value - first.astype(F32)
     second = rest.astype(BF16)
     third = (rest - second.astype(F32)).astype(BF16)
-    picked = [jnp.dot(part, picks[...], preferred_element_type=F32) for part in (first, second, third)]
-    value = picked[0] + picked[1] + picked[2]
+    parts = jnp.concatenate([first, second, third], axis=0)
+    parts = jnp.dot(parts, picks[...], preferred_element_type=F32)
+    n = value.shape[0]
+    return parts[:n] + parts[n : 2 * n] + parts[2 * n :]
+
+
+def near_kernel(lags, *refs):
+    pieces, (block, lnorm, picks, out, acc) = refs[:6], refs[6:]
+    values = cross_rows(lags, pieces, block, lnorm, acc)
+    out[...] = at_anchors(jnp.concatenate(values, axis=0), picks)
+
+
+def away_kernel(lags, *refs):
+    pieces, (block, lnorm, picks, near, out, acc) = refs[:6], refs[6:]
+    values = cross_rows(lags, pieces, block, lnorm, acc)
+    count = values[0].shape[0]
+    value = at_anchors(jnp.concatenate(values, axis=0), picks)
+    y, xh = place_on_y(), lax.axis_index("xh")
     for r, (dy, dx) in enumerate(NEAR + AWAY):
-        owner = lax.rem(place[0] + dy, 4) * 2 + lax.rem(place[1] + dx, 2)
-        out[pl.ds(pl.multiple_of(owner * count, count), count), :] = value[r * count : (r + 1) * count, :]
-
-
-def weights_kernel(dist, scale, spots, out):
+        owner = lax.rem(y + dy, 4) * 2 + lax.rem(xh + dx, 2)
+        source, at = (near, r) if r < 4 else (value, r - 4)
+        out[pl.ds(pl.multiple_of(owner * count, count), count), :] = source[at * count : (at + 1) * count, :]
+
+
+def weights_kernel(dist, scale, picks, out):
     scores = -dist[...] / scale[:, :1]
     top = jnp.max(scores, axis=1, keepdims=True)
     top_hi, top_lo = halves(top)
     weights = jnp.exp(scores - (top_hi + top_lo)).astype(BF16)
     tot_hi, tot_lo = halves(jnp.sum(weights.astype(F32), axis=1, keepdims=True))
-    wide = spots.shape[1]
-    out[:, :wide] = jnp.dot(weights, spots[...], preferred_element_type=F32).astype(BF16)
+    wide = picks.shape[0]
+    spread_out = lax.dot_general(weights, picks[...], (((1,), (1,)), ((), ())), preferred_element_type=F32)
+    out[:, :wide] = spread_out.astype(BF16)
     out[:, wide:] = in_lanes((top_hi, top_lo, tot_hi, tot_lo)).astype(BF16)
 
 
@@ -111,18 +155,21 @@
     return value
 
 
-def compose_kernel(leads, place, own, up, down, perm, block, block_up, block_down, out):
+def compose_kernel(leads, own, up, down, block, block_up, block_down, out):
     rows, quarter = block_up.shape
     targets, wide = own.shape[0], own.shape[1] - 128
     count = leads.shape[0]
-    odd = lax.rem(place[0], 2)
+    odd = lax.axis_index("yl")
+    shape = (count * targets, count * targets)
+    row, col = lax.broadcasted_iota(jnp.int32, shape, 0), lax.broadcasted_iota(jnp.int32, shape, 1)
+    perm = jnp.where(lax.rem(row, count) * targets + lax.div(row, count) == col, 1.0, 0.0).astype(BF16)
     mixed, facts = [], []
     for w in (own, up, down):
         weights = w[:, :wide].astype(F32)
         stack = jnp.concatenate([pltpu.roll(weights, leads[k], 1) for k in range(count)], axis=0).astype(BF16)
-        mixed.append(jnp.dot(perm[...], stack, preferred_element_type=F32).astype(BF16)[:, :rows])
+        mixed.append(jnp.dot(perm, stack, preferred_element_type=F32).astype(BF16)[:, :rows])
         fact = jnp.concatenate([w[:, wide:]] * count, axis=0)
-        facts.append(jnp.dot(perm[...], fact, preferred_element_type=F32))
+        facts.append(jnp.dot(perm, fact, preferred_element_type=F32))
     tops = [f[:, 0:1] + f[:, 1:2] for f in facts]
     totals = [f[:, 2:3] + f[:, 3:4] for f in facts]
     step = 512
@@ -185,51 +232,51 @@
     scale = math.sqrt(lags * width * lax.axis_size(SPACE))
     quarter = width // 4
 
-    near, away = gather_targets(targets.reshape(lags * count, width))
-
-    y, xh = lax.axis_index(Y), lax.axis_index("xh")
-    place = jnp.stack([y, xh]).astype(jnp.int32)
-    norm = jnp.sum(jnp.square(library.astype(F32)), axis=1)
-    norm = jnp.pad(norm, (0, wide - rows))
-    lnorm = functools.reduce(jnp.add, [jnp.roll(norm, lag) for lag in range(lags)])
-    lnorm = jnp.broadcast_to(lnorm[None, :], (8, wide))
-    spots = lax.broadcasted_iota(jnp.int32, (anchors.shape[0], wide), 1)
-    spots = (spots == anchors[:, None]).astype(BF16)
-    picks = lax.broadcasted_iota(jnp.int32, (wide, anchors.shape[0]), 0)
-    picks = (picks == anchors[None, :]).astype(BF16)
-    scales = jnp.broadcast_to((spread * scale)[:, None], (n_target, 128))
-    row = lax.broadcasted_iota(jnp.int32, (lead_n * n_target, lead_n * n_target), 0)
-    col = lax.broadcasted_iota(jnp.int32, (lead_n * n_target, lead_n * n_target), 1)
-    perm = ((row % lead_n) * n_target + row // lead_n == col).astype(BF16)
+    near, away = gather_targets(targets)
+
+    n_anchor = anchors.shape[0]
+    lnorm, picks, scales, for_up, for_down = pl.pallas_call(
+        functools.partial(prepare_kernel, lags, scale),
+        out_shape=(
+            jax.ShapeDtypeStruct((8, wide), F32),
+            jax.ShapeDtypeStruct((wide, n_anchor), BF16),
+            jax.ShapeDtypeStruct((n_target, 128), F32),
+            jax.ShapeDtypeStruct((rows, quarter), BF16),
+            jax.ShapeDtypeStruct((rows, quarter), BF16),
+        ),
+        in_specs=[VM] * 3,
+        out_specs=(VM,) * 5,
+        compiler_params=PARAMS,
+        cost_estimate=pl.CostEstimate(flops=2 * rows * width, bytes_accessed=4 << 20, transcendentals=0),
+        name="prepare",
+    )(library, anchors.reshape(1, n_anchor), spread.reshape(1, n_target))
 
     flops = lags * n_target * wide * width
     near_dist = pl.pallas_call(
         functools.partial(near_kernel, lags),
-        out_shape=jax.ShapeDtypeStruct((n_target // 2, wide), F32),
-        in_specs=[VM] * 6,
+        out_shape=jax.ShapeDtypeStruct((n_target // 2, n_anchor), F32),
+        in_specs=[VM] * 9,
         out_specs=VM,
         scratch_shapes=[pltpu.VMEM((lags * n_target // 2, wide), F32)],
         compiler_params=PARAMS,
         cost_estimate=pl.CostEstimate(flops=flops, bytes_accessed=5 << 20, transcendentals=0),
         name="near",
-    )(*near, library, lnorm)
+    )(*near, library, lnorm, picks)
+
+    for_up, for_down, near_dist = lax.optimization_barrier((for_up, for_down, near_dist))
+    block_down = lax.ppermute(for_up, Y, turn(4, 1))
+    block_up = lax.ppermute(for_down, Y, turn(4, -1))
+
     partial_dist = pl.pallas_call(
         functools.partial(away_kernel, lags),
-        out_shape=jax.ShapeDtypeStruct((n_target, anchors.shape[0]), F32),
-        in_specs=[SM] + [VM] * 10,
+        out_shape=jax.ShapeDtypeStruct((n_target, n_anchor), F32),
+        in_specs=[VM] * 10,
         out_specs=VM,
         scratch_shapes=[pltpu.VMEM((lags * n_target // 2, wide), F32)],
         compiler_params=PARAMS,
         cost_estimate=pl.CostEstimate(flops=flops, bytes_accessed=5 << 20, transcendentals=0),
         name="away",
-    )(place, *away, library, lnorm, near_dist, picks)
-
-    odd = lax.rem(y, 2)
-    for_up = lax.dynamic_slice_in_dim(library, (1 + 2 * odd) * quarter, quarter, axis=1)
-    for_down = lax.dynamic_slice_in_dim(library, (2 - 2 * odd) * quarter, quarter, axis=1)
-    for_up, for_down, partial_dist = lax.optimization_barrier((for_up, for_down, partial_dist))
-    block_down = lax.ppermute(for_up, Y, turn(4, 1))
-    block_up = lax.ppermute(for_down, Y, turn(4, -1))
+    )(*away, library, lnorm, picks, near_dist)
 
     dist = total_over_space(partial_dist)
     own = pl.pallas_call(
@@ -240,19 +287,19 @@
         compiler_params=PARAMS,
         cost_estimate=pl.CostEstimate(flops=2 * n_target * wide * 256, bytes_accessed=1 << 20, transcendentals=n_target * 256),
         name="weights",
-    )(dist, scales, spots)
+    )(dist, scales, picks)
     down = lax.ppermute(own, Y, turn(4, 1))
     up = lax.ppermute(own, Y, turn(4, -1))
 
     parts = pl.pallas_call(
         compose_kernel,
         out_shape=jax.ShapeDtypeStruct((lead_n * n_target, 2 * quarter + 128), BF16),
-        in_specs=[SM] * 2 + [VM] * 7,
+        in_specs=[SM] + [VM] * 6,
         out_specs=VM,
         compiler_params=PARAMS,
         cost_estimate=pl.CostEstimate(flops=2 * lead_n * n_target * rows * width, bytes_accessed=5 << 20, transcendentals=n_target * wide),
         name="compose",
-    )(leads, place, own, up, down, perm, library, block_up, block_down)
+    )(leads, own, up, down, library, block_up, block_down)
 
     parts = parts.reshape(n_lib, lead_n * count, 2 * quarter + 128)
     parts = lax.all_to_all(parts, LIB, 0, 0, tiled=True)

time: 97.8 us -> 94.9 us (0.970)
  starting transfers between devices: 27.7 us -> 33.2 us
  waiting for transfers between devices: 36.4 us -> 31.8 us
  other arithmetic: 2.98 us -> 0.05 us
  Pallas kernels: 9.41 us -> 7.75 us
    ppermute x4 -> x6, starting transfers between devices: 6.47 us -> 10.1 us  [the longest x1 3.69 us: gather_targets(): far_b = lax.ppermute(above_b, Y, turn(4, -1))]
    ppermute x1, waiting for transfers between devices: 2.81 us -> 0.01 us  [gather_targets(): far_xb = lax.ppermute(far_b, 'xh', flip(2, 1))]
    reduce_sum x1 -> x0, other arithmetic: 2.35 us -> none  [per_device(): norm = jnp.sum(jnp.square(library.astype(F32)), axis=1)]
    pallas_call x1, Pallas kernels: 3.17 us -> 1.58 us  [per_device(): pl.pallas_call(functools.partial(away_kernel, lags), out_shape=jax.ShapeD...]
    unnamed x14 -> x12, local copies, waits for them, and re-layouts: 1.88 us -> 3.37 us
    ppermute x4 -> x6, waiting for transfers between devices: 12.2 us -> 11 us  [the longest x1 5.61 us: gather_targets(): below_b = lax.ppermute(late, Y, turn(4, 1))]
  transfers between devices with their start and end apart: 19 -> 21, of which waited for: 12 -> 12; matrix products, arithmetic and copies ran while one was open for 5% -> 1% of each run, Pallas kernels for 3% -> 3%
where the time goes in v5:
time: 94.9 us; the launch traced here: 94.2 us
  starting transfers between devices  33.2 us (35%)
  waiting for transfers between devices  31.8 us (34%)
  blocking collectives  16.9 us (18%)
  Pallas kernels  7.75 us (8%)
  local copies, waits for them, and re-layouts  4.44 us (5%)
    all_to_all x1, blocking collectives, per_device(): parts = lax.all_to_all(parts, LIB, 0, 0, tiled=True)  16.9 us
    ppermute x1, waiting for transfers between devices, gather_targets(): below_b = lax.ppermute(late, Y, turn(4, 1))  5.61 us
    ppermute x1, starting transfers between devices, total_over_space(): high = lax.ppermute(three, 'z', turn(8, -3))  5.02 us
    ppermute x1, waiting for transfers between devices, total_over_space(): low = lax.ppermute(two, 'z', turn(8, 3))  4.37 us
    ppermute x1, starting transfers between devices, gather_targets(): far_b = lax.ppermute(above_b, Y, turn(4, -1))  3.69 us
    ppermute x1, waiting for transfers between devices, total_over_space(): value = value + lax.ppermute(value, 'xl', flip(2, 1))  3.67 us
    ppermute x1, waiting for transfers between devices, per_device(): down = lax.ppermute(own, Y, turn(4, 1))  3.57 us
    ppermute x1, waiting for transfers between devices, gather_targets(): above_b = lax.ppermute(late, Y, turn(4, -1))  3.48 us
  transfers between devices with their start and end apart: 21, of which 12 were waited for; matrix products, arithmetic and copies ran while one was open for 1% of the time, Pallas kernels for 3%

profile of v5, /device:TPU:32, one launch (start us, length us, event | category | flops | bytes accessed | tf_op | source)
XLA Modules:
  0.0 94.2 jit_solution(13813442875518561300)
XLA Ops:
  0.0 3.0 %collective-permute-start = (bf16[64,4096]{1,0:T(8,128)(2,1)}, bf16[64,4096]{1,0:T(8,128)(2,1)S(1)}, u32[]{:S(2)}, u32[]{:S(2)}) collective-permute-start(bf16[64,4096]{1,0:T(8,128)(2,1)} %bitcast.9), channel_id=1, source_target_pairs={{0,1},{1,0},{2,3},{3,2},{4,5},{5,4},{6,7},{7,6},{8,9},{9,8},{10,11... | collective-permute-start | bytes 1572872 | tf_op jit(solution)/shard_map/ppermute | solution.py:36
  4.1 3.1 %collective-permute-start.7 = (bf16[32,4096]{1,0:T(8,128)(2,1)S(1)}, bf16[32,4096]{1,0:T(8,128)(2,1)S(1)}, u32[]{:S(2)}, u32[]{:S(2)}) collective-permute-start(bf16[32,4096]{1,0:T(8,128)(2,1)S(1)} %get-tuple-element.28), channel_id=1, source_target_pairs={{0,6},{2,0},{4,2},{6,4},{1,7},{3,1},{5,3},{7,5},{8,14},{10,8},{12,... | collective-permute-start | bytes 786440 | tf_op jit(solution)/shard_map/ppermute | solution.py:38
  7.8 2.7 %collective-permute-start.2 = (bf16[32,4096]{1,0:T(8,128)(2,1)S(1)}, bf16[32,4096]{1,0:T(8,128)(2,1)S(1)}, u32[]{:S(2)}, u32[]{:S(2)}) collective-permute-start(bf16[32,4096]{1,0:T(8,128)(2,1)S(1)} %get-tuple-element.27), channel_id=1, source_target_pairs={{0,6},{2,0},{4,2},{6,4},{1,7},{3,1},{5,3},{7,5},{8,14},{10,8},{12,... | collective-permute-start | bytes 786440 | tf_op jit(solution)/shard_map/ppermute | solution.py:40
  10.5 3.5 %collective-permute-done.7.refs_5_ = bf16[32,4096]{1,0:T(8,128)(2,1)S(1)} collective-permute-done((bf16[32,4096]{1,0:T(8,128)(2,1)S(1)}, bf16[32,4096]{1,0:T(8,128)(2,1)S(1)}, u32[]{:S(2)}, u32[]{:S(2)}) %collective-permute-start.7) | collective-permute-done | bytes 262176 | tf_op jit(solution)/shard_map/ppermute | solution.py:38
  13.9 3.7 %collective-permute-start.8 = (bf16[32,4096]{1,0:T(8,128)(2,1)S(1)}, bf16[32,4096]{1,0:T(8,128)(2,1)S(1)}, u32[]{:S(2)}, u32[]{:S(2)}) collective-permute-start(bf16[32,4096]{1,0:T(8,128)(2,1)S(1)} %collective-permute-done.7.refs_5_), channel_id=1, source_target_pairs={{0,6},{2,0},{4,2},{6,4},{1,7},{3,1},{5,3},{7,5},{8,14},{10,8},{12,... | collective-permute-start | bytes 786440 | tf_op jit(solution)/shard_map/ppermute | solution.py:42
  17.6 5.6 %collective-permute-done.1.refs_3_ = bf16[32,4096]{1,0:T(8,128)(2,1)S(1)} collective-permute-done((bf16[32,4096]{1,0:T(8,128)(2,1)S(1)}, bf16[32,4096]{1,0:T(8,128)(2,1)S(1)}, u32[]{:S(2)}, u32[]{:S(2)}) %collective-permute-start.1) | collective-permute-done | bytes 262176 | tf_op jit(solution)/shard_map/ppermute | solution.py:39
  23.3 3.2 %collective-permute-start.4 = (bf16[64,4096]{1,0:T(8,128)(2,1)S(1)}, bf16[64,4096]{1,0:T(8,128)(2,1)S(1)}, u32[]{:S(2)}, u32[]{:S(2)}) collective-permute-start(bf16[64,4096]{1,0:T(8,128)(2,1)S(1)} %collective-permute-done.refs_1_), channel_id=1, source_target_pairs={{0,6},{2,0},{4,2},{6,4},{1,7},{3,1},{5,3},{7,5},{8,14},{10,8},{12,... | collective-permute-start | bytes 1572872 | tf_op jit(solution)/shard_map/ppermute | solution.py:45
  27.0 1.9 %collective-permute-done.6.refs_2_ = bf16[32,4096]{1,0:T(8,128)(2,1)S(1)} collective-permute-done((bf16[32,4096]{1,0:T(8,128)(2,1)S(1)}, bf16[32,4096]{1,0:T(8,128)(2,1)S(1)}, u32[]{:S(2)}, u32[]{:S(2)}) %collective-permute-start.6) | collective-permute-done | bytes 262176 | tf_op jit(solution)/shard_map/ppermute | solution.py:41
  30.0 1.7 %copy-done = bf16[320,4096]{1,0:T(8,128)(2,1)S(1)} copy-done((bf16[320,4096]{1,0:T(8,128)(2,1)S(1)}, bf16[320,4096]{1,0:T(8,128)(2,1)}, u32[]{:S(2)}) %copy-start) | copy-done | bytes 2621464
  34.2 1.6 %near.1.refs_9_ = f32[32,256]{1,0:T(8,128)S(1)} custom-call(bf16[64,4096]{1,0:T(8,128)(2,1)S(1)} %bitcast.10, bf16[64,4096]{1,0:T(8,128)(2,1)S(1)} %collective-permute-done.refs_1_, bf16[32,4096]{1,0:T(8,128)(2,1)S(1)} %collective-permute-done.5.refs_2_, bf16[32,4096]{1,0:T(8,128)(2,1)S(1)} %collective-permute-done.1.refs_3_, ...), custom_call_target="tpu_custom_call" | custom-call | flops 805306368 | bytes 5242880 | tf_op jit(solution)/shard_map/near/pallas_call | solution.py:255
  35.7 2.3 %collective-permute-done.9.refs_4_ = bf16[32,4096]{1,0:T(8,128)(2,1)S(1)} collective-permute-done((bf16[32,4096]{1,0:T(8,128)(2,1)S(1)}, bf16[32,4096]{1,0:T(8,128)(2,1)S(1)}, u32[]{:S(2)}, u32[]{:S(2)}) %collective-permute-start.9) | collective-permute-done | bytes 262176 | tf_op jit(solution)/shard_map/ppermute | solution.py:46
  38.4 1.6 %away.1 = f32[64,256]{1,0:T(8,128)S(1)} custom-call(bf16[64,4096]{1,0:T(8,128)(2,1)S(1)} %collective-permute-done.3.refs_0_, bf16[64,4096]{1,0:T(8,128)(2,1)S(1)} %collective-permute-done.4.refs_1_, bf16[32,4096]{1,0:T(8,128)(2,1)S(1)} %collective-permute-done.6.refs_2_, bf16[32,4096]{1,0:T(8,128)(2,1)S(1)} %collective-permute-done.8.refs_3_, ...), custom_call_target="tpu_custom_call" | custom-call | flops 805306368 | bytes 5242880 | tf_op jit(solution)/shard_map/away/pallas_call | solution.py:270
  40.0 1.3 %collective-permute-done.11 = f32[64,256]{1,0:T(8,128)S(1)} collective-permute-done((f32[64,256]{1,0:T(8,128)S(1)}, f32[64,256]{1,0:T(8,128)S(1)}, u32[]{:S(2)}, u32[]{:S(2)}) %collective-permute-start.11) | collective-permute-done | bytes 65568 | tf_op jit(solution)/shard_map/ppermute | solution.py:215
  42.1 3.7 %collective-permute-done.12 = f32[64,256]{1,0:T(8,128)S(1)} collective-permute-done((f32[64,256]{1,0:T(8,128)S(1)}, f32[64,256]{1,0:T(8,128)S(1)}, u32[]{:S(2)}, u32[]{:S(2)}) %collective-permute-start.12) | collective-permute-done | bytes 65568 | tf_op jit(solution)/shard_map/ppermute | solution.py:216
  45.8 2.0 %collective-permute-start.13 = (f32[64,256]{1,0:T(8,128)S(1)}, f32[64,256]{1,0:T(8,128)S(1)}, u32[]{:S(2)}, u32[]{:S(2)}) collective-permute-start(f32[64,256]{1,0:T(8,128)S(1)} %add.22), channel_id=1, source_target_pairs={{0,32},{32,64},{64,96},{96,128},{128,160},{160,192},{192,224},{224... | collective-permute-start | bytes 196616 | tf_op jit(solution)/shard_map/ppermute | solution.py:217
  47.9 3.0 %collective-permute-start.19 = (bf16[320,1024]{1,0:T(8,128)(2,1)S(1)}, bf16[320,1024]{1,0:T(8,128)(2,1)S(1)}, u32[]{:S(2)}, u32[]{:S(2)}) collective-permute-start(bf16[320,1024]{1,0:T(8,128)(2,1)S(1)} %get-tuple-element.25), channel_id=1, source_target_pairs={{0,6},{2,0},{4,2},{6,4},{1,7},{3,1},{5,3},{7,5},{8,14},{10,8},{12,... | collective-permute-start | bytes 1966088 | tf_op jit(solution)/shard_map/ppermute | solution.py:268
  52.1 5.0 %collective-permute-start.15 = (f32[64,256]{1,0:T(8,128)S(1)}, f32[64,256]{1,0:T(8,128)S(1)}, u32[]{:S(2)}, u32[]{:S(2)}) collective-permute-start(f32[64,256]{1,0:T(8,128)S(1)} %get-tuple-element.29), channel_id=1, source_target_pairs={{0,160},{32,192},{64,224},{96,0},{128,32},{160,64},{192,96},{224,1... | collective-permute-start | bytes 196616 | tf_op jit(solution)/shard_map/ppermute | solution.py:220
  58.2 2.3 %collective-permute-done.15 = f32[64,256]{1,0:T(8,128)S(1)} collective-permute-done((f32[64,256]{1,0:T(8,128)S(1)}, f32[64,256]{1,0:T(8,128)S(1)}, u32[]{:S(2)}, u32[]{:S(2)}) %collective-permute-start.15) | collective-permute-done | bytes 65568 | tf_op jit(solution)/shard_map/ppermute | solution.py:220
  60.5 4.4 %collective-permute-done.16 = f32[64,256]{1,0:T(8,128)S(1)} collective-permute-done((f32[64,256]{1,0:T(8,128)S(1)}, f32[64,256]{1,0:T(8,128)S(1)}, u32[]{:S(2)}, u32[]{:S(2)}) %collective-permute-start.16) | collective-permute-done | bytes 65568 | tf_op jit(solution)/shard_map/ppermute | solution.py:221
  65.2 3.1 %collective-permute-start.17 = (bf16[64,512]{1,0:T(8,128)(2,1)S(1)}, bf16[64,512]{1,0:T(8,128)(2,1)S(1)}, u32[]{:S(2)}, u32[]{:S(2)}) collective-permute-start(bf16[64,512]{1,0:T(8,128)(2,1)S(1)} %weights.1.own), channel_id=1, source_target_pairs={{0,6},{2,0},{4,2},{6,4},{1,7},{3,1},{5,3},{7,5},{8,14},{10,8},{12,... | collective-permute-start | bytes 196616 | tf_op jit(solution)/shard_map/ppermute | solution.py:292
  68.2 1.9 %collective-permute-done.17.up = bf16[64,512]{1,0:T(8,128)(2,1)S(1)} collective-permute-done((bf16[64,512]{1,0:T(8,128)(2,1)S(1)}, bf16[64,512]{1,0:T(8,128)(2,1)S(1)}, u32[]{:S(2)}, u32[]{:S(2)}) %collective-permute-start.17) | collective-permute-done | bytes 65568 | tf_op jit(solution)/shard_map/ppermute | solution.py:292
  70.1 3.6 %collective-permute-done.18.down = bf16[64,512]{1,0:T(8,128)(2,1)S(1)} collective-permute-done((bf16[64,512]{1,0:T(8,128)(2,1)S(1)}, bf16[64,512]{1,0:T(8,128)(2,1)S(1)}, u32[]{:S(2)}, u32[]{:S(2)}) %collective-permute-start.18) | collective-permute-done | bytes 65568 | tf_op jit(solution)/shard_map/ppermute | solution.py:291
  73.7 2.4 %compose.1 = bf16[256,2176]{1,0:T(8,128)(2,1)S(1)} custom-call(s32[4]{0:T(128)S(1)} %copy-done.5, bf16[64,512]{1,0:T(8,128)(2,1)S(1)} %weights.1.own, bf16[64,512]{1,0:T(8,128)(2,1)S(1)} %collective-permute-done.17.up, bf16[64,512]{1,0:T(8,128)(2,1)S(1)} %collective-permute-done.18.down, bf16[320,4096]{1,0:T(8,128)(2,1)S(1)} %copy-done.1, ...), custom_call_target="tpu_custom_call" | custom-call | flops 671088640 | bytes 5242880 | tf_op jit(solution)/shard_map/compose/pallas_call | solution.py:294
  76.1 16.9 %all_to_all.5.parts = bf16[8,32,2176]{2,1,0:T(8,128)(2,1)S(1)} all-to-all(bf16[8,32,2176]{2,1,0:T(8,128)(2,1)S(1)} %bitcast.8), channel_id=1, replica_groups=mesh['z'=8,'xl'=2,'co'=2,'yh'=2,'yl'=2,'xh'=2] {'yh','yl','xh'}, dimensions={0} | all-to-all | bytes 2228224 | tf_op jit(solution)/shard_map/all_to_all | solution.py:305
  (42 shorter events, 10.9 us)
Async XLA Ops:
  0.0 23.3 %collective-permute-start = (bf16[64,4096]{1,0:T(8,128)(2,1)}, bf16[64,4096]{1,0:T(8,128)(2,1)S(1)}, u32[]{:S(2)}, u32[]{:S(2)}) collective-permute-start(bf16[64,4096]{1,0:T(8,128)(2,1)} %bitcast.9), channel_id=1, source_target_pairs={{0,1},{1,0},{2,3},{3,2},{4,5},{5,4},{6,7},{7,6},{8,9},{9,8},{10,11... | collective-permute-start | bytes 1572872 | tf_op jit(solution)/shard_map/ppermute | solution.py:36
  4.1 9.8 %collective-permute-start.7 = (bf16[32,4096]{1,0:T(8,128)(2,1)S(1)}, bf16[32,4096]{1,0:T(8,128)(2,1)S(1)}, u32[]{:S(2)}, u32[]{:S(2)}) collective-permute-start(bf16[32,4096]{1,0:T(8,128)(2,1)S(1)} %get-tuple-element.28), channel_id=1, source_target_pairs={{0,6},{2,0},{4,2},{6,4},{1,7},{3,1},{5,3},{7,5},{8,14},{10,8},{12,... | collective-permute-start | bytes 786440 | tf_op jit(solution)/shard_map/ppermute | solution.py:38
  7.2 10.5 %collective-permute-start.5 = (bf16[32,4096]{1,0:T(8,128)(2,1)S(1)}, bf16[32,4096]{1,0:T(8,128)(2,1)S(1)}, u32[]{:S(2)}, u32[]{:S(2)}) collective-permute-start(bf16[32,4096]{1,0:T(8,128)(2,1)S(1)} %get-tuple-element.27), channel_id=1, source_target_pairs={{0,2},{2,4},{4,6},{6,0},{1,3},{3,5},{5,7},{7,1},{8,10},{10,12},{12... | collective-permute-start | bytes 786440 | tf_op jit(solution)/shard_map/ppermute | solution.py:37
  7.2 16.1 %collective-permute-start.1 = (bf16[32,4096]{1,0:T(8,128)(2,1)S(1)}, bf16[32,4096]{1,0:T(8,128)(2,1)S(1)}, u32[]{:S(2)}, u32[]{:S(2)}) collective-permute-start(bf16[32,4096]{1,0:T(8,128)(2,1)S(1)} %get-tuple-element.28), channel_id=1, source_target_pairs={{0,2},{2,4},{4,6},{6,0},{1,3},{3,5},{5,7},{7,1},{8,10},{10,12},{12... | collective-permute-start | bytes 786440 | tf_op jit(solution)/shard_map/ppermute | solution.py:39
  7.8 15.5 %collective-permute-start.2 = (bf16[32,4096]{1,0:T(8,128)(2,1)S(1)}, bf16[32,4096]{1,0:T(8,128)(2,1)S(1)}, u32[]{:S(2)}, u32[]{:S(2)}) collective-permute-start(bf16[32,4096]{1,0:T(8,128)(2,1)S(1)} %get-tuple-element.27), channel_id=1, source_target_pairs={{0,6},{2,0},{4,2},{6,4},{1,7},{3,1},{5,3},{7,5},{8,14},{10,8},{12,... | collective-permute-start | bytes 786440 | tf_op jit(solution)/shard_map/ppermute | solution.py:40
  13.9 12.6 %collective-permute-start.8 = (bf16[32,4096]{1,0:T(8,128)(2,1)S(1)}, bf16[32,4096]{1,0:T(8,128)(2,1)S(1)}, u32[]{:S(2)}, u32[]{:S(2)}) collective-permute-start(bf16[32,4096]{1,0:T(8,128)(2,1)S(1)} %collective-permute-done.7.refs_5_), channel_id=1, source_target_pairs={{0,6},{2,0},{4,2},{6,4},{1,7},{3,1},{5,3},{7,5},{8,14},{10,8},{12,... | collective-permute-start | bytes 786440 | tf_op jit(solution)/shard_map/ppermute | solution.py:42
  17.6 11.2 %collective-permute-start.6 = (bf16[32,4096]{1,0:T(8,128)(2,1)S(1)}, bf16[32,4096]{1,0:T(8,128)(2,1)S(1)}, u32[]{:S(2)}, u32[]{:S(2)}) collective-permute-start(bf16[32,4096]{1,0:T(8,128)(2,1)S(1)} %collective-permute-done.5.refs_2_), channel_id=1, source_target_pairs={{0,2},{2,4},{4,6},{6,0},{1,3},{3,5},{5,7},{7,1},{8,10},{10,12},{12... | collective-permute-start | bytes 786440 | tf_op jit(solution)/shard_map/ppermute | solution.py:41
  23.3 15.1 %collective-permute-start.3 = (bf16[64,4096]{1,0:T(8,128)(2,1)S(1)}, bf16[64,4096]{1,0:T(8,128)(2,1)S(1)}, u32[]{:S(2)}, u32[]{:S(2)}) collective-permute-start(bf16[64,4096]{1,0:T(8,128)(2,1)S(1)} %collective-permute-done.refs_1_), channel_id=1, source_target_pairs={{0,2},{2,4},{4,6},{6,0},{1,3},{3,5},{5,7},{7,1},{8,10},{10,12},{12... | collective-permute-start | bytes 1572872 | tf_op jit(solution)/shard_map/ppermute | solution.py:44
  23.3 15.1 %collective-permute-start.4 = (bf16[64,4096]{1,0:T(8,128)(2,1)S(1)}, bf16[64,4096]{1,0:T(8,128)(2,1)S(1)}, u32[]{:S(2)}, u32[]{:S(2)}) collective-permute-start(bf16[64,4096]{1,0:T(8,128)(2,1)S(1)} %collective-permute-done.refs_1_), channel_id=1, source_target_pairs={{0,6},{2,0},{4,2},{6,4},{1,7},{3,1},{5,3},{7,5},{8,14},{10,8},{12,... | collective-permute-start | bytes 1572872 | tf_op jit(solution)/shard_map/ppermute | solution.py:45
  26.5 9.2 %collective-permute-start.10 = (bf16[32,4096]{1,0:T(8,128)(2,1)S(1)}, bf16[32,4096]{1,0:T(8,128)(2,1)S(1)}, u32[]{:S(2)}, u32[]{:S(2)}) collective-permute-start(bf16[32,4096]{1,0:T(8,128)(2,1)S(1)} %collective-permute-done.8.refs_3_), channel_id=1, source_target_pairs={{0,1},{1,0},{2,3},{3,2},{4,5},{5,4},{6,7},{7,6},{8,9},{9,8},{10,11... | collective-permute-start | bytes 786440 | tf_op jit(solution)/shard_map/ppermute | solution.py:47
  28.9 9.1 %collective-permute-start.9 = (bf16[32,4096]{1,0:T(8,128)(2,1)S(1)}, bf16[32,4096]{1,0:T(8,128)(2,1)S(1)}, u32[]{:S(2)}, u32[]{:S(2)}) collective-permute-start(bf16[32,4096]{1,0:T(8,128)(2,1)S(1)} %collective-permute-done.6.refs_2_), channel_id=1, source_target_pairs={{0,1},{1,0},{2,3},{3,2},{4,5},{5,4},{6,7},{7,6},{8,9},{9,8},{10,11... | collective-permute-start | bytes 786440 | tf_op jit(solution)/shard_map/ppermute | solution.py:46
  30.0 1.7 %copy-start = (bf16[320,4096]{1,0:T(8,128)(2,1)S(1)}, bf16[320,4096]{1,0:T(8,128)(2,1)}, u32[]{:S(2)}) copy-start(bf16[320,4096]{1,0:T(8,128)(2,1)} %block.1) | copy-start | bytes 7864324
  38.4 35.3 %copy-start.1 = (bf16[320,4096]{1,0:T(8,128)(2,1)S(1)}, bf16[320,4096]{1,0:T(8,128)(2,1)}, u32[]{:S(2)}) copy-start(bf16[320,4096]{1,0:T(8,128)(2,1)} %block.1) | copy-start | bytes 7864324
  39.9 33.8 %copy-start.5 = (s32[4]{0:T(128)S(1)}, s32[4]{0:T(128)}, u32[]{:S(2)}) copy-start(s32[4]{0:T(128)} %leads.1) | copy-start | bytes 52
  39.9 1.3 %collective-permute-start.11 = (f32[64,256]{1,0:T(8,128)S(1)}, f32[64,256]{1,0:T(8,128)S(1)}, u32[]{:S(2)}, u32[]{:S(2)}) collective-permute-start(f32[64,256]{1,0:T(8,128)S(1)} %away.1), channel_id=1, source_target_pairs={{0,8},{8,0},{1,9},{9,1},{2,10},{10,2},{3,11},{11,3},{4,12},{12,4},... | collective-permute-start | bytes 196616 | tf_op jit(solution)/shard_map/ppermute | solution.py:215
  41.2 4.5 %collective-permute-start.12 = (f32[64,256]{1,0:T(8,128)S(1)}, f32[64,256]{1,0:T(8,128)S(1)}, u32[]{:S(2)}, u32[]{:S(2)}) collective-permute-start(f32[64,256]{1,0:T(8,128)S(1)} %add.21), channel_id=1, source_target_pairs={{0,16},{16,0},{1,17},{17,1},{2,18},{18,2},{3,19},{19,3},{4,20},{20... | collective-permute-start | bytes 196616 | tf_op jit(solution)/shard_map/ppermute | solution.py:216
  45.8 5.1 %collective-permute-start.13 = (f32[64,256]{1,0:T(8,128)S(1)}, f32[64,256]{1,0:T(8,128)S(1)}, u32[]{:S(2)}, u32[]{:S(2)}) collective-permute-start(f32[64,256]{1,0:T(8,128)S(1)} %add.22), channel_id=1, source_target_pairs={{0,32},{32,64},{64,96},{96,128},{128,160},{160,192},{192,224},{224... | collective-permute-start | bytes 196616 | tf_op jit(solution)/shard_map/ppermute | solution.py:217
  47.8 4.3 %collective-permute-start.14 = (f32[64,256]{1,0:T(8,128)S(1)}, f32[64,256]{1,0:T(8,128)S(1)}, u32[]{:S(2)}, u32[]{:S(2)}) collective-permute-start(f32[64,256]{1,0:T(8,128)S(1)} %add.22), channel_id=1, source_target_pairs={{0,224},{32,0},{64,32},{96,64},{128,96},{160,128},{192,160},{224,1... | collective-permute-start | bytes 196616 | tf_op jit(solution)/shard_map/ppermute | solution.py:218
  47.9 20.3 %collective-permute-start.19 = (bf16[320,1024]{1,0:T(8,128)(2,1)S(1)}, bf16[320,1024]{1,0:T(8,128)(2,1)S(1)}, u32[]{:S(2)}, u32[]{:S(2)}) collective-permute-start(bf16[320,1024]{1,0:T(8,128)(2,1)S(1)} %get-tuple-element.25), channel_id=1, source_target_pairs={{0,6},{2,0},{4,2},{6,4},{1,7},{3,1},{5,3},{7,5},{8,14},{10,8},{12,... | collective-permute-start | bytes 1966088 | tf_op jit(solution)/shard_map/ppermute | solution.py:268
  50.9 17.3 %collective-permute-start.20 = (bf16[320,1024]{1,0:T(8,128)(2,1)S(1)}, bf16[320,1024]{1,0:T(8,128)(2,1)S(1)}, u32[]{:S(2)}, u32[]{:S(2)}) collective-permute-start(bf16[320,1024]{1,0:T(8,128)(2,1)S(1)} %get-tuple-element.26), channel_id=1, source_target_pairs={{0,2},{2,4},{4,6},{6,0},{1,3},{3,5},{5,7},{7,1},{8,10},{10,12},{12... | collective-permute-start | bytes 1966088 | tf_op jit(solution)/shard_map/ppermute | solution.py:267
  52.1 8.4 %collective-permute-start.15 = (f32[64,256]{1,0:T(8,128)S(1)}, f32[64,256]{1,0:T(8,128)S(1)}, u32[]{:S(2)}, u32[]{:S(2)}) collective-permute-start(f32[64,256]{1,0:T(8,128)S(1)} %get-tuple-element.29), channel_id=1, source_target_pairs={{0,160},{32,192},{64,224},{96,0},{128,32},{160,64},{192,96},{224,1... | collective-permute-start | bytes 196616 | tf_op jit(solution)/shard_map/ppermute | solution.py:220
  57.1 7.8 %collective-permute-start.16 = (f32[64,256]{1,0:T(8,128)S(1)}, f32[64,256]{1,0:T(8,128)S(1)}, u32[]{:S(2)}, u32[]{:S(2)}) collective-permute-start(f32[64,256]{1,0:T(8,128)S(1)} %get-tuple-element.30), channel_id=1, source_target_pairs={{0,96},{32,128},{64,160},{96,192},{128,224},{160,0},{192,32},{224,... | collective-permute-start | bytes 196616 | tf_op jit(solution)/shard_map/ppermute | solution.py:221
  65.2 5.0 %collective-permute-start.17 = (bf16[64,512]{1,0:T(8,128)(2,1)S(1)}, bf16[64,512]{1,0:T(8,128)(2,1)S(1)}, u32[]{:S(2)}, u32[]{:S(2)}) collective-permute-start(bf16[64,512]{1,0:T(8,128)(2,1)S(1)} %weights.1.own), channel_id=1, source_target_pairs={{0,6},{2,0},{4,2},{6,4},{1,7},{3,1},{5,3},{7,5},{8,14},{10,8},{12,... | collective-permute-start | bytes 196616 | tf_op jit(solution)/shard_map/ppermute | solution.py:292
  68.2 5.5 %collective-permute-start.18 = (bf16[64,512]{1,0:T(8,128)(2,1)S(1)}, bf16[64,512]{1,0:T(8,128)(2,1)S(1)}, u32[]{:S(2)}, u32[]{:S(2)}) collective-permute-start(bf16[64,512]{1,0:T(8,128)(2,1)S(1)} %weights.1.own), channel_id=1, source_target_pairs={{0,2},{2,4},{4,6},{6,0},{1,3},{3,5},{5,7},{7,1},{8,10},{10,12},{12... | collective-permute-start | bytes 196616 | tf_op jit(solution)/shard_map/ppermute | solution.py:291
  (3 other events, 2.4 us)

commit v6 on v5

--- a/solution.py
+++ b/solution.py
@@ -28,7 +28,7 @@
     return [(i, (i + by) % n) for i in range(n)]
 
 
-def gather_targets(targets):
+def gather_targets(targets, ready):
     lags, count, width = targets.shape
     own = targets.reshape(lags * count, width)
     half = lags * count // 2
@@ -38,6 +38,7 @@
     above_b = lax.ppermute(late, Y, turn(4, -1))
     below_b = lax.ppermute(late, Y, turn(4, 1))
     above_a = lax.ppermute(early, Y, turn(4, -1))
+    below_a, above_b, ready = lax.optimization_barrier((below_a, above_b, ready))
     far_a = lax.ppermute(below_a, Y, turn(4, 1))
     far_b = lax.ppermute(above_b, Y, turn(4, -1))
     across, below_b, above_a = lax.optimization_barrier((across, below_b, above_a))
@@ -45,7 +46,7 @@
     above_x = lax.ppermute(across, Y, turn(4, -1))
     far_xa = lax.ppermute(far_a, "xh", flip(2, 1))
     far_xb = lax.ppermute(far_b, "xh", flip(2, 1))
-    return (own, across, below_a, below_b, above_a, above_b), (below_x, above_x, far_a, far_b, far_xa, far_xb)
+    return (own, across, below_a, below_b, above_a, above_b), (below_x, above_x, far_a, far_b, far_xa, far_xb), ready
 
 
 def place_on_y():
@@ -211,15 +212,16 @@
             out[:, :, q * quarter + c : q * quarter + c + step] = summed
 
 
-def total_over_space(value):
+def total_over_space(value, arriving):
     value = value + lax.ppermute(value, "co", flip(2, 1))
     value = value + lax.ppermute(value, "xl", flip(2, 1))
     down = lax.ppermute(value, "z", turn(8, 1))
     up = lax.ppermute(value, "z", turn(8, -1))
     three, two = value + down + up, value + up
+    three, two, arriving = lax.optimization_barrier((three, two, arriving))
     high = lax.ppermute(three, "z", turn(8, -3))
     low = lax.ppermute(two, "z", turn(8, 3))
-    return three + high + low
+    return three + high + low, arriving
 
 
 def per_device(targets, library, anchors, leads, spread):
@@ -232,10 +234,8 @@
     scale = math.sqrt(lags * width * lax.axis_size(SPACE))
     quarter = width // 4
 
-    near, away = gather_targets(targets)
-
     n_anchor = anchors.shape[0]
-    lnorm, picks, scales, for_up, for_down = pl.pallas_call(
+    ready = pl.pallas_call(
         functools.partial(prepare_kernel, lags, scale),
         out_shape=(
             jax.ShapeDtypeStruct((8, wide), F32),
@@ -250,6 +250,8 @@
         cost_estimate=pl.CostEstimate(flops=2 * rows * width, bytes_accessed=4 << 20, transcendentals=0),
         name="prepare",
     )(library, anchors.reshape(1, n_anchor), spread.reshape(1, n_target))
+    near, away, ready = gather_targets(targets, ready)
+    lnorm, picks, scales, for_up, for_down = ready
 
     flops = lags * n_target * wide * width
     near_dist = pl.pallas_call(
@@ -278,7 +280,7 @@
         name="away",
     )(*away, library, lnorm, picks, near_dist)
 
-    dist = total_over_space(partial_dist)
+    dist, (block_up, block_down) = total_over_space(partial_dist, (block_up, block_down))
     own = pl.pallas_call(
         weights_kernel,
         out_shape=jax.ShapeDtypeStruct((n_target, wide + 128), BF16),

time: 94.9 us -> 93 us (0.980)
  starting transfers between devices: 33.2 us -> 31.5 us
  blocking collectives: 16.9 us -> 17.9 us
    ppermute x1, waiting for transfers between devices: 5.61 us -> 0.01 us  [gather_targets(): below_b = lax.ppermute(late, Y, turn(4, 1))]
    ppermute x1, waiting for transfers between devices: 0.01 us -> 3.94 us  [total_over_space(): down = lax.ppermute(value, 'z', turn(8, 1))]
    ppermute x1, starting transfers between devices: 5.02 us -> 1.82 us  [total_over_space(): high = lax.ppermute(three, 'z', turn(8, -3))]
    ppermute x1, waiting for transfers between devices: 3.48 us -> 0.38 us  [gather_targets(): above_b = lax.ppermute(late, Y, turn(4, -1))]
    ppermute x1, waiting for transfers between devices: 0.01 us -> 2.57 us  [gather_targets(): far_xb = lax.ppermute(far_b, 'xh', flip(2, 1))]
    ppermute x1, waiting for transfers between devices: 0.01 us -> 2.38 us  [gather_targets(): above_a = lax.ppermute(early, Y, turn(4, -1))]
    ppermute x1, starting transfers between devices: 1.09 us -> 3.29 us  [total_over_space(): low = lax.ppermute(two, 'z', turn(8, 3))]
    ppermute x1, starting transfers between devices: 3.69 us -> 1.66 us  [gather_targets(): far_b = lax.ppermute(above_b, Y, turn(4, -1))]
  transfers between devices with their start and end apart: 21 -> 21, of which waited for: 12 -> 14; matrix products, arithmetic and copies ran while one was open for 1% -> 1% of each run, Pallas kernels for 3% -> 4%
where the time goes in v6:
time: 93 us; the launch traced here: 92.8 us
  starting transfers between devices  31.5 us (34%)
  waiting for transfers between devices  31.4 us (34%)
  blocking collectives  17.9 us (19%)
  Pallas kernels  7.77 us (8%)
  local copies, waits for them, and re-layouts  4.15 us (4%)
    all_to_all x1, blocking collectives, per_device(): parts = lax.all_to_all(parts, LIB, 0, 0, tiled=True)  17.9 us
    ppermute x1, waiting for transfers between devices, total_over_space(): down = lax.ppermute(value, 'z', turn(8, 1))  3.94 us
    ppermute x1, waiting for transfers between devices, total_over_space(): value = value + lax.ppermute(value, 'xl', flip(2, 1))  3.67 us
    ppermute x1, waiting for transfers between devices, total_over_space(): low = lax.ppermute(two, 'z', turn(8, 3))  3.6 us
    ppermute x1, starting transfers between devices, total_over_space(): low = lax.ppermute(two, 'z', turn(8, 3))  3.29 us
    unnamed x12, local copies, waits for them, and re-layouts  3.08 us
    ppermute x1, starting transfers between devices, gather_targets(): across = lax.ppermute(own, 'xh', flip(2, 1))  3.02 us
    ppermute x1, waiting for transfers between devices, gather_targets(): far_xa = lax.ppermute(far_a, 'xh', flip(2, 1))  2.88 us
  transfers between devices with their start and end apart: 21, of which 14 were waited for; matrix products, arithmetic and copies ran while one was open for 1% of the time, Pallas kernels for 4%

profile of v6, /device:TPU:32, one launch (start us, length us, event | category | flops | bytes accessed | tf_op | source)
XLA Modules:
  0.0 92.8 jit_solution(279710323687582144)
XLA Ops:
  0.0 3.0 %collective-permute-start = (bf16[64,4096]{1,0:T(8,128)(2,1)}, bf16[64,4096]{1,0:T(8,128)(2,1)S(1)}, u32[]{:S(2)}, u32[]{:S(2)}) collective-permute-start(bf16[64,4096]{1,0:T(8,128)(2,1)} %bitcast.9), channel_id=1, source_target_pairs={{0,1},{1,0},{2,3},{3,2},{4,5},{5,4},{6,7},{7,6},{8,9},{9,8},{10,11... | collective-permute-start | bytes 1572872 | tf_op jit(solution)/shard_map/ppermute | solution.py:36
  4.1 1.7 %collective-permute-start.5 = (bf16[32,4096]{1,0:T(8,128)(2,1)S(1)}, bf16[32,4096]{1,0:T(8,128)(2,1)S(1)}, u32[]{:S(2)}, u32[]{:S(2)}) collective-permute-start(bf16[32,4096]{1,0:T(8,128)(2,1)S(1)} %get-tuple-element.49), channel_id=1, source_target_pairs={{0,2},{2,4},{4,6},{6,0},{1,3},{3,5},{5,7},{7,1},{8,10},{10,12},{12... | collective-permute-start | bytes 786440 | tf_op jit(solution)/shard_map/ppermute | solution.py:37
  5.7 1.7 %collective-permute-start.6 = (bf16[32,4096]{1,0:T(8,128)(2,1)S(1)}, bf16[32,4096]{1,0:T(8,128)(2,1)S(1)}, u32[]{:S(2)}, u32[]{:S(2)}) collective-permute-start(bf16[32,4096]{1,0:T(8,128)(2,1)S(1)} %get-tuple-element.50), channel_id=1, source_target_pairs={{0,6},{2,0},{4,2},{6,4},{1,7},{3,1},{5,3},{7,5},{8,14},{10,8},{12,... | collective-permute-start | bytes 786440 | tf_op jit(solution)/shard_map/ppermute | solution.py:38
  7.4 1.8 %collective-permute-start.2 = (bf16[32,4096]{1,0:T(8,128)(2,1)S(1)}, bf16[32,4096]{1,0:T(8,128)(2,1)S(1)}, u32[]{:S(2)}, u32[]{:S(2)}) collective-permute-start(bf16[32,4096]{1,0:T(8,128)(2,1)S(1)} %get-tuple-element.49), channel_id=1, source_target_pairs={{0,6},{2,0},{4,2},{6,4},{1,7},{3,1},{5,3},{7,5},{8,14},{10,8},{12,... | collective-permute-start | bytes 786440 | tf_op jit(solution)/shard_map/ppermute | solution.py:40
  9.4 1.7 %copy-done = bf16[320,4096]{1,0:T(8,128)(2,1)S(1)} copy-done((bf16[320,4096]{1,0:T(8,128)(2,1)S(1)}, bf16[320,4096]{1,0:T(8,128)(2,1)}, u32[]{:S(2)}) %copy-start) | copy-done | bytes 2621464
  16.6 1.7 %collective-permute-start.8 = (bf16[32,4096]{1,0:T(8,128)(2,1)S(1)}, bf16[32,4096]{1,0:T(8,128)(2,1)S(1)}, u32[]{:S(2)}, u32[]{:S(2)}) collective-permute-start(bf16[32,4096]{1,0:T(8,128)(2,1)S(1)} %collective-permute-done.6.refs_5_), channel_id=1, source_target_pairs={{0,6},{2,0},{4,2},{6,4},{1,7},{3,1},{5,3},{7,5},{8,14},{10,8},{12,... | collective-permute-start | bytes 786440 | tf_op jit(solution)/shard_map/ppermute | solution.py:43
  18.2 2.4 %collective-permute-done.2.refs_4_ = bf16[32,4096]{1,0:T(8,128)(2,1)S(1)} collective-permute-done((bf16[32,4096]{1,0:T(8,128)(2,1)S(1)}, bf16[32,4096]{1,0:T(8,128)(2,1)S(1)}, u32[]{:S(2)}, u32[]{:S(2)}) %collective-permute-start.2) | collective-permute-done | bytes 262176 | tf_op jit(solution)/shard_map/ppermute | solution.py:40
  20.6 2.9 %collective-permute-start.4 = (bf16[64,4096]{1,0:T(8,128)(2,1)S(1)}, bf16[64,4096]{1,0:T(8,128)(2,1)S(1)}, u32[]{:S(2)}, u32[]{:S(2)}) collective-permute-start(bf16[64,4096]{1,0:T(8,128)(2,1)S(1)} %collective-permute-done.refs_1_), channel_id=1, source_target_pairs={{0,6},{2,0},{4,2},{6,4},{1,7},{3,1},{5,3},{7,5},{8,14},{10,8},{12,... | collective-permute-start | bytes 1572872 | tf_op jit(solution)/shard_map/ppermute | solution.py:46
  26.2 2.2 %collective-permute-start.10 = (bf16[32,4096]{1,0:T(8,128)(2,1)S(1)}, bf16[32,4096]{1,0:T(8,128)(2,1)S(1)}, u32[]{:S(2)}, u32[]{:S(2)}) collective-permute-start(bf16[32,4096]{1,0:T(8,128)(2,1)S(1)} %collective-permute-done.8.refs_3_), channel_id=1, source_target_pairs={{0,1},{1,0},{2,3},{3,2},{4,5},{5,4},{6,7},{7,6},{8,9},{9,8},{10,11... | collective-permute-start | bytes 786440 | tf_op jit(solution)/shard_map/ppermute | solution.py:48
  30.0 2.8 %collective-permute-start.15 = (bf16[320,1024]{1,0:T(8,128)(2,1)S(1)}, bf16[320,1024]{1,0:T(8,128)(2,1)S(1)}, u32[]{:S(2)}, u32[]{:S(2)}) collective-permute-start(bf16[320,1024]{1,0:T(8,128)(2,1)S(1)} %get-tuple-element.42), channel_id=1, source_target_pairs={{0,6},{2,0},{4,2},{6,4},{1,7},{3,1},{5,3},{7,5},{8,14},{10,8},{12,... | collective-permute-start | bytes 1966088 | tf_op jit(solution)/shard_map/ppermute | solution.py:270
  32.8 2.9 %collective-permute-done.9.refs_4_ = bf16[32,4096]{1,0:T(8,128)(2,1)S(1)} collective-permute-done((bf16[32,4096]{1,0:T(8,128)(2,1)S(1)}, bf16[32,4096]{1,0:T(8,128)(2,1)S(1)}, u32[]{:S(2)}, u32[]{:S(2)}) %collective-permute-start.9) | collective-permute-done | bytes 262176 | tf_op jit(solution)/shard_map/ppermute | solution.py:47
  35.9 2.6 %collective-permute-done.10.refs_5_ = bf16[32,4096]{1,0:T(8,128)(2,1)S(1)} collective-permute-done((bf16[32,4096]{1,0:T(8,128)(2,1)S(1)}, bf16[32,4096]{1,0:T(8,128)(2,1)S(1)}, u32[]{:S(2)}, u32[]{:S(2)}) %collective-permute-start.10) | collective-permute-done | bytes 262176 | tf_op jit(solution)/shard_map/ppermute | solution.py:48
  42.1 3.7 %collective-permute-done.12 = f32[64,256]{1,0:T(8,128)S(1)} collective-permute-done((f32[64,256]{1,0:T(8,128)S(1)}, f32[64,256]{1,0:T(8,128)S(1)}, u32[]{:S(2)}, u32[]{:S(2)}) %collective-permute-start.12) | collective-permute-done | bytes 65568 | tf_op jit(solution)/shard_map/ppermute | solution.py:217
  45.9 1.9 %collective-permute-start.13 = (f32[64,256]{1,0:T(8,128)S(1)}, f32[64,256]{1,0:T(8,128)S(1)}, u32[]{:S(2)}, u32[]{:S(2)}) collective-permute-start(f32[64,256]{1,0:T(8,128)S(1)} %add.22), channel_id=1, source_target_pairs={{0,32},{32,64},{64,96},{96,128},{128,160},{160,192},{192,224},{224... | collective-permute-start | bytes 196616 | tf_op jit(solution)/shard_map/ppermute | solution.py:218
  47.9 2.2 %collective-permute-done.14 = f32[64,256]{1,0:T(8,128)S(1)} collective-permute-done((f32[64,256]{1,0:T(8,128)S(1)}, f32[64,256]{1,0:T(8,128)S(1)}, u32[]{:S(2)}, u32[]{:S(2)}) %collective-permute-start.14) | collective-permute-done | bytes 65568 | tf_op jit(solution)/shard_map/ppermute | solution.py:219
  50.1 3.9 %collective-permute-done.13 = f32[64,256]{1,0:T(8,128)S(1)} collective-permute-done((f32[64,256]{1,0:T(8,128)S(1)}, f32[64,256]{1,0:T(8,128)S(1)}, u32[]{:S(2)}, u32[]{:S(2)}) %collective-permute-start.13) | collective-permute-done | bytes 65568 | tf_op jit(solution)/shard_map/ppermute | solution.py:218
  54.1 3.3 %collective-permute-start.18 = (f32[64,256]{1,0:T(8,128)S(1)}, f32[64,256]{1,0:T(8,128)S(1)}, u32[]{:S(2)}, u32[]{:S(2)}) collective-permute-start(f32[64,256]{1,0:T(8,128)S(1)} %get-tuple-element.45), channel_id=1, source_target_pairs={{0,96},{32,128},{64,160},{96,192},{128,224},{160,0},{192,32},{224,... | collective-permute-start | bytes 196616 | tf_op jit(solution)/shard_map/ppermute | solution.py:223
  57.4 1.8 %collective-permute-start.17 = (f32[64,256]{1,0:T(8,128)S(1)}, f32[64,256]{1,0:T(8,128)S(1)}, u32[]{:S(2)}, u32[]{:S(2)}) collective-permute-start(f32[64,256]{1,0:T(8,128)S(1)} %get-tuple-element.44), channel_id=1, source_target_pairs={{0,160},{32,192},{64,224},{96,0},{128,32},{160,64},{192,96},{224,1... | collective-permute-start | bytes 196616 | tf_op jit(solution)/shard_map/ppermute | solution.py:222
  59.2 3.6 %collective-permute-done.18 = f32[64,256]{1,0:T(8,128)S(1)} collective-permute-done((f32[64,256]{1,0:T(8,128)S(1)}, f32[64,256]{1,0:T(8,128)S(1)}, u32[]{:S(2)}, u32[]{:S(2)}) %collective-permute-start.18) | collective-permute-done | bytes 65568 | tf_op jit(solution)/shard_map/ppermute | solution.py:223
  62.8 2.6 %collective-permute-done.17 = f32[64,256]{1,0:T(8,128)S(1)} collective-permute-done((f32[64,256]{1,0:T(8,128)S(1)}, f32[64,256]{1,0:T(8,128)S(1)}, u32[]{:S(2)}, u32[]{:S(2)}) %collective-permute-start.17) | collective-permute-done | bytes 65568 | tf_op jit(solution)/shard_map/ppermute | solution.py:222
  66.4 2.7 %collective-permute-start.19 = (bf16[64,512]{1,0:T(8,128)(2,1)S(1)}, bf16[64,512]{1,0:T(8,128)(2,1)S(1)}, u32[]{:S(2)}, u32[]{:S(2)}) collective-permute-start(bf16[64,512]{1,0:T(8,128)(2,1)S(1)} %weights.1.own), channel_id=1, source_target_pairs={{0,6},{2,0},{4,2},{6,4},{1,7},{3,1},{5,3},{7,5},{8,14},{10,8},{12,... | collective-permute-start | bytes 196616 | tf_op jit(solution)/shard_map/ppermute | solution.py:294
  69.1 2.2 %collective-permute-done.20.down = bf16[64,512]{1,0:T(8,128)(2,1)S(1)} collective-permute-done((bf16[64,512]{1,0:T(8,128)(2,1)S(1)}, bf16[64,512]{1,0:T(8,128)(2,1)S(1)}, u32[]{:S(2)}, u32[]{:S(2)}) %collective-permute-start.20) | collective-permute-done | bytes 65568 | tf_op jit(solution)/shard_map/ppermute | solution.py:293
  71.3 2.4 %compose.1 = bf16[256,2176]{1,0:T(8,128)(2,1)S(1)} custom-call(s32[4]{0:T(128)S(1)} %copy-done.5, bf16[64,512]{1,0:T(8,128)(2,1)S(1)} %weights.1.own, bf16[64,512]{1,0:T(8,128)(2,1)S(1)} %collective-permute-done.19.up, bf16[64,512]{1,0:T(8,128)(2,1)S(1)} %collective-permute-done.20.down, bf16[320,4096]{1,0:T(8,128)(2,1)S(1)} %copy-done.1, ...), custom_call_target="tpu_custom_call" | custom-call | flops 671088640 | bytes 5242880 | tf_op jit(solution)/shard_map/compose/pallas_call | solution.py:296
  73.7 17.9 %all_to_all.5.parts = bf16[8,32,2176]{2,1,0:T(8,128)(2,1)S(1)} all-to-all(bf16[8,32,2176]{2,1,0:T(8,128)(2,1)S(1)} %bitcast.8), channel_id=1, replica_groups=mesh['z'=8,'xl'=2,'co'=2,'yh'=2,'yl'=2,'xh'=2] {'yh','yl','xh'}, dimensions={0} | all-to-all | bytes 2228224 | tf_op jit(solution)/shard_map/all_to_all | solution.py:307
  (42 shorter events, 17.1 us)
Async XLA Ops:
  0.0 20.6 %collective-permute-start = (bf16[64,4096]{1,0:T(8,128)(2,1)}, bf16[64,4096]{1,0:T(8,128)(2,1)S(1)}, u32[]{:S(2)}, u32[]{:S(2)}) collective-permute-start(bf16[64,4096]{1,0:T(8,128)(2,1)} %bitcast.9), channel_id=1, source_target_pairs={{0,1},{1,0},{2,3},{3,2},{4,5},{5,4},{6,7},{7,6},{8,9},{9,8},{10,11... | collective-permute-start | bytes 1572872 | tf_op jit(solution)/shard_map/ppermute | solution.py:36
  4.1 10.5 %collective-permute-start.5 = (bf16[32,4096]{1,0:T(8,128)(2,1)S(1)}, bf16[32,4096]{1,0:T(8,128)(2,1)S(1)}, u32[]{:S(2)}, u32[]{:S(2)}) collective-permute-start(bf16[32,4096]{1,0:T(8,128)(2,1)S(1)} %get-tuple-element.49), channel_id=1, source_target_pairs={{0,2},{2,4},{4,6},{6,0},{1,3},{3,5},{5,7},{7,1},{8,10},{10,12},{12... | collective-permute-start | bytes 786440 | tf_op jit(solution)/shard_map/ppermute | solution.py:37
  5.7 9.2 %collective-permute-start.6 = (bf16[32,4096]{1,0:T(8,128)(2,1)S(1)}, bf16[32,4096]{1,0:T(8,128)(2,1)S(1)}, u32[]{:S(2)}, u32[]{:S(2)}) collective-permute-start(bf16[32,4096]{1,0:T(8,128)(2,1)S(1)} %get-tuple-element.50), channel_id=1, source_target_pairs={{0,6},{2,0},{4,2},{6,4},{1,7},{3,1},{5,3},{7,5},{8,14},{10,8},{12,... | collective-permute-start | bytes 786440 | tf_op jit(solution)/shard_map/ppermute | solution.py:38
  7.4 13.2 %collective-permute-start.2 = (bf16[32,4096]{1,0:T(8,128)(2,1)S(1)}, bf16[32,4096]{1,0:T(8,128)(2,1)S(1)}, u32[]{:S(2)}, u32[]{:S(2)}) collective-permute-start(bf16[32,4096]{1,0:T(8,128)(2,1)S(1)} %get-tuple-element.49), channel_id=1, source_target_pairs={{0,6},{2,0},{4,2},{6,4},{1,7},{3,1},{5,3},{7,5},{8,14},{10,8},{12,... | collective-permute-start | bytes 786440 | tf_op jit(solution)/shard_map/ppermute | solution.py:40
  9.2 11.4 %collective-permute-start.1 = (bf16[32,4096]{1,0:T(8,128)(2,1)S(1)}, bf16[32,4096]{1,0:T(8,128)(2,1)S(1)}, u32[]{:S(2)}, u32[]{:S(2)}) collective-permute-start(bf16[32,4096]{1,0:T(8,128)(2,1)S(1)} %get-tuple-element.50), channel_id=1, source_target_pairs={{0,2},{2,4},{4,6},{6,0},{1,3},{3,5},{5,7},{7,1},{8,10},{10,12},{12... | collective-permute-start | bytes 786440 | tf_op jit(solution)/shard_map/ppermute | solution.py:39
  12.5 15.9 %copy-start.2 = (bf16[8,8,4096]{2,1,0:T(8,128)(2,1)S(1)}, bf16[8,8,4096]{2,1,0:T(8,128)(2,1)}, u32[]{:S(2)}) copy-start(bf16[8,8,4096]{2,1,0:T(8,128)(2,1)} %param.5) | copy-start | bytes 1572868
  15.0 9.9 %collective-permute-start.7 = (bf16[32,4096]{1,0:T(8,128)(2,1)S(1)}, bf16[32,4096]{1,0:T(8,128)(2,1)S(1)}, u32[]{:S(2)}, u32[]{:S(2)}) collective-permute-start(bf16[32,4096]{1,0:T(8,128)(2,1)S(1)} %collective-permute-done.5.refs_2_), channel_id=1, source_target_pairs={{0,2},{2,4},{4,6},{6,0},{1,3},{3,5},{5,7},{7,1},{8,10},{10,12},{12... | collective-permute-start | bytes 786440 | tf_op jit(solution)/shard_map/ppermute | solution.py:42
  16.6 9.7 %collective-permute-start.8 = (bf16[32,4096]{1,0:T(8,128)(2,1)S(1)}, bf16[32,4096]{1,0:T(8,128)(2,1)S(1)}, u32[]{:S(2)}, u32[]{:S(2)}) collective-permute-start(bf16[32,4096]{1,0:T(8,128)(2,1)S(1)} %collective-permute-done.6.refs_5_), channel_id=1, source_target_pairs={{0,6},{2,0},{4,2},{6,4},{1,7},{3,1},{5,3},{7,5},{8,14},{10,8},{12,... | collective-permute-start | bytes 786440 | tf_op jit(solution)/shard_map/ppermute | solution.py:43
  20.6 17.9 %collective-permute-start.4 = (bf16[64,4096]{1,0:T(8,128)(2,1)S(1)}, bf16[64,4096]{1,0:T(8,128)(2,1)S(1)}, u32[]{:S(2)}, u32[]{:S(2)}) collective-permute-start(bf16[64,4096]{1,0:T(8,128)(2,1)S(1)} %collective-permute-done.refs_1_), channel_id=1, source_target_pairs={{0,6},{2,0},{4,2},{6,4},{1,7},{3,1},{5,3},{7,5},{8,14},{10,8},{12,... | collective-permute-start | bytes 1572872 | tf_op jit(solution)/shard_map/ppermute | solution.py:46
  23.5 15.0 %collective-permute-start.3 = (bf16[64,4096]{1,0:T(8,128)(2,1)S(1)}, bf16[64,4096]{1,0:T(8,128)(2,1)S(1)}, u32[]{:S(2)}, u32[]{:S(2)}) collective-permute-start(bf16[64,4096]{1,0:T(8,128)(2,1)S(1)} %collective-permute-done.refs_1_), channel_id=1, source_target_pairs={{0,2},{2,4},{4,6},{6,0},{1,3},{3,5},{5,7},{7,1},{8,10},{10,12},{12... | collective-permute-start | bytes 1572872 | tf_op jit(solution)/shard_map/ppermute | solution.py:45
  24.9 10.7 %collective-permute-start.9 = (bf16[32,4096]{1,0:T(8,128)(2,1)S(1)}, bf16[32,4096]{1,0:T(8,128)(2,1)S(1)}, u32[]{:S(2)}, u32[]{:S(2)}) collective-permute-start(bf16[32,4096]{1,0:T(8,128)(2,1)S(1)} %collective-permute-done.7.refs_2_), channel_id=1, source_target_pairs={{0,1},{1,0},{2,3},{3,2},{4,5},{5,4},{6,7},{7,6},{8,9},{9,8},{10,11... | collective-permute-start | bytes 786440 | tf_op jit(solution)/shard_map/ppermute | solution.py:47
  26.2 12.3 %collective-permute-start.10 = (bf16[32,4096]{1,0:T(8,128)(2,1)S(1)}, bf16[32,4096]{1,0:T(8,128)(2,1)S(1)}, u32[]{:S(2)}, u32[]{:S(2)}) collective-permute-start(bf16[32,4096]{1,0:T(8,128)(2,1)S(1)} %collective-permute-done.8.refs_3_), channel_id=1, source_target_pairs={{0,1},{1,0},{2,3},{3,2},{4,5},{5,4},{6,7},{7,6},{8,9},{9,8},{10,11... | collective-permute-start | bytes 786440 | tf_op jit(solution)/shard_map/ppermute | solution.py:48
  30.0 24.0 %collective-permute-start.15 = (bf16[320,1024]{1,0:T(8,128)(2,1)S(1)}, bf16[320,1024]{1,0:T(8,128)(2,1)S(1)}, u32[]{:S(2)}, u32[]{:S(2)}) collective-permute-start(bf16[320,1024]{1,0:T(8,128)(2,1)S(1)} %get-tuple-element.42), channel_id=1, source_target_pairs={{0,6},{2,0},{4,2},{6,4},{1,7},{3,1},{5,3},{7,5},{8,14},{10,8},{12,... | collective-permute-start | bytes 1966088 | tf_op jit(solution)/shard_map/ppermute | solution.py:270
  35.7 18.4 %collective-permute-start.16 = (bf16[320,1024]{1,0:T(8,128)(2,1)S(1)}, bf16[320,1024]{1,0:T(8,128)(2,1)S(1)}, u32[]{:S(2)}, u32[]{:S(2)}) collective-permute-start(bf16[320,1024]{1,0:T(8,128)(2,1)S(1)} %get-tuple-element.43), channel_id=1, source_target_pairs={{0,2},{2,4},{4,6},{6,0},{1,3},{3,5},{5,7},{7,1},{8,10},{10,12},{12... | collective-permute-start | bytes 1966088 | tf_op jit(solution)/shard_map/ppermute | solution.py:269
  38.5 32.8 %copy-start.1 = (bf16[320,4096]{1,0:T(8,128)(2,1)S(1)}, bf16[320,4096]{1,0:T(8,128)(2,1)}, u32[]{:S(2)}) copy-start(bf16[320,4096]{1,0:T(8,128)(2,1)} %block.1) | copy-start | bytes 7864324
  40.1 31.2 %copy-start.5 = (s32[4]{0:T(128)S(1)}, s32[4]{0:T(128)}, u32[]{:S(2)}) copy-start(s32[4]{0:T(128)} %leads.1) | copy-start | bytes 52
  40.1 1.3 %collective-permute-start.11 = (f32[64,256]{1,0:T(8,128)S(1)}, f32[64,256]{1,0:T(8,128)S(1)}, u32[]{:S(2)}, u32[]{:S(2)}) collective-permute-start(f32[64,256]{1,0:T(8,128)S(1)} %away.1), channel_id=1, source_target_pairs={{0,8},{8,0},{1,9},{9,1},{2,10},{10,2},{3,11},{11,3},{4,12},{12,4},... | collective-permute-start | bytes 196616 | tf_op jit(solution)/shard_map/ppermute | solution.py:216
  41.4 4.4 %collective-permute-start.12 = (f32[64,256]{1,0:T(8,128)S(1)}, f32[64,256]{1,0:T(8,128)S(1)}, u32[]{:S(2)}, u32[]{:S(2)}) collective-permute-start(f32[64,256]{1,0:T(8,128)S(1)} %add.21), channel_id=1, source_target_pairs={{0,16},{16,0},{1,17},{17,1},{2,18},{18,2},{3,19},{19,3},{4,20},{20... | collective-permute-start | bytes 196616 | tf_op jit(solution)/shard_map/ppermute | solution.py:217
  45.8 4.3 %collective-permute-start.14 = (f32[64,256]{1,0:T(8,128)S(1)}, f32[64,256]{1,0:T(8,128)S(1)}, u32[]{:S(2)}, u32[]{:S(2)}) collective-permute-start(f32[64,256]{1,0:T(8,128)S(1)} %add.22), channel_id=1, source_target_pairs={{0,224},{32,0},{64,32},{96,64},{128,96},{160,128},{192,160},{224,1... | collective-permute-start | bytes 196616 | tf_op jit(solution)/shard_map/ppermute | solution.py:219
  45.9 8.1 %collective-permute-start.13 = (f32[64,256]{1,0:T(8,128)S(1)}, f32[64,256]{1,0:T(8,128)S(1)}, u32[]{:S(2)}, u32[]{:S(2)}) collective-permute-start(f32[64,256]{1,0:T(8,128)S(1)} %add.22), channel_id=1, source_target_pairs={{0,32},{32,64},{64,96},{96,128},{128,160},{160,192},{192,224},{224... | collective-permute-start | bytes 196616 | tf_op jit(solution)/shard_map/ppermute | solution.py:218
  54.1 8.7 %collective-permute-start.18 = (f32[64,256]{1,0:T(8,128)S(1)}, f32[64,256]{1,0:T(8,128)S(1)}, u32[]{:S(2)}, u32[]{:S(2)}) collective-permute-start(f32[64,256]{1,0:T(8,128)S(1)} %get-tuple-element.45), channel_id=1, source_target_pairs={{0,96},{32,128},{64,160},{96,192},{128,224},{160,0},{192,32},{224,... | collective-permute-start | bytes 196616 | tf_op jit(solution)/shard_map/ppermute | solution.py:223
  57.4 8.1 %collective-permute-start.17 = (f32[64,256]{1,0:T(8,128)S(1)}, f32[64,256]{1,0:T(8,128)S(1)}, u32[]{:S(2)}, u32[]{:S(2)}) collective-permute-start(f32[64,256]{1,0:T(8,128)S(1)} %get-tuple-element.44), channel_id=1, source_target_pairs={{0,160},{32,192},{64,224},{96,0},{128,32},{160,64},{192,96},{224,1... | collective-permute-start | bytes 196616 | tf_op jit(solution)/shard_map/ppermute | solution.py:222
  65.8 5.6 %collective-permute-start.20 = (bf16[64,512]{1,0:T(8,128)(2,1)S(1)}, bf16[64,512]{1,0:T(8,128)(2,1)S(1)}, u32[]{:S(2)}, u32[]{:S(2)}) collective-permute-start(bf16[64,512]{1,0:T(8,128)(2,1)S(1)} %weights.1.own), channel_id=1, source_target_pairs={{0,2},{2,4},{4,6},{6,0},{1,3},{3,5},{5,7},{7,1},{8,10},{10,12},{12... | collective-permute-start | bytes 196616 | tf_op jit(solution)/shard_map/ppermute | solution.py:293
  66.4 4.9 %collective-permute-start.19 = (bf16[64,512]{1,0:T(8,128)(2,1)S(1)}, bf16[64,512]{1,0:T(8,128)(2,1)S(1)}, u32[]{:S(2)}, u32[]{:S(2)}) collective-permute-start(bf16[64,512]{1,0:T(8,128)(2,1)S(1)} %weights.1.own), channel_id=1, source_target_pairs={{0,6},{2,0},{4,2},{6,4},{1,7},{3,1},{5,3},{7,5},{8,14},{10,8},{12,... | collective-permute-start | bytes 196616 | tf_op jit(solution)/shard_map/ppermute | solution.py:294
  (3 other events, 3.1 us)

commit v7 on v6

--- a/solution.py
+++ b/solution.py
@@ -156,37 +156,47 @@
     return value
 
 
-def compose_kernel(leads, own, up, down, block, block_up, block_down, out):
-    rows, quarter = block_up.shape
-    targets, wide = own.shape[0], own.shape[1] - 128
+def mixing(leads, w, rows):
+    targets, wide = w.shape[0], w.shape[1] - 128
     count = leads.shape[0]
-    odd = lax.axis_index("yl")
     shape = (count * targets, count * targets)
     row, col = lax.broadcasted_iota(jnp.int32, shape, 0), lax.broadcasted_iota(jnp.int32, shape, 1)
     perm = jnp.where(lax.rem(row, count) * targets + lax.div(row, count) == col, 1.0, 0.0).astype(BF16)
-    mixed, facts = [], []
-    for w in (own, up, down):
-        weights = w[:, :wide].astype(F32)
-        stack = jnp.concatenate([pltpu.roll(weights, leads[k], 1) for k in range(count)], axis=0).astype(BF16)
-        mixed.append(jnp.dot(perm, stack, preferred_element_type=F32).astype(BF16)[:, :rows])
-        fact = jnp.concatenate([w[:, wide:]] * count, axis=0)
-        facts.append(jnp.dot(perm, fact, preferred_element_type=F32))
-    tops = [f[:, 0:1] + f[:, 1:2] for f in facts]
-    totals = [f[:, 2:3] + f[:, 3:4] for f in facts]
+    weights = w[:, :wide].astype(F32)
+    stack = jnp.concatenate([pltpu.roll(weights, leads[k], 1) for k in range(count)], axis=0).astype(BF16)
+    mixed = jnp.dot(perm, stack, preferred_element_type=F32).astype(BF16)[:, :rows]
+    fact = jnp.concatenate([w[:, wide:]] * count, axis=0)
+    return mixed, jnp.dot(perm, fact, preferred_element_type=F32)
+
+
+def compose_own_kernel(leads, own, block, out, facts):
+    rows = block.shape[0]
+    quarter = out.shape[1] // 2
+    mixed, facts[...] = mixing(leads, own, rows)
+    odd = lax.axis_index("yl")
+    for side, start in enumerate((2 * odd, 3 - 2 * odd)):
+        mine = block[:, pl.ds(pl.multiple_of(start * quarter, quarter), quarter)]
+        out[:, side * quarter : (side + 1) * quarter] = jnp.dot(mixed, mine, preferred_element_type=F32)
+
+
+def compose_kernel(leads, partial, own_facts, up, down, block_up, block_down, out):
+    rows, quarter = block_up.shape
+    fact = own_facts[...]
     step = 512
     columns = []
-    for side, (other, start) in enumerate(((block_up, 2 * odd), (block_down, 3 - 2 * odd))):
-        i = side + 1
-        larger = tops[0] >= tops[i]
-        top = jnp.where(larger, tops[0], tops[i])
-        first, second = jnp.exp(tops[0] - top), jnp.exp(tops[i] - top)
-        columns += [jnp.where(larger, facts[0][:, j : j + 1], facts[i][:, j : j + 1]) for j in range(2)]
-        columns += halves(first * totals[0] + second * totals[i])
+    for side, (w, other) in enumerate(((up, block_up), (down, block_down))):
+        mixed, there = mixing(leads, w, rows)
+        tops = [f[:, 0:1] + f[:, 1:2] for f in (fact, there)]
+        totals = [f[:, 2:3] + f[:, 3:4] for f in (fact, there)]
+        larger = tops[0] >= tops[1]
+        top = jnp.where(larger, tops[0], tops[1])
+        first, second = jnp.exp(tops[0] - top), jnp.exp(tops[1] - top)
+        columns += [jnp.where(larger, fact[:, j : j + 1], there[:, j : j + 1]) for j in range(2)]
+        columns += halves(first * totals[0] + second * totals[1])
         for c in range(0, quarter, step):
-            mine = block[:, pl.ds(pl.multiple_of(start * quarter + c, step), step)]
-            value = first * jnp.dot(mixed[0], mine, preferred_element_type=F32)
-            value = value + second * jnp.dot(mixed[i], other[:, c : c + step], preferred_element_type=F32)
-            out[:, side * quarter + c : side * quarter + c + step] = value.astype(BF16)
+            at = side * quarter + c
+            value = second * jnp.dot(mixed, other[:, c : c + step], preferred_element_type=F32)
+            out[:, at : at + step] = (value + first * partial[:, at : at + step]).astype(BF16)
     out[:, 2 * quarter :] = in_lanes(columns).astype(BF16)
 
 
@@ -214,14 +224,13 @@
 
 def total_over_space(value, arriving):
     value = value + lax.ppermute(value, "co", flip(2, 1))
-    value = value + lax.ppermute(value, "xl", flip(2, 1))
-    down = lax.ppermute(value, "z", turn(8, 1))
-    up = lax.ppermute(value, "z", turn(8, -1))
-    three, two = value + down + up, value + up
-    three, two, arriving = lax.optimization_barrier((three, two, arriving))
-    high = lax.ppermute(three, "z", turn(8, -3))
-    low = lax.ppermute(two, "z", turn(8, 3))
-    return three + high + low, arriving
+    both = [(z * 2 + x, (z ^ 1) * 2 + (x ^ 1)) for z in range(8) for x in range(2)]
+    value = (value + lax.ppermute(value, ("z", "xl"), both)) + (lax.ppermute(value, "z", flip(8, 1)) + lax.ppermute(value, "xl", flip(2, 1)))
+    value, arriving = lax.optimization_barrier((value, arriving))
+    three = lax.ppermute(value, "z", [(z, (z - 3) % 8 if z % 2 == 0 else (z + 3) % 8) for z in range(8)])
+    two = lax.ppermute(value, "z", [(z, (z - 2) % 8 if z % 2 == 0 else (z + 2) % 8) for z in range(8)])
+    one = lax.ppermute(value, "z", [(z, (z - 1) % 8 if z % 2 == 0 else (z + 1) % 8) for z in range(8)])
+    return value + one + two + three, arriving
 
 
 def per_device(targets, library, anchors, leads, spread):
@@ -293,15 +302,27 @@
     down = lax.ppermute(own, Y, turn(4, 1))
     up = lax.ppermute(own, Y, turn(4, -1))
 
+    partial, facts = pl.pallas_call(
+        compose_own_kernel,
+        out_shape=(
+            jax.ShapeDtypeStruct((lead_n * n_target, 2 * quarter), F32),
+            jax.ShapeDtypeStruct((lead_n * n_target, 128), F32),
+        ),
+        in_specs=[SM] + [VM] * 2,
+        out_specs=(VM,) * 2,
+        compiler_params=PARAMS,
+        cost_estimate=pl.CostEstimate(flops=lead_n * n_target * rows * width, bytes_accessed=5 << 20, transcendentals=0),
+        name="compose_own",
+    )(leads, own, library)
     parts = pl.pallas_call(
         compose_kernel,
         out_shape=jax.ShapeDtypeStruct((lead_n * n_target, 2 * quarter + 128), BF16),
         in_specs=[SM] + [VM] * 6,
         out_specs=VM,
         compiler_params=PARAMS,
-        cost_estimate=pl.CostEstimate(flops=2 * lead_n * n_target * rows * width, bytes_accessed=5 << 20, transcendentals=n_target * wide),
+        cost_estimate=pl.CostEstimate(flops=lead_n * n_target * rows * width, bytes_accessed=5 << 20, transcendentals=0),
         name="compose",
-    )(leads, own, up, down, library, block_up, block_down)
+    )(leads, partial, facts, up, down, block_up, block_down)
 
     parts = parts.reshape(n_lib, lead_n * count, 2 * quarter + 128)
     parts = lax.all_to_all(parts, LIB, 0, 0, tiled=True)

time: 93 us -> 90.6 us (0.974)
  waiting for transfers between devices: 31.4 us -> 22.8 us
  starting transfers between devices: 31.5 us -> 35.5 us
    ppermute x5 -> x6, waiting for transfers between devices: 16.1 us -> 7.15 us  [the longest x1 3.89 us: total_over_space(): lax.ppermute(value, 'z', [(z, (z - 2) % 8 if z % 2 == 0 else (z + 2) % 8)...]
    ppermute x5 -> x6, starting transfers between devices: 7.9 us -> 11.9 us  [the longest x1 5.84 us: total_over_space(): lax.ppermute(value, 'z', [(z, (z - 3) % 8 if z % 2 == 0 else (z + 3) % 8)...]
    ppermute x1, waiting for transfers between devices: 0.01 us -> 1.53 us  [per_device(): block_up = lax.ppermute(for_down, Y, turn(4, -1))]
    ppermute x1, waiting for transfers between devices: 2.24 us -> 0.73 us  [per_device(): down = lax.ppermute(own, Y, turn(4, 1))]
    pallas_call x0 -> x1, Pallas kernels: none -> 1.5 us  [per_device(): pl.pallas_call(compose_own_kernel, out_shape=(jax.ShapeDtypeStruct((lead_...]
    ppermute x1, starting transfers between devices: 0.62 us -> 1.65 us  [per_device(): down = lax.ppermute(own, Y, turn(4, 1))]
    ppermute x1, starting transfers between devices: 2.69 us -> 1.66 us  [per_device(): up = lax.ppermute(own, Y, turn(4, -1))]
  transfers between devices with their start and end apart: 21 -> 22, of which waited for: 14 -> 15; matrix products, arithmetic and copies ran while one was open for 1% -> 1% of each run, Pallas kernels for 4% -> 6%
where the time goes in v7:
time: 90.6 us; the launch traced here: 90 us
  starting transfers between devices  35.5 us (39%)
  waiting for transfers between devices  22.8 us (25%)
  blocking collectives  18.7 us (21%)
  Pallas kernels  8.68 us (10%)
  local copies, waits for them, and re-layouts  4.15 us (5%)
    all_to_all x1, blocking collectives, per_device(): parts = lax.all_to_all(parts, LIB, 0, 0, tiled=True)  18.7 us
    ppermute x1, starting transfers between devices, total_over_space(): lax.ppermute(value, 'z', [(z, (z - 3) % 8 if z % 2 == 0 else (z + 3) % 8)...  5.84 us
    ppermute x1, waiting for transfers between devices, total_over_space(): lax.ppermute(value, 'z', [(z, (z - 2) % 8 if z % 2 == 0 else (z + 2) % 8)...  3.89 us
    unnamed x12, local copies, waits for them, and re-layouts  3.08 us
    ppermute x1, starting transfers between devices, gather_targets(): across = lax.ppermute(own, 'xh', flip(2, 1))  3.02 us
    ppermute x1, starting transfers between devices, gather_targets(): above_x = lax.ppermute(across, Y, turn(4, -1))  2.87 us
    ppermute x1, waiting for transfers between devices, gather_targets(): far_xa = lax.ppermute(far_a, 'xh', flip(2, 1))  2.81 us
    ppermute x1, starting transfers between devices, per_device(): block_up = lax.ppermute(for_down, Y, turn(4, -1))  2.8 us
  transfers between devices with their start and end apart: 22, of which 15 were waited for; matrix products, arithmetic and copies ran while one was open for 1% of the time, Pallas kernels for 6%

profile of v7, /device:TPU:32, one launch (start us, length us, event | category | flops | bytes accessed | tf_op | source)
XLA Modules:
  0.0 90.0 jit_solution(5417587889934564837)
XLA Ops:
  0.0 3.0 %collective-permute-start = (bf16[64,4096]{1,0:T(8,128)(2,1)}, bf16[64,4096]{1,0:T(8,128)(2,1)S(1)}, u32[]{:S(2)}, u32[]{:S(2)}) collective-permute-start(bf16[64,4096]{1,0:T(8,128)(2,1)} %bitcast.9), channel_id=1, source_target_pairs={{0,1},{1,0},{2,3},{3,2},{4,5},{5,4},{6,7},{7,6},{8,9},{9,8},{10,11... | collective-permute-start | bytes 1572872 | tf_op jit(solution)/shard_map/ppermute | solution.py:36
  4.1 1.7 %collective-permute-start.5 = (bf16[32,4096]{1,0:T(8,128)(2,1)S(1)}, bf16[32,4096]{1,0:T(8,128)(2,1)S(1)}, u32[]{:S(2)}, u32[]{:S(2)}) collective-permute-start(bf16[32,4096]{1,0:T(8,128)(2,1)S(1)} %get-tuple-element.51), channel_id=1, source_target_pairs={{0,2},{2,4},{4,6},{6,0},{1,3},{3,5},{5,7},{7,1},{8,10},{10,12},{12... | collective-permute-start | bytes 786440 | tf_op jit(solution)/shard_map/ppermute | solution.py:37
  5.7 1.7 %collective-permute-start.6 = (bf16[32,4096]{1,0:T(8,128)(2,1)S(1)}, bf16[32,4096]{1,0:T(8,128)(2,1)S(1)}, u32[]{:S(2)}, u32[]{:S(2)}) collective-permute-start(bf16[32,4096]{1,0:T(8,128)(2,1)S(1)} %get-tuple-element.52), channel_id=1, source_target_pairs={{0,6},{2,0},{4,2},{6,4},{1,7},{3,1},{5,3},{7,5},{8,14},{10,8},{12,... | collective-permute-start | bytes 786440 | tf_op jit(solution)/shard_map/ppermute | solution.py:38
  7.4 1.8 %collective-permute-start.2 = (bf16[32,4096]{1,0:T(8,128)(2,1)S(1)}, bf16[32,4096]{1,0:T(8,128)(2,1)S(1)}, u32[]{:S(2)}, u32[]{:S(2)}) collective-permute-start(bf16[32,4096]{1,0:T(8,128)(2,1)S(1)} %get-tuple-element.51), channel_id=1, source_target_pairs={{0,6},{2,0},{4,2},{6,4},{1,7},{3,1},{5,3},{7,5},{8,14},{10,8},{12,... | collective-permute-start | bytes 786440 | tf_op jit(solution)/shard_map/ppermute | solution.py:40
  9.4 1.7 %copy-done = bf16[320,4096]{1,0:T(8,128)(2,1)S(1)} copy-done((bf16[320,4096]{1,0:T(8,128)(2,1)S(1)}, bf16[320,4096]{1,0:T(8,128)(2,1)}, u32[]{:S(2)}) %copy-start) | copy-done | bytes 2621464
  15.0 1.6 %collective-permute-start.7 = (bf16[32,4096]{1,0:T(8,128)(2,1)S(1)}, bf16[32,4096]{1,0:T(8,128)(2,1)S(1)}, u32[]{:S(2)}, u32[]{:S(2)}) collective-permute-start(bf16[32,4096]{1,0:T(8,128)(2,1)S(1)} %collective-permute-done.5.refs_2_), channel_id=1, source_target_pairs={{0,2},{2,4},{4,6},{6,0},{1,3},{3,5},{5,7},{7,1},{8,10},{10,12},{12... | collective-permute-start | bytes 786440 | tf_op jit(solution)/shard_map/ppermute | solution.py:42
  16.6 1.7 %collective-permute-start.8 = (bf16[32,4096]{1,0:T(8,128)(2,1)S(1)}, bf16[32,4096]{1,0:T(8,128)(2,1)S(1)}, u32[]{:S(2)}, u32[]{:S(2)}) collective-permute-start(bf16[32,4096]{1,0:T(8,128)(2,1)S(1)} %collective-permute-done.6.refs_5_), channel_id=1, source_target_pairs={{0,6},{2,0},{4,2},{6,4},{1,7},{3,1},{5,3},{7,5},{8,14},{10,8},{12,... | collective-permute-start | bytes 786440 | tf_op jit(solution)/shard_map/ppermute | solution.py:43
  18.2 2.4 %collective-permute-done.2.refs_4_ = bf16[32,4096]{1,0:T(8,128)(2,1)S(1)} collective-permute-done((bf16[32,4096]{1,0:T(8,128)(2,1)S(1)}, bf16[32,4096]{1,0:T(8,128)(2,1)S(1)}, u32[]{:S(2)}, u32[]{:S(2)}) %collective-permute-start.2) | collective-permute-done | bytes 262176 | tf_op jit(solution)/shard_map/ppermute | solution.py:40
  20.6 2.9 %collective-permute-start.4 = (bf16[64,4096]{1,0:T(8,128)(2,1)S(1)}, bf16[64,4096]{1,0:T(8,128)(2,1)S(1)}, u32[]{:S(2)}, u32[]{:S(2)}) collective-permute-start(bf16[64,4096]{1,0:T(8,128)(2,1)S(1)} %collective-permute-done.refs_1_), channel_id=1, source_target_pairs={{0,6},{2,0},{4,2},{6,4},{1,7},{3,1},{5,3},{7,5},{8,14},{10,8},{12,... | collective-permute-start | bytes 1572872 | tf_op jit(solution)/shard_map/ppermute | solution.py:46
  26.2 2.2 %collective-permute-start.10 = (bf16[32,4096]{1,0:T(8,128)(2,1)S(1)}, bf16[32,4096]{1,0:T(8,128)(2,1)S(1)}, u32[]{:S(2)}, u32[]{:S(2)}) collective-permute-start(bf16[32,4096]{1,0:T(8,128)(2,1)S(1)} %collective-permute-done.8.refs_3_), channel_id=1, source_target_pairs={{0,1},{1,0},{2,3},{3,2},{4,5},{5,4},{6,7},{7,6},{8,9},{9,8},{10,11... | collective-permute-start | bytes 786440 | tf_op jit(solution)/shard_map/ppermute | solution.py:48
  28.5 1.6 %near.1.refs_9_ = f32[32,256]{1,0:T(8,128)S(1)} custom-call(bf16[64,4096]{1,0:T(8,128)(2,1)S(1)} %bitcast.10, bf16[64,4096]{1,0:T(8,128)(2,1)S(1)} %collective-permute-done.refs_1_, bf16[32,4096]{1,0:T(8,128)(2,1)S(1)} %collective-permute-done.5.refs_2_, bf16[32,4096]{1,0:T(8,128)(2,1)S(1)} %collective-permute-done.1.refs_3_, ...), custom_call_target="tpu_custom_call" | custom-call | flops 805306368 | bytes 5242880 | tf_op jit(solution)/shard_map/near/pallas_call | solution.py:266
  30.1 2.8 %collective-permute-start.15 = (bf16[320,1024]{1,0:T(8,128)(2,1)S(1)}, bf16[320,1024]{1,0:T(8,128)(2,1)S(1)}, u32[]{:S(2)}, u32[]{:S(2)}) collective-permute-start(bf16[320,1024]{1,0:T(8,128)(2,1)S(1)} %get-tuple-element.43), channel_id=1, source_target_pairs={{0,6},{2,0},{4,2},{6,4},{1,7},{3,1},{5,3},{7,5},{8,14},{10,8},{12,... | collective-permute-start | bytes 1966088 | tf_op jit(solution)/shard_map/ppermute | solution.py:279
  32.9 2.8 %collective-permute-done.9.refs_4_ = bf16[32,4096]{1,0:T(8,128)(2,1)S(1)} collective-permute-done((bf16[32,4096]{1,0:T(8,128)(2,1)S(1)}, bf16[32,4096]{1,0:T(8,128)(2,1)S(1)}, u32[]{:S(2)}, u32[]{:S(2)}) %collective-permute-start.9) | collective-permute-done | bytes 262176 | tf_op jit(solution)/shard_map/ppermute | solution.py:47
  35.9 2.6 %collective-permute-done.10.refs_5_ = bf16[32,4096]{1,0:T(8,128)(2,1)S(1)} collective-permute-done((bf16[32,4096]{1,0:T(8,128)(2,1)S(1)}, bf16[32,4096]{1,0:T(8,128)(2,1)S(1)}, u32[]{:S(2)}, u32[]{:S(2)}) %collective-permute-start.10) | collective-permute-done | bytes 262176 | tf_op jit(solution)/shard_map/ppermute | solution.py:48
  38.5 1.6 %away.1 = f32[64,256]{1,0:T(8,128)S(1)} custom-call(bf16[64,4096]{1,0:T(8,128)(2,1)S(1)} %collective-permute-done.3.refs_0_, bf16[64,4096]{1,0:T(8,128)(2,1)S(1)} %collective-permute-done.4.refs_1_, bf16[32,4096]{1,0:T(8,128)(2,1)S(1)} %collective-permute-done.7.refs_2_, bf16[32,4096]{1,0:T(8,128)(2,1)S(1)} %collective-permute-done.8.refs_3_, ...), custom_call_target="tpu_custom_call" | custom-call | flops 805306368 | bytes 5242880 | tf_op jit(solution)/shard_map/away/pallas_call | solution.py:281
  42.2 2.8 %collective-permute-start.12 = (f32[64,256]{1,0:T(8,128)S(1)}, f32[64,256]{1,0:T(8,128)S(1)}, u32[]{:S(2)}, u32[]{:S(2)}) collective-permute-start(f32[64,256]{1,0:T(8,128)S(1)} %add.21), channel_id=1, source_target_pairs={{0,48},{16,32},{32,16},{48,0},{64,112},{80,96},{96,80},{112,64},{1... | collective-permute-start | bytes 196616 | tf_op jit(solution)/shard_map/ppermute | solution.py:228
  48.2 1.5 %collective-permute-done.15.block_up = bf16[320,1024]{1,0:T(8,128)(2,1)S(1)} collective-permute-done((bf16[320,1024]{1,0:T(8,128)(2,1)S(1)}, bf16[320,1024]{1,0:T(8,128)(2,1)S(1)}, u32[]{:S(2)}, u32[]{:S(2)}) %collective-permute-start.15) | collective-permute-done | bytes 655392 | tf_op jit(solution)/shard_map/ppermute | solution.py:279
  49.8 5.8 %collective-permute-start.19 = (f32[64,256]{1,0:T(8,128)S(1)}, f32[64,256]{1,0:T(8,128)S(1)}, u32[]{:S(2)}, u32[]{:S(2)}) collective-permute-start(f32[64,256]{1,0:T(8,128)S(1)} %add_add_fusion.1), channel_id=1, source_target_pairs={{0,160},{32,128},{64,224},{96,192},{128,32},{160,0},{192,96},{224,... | collective-permute-start | bytes 196616 | tf_op jit(solution)/shard_map/ppermute | solution.py:230
  58.1 3.9 %collective-permute-done.18 = f32[64,256]{1,0:T(8,128)S(1)} collective-permute-done((f32[64,256]{1,0:T(8,128)S(1)}, f32[64,256]{1,0:T(8,128)S(1)}, u32[]{:S(2)}, u32[]{:S(2)}) %collective-permute-start.18) | collective-permute-done | bytes 65568 | tf_op jit(solution)/shard_map/ppermute | solution.py:231
  62.3 1.7 %collective-permute-start.21 = (bf16[64,512]{1,0:T(8,128)(2,1)S(1)}, bf16[64,512]{1,0:T(8,128)(2,1)S(1)}, u32[]{:S(2)}, u32[]{:S(2)}) collective-permute-start(bf16[64,512]{1,0:T(8,128)(2,1)S(1)} %weights.1.own), channel_id=1, source_target_pairs={{0,2},{2,4},{4,6},{6,0},{1,3},{3,5},{5,7},{7,1},{8,10},{10,12},{12... | collective-permute-start | bytes 196616 | tf_op jit(solution)/shard_map/ppermute | solution.py:302
  64.0 1.7 %collective-permute-start.20 = (bf16[64,512]{1,0:T(8,128)(2,1)S(1)}, bf16[64,512]{1,0:T(8,128)(2,1)S(1)}, u32[]{:S(2)}, u32[]{:S(2)}) collective-permute-start(bf16[64,512]{1,0:T(8,128)(2,1)S(1)} %weights.1.own), channel_id=1, source_target_pairs={{0,6},{2,0},{4,2},{6,4},{1,7},{3,1},{5,3},{7,5},{8,14},{10,8},{12,... | collective-permute-start | bytes 196616 | tf_op jit(solution)/shard_map/ppermute | solution.py:303
  65.6 1.5 %compose_own.1 = (f32[256,2048]{1,0:T(8,128)S(1)}, f32[256,128]{1,0:T(8,128)S(1)}) custom-call(s32[4]{0:T(128)S(1)} %copy-done.3, bf16[64,512]{1,0:T(8,128)(2,1)S(1)} %weights.1.own, bf16[320,4096]{1,0:T(8,128)(2,1)S(1)} %copy-done.1), custom_call_target="tpu_custom_call" | custom-call | flops 335544320 | bytes 5242880 | tf_op jit(solution)/shard_map/compose_own/pallas_call | solution.py:305
  68.2 1.8 %compose.1 = bf16[256,2176]{1,0:T(8,128)(2,1)S(1)} custom-call(s32[4]{0:T(128)S(1)} %copy-done.3, f32[256,2048]{1,0:T(8,128)S(1)} %get-tuple-element.47.partial, f32[256,128]{1,0:T(8,128)S(1)} %get-tuple-element.48.own_facts, bf16[64,512]{1,0:T(8,128)(2,1)S(1)} %collective-permute-done.20.up, bf16[64,512]{1,0:T(8,128)(2,1)S(1)} %collective-permute-done.21.down, ...), custom_call_target="tpu_custom_call" | custom-call | flops 335544320 | bytes 5242880 | tf_op jit(solution)/shard_map/compose/pallas_call | solution.py:317
  70.0 18.7 %all_to_all.5.parts = bf16[8,32,2176]{2,1,0:T(8,128)(2,1)S(1)} all-to-all(bf16[8,32,2176]{2,1,0:T(8,128)(2,1)S(1)} %bitcast.8), channel_id=1, replica_groups=mesh['z'=8,'xl'=2,'co'=2,'yh'=2,'yl'=2,'xh'=2] {'yh','yl','xh'}, dimensions={0} | all-to-all | bytes 2228224 | tf_op jit(solution)/shard_map/all_to_all | solution.py:328
  (44 shorter events, 18.5 us)
Async XLA Ops:
  0.0 20.6 %collective-permute-start = (bf16[64,4096]{1,0:T(8,128)(2,1)}, bf16[64,4096]{1,0:T(8,128)(2,1)S(1)}, u32[]{:S(2)}, u32[]{:S(2)}) collective-permute-start(bf16[64,4096]{1,0:T(8,128)(2,1)} %bitcast.9), channel_id=1, source_target_pairs={{0,1},{1,0},{2,3},{3,2},{4,5},{5,4},{6,7},{7,6},{8,9},{9,8},{10,11... | collective-permute-start | bytes 1572872 | tf_op jit(solution)/shard_map/ppermute | solution.py:36
  4.1 10.5 %collective-permute-start.5 = (bf16[32,4096]{1,0:T(8,128)(2,1)S(1)}, bf16[32,4096]{1,0:T(8,128)(2,1)S(1)}, u32[]{:S(2)}, u32[]{:S(2)}) collective-permute-start(bf16[32,4096]{1,0:T(8,128)(2,1)S(1)} %get-tuple-element.51), channel_id=1, source_target_pairs={{0,2},{2,4},{4,6},{6,0},{1,3},{3,5},{5,7},{7,1},{8,10},{10,12},{12... | collective-permute-start | bytes 786440 | tf_op jit(solution)/shard_map/ppermute | solution.py:37
  5.7 9.2 %collective-permute-start.6 = (bf16[32,4096]{1,0:T(8,128)(2,1)S(1)}, bf16[32,4096]{1,0:T(8,128)(2,1)S(1)}, u32[]{:S(2)}, u32[]{:S(2)}) collective-permute-start(bf16[32,4096]{1,0:T(8,128)(2,1)S(1)} %get-tuple-element.52), channel_id=1, source_target_pairs={{0,6},{2,0},{4,2},{6,4},{1,7},{3,1},{5,3},{7,5},{8,14},{10,8},{12,... | collective-permute-start | bytes 786440 | tf_op jit(solution)/shard_map/ppermute | solution.py:38
  7.4 13.2 %collective-permute-start.2 = (bf16[32,4096]{1,0:T(8,128)(2,1)S(1)}, bf16[32,4096]{1,0:T(8,128)(2,1)S(1)}, u32[]{:S(2)}, u32[]{:S(2)}) collective-permute-start(bf16[32,4096]{1,0:T(8,128)(2,1)S(1)} %get-tuple-element.51), channel_id=1, source_target_pairs={{0,6},{2,0},{4,2},{6,4},{1,7},{3,1},{5,3},{7,5},{8,14},{10,8},{12,... | collective-permute-start | bytes 786440 | tf_op jit(solution)/shard_map/ppermute | solution.py:40
  9.2 11.4 %collective-permute-start.1 = (bf16[32,4096]{1,0:T(8,128)(2,1)S(1)}, bf16[32,4096]{1,0:T(8,128)(2,1)S(1)}, u32[]{:S(2)}, u32[]{:S(2)}) collective-permute-start(bf16[32,4096]{1,0:T(8,128)(2,1)S(1)} %get-tuple-element.52), channel_id=1, source_target_pairs={{0,2},{2,4},{4,6},{6,0},{1,3},{3,5},{5,7},{7,1},{8,10},{10,12},{12... | collective-permute-start | bytes 786440 | tf_op jit(solution)/shard_map/ppermute | solution.py:39
  15.0 9.9 %collective-permute-start.7 = (bf16[32,4096]{1,0:T(8,128)(2,1)S(1)}, bf16[32,4096]{1,0:T(8,128)(2,1)S(1)}, u32[]{:S(2)}, u32[]{:S(2)}) collective-permute-start(bf16[32,4096]{1,0:T(8,128)(2,1)S(1)} %collective-permute-done.5.refs_2_), channel_id=1, source_target_pairs={{0,2},{2,4},{4,6},{6,0},{1,3},{3,5},{5,7},{7,1},{8,10},{10,12},{12... | collective-permute-start | bytes 786440 | tf_op jit(solution)/shard_map/ppermute | solution.py:42
  16.6 9.7 %collective-permute-start.8 = (bf16[32,4096]{1,0:T(8,128)(2,1)S(1)}, bf16[32,4096]{1,0:T(8,128)(2,1)S(1)}, u32[]{:S(2)}, u32[]{:S(2)}) collective-permute-start(bf16[32,4096]{1,0:T(8,128)(2,1)S(1)} %collective-permute-done.6.refs_5_), channel_id=1, source_target_pairs={{0,6},{2,0},{4,2},{6,4},{1,7},{3,1},{5,3},{7,5},{8,14},{10,8},{12,... | collective-permute-start | bytes 786440 | tf_op jit(solution)/shard_map/ppermute | solution.py:43
  20.6 17.9 %collective-permute-start.4 = (bf16[64,4096]{1,0:T(8,128)(2,1)S(1)}, bf16[64,4096]{1,0:T(8,128)(2,1)S(1)}, u32[]{:S(2)}, u32[]{:S(2)}) collective-permute-start(bf16[64,4096]{1,0:T(8,128)(2,1)S(1)} %collective-permute-done.refs_1_), channel_id=1, source_target_pairs={{0,6},{2,0},{4,2},{6,4},{1,7},{3,1},{5,3},{7,5},{8,14},{10,8},{12,... | collective-permute-start | bytes 1572872 | tf_op jit(solution)/shard_map/ppermute | solution.py:46
  23.5 15.0 %collective-permute-start.3 = (bf16[64,4096]{1,0:T(8,128)(2,1)S(1)}, bf16[64,4096]{1,0:T(8,128)(2,1)S(1)}, u32[]{:S(2)}, u32[]{:S(2)}) collective-permute-start(bf16[64,4096]{1,0:T(8,128)(2,1)S(1)} %collective-permute-done.refs_1_), channel_id=1, source_target_pairs={{0,2},{2,4},{4,6},{6,0},{1,3},{3,5},{5,7},{7,1},{8,10},{10,12},{12... | collective-permute-start | bytes 1572872 | tf_op jit(solution)/shard_map/ppermute | solution.py:45
  24.9 10.7 %collective-permute-start.9 = (bf16[32,4096]{1,0:T(8,128)(2,1)S(1)}, bf16[32,4096]{1,0:T(8,128)(2,1)S(1)}, u32[]{:S(2)}, u32[]{:S(2)}) collective-permute-start(bf16[32,4096]{1,0:T(8,128)(2,1)S(1)} %collective-permute-done.7.refs_2_), channel_id=1, source_target_pairs={{0,1},{1,0},{2,3},{3,2},{4,5},{5,4},{6,7},{7,6},{8,9},{9,8},{10,11... | collective-permute-start | bytes 786440 | tf_op jit(solution)/shard_map/ppermute | solution.py:47
  26.2 12.3 %collective-permute-start.10 = (bf16[32,4096]{1,0:T(8,128)(2,1)S(1)}, bf16[32,4096]{1,0:T(8,128)(2,1)S(1)}, u32[]{:S(2)}, u32[]{:S(2)}) collective-permute-start(bf16[32,4096]{1,0:T(8,128)(2,1)S(1)} %collective-permute-done.8.refs_3_), channel_id=1, source_target_pairs={{0,1},{1,0},{2,3},{3,2},{4,5},{5,4},{6,7},{7,6},{8,9},{9,8},{10,11... | collective-permute-start | bytes 786440 | tf_op jit(solution)/shard_map/ppermute | solution.py:48
  30.0 35.6 %copy-start.1 = (bf16[320,4096]{1,0:T(8,128)(2,1)S(1)}, bf16[320,4096]{1,0:T(8,128)(2,1)}, u32[]{:S(2)}) copy-start(bf16[320,4096]{1,0:T(8,128)(2,1)} %block.1) | copy-start | bytes 7864324
  30.0 35.6 %copy-start.3 = (s32[4]{0:T(128)S(1)}, s32[4]{0:T(128)}, u32[]{:S(2)}) copy-start(s32[4]{0:T(128)} %leads.3) | copy-start | bytes 52
  30.1 19.7 %collective-permute-start.15 = (bf16[320,1024]{1,0:T(8,128)(2,1)S(1)}, bf16[320,1024]{1,0:T(8,128)(2,1)S(1)}, u32[]{:S(2)}, u32[]{:S(2)}) collective-permute-start(bf16[320,1024]{1,0:T(8,128)(2,1)S(1)} %get-tuple-element.43), channel_id=1, source_target_pairs={{0,6},{2,0},{4,2},{6,4},{1,7},{3,1},{5,3},{7,5},{8,14},{10,8},{12,... | collective-permute-start | bytes 1966088 | tf_op jit(solution)/shard_map/ppermute | solution.py:279
  35.7 14.1 %collective-permute-start.16 = (bf16[320,1024]{1,0:T(8,128)(2,1)S(1)}, bf16[320,1024]{1,0:T(8,128)(2,1)S(1)}, u32[]{:S(2)}, u32[]{:S(2)}) collective-permute-start(bf16[320,1024]{1,0:T(8,128)(2,1)S(1)} %get-tuple-element.44), channel_id=1, source_target_pairs={{0,2},{2,4},{4,6},{6,0},{1,3},{3,5},{5,7},{7,1},{8,10},{10,12},{12... | collective-permute-start | bytes 1966088 | tf_op jit(solution)/shard_map/ppermute | solution.py:278
  40.1 1.3 %collective-permute-start.11 = (f32[64,256]{1,0:T(8,128)S(1)}, f32[64,256]{1,0:T(8,128)S(1)}, u32[]{:S(2)}, u32[]{:S(2)}) collective-permute-start(f32[64,256]{1,0:T(8,128)S(1)} %away.1), channel_id=1, source_target_pairs={{0,8},{8,0},{1,9},{9,1},{2,10},{10,2},{3,11},{11,3},{4,12},{12,4},... | collective-permute-start | bytes 196616 | tf_op jit(solution)/shard_map/ppermute | solution.py:226
  41.4 4.4 %collective-permute-start.14 = (f32[64,256]{1,0:T(8,128)S(1)}, f32[64,256]{1,0:T(8,128)S(1)}, u32[]{:S(2)}, u32[]{:S(2)}) collective-permute-start(f32[64,256]{1,0:T(8,128)S(1)} %add.21), channel_id=1, source_target_pairs={{0,16},{16,0},{1,17},{17,1},{2,18},{18,2},{3,19},{19,3},{4,20},{20... | collective-permute-start | bytes 196616 | tf_op jit(solution)/shard_map/ppermute | solution.py:228
  42.0 4.8 %collective-permute-start.13 = (f32[64,256]{1,0:T(8,128)S(1)}, f32[64,256]{1,0:T(8,128)S(1)}, u32[]{:S(2)}, u32[]{:S(2)}) collective-permute-start(f32[64,256]{1,0:T(8,128)S(1)} %add.21), channel_id=1, source_target_pairs={{0,32},{32,0},{64,96},{96,64},{128,160},{160,128},{192,224},{224,1... | collective-permute-start | bytes 196616 | tf_op jit(solution)/shard_map/ppermute | solution.py:228
  42.2 6.0 %collective-permute-start.12 = (f32[64,256]{1,0:T(8,128)S(1)}, f32[64,256]{1,0:T(8,128)S(1)}, u32[]{:S(2)}, u32[]{:S(2)}) collective-permute-start(f32[64,256]{1,0:T(8,128)S(1)} %add.21), channel_id=1, source_target_pairs={{0,48},{16,32},{32,16},{48,0},{64,112},{80,96},{96,80},{112,64},{1... | collective-permute-start | bytes 196616 | tf_op jit(solution)/shard_map/ppermute | solution.py:228
  49.8 8.3 %collective-permute-start.19 = (f32[64,256]{1,0:T(8,128)S(1)}, f32[64,256]{1,0:T(8,128)S(1)}, u32[]{:S(2)}, u32[]{:S(2)}) collective-permute-start(f32[64,256]{1,0:T(8,128)S(1)} %add_add_fusion.1), channel_id=1, source_target_pairs={{0,160},{32,128},{64,224},{96,192},{128,32},{160,0},{192,96},{224,... | collective-permute-start | bytes 196616 | tf_op jit(solution)/shard_map/ppermute | solution.py:230
  55.6 6.4 %collective-permute-start.18 = (f32[64,256]{1,0:T(8,128)S(1)}, f32[64,256]{1,0:T(8,128)S(1)}, u32[]{:S(2)}, u32[]{:S(2)}) collective-permute-start(f32[64,256]{1,0:T(8,128)S(1)} %add_add_fusion.1), channel_id=1, source_target_pairs={{0,192},{32,96},{64,0},{96,160},{128,64},{160,224},{192,128},{224,... | collective-permute-start | bytes 196616 | tf_op jit(solution)/shard_map/ppermute | solution.py:231
  57.1 4.9 %collective-permute-start.17 = (f32[64,256]{1,0:T(8,128)S(1)}, f32[64,256]{1,0:T(8,128)S(1)}, u32[]{:S(2)}, u32[]{:S(2)}) collective-permute-start(f32[64,256]{1,0:T(8,128)S(1)} %add_add_fusion.1), channel_id=1, source_target_pairs={{0,224},{32,64},{64,32},{96,128},{128,96},{160,192},{192,160},{224... | collective-permute-start | bytes 196616 | tf_op jit(solution)/shard_map/ppermute | solution.py:232
  62.3 5.6 %collective-permute-start.21 = (bf16[64,512]{1,0:T(8,128)(2,1)S(1)}, bf16[64,512]{1,0:T(8,128)(2,1)S(1)}, u32[]{:S(2)}, u32[]{:S(2)}) collective-permute-start(bf16[64,512]{1,0:T(8,128)(2,1)S(1)} %weights.1.own), channel_id=1, source_target_pairs={{0,2},{2,4},{4,6},{6,0},{1,3},{3,5},{5,7},{7,1},{8,10},{10,12},{12... | collective-permute-start | bytes 196616 | tf_op jit(solution)/shard_map/ppermute | solution.py:302
  64.0 4.3 %collective-permute-start.20 = (bf16[64,512]{1,0:T(8,128)(2,1)S(1)}, bf16[64,512]{1,0:T(8,128)(2,1)S(1)}, u32[]{:S(2)}, u32[]{:S(2)}) collective-permute-start(bf16[64,512]{1,0:T(8,128)(2,1)S(1)} %weights.1.own), channel_id=1, source_target_pairs={{0,6},{2,0},{4,2},{6,4},{1,7},{3,1},{5,3},{7,5},{8,14},{10,8},{12,... | collective-permute-start | bytes 196616 | tf_op jit(solution)/shard_map/ppermute | solution.py:303
  (4 other events, 31.5 us)

commit v8 on v7

--- a/solution.py
+++ b/solution.py
@@ -15,6 +15,7 @@
 SPACE = ("z", "xl", "co")
 VM = pl.BlockSpec(memory_space=pltpu.VMEM)
 SM = pl.BlockSpec(memory_space=pltpu.SMEM)
+HB = pl.BlockSpec(memory_space=pltpu.HBM)
 PARAMS = pltpu.CompilerParams(vmem_limit_bytes=16 * 1024 * 1024)
 NEAR = ((0, 0), (0, 1), (3, 0), (1, 0))
 AWAY = ((3, 1), (1, 1), (2, 0), (2, 1))
@@ -32,10 +33,19 @@
     lags, count, width = targets.shape
     own = targets.reshape(lags * count, width)
     half = lags * count // 2
-    early, late = own[:half], own[half:]
-    across = lax.ppermute(own, "xh", flip(2, 1))
+    early, late = pl.pallas_call(
+        split_kernel,
+        out_shape=(jax.ShapeDtypeStruct((half, width), BF16),) * 2,
+        in_specs=[HB],
+        out_specs=(VM,) * 2,
+        scratch_shapes=[pltpu.SemaphoreType.DMA((2,))],
+        compiler_params=PARAMS,
+        name="split",
+    )(own)
     below_a = lax.ppermute(early, Y, turn(4, 1))
     above_b = lax.ppermute(late, Y, turn(4, -1))
+    sent, early, late = lax.optimization_barrier((own, early, late))
+    across = lax.ppermute(sent, "xh", flip(2, 1))
     below_b = lax.ppermute(late, Y, turn(4, 1))
     above_a = lax.ppermute(early, Y, turn(4, -1))
     below_a, above_b, ready = lax.optimization_barrier((below_a, above_b, ready))
@@ -47,6 +57,16 @@
     far_xa = lax.ppermute(far_a, "xh", flip(2, 1))
     far_xb = lax.ppermute(far_b, "xh", flip(2, 1))
     return (own, across, below_a, below_b, above_a, above_b), (below_x, above_x, far_a, far_b, far_xa, far_xb), ready
+
+
+def split_kernel(whole, early, late, sems):
+    half = early.shape[0]
+    first = pltpu.make_async_copy(whole.at[pl.ds(0, half), :], early, sems.at[0])
+    second = pltpu.make_async_copy(whole.at[pl.ds(half, half), :], late, sems.at[1])
+    first.start()
+    second.start()
+    first.wait()
+    second.wait()
 
 
 def place_on_y():
@@ -225,11 +245,11 @@
 def total_over_space(value, arriving):
     value = value + lax.ppermute(value, "co", flip(2, 1))
     both = [(z * 2 + x, (z ^ 1) * 2 + (x ^ 1)) for z in range(8) for x in range(2)]
-    value = (value + lax.ppermute(value, ("z", "xl"), both)) + (lax.ppermute(value, "z", flip(8, 1)) + lax.ppermute(value, "xl", flip(2, 1)))
-    value, arriving = lax.optimization_barrier((value, arriving))
+    value = (value + lax.ppermute(value, "xl", flip(2, 1))) + (lax.ppermute(value, "z", flip(8, 1)) + lax.ppermute(value, ("z", "xl"), both))
     three = lax.ppermute(value, "z", [(z, (z - 3) % 8 if z % 2 == 0 else (z + 3) % 8) for z in range(8)])
     two = lax.ppermute(value, "z", [(z, (z - 2) % 8 if z % 2 == 0 else (z + 2) % 8) for z in range(8)])
-    one = lax.ppermute(value, "z", [(z, (z - 1) % 8 if z % 2 == 0 else (z + 1) % 8) for z in range(8)])
+    last, arriving = lax.optimization_barrier((value, arriving))
+    one = lax.ppermute(last, "z", [(z, (z - 1) % 8 if z % 2 == 0 else (z + 1) % 8) for z in range(8)])
     return value + one + two + three, arriving
 
 

time: 90.6 us -> 90 us (level)
  waiting for transfers between devices: 22.8 us -> 18.9 us
  Pallas kernels: 8.68 us -> 10.8 us
  blocking collectives: 18.7 us -> 20.4 us
  local copies, waits for them, and re-layouts: 4.15 us -> 3.08 us
    ppermute x1, starting transfers between devices: 2.79 us -> 0.22 us  [total_over_space(): lax.ppermute(value, ('z', 'xl'), both)]
    ppermute x1, waiting for transfers between devices: 2.38 us -> 0.39 us  [gather_targets(): above_a = lax.ppermute(early, Y, turn(4, -1))]
    ppermute x1, waiting for transfers between devices: 0.01 us -> 1.99 us  [gather_targets(): below_b = lax.ppermute(late, Y, turn(4, 1))]
    ppermute x3, starting transfers between devices: 4.14 us -> 6.04 us  [the longest x1 3.11 us: gather_targets(): across = lax.ppermute(sent, 'xh', flip(2, 1))]
    all_to_all x1, blocking collectives: 18.7 us -> 20.4 us  [per_device(): parts = lax.all_to_all(parts, LIB, 0, 0, tiled=True)]
    ppermute x1, waiting for transfers between devices: 1.53 us -> 0.01 us  [per_device(): block_up = lax.ppermute(for_down, Y, turn(4, -1))]
    ppermute x1, waiting for transfers between devices: 1.35 us -> 0.14 us  [gather_targets(): below_a = lax.ppermute(early, Y, turn(4, 1))]
    ppermute x3, waiting for transfers between devices: 1.08 us -> 0.01 us  [the longest x1 0.01 us: gather_targets(): across = lax.ppermute(sent, 'xh', flip(2, 1))]
  transfers between devices with their start and end apart: 22 -> 22, of which waited for: 15 -> 14; matrix products, arithmetic and copies ran while one was open for 1% -> 0% of each run, Pallas kernels for 6% -> 7%
where the time goes in v8:
time: 90 us; the launch traced here: 89.5 us
  starting transfers between devices  36.2 us (40%)
  blocking collectives  20.4 us (23%)
  waiting for transfers between devices  18.9 us (21%)
  Pallas kernels  10.8 us (12%)
  local copies, waits for them, and re-layouts  3.08 us (3%)
    all_to_all x1, blocking collectives, per_device(): parts = lax.all_to_all(parts, LIB, 0, 0, tiled=True)  20.4 us
    ppermute x1, starting transfers between devices, total_over_space(): lax.ppermute(value, 'z', [(z, (z - 3) % 8 if z % 2 == 0 else (z + 3) % 8)...  5.92 us
    ppermute x1, waiting for transfers between devices, total_over_space(): lax.ppermute(value, 'z', [(z, (z - 2) % 8 if z % 2 == 0 else (z + 2) % 8)...  3.33 us
    ppermute x1, starting transfers between devices, gather_targets(): across = lax.ppermute(sent, 'xh', flip(2, 1))  3.11 us
    unnamed x10, local copies, waits for them, and re-layouts  3.08 us
    ppermute x1, starting transfers between devices, gather_targets(): above_a = lax.ppermute(early, Y, turn(4, -1))  2.87 us
    ppermute x1, starting transfers between devices, gather_targets(): above_x = lax.ppermute(across, Y, turn(4, -1))  2.87 us
    ppermute x1, starting transfers between devices, per_device(): up = lax.ppermute(own, Y, turn(4, -1))  2.69 us
  transfers between devices with their start and end apart: 22, of which 14 were waited for; matrix products, arithmetic and copies ran while one was open for 0% of the time, Pallas kernels for 7%

profile of v8, /device:TPU:32, one launch (start us, length us, event | category | flops | bytes accessed | tf_op | source)
XLA Modules:
  0.0 89.5 jit_solution(8023218756062998124)
XLA Ops:
  1.1 3.1 %collective-permute-start = (bf16[64,4096]{1,0:T(8,128)(2,1)}, bf16[64,4096]{1,0:T(8,128)(2,1)S(1)}, u32[]{:S(2)}, u32[]{:S(2)}) collective-permute-start(bf16[64,4096]{1,0:T(8,128)(2,1)} %bitcast.whole.refs_0_), channel_id=1, source_target_pairs={{0,1},{1,0},{2,3},{3,2},{4,5},{5,4},{6,7},{7,6},{8,9},{9,8},{10,11... | collective-permute-start | bytes 1572872 | tf_op jit(solution)/shard_map/ppermute | solution.py:48
  4.2 1.6 %collective-permute-start.5 = (bf16[32,4096]{1,0:T(8,128)(2,1)S(1)}, bf16[32,4096]{1,0:T(8,128)(2,1)S(1)}, u32[]{:S(2)}, u32[]{:S(2)}) collective-permute-start(bf16[32,4096]{1,0:T(8,128)(2,1)S(1)} %get-tuple-element.37), channel_id=1, source_target_pairs={{0,2},{2,4},{4,6},{6,0},{1,3},{3,5},{5,7},{7,1},{8,10},{10,12},{12... | collective-permute-start | bytes 786440 | tf_op jit(solution)/shard_map/ppermute | solution.py:45
  5.7 1.7 %collective-permute-start.6 = (bf16[32,4096]{1,0:T(8,128)(2,1)S(1)}, bf16[32,4096]{1,0:T(8,128)(2,1)S(1)}, u32[]{:S(2)}, u32[]{:S(2)}) collective-permute-start(bf16[32,4096]{1,0:T(8,128)(2,1)S(1)} %get-tuple-element.36), channel_id=1, source_target_pairs={{0,6},{2,0},{4,2},{6,4},{1,7},{3,1},{5,3},{7,5},{8,14},{10,8},{12,... | collective-permute-start | bytes 786440 | tf_op jit(solution)/shard_map/ppermute | solution.py:46
  7.8 2.9 %collective-permute-start.2 = (bf16[32,4096]{1,0:T(8,128)(2,1)S(1)}, bf16[32,4096]{1,0:T(8,128)(2,1)S(1)}, u32[]{:S(2)}, u32[]{:S(2)}) collective-permute-start(bf16[32,4096]{1,0:T(8,128)(2,1)S(1)} %get-tuple-element.37), channel_id=1, source_target_pairs={{0,6},{2,0},{4,2},{6,4},{1,7},{3,1},{5,3},{7,5},{8,14},{10,8},{12,... | collective-permute-start | bytes 786440 | tf_op jit(solution)/shard_map/ppermute | solution.py:50
  10.6 1.7 %copy-done = bf16[320,4096]{1,0:T(8,128)(2,1)S(1)} copy-done((bf16[320,4096]{1,0:T(8,128)(2,1)S(1)}, bf16[320,4096]{1,0:T(8,128)(2,1)}, u32[]{:S(2)}) %copy-start) | copy-done | bytes 2621464
  15.0 1.6 %collective-permute-start.7 = (bf16[32,4096]{1,0:T(8,128)(2,1)S(1)}, bf16[32,4096]{1,0:T(8,128)(2,1)S(1)}, u32[]{:S(2)}, u32[]{:S(2)}) collective-permute-start(bf16[32,4096]{1,0:T(8,128)(2,1)S(1)} %collective-permute-done.5.refs_2_), channel_id=1, source_target_pairs={{0,2},{2,4},{4,6},{6,0},{1,3},{3,5},{5,7},{7,1},{8,10},{10,12},{12... | collective-permute-start | bytes 786440 | tf_op jit(solution)/shard_map/ppermute | solution.py:52
  16.6 1.7 %collective-permute-start.8 = (bf16[32,4096]{1,0:T(8,128)(2,1)S(1)}, bf16[32,4096]{1,0:T(8,128)(2,1)S(1)}, u32[]{:S(2)}, u32[]{:S(2)}) collective-permute-start(bf16[32,4096]{1,0:T(8,128)(2,1)S(1)} %collective-permute-done.6.refs_5_), channel_id=1, source_target_pairs={{0,6},{2,0},{4,2},{6,4},{1,7},{3,1},{5,3},{7,5},{8,14},{10,8},{12,... | collective-permute-start | bytes 786440 | tf_op jit(solution)/shard_map/ppermute | solution.py:53
  18.2 2.0 %collective-permute-done.1.refs_3_ = bf16[32,4096]{1,0:T(8,128)(2,1)S(1)} collective-permute-done((bf16[32,4096]{1,0:T(8,128)(2,1)S(1)}, bf16[32,4096]{1,0:T(8,128)(2,1)S(1)}, u32[]{:S(2)}, u32[]{:S(2)}) %collective-permute-start.1) | collective-permute-done | bytes 262176 | tf_op jit(solution)/shard_map/ppermute | solution.py:49
  20.6 2.9 %collective-permute-start.4 = (bf16[64,4096]{1,0:T(8,128)(2,1)S(1)}, bf16[64,4096]{1,0:T(8,128)(2,1)S(1)}, u32[]{:S(2)}, u32[]{:S(2)}) collective-permute-start(bf16[64,4096]{1,0:T(8,128)(2,1)S(1)} %collective-permute-done.refs_1_), channel_id=1, source_target_pairs={{0,6},{2,0},{4,2},{6,4},{1,7},{3,1},{5,3},{7,5},{8,14},{10,8},{12,... | collective-permute-start | bytes 1572872 | tf_op jit(solution)/shard_map/ppermute | solution.py:56
  23.5 1.6 %collective-permute-done.7.refs_2_ = bf16[32,4096]{1,0:T(8,128)(2,1)S(1)} collective-permute-done((bf16[32,4096]{1,0:T(8,128)(2,1)S(1)}, bf16[32,4096]{1,0:T(8,128)(2,1)S(1)}, u32[]{:S(2)}, u32[]{:S(2)}) %collective-permute-start.7) | collective-permute-done | bytes 262176 | tf_op jit(solution)/shard_map/ppermute | solution.py:52
  26.2 2.4 %collective-permute-start.10 = (bf16[32,4096]{1,0:T(8,128)(2,1)S(1)}, bf16[32,4096]{1,0:T(8,128)(2,1)S(1)}, u32[]{:S(2)}, u32[]{:S(2)}) collective-permute-start(bf16[32,4096]{1,0:T(8,128)(2,1)S(1)} %collective-permute-done.8.refs_3_), channel_id=1, source_target_pairs={{0,1},{1,0},{2,3},{3,2},{4,5},{5,4},{6,7},{7,6},{8,9},{9,8},{10,11... | collective-permute-start | bytes 786440 | tf_op jit(solution)/shard_map/ppermute | solution.py:58
  28.6 2.6 %near.1.refs_9_ = f32[32,256]{1,0:T(8,128)S(1)} custom-call(bf16[64,4096]{1,0:T(8,128)(2,1)} %bitcast.whole.refs_0_, bf16[64,4096]{1,0:T(8,128)(2,1)S(1)} %collective-permute-done.refs_1_, bf16[32,4096]{1,0:T(8,128)(2,1)S(1)} %collective-permute-done.5.refs_2_, bf16[32,4096]{1,0:T(8,128)(2,1)S(1)} %collective-permute-done.1.refs_3_, ...), custom_call_target="tpu_custom_call" | custom-call | flops 805306368 | bytes 5242880 | tf_op jit(solution)/shard_map/near/pallas_call | solution.py:286
  31.2 2.6 %collective-permute-start.15 = (bf16[320,1024]{1,0:T(8,128)(2,1)S(1)}, bf16[320,1024]{1,0:T(8,128)(2,1)S(1)}, u32[]{:S(2)}, u32[]{:S(2)}) collective-permute-start(bf16[320,1024]{1,0:T(8,128)(2,1)S(1)} %get-tuple-element.53), channel_id=1, source_target_pairs={{0,6},{2,0},{4,2},{6,4},{1,7},{3,1},{5,3},{7,5},{8,14},{10,8},{12,... | collective-permute-start | bytes 1966088 | tf_op jit(solution)/shard_map/ppermute | solution.py:299
  33.8 1.8 %collective-permute-done.9.refs_4_ = bf16[32,4096]{1,0:T(8,128)(2,1)S(1)} collective-permute-done((bf16[32,4096]{1,0:T(8,128)(2,1)S(1)}, bf16[32,4096]{1,0:T(8,128)(2,1)S(1)}, u32[]{:S(2)}, u32[]{:S(2)}) %collective-permute-start.9) | collective-permute-done | bytes 262176 | tf_op jit(solution)/shard_map/ppermute | solution.py:57
  35.9 2.6 %collective-permute-done.10.refs_5_ = bf16[32,4096]{1,0:T(8,128)(2,1)S(1)} collective-permute-done((bf16[32,4096]{1,0:T(8,128)(2,1)S(1)}, bf16[32,4096]{1,0:T(8,128)(2,1)S(1)}, u32[]{:S(2)}, u32[]{:S(2)}) %collective-permute-start.10) | collective-permute-done | bytes 262176 | tf_op jit(solution)/shard_map/ppermute | solution.py:58
  38.5 1.6 %away.1 = f32[64,256]{1,0:T(8,128)S(1)} custom-call(bf16[64,4096]{1,0:T(8,128)(2,1)S(1)} %collective-permute-done.3.refs_0_, bf16[64,4096]{1,0:T(8,128)(2,1)S(1)} %collective-permute-done.4.refs_1_, bf16[32,4096]{1,0:T(8,128)(2,1)S(1)} %collective-permute-done.7.refs_2_, bf16[32,4096]{1,0:T(8,128)(2,1)S(1)} %collective-permute-done.8.refs_3_, ...), custom_call_target="tpu_custom_call" | custom-call | flops 805306368 | bytes 5242880 | tf_op jit(solution)/shard_map/away/pallas_call | solution.py:301
  41.6 1.9 %collective-permute-start.13 = (f32[64,256]{1,0:T(8,128)S(1)}, f32[64,256]{1,0:T(8,128)S(1)}, u32[]{:S(2)}, u32[]{:S(2)}) collective-permute-start(f32[64,256]{1,0:T(8,128)S(1)} %add.21), channel_id=1, source_target_pairs={{0,32},{32,0},{64,96},{96,64},{128,160},{160,128},{192,224},{224,1... | collective-permute-start | bytes 196616 | tf_op jit(solution)/shard_map/ppermute | solution.py:248
  45.0 2.3 %collective-permute-done.14 = f32[64,256]{1,0:T(8,128)S(1)} collective-permute-done((f32[64,256]{1,0:T(8,128)S(1)}, f32[64,256]{1,0:T(8,128)S(1)}, u32[]{:S(2)}, u32[]{:S(2)}) %collective-permute-start.14) | collective-permute-done | bytes 65568 | tf_op jit(solution)/shard_map/ppermute | solution.py:248
  47.9 5.9 %collective-permute-start.19 = (f32[64,256]{1,0:T(8,128)S(1)}, f32[64,256]{1,0:T(8,128)S(1)}, u32[]{:S(2)}, u32[]{:S(2)}) collective-permute-start(f32[64,256]{1,0:T(8,128)S(1)} %add_add_fusion.1), channel_id=1, source_target_pairs={{0,160},{32,128},{64,224},{96,192},{128,32},{160,0},{192,96},{224,... | collective-permute-start | bytes 196616 | tf_op jit(solution)/shard_map/ppermute | solution.py:249
  56.9 3.3 %collective-permute-done.18 = f32[64,256]{1,0:T(8,128)S(1)} collective-permute-done((f32[64,256]{1,0:T(8,128)S(1)}, f32[64,256]{1,0:T(8,128)S(1)}, u32[]{:S(2)}, u32[]{:S(2)}) %collective-permute-start.18) | collective-permute-done | bytes 65568 | tf_op jit(solution)/shard_map/ppermute | solution.py:250
  61.2 2.7 %collective-permute-start.20 = (bf16[64,512]{1,0:T(8,128)(2,1)S(1)}, bf16[64,512]{1,0:T(8,128)(2,1)S(1)}, u32[]{:S(2)}, u32[]{:S(2)}) collective-permute-start(bf16[64,512]{1,0:T(8,128)(2,1)S(1)} %weights.1.own), channel_id=1, source_target_pairs={{0,6},{2,0},{4,2},{6,4},{1,7},{3,1},{5,3},{7,5},{8,14},{10,8},{12,... | collective-permute-start | bytes 196616 | tf_op jit(solution)/shard_map/ppermute | solution.py:323
  63.9 1.5 %compose_own.1 = (f32[256,2048]{1,0:T(8,128)S(1)}, f32[256,128]{1,0:T(8,128)S(1)}) custom-call(s32[4]{0:T(128)S(1)} %copy-done.2, bf16[64,512]{1,0:T(8,128)(2,1)S(1)} %weights.1.own, bf16[320,4096]{1,0:T(8,128)(2,1)S(1)} %copy-done.1), custom_call_target="tpu_custom_call" | custom-call | flops 335544320 | bytes 5242880 | tf_op jit(solution)/shard_map/compose_own/pallas_call | solution.py:325
  66.1 1.8 %compose.1 = bf16[256,2176]{1,0:T(8,128)(2,1)S(1)} custom-call(s32[4]{0:T(128)S(1)} %copy-done.2, f32[256,2048]{1,0:T(8,128)S(1)} %get-tuple-element.57.partial, f32[256,128]{1,0:T(8,128)S(1)} %get-tuple-element.58.own_facts, bf16[64,512]{1,0:T(8,128)(2,1)S(1)} %collective-permute-done.20.up, bf16[64,512]{1,0:T(8,128)(2,1)S(1)} %collective-permute-done.21.down, ...), custom_call_target="tpu_custom_call" | custom-call | flops 335544320 | bytes 5242880 | tf_op jit(solution)/shard_map/compose/pallas_call | solution.py:337
  68.0 20.4 %all_to_all.5.parts = bf16[8,32,2176]{2,1,0:T(8,128)(2,1)S(1)} all-to-all(bf16[8,32,2176]{2,1,0:T(8,128)(2,1)S(1)} %bitcast.4), channel_id=1, replica_groups=mesh['z'=8,'xl'=2,'co'=2,'yh'=2,'yl'=2,'xh'=2] {'yh','yl','xh'}, dimensions={0} | all-to-all | bytes 2228224 | tf_op jit(solution)/shard_map/all_to_all | solution.py:348
  (42 shorter events, 15.4 us)
Async XLA Ops:
  1.1 19.6 %collective-permute-start = (bf16[64,4096]{1,0:T(8,128)(2,1)}, bf16[64,4096]{1,0:T(8,128)(2,1)S(1)}, u32[]{:S(2)}, u32[]{:S(2)}) collective-permute-start(bf16[64,4096]{1,0:T(8,128)(2,1)} %bitcast.whole.refs_0_), channel_id=1, source_target_pairs={{0,1},{1,0},{2,3},{3,2},{4,5},{5,4},{6,7},{7,6},{8,9},{9,8},{10,11... | collective-permute-start | bytes 1572872 | tf_op jit(solution)/shard_map/ppermute | solution.py:48
  4.2 10.4 %collective-permute-start.5 = (bf16[32,4096]{1,0:T(8,128)(2,1)S(1)}, bf16[32,4096]{1,0:T(8,128)(2,1)S(1)}, u32[]{:S(2)}, u32[]{:S(2)}) collective-permute-start(bf16[32,4096]{1,0:T(8,128)(2,1)S(1)} %get-tuple-element.37), channel_id=1, source_target_pairs={{0,2},{2,4},{4,6},{6,0},{1,3},{3,5},{5,7},{7,1},{8,10},{10,12},{12... | collective-permute-start | bytes 786440 | tf_op jit(solution)/shard_map/ppermute | solution.py:45
  5.7 9.2 %collective-permute-start.6 = (bf16[32,4096]{1,0:T(8,128)(2,1)S(1)}, bf16[32,4096]{1,0:T(8,128)(2,1)S(1)}, u32[]{:S(2)}, u32[]{:S(2)}) collective-permute-start(bf16[32,4096]{1,0:T(8,128)(2,1)S(1)} %get-tuple-element.36), channel_id=1, source_target_pairs={{0,6},{2,0},{4,2},{6,4},{1,7},{3,1},{5,3},{7,5},{8,14},{10,8},{12,... | collective-permute-start | bytes 786440 | tf_op jit(solution)/shard_map/ppermute | solution.py:46
  7.4 12.8 %collective-permute-start.1 = (bf16[32,4096]{1,0:T(8,128)(2,1)S(1)}, bf16[32,4096]{1,0:T(8,128)(2,1)S(1)}, u32[]{:S(2)}, u32[]{:S(2)}) collective-permute-start(bf16[32,4096]{1,0:T(8,128)(2,1)S(1)} %get-tuple-element.36), channel_id=1, source_target_pairs={{0,2},{2,4},{4,6},{6,0},{1,3},{3,5},{5,7},{7,1},{8,10},{10,12},{12... | collective-permute-start | bytes 786440 | tf_op jit(solution)/shard_map/ppermute | solution.py:49
  7.8 12.8 %collective-permute-start.2 = (bf16[32,4096]{1,0:T(8,128)(2,1)S(1)}, bf16[32,4096]{1,0:T(8,128)(2,1)S(1)}, u32[]{:S(2)}, u32[]{:S(2)}) collective-permute-start(bf16[32,4096]{1,0:T(8,128)(2,1)S(1)} %get-tuple-element.37), channel_id=1, source_target_pairs={{0,6},{2,0},{4,2},{6,4},{1,7},{3,1},{5,3},{7,5},{8,14},{10,8},{12,... | collective-permute-start | bytes 786440 | tf_op jit(solution)/shard_map/ppermute | solution.py:50
  13.7 14.9 %copy-start.1 = (bf16[320,4096]{1,0:T(8,128)(2,1)S(1)}, bf16[320,4096]{1,0:T(8,128)(2,1)}, u32[]{:S(2)}) copy-start(bf16[320,4096]{1,0:T(8,128)(2,1)} %block.1) | copy-start | bytes 7864324
  15.0 10.1 %collective-permute-start.7 = (bf16[32,4096]{1,0:T(8,128)(2,1)S(1)}, bf16[32,4096]{1,0:T(8,128)(2,1)S(1)}, u32[]{:S(2)}, u32[]{:S(2)}) collective-permute-start(bf16[32,4096]{1,0:T(8,128)(2,1)S(1)} %collective-permute-done.5.refs_2_), channel_id=1, source_target_pairs={{0,2},{2,4},{4,6},{6,0},{1,3},{3,5},{5,7},{7,1},{8,10},{10,12},{12... | collective-permute-start | bytes 786440 | tf_op jit(solution)/shard_map/ppermute | solution.py:52
  16.6 9.7 %collective-permute-start.8 = (bf16[32,4096]{1,0:T(8,128)(2,1)S(1)}, bf16[32,4096]{1,0:T(8,128)(2,1)S(1)}, u32[]{:S(2)}, u32[]{:S(2)}) collective-permute-start(bf16[32,4096]{1,0:T(8,128)(2,1)S(1)} %collective-permute-done.6.refs_5_), channel_id=1, source_target_pairs={{0,6},{2,0},{4,2},{6,4},{1,7},{3,1},{5,3},{7,5},{8,14},{10,8},{12,... | collective-permute-start | bytes 786440 | tf_op jit(solution)/shard_map/ppermute | solution.py:53
  20.6 17.9 %collective-permute-start.4 = (bf16[64,4096]{1,0:T(8,128)(2,1)S(1)}, bf16[64,4096]{1,0:T(8,128)(2,1)S(1)}, u32[]{:S(2)}, u32[]{:S(2)}) collective-permute-start(bf16[64,4096]{1,0:T(8,128)(2,1)S(1)} %collective-permute-done.refs_1_), channel_id=1, source_target_pairs={{0,6},{2,0},{4,2},{6,4},{1,7},{3,1},{5,3},{7,5},{8,14},{10,8},{12,... | collective-permute-start | bytes 1572872 | tf_op jit(solution)/shard_map/ppermute | solution.py:56
  23.5 15.0 %collective-permute-start.3 = (bf16[64,4096]{1,0:T(8,128)(2,1)S(1)}, bf16[64,4096]{1,0:T(8,128)(2,1)S(1)}, u32[]{:S(2)}, u32[]{:S(2)}) collective-permute-start(bf16[64,4096]{1,0:T(8,128)(2,1)S(1)} %collective-permute-done.refs_1_), channel_id=1, source_target_pairs={{0,2},{2,4},{4,6},{6,0},{1,3},{3,5},{5,7},{7,1},{8,10},{10,12},{12... | collective-permute-start | bytes 1572872 | tf_op jit(solution)/shard_map/ppermute | solution.py:55
  25.1 10.6 %collective-permute-start.9 = (bf16[32,4096]{1,0:T(8,128)(2,1)S(1)}, bf16[32,4096]{1,0:T(8,128)(2,1)S(1)}, u32[]{:S(2)}, u32[]{:S(2)}) collective-permute-start(bf16[32,4096]{1,0:T(8,128)(2,1)S(1)} %collective-permute-done.7.refs_2_), channel_id=1, source_target_pairs={{0,1},{1,0},{2,3},{3,2},{4,5},{5,4},{6,7},{7,6},{8,9},{9,8},{10,11... | collective-permute-start | bytes 786440 | tf_op jit(solution)/shard_map/ppermute | solution.py:57
  26.2 12.3 %collective-permute-start.10 = (bf16[32,4096]{1,0:T(8,128)(2,1)S(1)}, bf16[32,4096]{1,0:T(8,128)(2,1)S(1)}, u32[]{:S(2)}, u32[]{:S(2)}) collective-permute-start(bf16[32,4096]{1,0:T(8,128)(2,1)S(1)} %collective-permute-done.8.refs_3_), channel_id=1, source_target_pairs={{0,1},{1,0},{2,3},{3,2},{4,5},{5,4},{6,7},{7,6},{8,9},{9,8},{10,11... | collective-permute-start | bytes 786440 | tf_op jit(solution)/shard_map/ppermute | solution.py:58
  31.2 32.7 %copy-start.2 = (s32[4]{0:T(128)S(1)}, s32[4]{0:T(128)}, u32[]{:S(2)}) copy-start(s32[4]{0:T(128)} %leads.3) | copy-start | bytes 52
  31.2 24.1 %collective-permute-start.15 = (bf16[320,1024]{1,0:T(8,128)(2,1)S(1)}, bf16[320,1024]{1,0:T(8,128)(2,1)S(1)}, u32[]{:S(2)}, u32[]{:S(2)}) collective-permute-start(bf16[320,1024]{1,0:T(8,128)(2,1)S(1)} %get-tuple-element.53), channel_id=1, source_target_pairs={{0,6},{2,0},{4,2},{6,4},{1,7},{3,1},{5,3},{7,5},{8,14},{10,8},{12,... | collective-permute-start | bytes 1966088 | tf_op jit(solution)/shard_map/ppermute | solution.py:299
  35.7 19.7 %collective-permute-start.16 = (bf16[320,1024]{1,0:T(8,128)(2,1)S(1)}, bf16[320,1024]{1,0:T(8,128)(2,1)S(1)}, u32[]{:S(2)}, u32[]{:S(2)}) collective-permute-start(bf16[320,1024]{1,0:T(8,128)(2,1)S(1)} %get-tuple-element.54), channel_id=1, source_target_pairs={{0,2},{2,4},{4,6},{6,0},{1,3},{3,5},{5,7},{7,1},{8,10},{10,12},{12... | collective-permute-start | bytes 1966088 | tf_op jit(solution)/shard_map/ppermute | solution.py:298
  40.1 1.3 %collective-permute-start.11 = (f32[64,256]{1,0:T(8,128)S(1)}, f32[64,256]{1,0:T(8,128)S(1)}, u32[]{:S(2)}, u32[]{:S(2)}) collective-permute-start(f32[64,256]{1,0:T(8,128)S(1)} %away.1), channel_id=1, source_target_pairs={{0,8},{8,0},{1,9},{9,1},{2,10},{10,2},{3,11},{11,3},{4,12},{12,4},... | collective-permute-start | bytes 196616 | tf_op jit(solution)/shard_map/ppermute | solution.py:246
  41.4 5.8 %collective-permute-start.14 = (f32[64,256]{1,0:T(8,128)S(1)}, f32[64,256]{1,0:T(8,128)S(1)}, u32[]{:S(2)}, u32[]{:S(2)}) collective-permute-start(f32[64,256]{1,0:T(8,128)S(1)} %add.21), channel_id=1, source_target_pairs={{0,48},{16,32},{32,16},{48,0},{64,112},{80,96},{96,80},{112,64},{1... | collective-permute-start | bytes 196616 | tf_op jit(solution)/shard_map/ppermute | solution.py:248
  41.6 5.6 %collective-permute-start.13 = (f32[64,256]{1,0:T(8,128)S(1)}, f32[64,256]{1,0:T(8,128)S(1)}, u32[]{:S(2)}, u32[]{:S(2)}) collective-permute-start(f32[64,256]{1,0:T(8,128)S(1)} %add.21), channel_id=1, source_target_pairs={{0,32},{32,0},{64,96},{96,64},{128,160},{160,128},{192,224},{224,1... | collective-permute-start | bytes 196616 | tf_op jit(solution)/shard_map/ppermute | solution.py:248
  43.5 4.4 %collective-permute-start.12 = (f32[64,256]{1,0:T(8,128)S(1)}, f32[64,256]{1,0:T(8,128)S(1)}, u32[]{:S(2)}, u32[]{:S(2)}) collective-permute-start(f32[64,256]{1,0:T(8,128)S(1)} %add.21), channel_id=1, source_target_pairs={{0,16},{16,0},{1,17},{17,1},{2,18},{18,2},{3,19},{19,3},{4,20},{20... | collective-permute-start | bytes 196616 | tf_op jit(solution)/shard_map/ppermute | solution.py:248
  47.9 9.0 %collective-permute-start.19 = (f32[64,256]{1,0:T(8,128)S(1)}, f32[64,256]{1,0:T(8,128)S(1)}, u32[]{:S(2)}, u32[]{:S(2)}) collective-permute-start(f32[64,256]{1,0:T(8,128)S(1)} %add_add_fusion.1), channel_id=1, source_target_pairs={{0,160},{32,128},{64,224},{96,192},{128,32},{160,0},{192,96},{224,... | collective-permute-start | bytes 196616 | tf_op jit(solution)/shard_map/ppermute | solution.py:249
  53.9 6.4 %collective-permute-start.18 = (f32[64,256]{1,0:T(8,128)S(1)}, f32[64,256]{1,0:T(8,128)S(1)}, u32[]{:S(2)}, u32[]{:S(2)}) collective-permute-start(f32[64,256]{1,0:T(8,128)S(1)} %add_add_fusion.1), channel_id=1, source_target_pairs={{0,192},{32,96},{64,0},{96,160},{128,64},{160,224},{192,128},{224,... | collective-permute-start | bytes 196616 | tf_op jit(solution)/shard_map/ppermute | solution.py:250
  55.3 4.9 %collective-permute-start.17 = (f32[64,256]{1,0:T(8,128)S(1)}, f32[64,256]{1,0:T(8,128)S(1)}, u32[]{:S(2)}, u32[]{:S(2)}) collective-permute-start(f32[64,256]{1,0:T(8,128)S(1)} %add_add_fusion.1), channel_id=1, source_target_pairs={{0,224},{32,64},{64,32},{96,128},{128,96},{160,192},{192,160},{224... | collective-permute-start | bytes 196616 | tf_op jit(solution)/shard_map/ppermute | solution.py:252
  60.6 5.6 %collective-permute-start.21 = (bf16[64,512]{1,0:T(8,128)(2,1)S(1)}, bf16[64,512]{1,0:T(8,128)(2,1)S(1)}, u32[]{:S(2)}, u32[]{:S(2)}) collective-permute-start(bf16[64,512]{1,0:T(8,128)(2,1)S(1)} %weights.1.own), channel_id=1, source_target_pairs={{0,2},{2,4},{4,6},{6,0},{1,3},{3,5},{5,7},{7,1},{8,10},{10,12},{12... | collective-permute-start | bytes 196616 | tf_op jit(solution)/shard_map/ppermute | solution.py:322
  61.2 4.9 %collective-permute-start.20 = (bf16[64,512]{1,0:T(8,128)(2,1)S(1)}, bf16[64,512]{1,0:T(8,128)(2,1)S(1)}, u32[]{:S(2)}, u32[]{:S(2)}) collective-permute-start(bf16[64,512]{1,0:T(8,128)(2,1)S(1)} %weights.1.own), channel_id=1, source_target_pairs={{0,6},{2,0},{4,2},{6,4},{1,7},{3,1},{5,3},{7,5},{8,14},{10,8},{12,... | collective-permute-start | bytes 196616 | tf_op jit(solution)/shard_map/ppermute | solution.py:323
  (3 other events, 3.1 us)

commit v9 on v8

--- a/solution.py
+++ b/solution.py
@@ -16,6 +16,7 @@
 VM = pl.BlockSpec(memory_space=pltpu.VMEM)
 SM = pl.BlockSpec(memory_space=pltpu.SMEM)
 HB = pl.BlockSpec(memory_space=pltpu.HBM)
+ANY = pl.BlockSpec(memory_space=pl.ANY)
 PARAMS = pltpu.CompilerParams(vmem_limit_bytes=16 * 1024 * 1024)
 NEAR = ((0, 0), (0, 1), (3, 0), (1, 0))
 AWAY = ((3, 1), (1, 1), (2, 0), (2, 1))
@@ -49,6 +50,16 @@
     below_b = lax.ppermute(late, Y, turn(4, 1))
     above_a = lax.ppermute(early, Y, turn(4, -1))
     below_a, above_b, ready = lax.optimization_barrier((below_a, above_b, ready))
+    below_a, above_b = pl.pallas_call(
+        stay_kernel,
+        out_shape=(jax.ShapeDtypeStruct(below_a.shape, BF16),) * 2,
+        in_specs=[ANY] * 2,
+        out_specs=(ANY,) * 2,
+        input_output_aliases={0: 0, 1: 1},
+        compiler_params=PARAMS,
+        cost_estimate=pl.CostEstimate(flops=1 << 30, bytes_accessed=1 << 20, transcendentals=0),
+        name="stay",
+    )(below_a, above_b)
     far_a = lax.ppermute(below_a, Y, turn(4, 1))
     far_b = lax.ppermute(above_b, Y, turn(4, -1))
     across, below_b, above_a = lax.optimization_barrier((across, below_b, above_a))
@@ -57,6 +68,10 @@
     far_xa = lax.ppermute(far_a, "xh", flip(2, 1))
     far_xb = lax.ppermute(far_b, "xh", flip(2, 1))
     return (own, across, below_a, below_b, above_a, above_b), (below_x, above_x, far_a, far_b, far_xa, far_xb), ready
+
+
+def stay_kernel(*refs):
+    pass
 
 
 def split_kernel(whole, early, late, sems):
@@ -176,12 +191,15 @@
     return value
 
 
-def mixing(leads, w, rows):
-    targets, wide = w.shape[0], w.shape[1] - 128
+def by_target(shape, count):
+    row, col = lax.broadcasted_iota(jnp.int32, shape, 0), lax.broadcasted_iota(jnp.int32, shape, 1)
+    targets = shape[0] // count
+    return jnp.where(lax.rem(row, count) * targets + lax.div(row, count) == col, 1.0, 0.0).astype(BF16)
+
+
+def mixing(leads, w, perm, rows):
+    wide = w.shape[1] - 128
     count = leads.shape[0]
-    shape = (count * targets, count * targets)
-    row, col = lax.broadcasted_iota(jnp.int32, shape, 0), lax.broadcasted_iota(jnp.int32, shape, 1)
-    perm = jnp.where(lax.rem(row, count) * targets + lax.div(row, count) == col, 1.0, 0.0).astype(BF16)
     weights = w[:, :wide].astype(F32)
     stack = jnp.concatenate([pltpu.roll(weights, leads[k], 1) for k in range(count)], axis=0).astype(BF16)
     mixed = jnp.dot(perm, stack, preferred_element_type=F32).astype(BF16)[:, :rows]
@@ -189,23 +207,26 @@
     return mixed, jnp.dot(perm, fact, preferred_element_type=F32)
 
 
-def compose_own_kernel(leads, own, block, out, facts):
+def compose_own_kernel(leads, own, block, out, facts, order):
     rows = block.shape[0]
     quarter = out.shape[1] // 2
-    mixed, facts[...] = mixing(leads, own, rows)
+    perm = by_target(order.shape, leads.shape[0])
+    order[...] = perm
+    mixed, facts[...] = mixing(leads, own, perm, rows)
     odd = lax.axis_index("yl")
     for side, start in enumerate((2 * odd, 3 - 2 * odd)):
         mine = block[:, pl.ds(pl.multiple_of(start * quarter, quarter), quarter)]
         out[:, side * quarter : (side + 1) * quarter] = jnp.dot(mixed, mine, preferred_element_type=F32)
 
 
-def compose_kernel(leads, partial, own_facts, up, down, block_up, block_down, out):
+def compose_kernel(leads, partial, own_facts, order, up, down, block_up, block_down, out):
     rows, quarter = block_up.shape
     fact = own_facts[...]
+    perm = order[...]
     step = 512
     columns = []
     for side, (w, other) in enumerate(((up, block_up), (down, block_down))):
-        mixed, there = mixing(leads, w, rows)
+        mixed, there = mixing(leads, w, perm, rows)
         tops = [f[:, 0:1] + f[:, 1:2] for f in (fact, there)]
         totals = [f[:, 2:3] + f[:, 3:4] for f in (fact, there)]
         larger = tops[0] >= tops[1]
@@ -322,14 +343,15 @@
     down = lax.ppermute(own, Y, turn(4, 1))
     up = lax.ppermute(own, Y, turn(4, -1))
 
-    partial, facts = pl.pallas_call(
+    partial, facts, order = pl.pallas_call(
         compose_own_kernel,
         out_shape=(
             jax.ShapeDtypeStruct((lead_n * n_target, 2 * quarter), F32),
             jax.ShapeDtypeStruct((lead_n * n_target, 128), F32),
+            jax.ShapeDtypeStruct((lead_n * n_target, lead_n * n_target), BF16),
         ),
         in_specs=[SM] + [VM] * 2,
-        out_specs=(VM,) * 2,
+        out_specs=(VM,) * 3,
         compiler_params=PARAMS,
         cost_estimate=pl.CostEstimate(flops=lead_n * n_target * rows * width, bytes_accessed=5 << 20, transcendentals=0),
         name="compose_own",
@@ -337,12 +359,12 @@
     parts = pl.pallas_call(
         compose_kernel,
         out_shape=jax.ShapeDtypeStruct((lead_n * n_target, 2 * quarter + 128), BF16),
-        in_specs=[SM] + [VM] * 6,
+        in_specs=[SM] + [VM] * 7,
         out_specs=VM,
         compiler_params=PARAMS,
         cost_estimate=pl.CostEstimate(flops=lead_n * n_target * rows * width, bytes_accessed=5 << 20, transcendentals=0),
         name="compose",
-    )(leads, partial, facts, up, down, block_up, block_down)
+    )(leads, partial, facts, order, up, down, block_up, block_down)
 
     parts = parts.reshape(n_lib, lead_n * count, 2 * quarter + 128)
     parts = lax.all_to_all(parts, LIB, 0, 0, tiled=True)

time: 90 us -> 89.6 us (level)
  waiting for transfers between devices: 18.9 us -> 17.2 us
  blocking collectives: 20.4 us -> 21.4 us
    ppermute x1, starting transfers between devices: 0.01 us -> 2.13 us  [gather_targets(): far_xa = lax.ppermute(far_a, 'xh', flip(2, 1))]
    ppermute x1, waiting for transfers between devices: 1.99 us -> 0.01 us  [gather_targets(): below_b = lax.ppermute(late, Y, turn(4, 1))]
    ppermute x1, starting transfers between devices: 1.66 us -> 3.22 us  [gather_targets(): far_b = lax.ppermute(above_b, Y, turn(4, -1))]
    ppermute x1, waiting for transfers between devices: 0.01 us -> 1.52 us  [gather_targets(): across = lax.ppermute(sent, 'xh', flip(2, 1))]
    ppermute x1, starting transfers between devices: 1.58 us -> 0.08 us  [gather_targets(): far_a = lax.ppermute(below_a, Y, turn(4, 1))]
    ppermute x1, starting transfers between devices: 0.22 us -> 1.69 us  [total_over_space(): lax.ppermute(value, ('z', 'xl'), both)]
    ppermute x1, starting transfers between devices: 1.44 us -> 0.01 us  [total_over_space(): lax.ppermute(value, 'xl', flip(2, 1))]
    ppermute x1, waiting for transfers between devices: 0.01 us -> 1.3 us  [total_over_space(): lax.ppermute(value, 'z', flip(8, 1))]
  transfers between devices with their start and end apart: 22 -> 22, of which waited for: 14 -> 11; matrix products, arithmetic and copies ran while one was open for 0% -> 0% of each run, Pallas kernels for 7% -> 7%
where the time goes in v9:
time: 89.6 us; the launch traced here: 89.4 us
  starting transfers between devices  36.8 us (41%)
  blocking collectives  21.4 us (24%)
  waiting for transfers between devices  17.2 us (19%)
  Pallas kernels  10.8 us (12%)
  local copies, waits for them, and re-layouts  3.08 us (3%)
    all_to_all x1, blocking collectives, per_device(): parts = lax.all_to_all(parts, LIB, 0, 0, tiled=True)  21.4 us
    ppermute x1, starting transfers between devices, total_over_space(): lax.ppermute(value, 'z', [(z, (z - 3) % 8 if z % 2 == 0 else (z + 3) % 8)...  5.92 us
    ppermute x1, waiting for transfers between devices, total_over_space(): lax.ppermute(value, 'z', [(z, (z - 2) % 8 if z % 2 == 0 else (z + 2) % 8)...  3.62 us
    ppermute x1, starting transfers between devices, gather_targets(): far_b = lax.ppermute(above_b, Y, turn(4, -1))  3.22 us
    ppermute x1, starting transfers between devices, per_device(): up = lax.ppermute(own, Y, turn(4, -1))  3.22 us
    unnamed x10, local copies, waits for them, and re-layouts  3.08 us
    ppermute x1, starting transfers between devices, gather_targets(): across = lax.ppermute(sent, 'xh', flip(2, 1))  3.02 us
    ppermute x1, starting transfers between devices, per_device(): block_up = lax.ppermute(for_down, Y, turn(4, -1))  2.98 us
  transfers between devices with their start and end apart: 22, of which 11 were waited for; matrix products, arithmetic and copies ran while one was open for 0% of the time, Pallas kernels for 7%

profile of v9, /device:TPU:32, one launch (start us, length us, event | category | flops | bytes accessed | tf_op | source)
XLA Modules:
  0.0 89.4 jit_solution(8947888627936442894)
XLA Ops:
  1.1 1.7 %collective-permute-start.5 = (bf16[32,4096]{1,0:T(8,128)(2,1)S(1)}, bf16[32,4096]{1,0:T(8,128)(2,1)S(1)}, u32[]{:S(2)}, u32[]{:S(2)}) collective-permute-start(bf16[32,4096]{1,0:T(8,128)(2,1)S(1)} %get-tuple-element.40), channel_id=1, source_target_pairs={{0,2},{2,4},{4,6},{6,0},{1,3},{3,5},{5,7},{7,1},{8,10},{10,12},{12... | collective-permute-start | bytes 786440 | tf_op jit(solution)/shard_map/ppermute | solution.py:46
  2.7 1.7 %collective-permute-start.6 = (bf16[32,4096]{1,0:T(8,128)(2,1)S(1)}, bf16[32,4096]{1,0:T(8,128)(2,1)S(1)}, u32[]{:S(2)}, u32[]{:S(2)}) collective-permute-start(bf16[32,4096]{1,0:T(8,128)(2,1)S(1)} %get-tuple-element.39), channel_id=1, source_target_pairs={{0,6},{2,0},{4,2},{6,4},{1,7},{3,1},{5,3},{7,5},{8,14},{10,8},{12,... | collective-permute-start | bytes 786440 | tf_op jit(solution)/shard_map/ppermute | solution.py:47
  4.4 3.0 %collective-permute-start = (bf16[64,4096]{1,0:T(8,128)(2,1)}, bf16[64,4096]{1,0:T(8,128)(2,1)S(1)}, u32[]{:S(2)}, u32[]{:S(2)}) collective-permute-start(bf16[64,4096]{1,0:T(8,128)(2,1)} %bitcast.whole.refs_0_), channel_id=1, source_target_pairs={{0,1},{1,0},{2,3},{3,2},{4,5},{5,4},{6,7},{7,6},{8,9},{9,8},{10,11... | collective-permute-start | bytes 1572872 | tf_op jit(solution)/shard_map/ppermute | solution.py:49
  7.8 2.9 %collective-permute-start.2 = (bf16[32,4096]{1,0:T(8,128)(2,1)S(1)}, bf16[32,4096]{1,0:T(8,128)(2,1)S(1)}, u32[]{:S(2)}, u32[]{:S(2)}) collective-permute-start(bf16[32,4096]{1,0:T(8,128)(2,1)S(1)} %get-tuple-element.40), channel_id=1, source_target_pairs={{0,6},{2,0},{4,2},{6,4},{1,7},{3,1},{5,3},{7,5},{8,14},{10,8},{12,... | collective-permute-start | bytes 786440 | tf_op jit(solution)/shard_map/ppermute | solution.py:51
  10.6 1.7 %copy-done = bf16[320,4096]{1,0:T(8,128)(2,1)S(1)} copy-done((bf16[320,4096]{1,0:T(8,128)(2,1)S(1)}, bf16[320,4096]{1,0:T(8,128)(2,1)}, u32[]{:S(2)}) %copy-start) | copy-done | bytes 2621464
  14.6 3.2 %collective-permute-start.8 = (bf16[32,4096]{1,0:T(8,128)(2,1)S(1)}, bf16[32,4096]{1,0:T(8,128)(2,1)S(1)}, u32[]{:S(2)}, u32[]{:S(2)}) collective-permute-start(bf16[32,4096]{1,0:T(8,128)(2,1)S(1)} %get-tuple-element.50.refs_5_), channel_id=1, source_target_pairs={{0,6},{2,0},{4,2},{6,4},{1,7},{3,1},{5,3},{7,5},{8,14},{10,8},{12,... | collective-permute-start | bytes 786440 | tf_op jit(solution)/shard_map/ppermute | solution.py:64
  17.8 1.5 %collective-permute-done.refs_1_ = bf16[64,4096]{1,0:T(8,128)(2,1)S(1)} collective-permute-done((bf16[64,4096]{1,0:T(8,128)(2,1)}, bf16[64,4096]{1,0:T(8,128)(2,1)S(1)}, u32[]{:S(2)}, u32[]{:S(2)}) %collective-permute-start) | collective-permute-done | bytes 524320 | tf_op jit(solution)/shard_map/ppermute | solution.py:49
  19.3 1.7 %collective-permute-start.4 = (bf16[64,4096]{1,0:T(8,128)(2,1)S(1)}, bf16[64,4096]{1,0:T(8,128)(2,1)S(1)}, u32[]{:S(2)}, u32[]{:S(2)}) collective-permute-start(bf16[64,4096]{1,0:T(8,128)(2,1)S(1)} %collective-permute-done.refs_1_), channel_id=1, source_target_pairs={{0,6},{2,0},{4,2},{6,4},{1,7},{3,1},{5,3},{7,5},{8,14},{10,8},{12,... | collective-permute-start | bytes 1572872 | tf_op jit(solution)/shard_map/ppermute | solution.py:67
  22.6 2.1 %collective-permute-start.9 = (bf16[32,4096]{1,0:T(8,128)(2,1)S(1)}, bf16[32,4096]{1,0:T(8,128)(2,1)S(1)}, u32[]{:S(2)}, u32[]{:S(2)}) collective-permute-start(bf16[32,4096]{1,0:T(8,128)(2,1)S(1)} %collective-permute-done.7.refs_2_), channel_id=1, source_target_pairs={{0,1},{1,0},{2,3},{3,2},{4,5},{5,4},{6,7},{7,6},{8,9},{9,8},{10,11... | collective-permute-start | bytes 786440 | tf_op jit(solution)/shard_map/ppermute | solution.py:68
  26.1 2.6 %near.1.refs_9_ = f32[32,256]{1,0:T(8,128)S(1)} custom-call(bf16[64,4096]{1,0:T(8,128)(2,1)} %bitcast.whole.refs_0_, bf16[64,4096]{1,0:T(8,128)(2,1)S(1)} %collective-permute-done.refs_1_, bf16[32,4096]{1,0:T(8,128)(2,1)S(1)} %get-tuple-element.49.refs_2_, bf16[32,4096]{1,0:T(8,128)(2,1)S(1)} %collective-permute-done.1.refs_3_, ...), custom_call_target="tpu_custom_call" | custom-call | flops 805306368 | bytes 5242880 | tf_op jit(solution)/shard_map/near/pallas_call | solution.py:307
  28.7 3.0 %collective-permute-start.15 = (bf16[320,1024]{1,0:T(8,128)(2,1)S(1)}, bf16[320,1024]{1,0:T(8,128)(2,1)S(1)}, u32[]{:S(2)}, u32[]{:S(2)}) collective-permute-start(bf16[320,1024]{1,0:T(8,128)(2,1)S(1)} %get-tuple-element.58), channel_id=1, source_target_pairs={{0,6},{2,0},{4,2},{6,4},{1,7},{3,1},{5,3},{7,5},{8,14},{10,8},{12,... | collective-permute-start | bytes 1966088 | tf_op jit(solution)/shard_map/ppermute | solution.py:320
  31.7 1.5 %collective-permute-done.9.refs_4_ = bf16[32,4096]{1,0:T(8,128)(2,1)S(1)} collective-permute-done((bf16[32,4096]{1,0:T(8,128)(2,1)S(1)}, bf16[32,4096]{1,0:T(8,128)(2,1)S(1)}, u32[]{:S(2)}, u32[]{:S(2)}) %collective-permute-start.9) | collective-permute-done | bytes 262176 | tf_op jit(solution)/shard_map/ppermute | solution.py:68
  33.2 2.8 %collective-permute-done.10.refs_5_ = bf16[32,4096]{1,0:T(8,128)(2,1)S(1)} collective-permute-done((bf16[32,4096]{1,0:T(8,128)(2,1)S(1)}, bf16[32,4096]{1,0:T(8,128)(2,1)S(1)}, u32[]{:S(2)}, u32[]{:S(2)}) %collective-permute-start.10) | collective-permute-done | bytes 262176 | tf_op jit(solution)/shard_map/ppermute | solution.py:69
  36.0 1.6 %away.1 = f32[64,256]{1,0:T(8,128)S(1)} custom-call(bf16[64,4096]{1,0:T(8,128)(2,1)S(1)} %collective-permute-done.3.refs_0_, bf16[64,4096]{1,0:T(8,128)(2,1)S(1)} %collective-permute-done.4.refs_1_, bf16[32,4096]{1,0:T(8,128)(2,1)S(1)} %collective-permute-done.7.refs_2_, bf16[32,4096]{1,0:T(8,128)(2,1)S(1)} %collective-permute-done.8.refs_3_, ...), custom_call_target="tpu_custom_call" | custom-call | flops 805306368 | bytes 5242880 | tf_op jit(solution)/shard_map/away/pallas_call | solution.py:322
  38.9 1.7 %collective-permute-start.14 = (f32[64,256]{1,0:T(8,128)S(1)}, f32[64,256]{1,0:T(8,128)S(1)}, u32[]{:S(2)}, u32[]{:S(2)}) collective-permute-start(f32[64,256]{1,0:T(8,128)S(1)} %add.21), channel_id=1, source_target_pairs={{0,48},{16,32},{32,16},{48,0},{64,112},{80,96},{96,80},{112,64},{1... | collective-permute-start | bytes 196616 | tf_op jit(solution)/shard_map/ppermute | solution.py:269
  40.6 1.9 %collective-permute-start.13 = (f32[64,256]{1,0:T(8,128)S(1)}, f32[64,256]{1,0:T(8,128)S(1)}, u32[]{:S(2)}, u32[]{:S(2)}) collective-permute-start(f32[64,256]{1,0:T(8,128)S(1)} %add.21), channel_id=1, source_target_pairs={{0,32},{32,0},{64,96},{96,64},{128,160},{160,128},{192,224},{224,1... | collective-permute-start | bytes 196616 | tf_op jit(solution)/shard_map/ppermute | solution.py:269
  42.5 2.2 %collective-permute-done.14 = f32[64,256]{1,0:T(8,128)S(1)} collective-permute-done((f32[64,256]{1,0:T(8,128)S(1)}, f32[64,256]{1,0:T(8,128)S(1)}, u32[]{:S(2)}, u32[]{:S(2)}) %collective-permute-start.14) | collective-permute-done | bytes 65568 | tf_op jit(solution)/shard_map/ppermute | solution.py:269
  46.8 5.9 %collective-permute-start.19 = (f32[64,256]{1,0:T(8,128)S(1)}, f32[64,256]{1,0:T(8,128)S(1)}, u32[]{:S(2)}, u32[]{:S(2)}) collective-permute-start(f32[64,256]{1,0:T(8,128)S(1)} %add_add_fusion.1), channel_id=1, source_target_pairs={{0,160},{32,128},{64,224},{96,192},{128,32},{160,0},{192,96},{224,... | collective-permute-start | bytes 196616 | tf_op jit(solution)/shard_map/ppermute | solution.py:270
  52.7 1.5 %collective-permute-start.18 = (f32[64,256]{1,0:T(8,128)S(1)}, f32[64,256]{1,0:T(8,128)S(1)}, u32[]{:S(2)}, u32[]{:S(2)}) collective-permute-start(f32[64,256]{1,0:T(8,128)S(1)} %add_add_fusion.1), channel_id=1, source_target_pairs={{0,192},{32,96},{64,0},{96,160},{128,64},{160,224},{192,128},{224,... | collective-permute-start | bytes 196616 | tf_op jit(solution)/shard_map/ppermute | solution.py:271
  55.5 3.6 %collective-permute-done.18 = f32[64,256]{1,0:T(8,128)S(1)} collective-permute-done((f32[64,256]{1,0:T(8,128)S(1)}, f32[64,256]{1,0:T(8,128)S(1)}, u32[]{:S(2)}, u32[]{:S(2)}) %collective-permute-start.18) | collective-permute-done | bytes 65568 | tf_op jit(solution)/shard_map/ppermute | solution.py:271
  59.5 3.2 %collective-permute-start.20 = (bf16[64,512]{1,0:T(8,128)(2,1)S(1)}, bf16[64,512]{1,0:T(8,128)(2,1)S(1)}, u32[]{:S(2)}, u32[]{:S(2)}) collective-permute-start(bf16[64,512]{1,0:T(8,128)(2,1)S(1)} %weights.1.own), channel_id=1, source_target_pairs={{0,6},{2,0},{4,2},{6,4},{1,7},{3,1},{5,3},{7,5},{8,14},{10,8},{12,... | collective-permute-start | bytes 196616 | tf_op jit(solution)/shard_map/ppermute | solution.py:344
  62.7 1.5 %compose_own.1 = (f32[256,2048]{1,0:T(8,128)S(1)}, f32[256,128]{1,0:T(8,128)S(1)}, bf16[256,256]{1,0:T(8,128)(2,1)S(1)}) custom-call(s32[4]{0:T(128)S(1)} %copy-done.2, bf16[64,512]{1,0:T(8,128)(2,1)S(1)} %weights.1.own, bf16[320,4096]{1,0:T(8,128)(2,1)S(1)} %copy-done.1), custom_call_target="tpu_custom_call" | custom-call | flops 335544320 | bytes 5242880 | tf_op jit(solution)/shard_map/compose_own/pallas_call | solution.py:346
  65.0 1.8 %compose.1 = bf16[256,2176]{1,0:T(8,128)(2,1)S(1)} custom-call(s32[4]{0:T(128)S(1)} %copy-done.2, f32[256,2048]{1,0:T(8,128)S(1)} %get-tuple-element.62.partial, f32[256,128]{1,0:T(8,128)S(1)} %get-tuple-element.63.own_facts, bf16[256,256]{1,0:T(8,128)(2,1)S(1)} %get-tuple-element.64.order, bf16[64,512]{1,0:T(8,128)(2,1)S(1)} %collective-permute-done.20.up, ...), custom_call_target="tpu_custom_call" | custom-call | flops 335544320 | bytes 5242880 | tf_op jit(solution)/shard_map/compose/pallas_call | solution.py:359
  66.8 21.4 %all_to_all.5.parts = bf16[8,32,2176]{2,1,0:T(8,128)(2,1)S(1)} all-to-all(bf16[8,32,2176]{2,1,0:T(8,128)(2,1)S(1)} %bitcast.4), channel_id=1, replica_groups=mesh['z'=8,'xl'=2,'co'=2,'yh'=2,'yl'=2,'xh'=2] {'yh','yl','xh'}, dimensions={0} | all-to-all | bytes 2228224 | tf_op jit(solution)/shard_map/all_to_all | solution.py:370
  (43 shorter events, 13.5 us)
Async XLA Ops:
  1.1 13.4 %collective-permute-start.5 = (bf16[32,4096]{1,0:T(8,128)(2,1)S(1)}, bf16[32,4096]{1,0:T(8,128)(2,1)S(1)}, u32[]{:S(2)}, u32[]{:S(2)}) collective-permute-start(bf16[32,4096]{1,0:T(8,128)(2,1)S(1)} %get-tuple-element.40), channel_id=1, source_target_pairs={{0,2},{2,4},{4,6},{6,0},{1,3},{3,5},{5,7},{7,1},{8,10},{10,12},{12... | collective-permute-start | bytes 786440 | tf_op jit(solution)/shard_map/ppermute | solution.py:46
  2.7 11.8 %collective-permute-start.6 = (bf16[32,4096]{1,0:T(8,128)(2,1)S(1)}, bf16[32,4096]{1,0:T(8,128)(2,1)S(1)}, u32[]{:S(2)}, u32[]{:S(2)}) collective-permute-start(bf16[32,4096]{1,0:T(8,128)(2,1)S(1)} %get-tuple-element.39), channel_id=1, source_target_pairs={{0,6},{2,0},{4,2},{6,4},{1,7},{3,1},{5,3},{7,5},{8,14},{10,8},{12,... | collective-permute-start | bytes 786440 | tf_op jit(solution)/shard_map/ppermute | solution.py:47
  4.4 15.0 %collective-permute-start = (bf16[64,4096]{1,0:T(8,128)(2,1)}, bf16[64,4096]{1,0:T(8,128)(2,1)S(1)}, u32[]{:S(2)}, u32[]{:S(2)}) collective-permute-start(bf16[64,4096]{1,0:T(8,128)(2,1)} %bitcast.whole.refs_0_), channel_id=1, source_target_pairs={{0,1},{1,0},{2,3},{3,2},{4,5},{5,4},{6,7},{7,6},{8,9},{9,8},{10,11... | collective-permute-start | bytes 1572872 | tf_op jit(solution)/shard_map/ppermute | solution.py:49
  7.4 10.4 %collective-permute-start.1 = (bf16[32,4096]{1,0:T(8,128)(2,1)S(1)}, bf16[32,4096]{1,0:T(8,128)(2,1)S(1)}, u32[]{:S(2)}, u32[]{:S(2)}) collective-permute-start(bf16[32,4096]{1,0:T(8,128)(2,1)S(1)} %get-tuple-element.39), channel_id=1, source_target_pairs={{0,2},{2,4},{4,6},{6,0},{1,3},{3,5},{5,7},{7,1},{8,10},{10,12},{12... | collective-permute-start | bytes 786440 | tf_op jit(solution)/shard_map/ppermute | solution.py:50
  7.8 10.1 %collective-permute-start.2 = (bf16[32,4096]{1,0:T(8,128)(2,1)S(1)}, bf16[32,4096]{1,0:T(8,128)(2,1)S(1)}, u32[]{:S(2)}, u32[]{:S(2)}) collective-permute-start(bf16[32,4096]{1,0:T(8,128)(2,1)S(1)} %get-tuple-element.40), channel_id=1, source_target_pairs={{0,6},{2,0},{4,2},{6,4},{1,7},{3,1},{5,3},{7,5},{8,14},{10,8},{12,... | collective-permute-start | bytes 786440 | tf_op jit(solution)/shard_map/ppermute | solution.py:51
  14.5 11.7 %copy-start.1 = (bf16[320,4096]{1,0:T(8,128)(2,1)S(1)}, bf16[320,4096]{1,0:T(8,128)(2,1)}, u32[]{:S(2)}) copy-start(bf16[320,4096]{1,0:T(8,128)(2,1)} %block.1) | copy-start | bytes 7864324
  14.5 8.1 %collective-permute-start.7 = (bf16[32,4096]{1,0:T(8,128)(2,1)S(1)}, bf16[32,4096]{1,0:T(8,128)(2,1)S(1)}, u32[]{:S(2)}, u32[]{:S(2)}) collective-permute-start(bf16[32,4096]{1,0:T(8,128)(2,1)S(1)} %get-tuple-element.49.refs_2_), channel_id=1, source_target_pairs={{0,2},{2,4},{4,6},{6,0},{1,3},{3,5},{5,7},{7,1},{8,10},{10,12},{12... | collective-permute-start | bytes 786440 | tf_op jit(solution)/shard_map/ppermute | solution.py:63
  14.6 10.1 %collective-permute-start.8 = (bf16[32,4096]{1,0:T(8,128)(2,1)S(1)}, bf16[32,4096]{1,0:T(8,128)(2,1)S(1)}, u32[]{:S(2)}, u32[]{:S(2)}) collective-permute-start(bf16[32,4096]{1,0:T(8,128)(2,1)S(1)} %get-tuple-element.50.refs_5_), channel_id=1, source_target_pairs={{0,6},{2,0},{4,2},{6,4},{1,7},{3,1},{5,3},{7,5},{8,14},{10,8},{12,... | collective-permute-start | bytes 786440 | tf_op jit(solution)/shard_map/ppermute | solution.py:64
  19.3 16.7 %collective-permute-start.4 = (bf16[64,4096]{1,0:T(8,128)(2,1)S(1)}, bf16[64,4096]{1,0:T(8,128)(2,1)S(1)}, u32[]{:S(2)}, u32[]{:S(2)}) collective-permute-start(bf16[64,4096]{1,0:T(8,128)(2,1)S(1)} %collective-permute-done.refs_1_), channel_id=1, source_target_pairs={{0,6},{2,0},{4,2},{6,4},{1,7},{3,1},{5,3},{7,5},{8,14},{10,8},{12,... | collective-permute-start | bytes 1572872 | tf_op jit(solution)/shard_map/ppermute | solution.py:67
  21.0 15.0 %collective-permute-start.3 = (bf16[64,4096]{1,0:T(8,128)(2,1)S(1)}, bf16[64,4096]{1,0:T(8,128)(2,1)S(1)}, u32[]{:S(2)}, u32[]{:S(2)}) collective-permute-start(bf16[64,4096]{1,0:T(8,128)(2,1)S(1)} %collective-permute-done.refs_1_), channel_id=1, source_target_pairs={{0,2},{2,4},{4,6},{6,0},{1,3},{3,5},{5,7},{7,1},{8,10},{10,12},{12... | collective-permute-start | bytes 1572872 | tf_op jit(solution)/shard_map/ppermute | solution.py:66
  22.6 10.6 %collective-permute-start.9 = (bf16[32,4096]{1,0:T(8,128)(2,1)S(1)}, bf16[32,4096]{1,0:T(8,128)(2,1)S(1)}, u32[]{:S(2)}, u32[]{:S(2)}) collective-permute-start(bf16[32,4096]{1,0:T(8,128)(2,1)S(1)} %collective-permute-done.7.refs_2_), channel_id=1, source_target_pairs={{0,1},{1,0},{2,3},{3,2},{4,5},{5,4},{6,7},{7,6},{8,9},{9,8},{10,11... | collective-permute-start | bytes 786440 | tf_op jit(solution)/shard_map/ppermute | solution.py:68
  24.7 11.3 %collective-permute-start.10 = (bf16[32,4096]{1,0:T(8,128)(2,1)S(1)}, bf16[32,4096]{1,0:T(8,128)(2,1)S(1)}, u32[]{:S(2)}, u32[]{:S(2)}) collective-permute-start(bf16[32,4096]{1,0:T(8,128)(2,1)S(1)} %collective-permute-done.8.refs_3_), channel_id=1, source_target_pairs={{0,1},{1,0},{2,3},{3,2},{4,5},{5,4},{6,7},{7,6},{8,9},{9,8},{10,11... | collective-permute-start | bytes 786440 | tf_op jit(solution)/shard_map/ppermute | solution.py:69
  28.7 34.0 %copy-start.2 = (s32[4]{0:T(128)S(1)}, s32[4]{0:T(128)}, u32[]{:S(2)}) copy-start(s32[4]{0:T(128)} %leads.3) | copy-start | bytes 52
  28.7 25.4 %collective-permute-start.15 = (bf16[320,1024]{1,0:T(8,128)(2,1)S(1)}, bf16[320,1024]{1,0:T(8,128)(2,1)S(1)}, u32[]{:S(2)}, u32[]{:S(2)}) collective-permute-start(bf16[320,1024]{1,0:T(8,128)(2,1)S(1)} %get-tuple-element.58), channel_id=1, source_target_pairs={{0,6},{2,0},{4,2},{6,4},{1,7},{3,1},{5,3},{7,5},{8,14},{10,8},{12,... | collective-permute-start | bytes 1966088 | tf_op jit(solution)/shard_map/ppermute | solution.py:320
  33.2 21.0 %collective-permute-start.16 = (bf16[320,1024]{1,0:T(8,128)(2,1)S(1)}, bf16[320,1024]{1,0:T(8,128)(2,1)S(1)}, u32[]{:S(2)}, u32[]{:S(2)}) collective-permute-start(bf16[320,1024]{1,0:T(8,128)(2,1)S(1)} %get-tuple-element.59), channel_id=1, source_target_pairs={{0,2},{2,4},{4,6},{6,0},{1,3},{3,5},{5,7},{7,1},{8,10},{10,12},{12... | collective-permute-start | bytes 1966088 | tf_op jit(solution)/shard_map/ppermute | solution.py:319
  37.6 1.3 %collective-permute-start.11 = (f32[64,256]{1,0:T(8,128)S(1)}, f32[64,256]{1,0:T(8,128)S(1)}, u32[]{:S(2)}, u32[]{:S(2)}) collective-permute-start(f32[64,256]{1,0:T(8,128)S(1)} %away.1), channel_id=1, source_target_pairs={{0,8},{8,0},{1,9},{9,1},{2,10},{10,2},{3,11},{11,3},{4,12},{12,4},... | collective-permute-start | bytes 196616 | tf_op jit(solution)/shard_map/ppermute | solution.py:267
  38.9 5.8 %collective-permute-start.14 = (f32[64,256]{1,0:T(8,128)S(1)}, f32[64,256]{1,0:T(8,128)S(1)}, u32[]{:S(2)}, u32[]{:S(2)}) collective-permute-start(f32[64,256]{1,0:T(8,128)S(1)} %add.21), channel_id=1, source_target_pairs={{0,48},{16,32},{32,16},{48,0},{64,112},{80,96},{96,80},{112,64},{1... | collective-permute-start | bytes 196616 | tf_op jit(solution)/shard_map/ppermute | solution.py:269
  40.6 5.5 %collective-permute-start.13 = (f32[64,256]{1,0:T(8,128)S(1)}, f32[64,256]{1,0:T(8,128)S(1)}, u32[]{:S(2)}, u32[]{:S(2)}) collective-permute-start(f32[64,256]{1,0:T(8,128)S(1)} %add.21), channel_id=1, source_target_pairs={{0,32},{32,0},{64,96},{96,64},{128,160},{160,128},{192,224},{224,1... | collective-permute-start | bytes 196616 | tf_op jit(solution)/shard_map/ppermute | solution.py:269
  42.5 4.3 %collective-permute-start.12 = (f32[64,256]{1,0:T(8,128)S(1)}, f32[64,256]{1,0:T(8,128)S(1)}, u32[]{:S(2)}, u32[]{:S(2)}) collective-permute-start(f32[64,256]{1,0:T(8,128)S(1)} %add.21), channel_id=1, source_target_pairs={{0,16},{16,0},{1,17},{17,1},{2,18},{18,2},{3,19},{19,3},{4,20},{20... | collective-permute-start | bytes 196616 | tf_op jit(solution)/shard_map/ppermute | solution.py:269
  46.8 8.7 %collective-permute-start.19 = (f32[64,256]{1,0:T(8,128)S(1)}, f32[64,256]{1,0:T(8,128)S(1)}, u32[]{:S(2)}, u32[]{:S(2)}) collective-permute-start(f32[64,256]{1,0:T(8,128)S(1)} %add_add_fusion.1), channel_id=1, source_target_pairs={{0,160},{32,128},{64,224},{96,192},{128,32},{160,0},{192,96},{224,... | collective-permute-start | bytes 196616 | tf_op jit(solution)/shard_map/ppermute | solution.py:270
  52.7 6.4 %collective-permute-start.18 = (f32[64,256]{1,0:T(8,128)S(1)}, f32[64,256]{1,0:T(8,128)S(1)}, u32[]{:S(2)}, u32[]{:S(2)}) collective-permute-start(f32[64,256]{1,0:T(8,128)S(1)} %add_add_fusion.1), channel_id=1, source_target_pairs={{0,192},{32,96},{64,0},{96,160},{128,64},{160,224},{192,128},{224,... | collective-permute-start | bytes 196616 | tf_op jit(solution)/shard_map/ppermute | solution.py:271
  54.2 4.9 %collective-permute-start.17 = (f32[64,256]{1,0:T(8,128)S(1)}, f32[64,256]{1,0:T(8,128)S(1)}, u32[]{:S(2)}, u32[]{:S(2)}) collective-permute-start(f32[64,256]{1,0:T(8,128)S(1)} %add_add_fusion.1), channel_id=1, source_target_pairs={{0,224},{32,64},{64,32},{96,128},{128,96},{160,192},{192,160},{224... | collective-permute-start | bytes 196616 | tf_op jit(solution)/shard_map/ppermute | solution.py:273
  59.4 5.6 %collective-permute-start.21 = (bf16[64,512]{1,0:T(8,128)(2,1)S(1)}, bf16[64,512]{1,0:T(8,128)(2,1)S(1)}, u32[]{:S(2)}, u32[]{:S(2)}) collective-permute-start(bf16[64,512]{1,0:T(8,128)(2,1)S(1)} %weights.1.own), channel_id=1, source_target_pairs={{0,2},{2,4},{4,6},{6,0},{1,3},{3,5},{5,7},{7,1},{8,10},{10,12},{12... | collective-permute-start | bytes 196616 | tf_op jit(solution)/shard_map/ppermute | solution.py:343
  59.5 5.5 %collective-permute-start.20 = (bf16[64,512]{1,0:T(8,128)(2,1)S(1)}, bf16[64,512]{1,0:T(8,128)(2,1)S(1)}, u32[]{:S(2)}, u32[]{:S(2)}) collective-permute-start(bf16[64,512]{1,0:T(8,128)(2,1)S(1)} %weights.1.own), channel_id=1, source_target_pairs={{0,6},{2,0},{4,2},{6,4},{1,7},{3,1},{5,3},{7,5},{8,14},{10,8},{12,... | collective-permute-start | bytes 196616 | tf_op jit(solution)/shard_map/ppermute | solution.py:344
  (3 other events, 3.1 us)

commit v10 on v9

--- a/solution.py
+++ b/solution.py
@@ -166,16 +166,17 @@
         out[pl.ds(pl.multiple_of(owner * count, count), count), :] = source[at * count : (at + 1) * count, :]
 
 
-def weights_kernel(dist, scale, picks, out):
+def weights_kernel(rows, dist, scale, picks, out):
     scores = -dist[...] / scale[:, :1]
     top = jnp.max(scores, axis=1, keepdims=True)
     top_hi, top_lo = halves(top)
     weights = jnp.exp(scores - (top_hi + top_lo)).astype(BF16)
     tot_hi, tot_lo = halves(jnp.sum(weights.astype(F32), axis=1, keepdims=True))
-    wide = picks.shape[0]
     spread_out = lax.dot_general(weights, picks[...], (((1,), (1,)), ((), ())), preferred_element_type=F32)
-    out[:, :wide] = spread_out.astype(BF16)
-    out[:, wide:] = in_lanes((top_hi, top_lo, tot_hi, tot_lo)).astype(BF16)
+    lane = lax.broadcasted_iota(jnp.int32, spread_out.shape, 1)
+    for at, fact in enumerate((top_hi, top_lo, tot_hi, tot_lo)):
+        spread_out = jnp.where(lane == rows + at, fact, spread_out)
+    out[...] = spread_out.astype(BF16)
 
 
 def halves(value):
@@ -198,13 +199,13 @@
 
 
 def mixing(leads, w, perm, rows):
-    wide = w.shape[1] - 128
+    wide = w.shape[1]
     count = leads.shape[0]
-    weights = w[:, :wide].astype(F32)
+    weights = w[...].astype(F32)
     stack = jnp.concatenate([pltpu.roll(weights, leads[k], 1) for k in range(count)], axis=0).astype(BF16)
     mixed = jnp.dot(perm, stack, preferred_element_type=F32).astype(BF16)[:, :rows]
-    fact = jnp.concatenate([w[:, wide:]] * count, axis=0)
-    return mixed, jnp.dot(perm, fact, preferred_element_type=F32)
+    fact = jnp.concatenate([w[:, wide - 128 :]] * count, axis=0)
+    return mixed, pltpu.roll(jnp.dot(perm, fact, preferred_element_type=F32), wide - rows, 1)
 
 
 def compose_own_kernel(leads, own, block, out, facts, order):
@@ -332,8 +333,8 @@
 
     dist, (block_up, block_down) = total_over_space(partial_dist, (block_up, block_down))
     own = pl.pallas_call(
-        weights_kernel,
-        out_shape=jax.ShapeDtypeStruct((n_target, wide + 128), BF16),
+        functools.partial(weights_kernel, rows),
+        out_shape=jax.ShapeDtypeStruct((n_target, wide), BF16),
         in_specs=[VM] * 3,
         out_specs=VM,
         compiler_params=PARAMS,

time: 89.6 us -> 89.6 us (level)
  no operation moved by 1% of the time
where the time goes in v10:
time: 89.6 us; the launch traced here: 89.3 us
  starting transfers between devices  36.8 us (41%)
  blocking collectives  21.5 us (24%)
  waiting for transfers between devices  17 us (19%)
  Pallas kernels  10.9 us (12%)
  local copies, waits for them, and re-layouts  3.08 us (3%)
    all_to_all x1, blocking collectives, per_device(): parts = lax.all_to_all(parts, LIB, 0, 0, tiled=True)  21.5 us
    ppermute x1, starting transfers between devices, total_over_space(): lax.ppermute(value, 'z', [(z, (z - 3) % 8 if z % 2 == 0 else (z + 3) % 8)...  5.92 us
    ppermute x1, waiting for transfers between devices, total_over_space(): lax.ppermute(value, 'z', [(z, (z - 2) % 8 if z % 2 == 0 else (z + 2) % 8)...  3.62 us
    ppermute x1, starting transfers between devices, gather_targets(): far_b = lax.ppermute(above_b, Y, turn(4, -1))  3.22 us
    ppermute x1, starting transfers between devices, per_device(): up = lax.ppermute(own, Y, turn(4, -1))  3.22 us
    unnamed x10, local copies, waits for them, and re-layouts  3.08 us
    ppermute x1, starting transfers between devices, gather_targets(): across = lax.ppermute(sent, 'xh', flip(2, 1))  3.02 us
    ppermute x1, starting transfers between devices, per_device(): block_up = lax.ppermute(for_down, Y, turn(4, -1))  2.98 us
  transfers between devices with their start and end apart: 22, of which 11 were waited for; matrix products, arithmetic and copies ran while one was open for 0% of the time, Pallas kernels for 7%

profile of v10, /device:TPU:32, one launch (start us, length us, event | category | flops | bytes accessed | tf_op | source)
XLA Modules:
  0.0 89.3 jit_solution(9579711415094895388)
XLA Ops:
  1.1 1.7 %collective-permute-start.5 = (bf16[32,4096]{1,0:T(8,128)(2,1)S(1)}, bf16[32,4096]{1,0:T(8,128)(2,1)S(1)}, u32[]{:S(2)}, u32[]{:S(2)}) collective-permute-start(bf16[32,4096]{1,0:T(8,128)(2,1)S(1)} %get-tuple-element.40), channel_id=1, source_target_pairs={{0,2},{2,4},{4,6},{6,0},{1,3},{3,5},{5,7},{7,1},{8,10},{10,12},{12... | collective-permute-start | bytes 786440 | tf_op jit(solution)/shard_map/ppermute | solution.py:46
  2.7 1.7 %collective-permute-start.6 = (bf16[32,4096]{1,0:T(8,128)(2,1)S(1)}, bf16[32,4096]{1,0:T(8,128)(2,1)S(1)}, u32[]{:S(2)}, u32[]{:S(2)}) collective-permute-start(bf16[32,4096]{1,0:T(8,128)(2,1)S(1)} %get-tuple-element.39), channel_id=1, source_target_pairs={{0,6},{2,0},{4,2},{6,4},{1,7},{3,1},{5,3},{7,5},{8,14},{10,8},{12,... | collective-permute-start | bytes 786440 | tf_op jit(solution)/shard_map/ppermute | solution.py:47
  4.4 3.0 %collective-permute-start = (bf16[64,4096]{1,0:T(8,128)(2,1)}, bf16[64,4096]{1,0:T(8,128)(2,1)S(1)}, u32[]{:S(2)}, u32[]{:S(2)}) collective-permute-start(bf16[64,4096]{1,0:T(8,128)(2,1)} %bitcast.whole.refs_0_), channel_id=1, source_target_pairs={{0,1},{1,0},{2,3},{3,2},{4,5},{5,4},{6,7},{7,6},{8,9},{9,8},{10,11... | collective-permute-start | bytes 1572872 | tf_op jit(solution)/shard_map/ppermute | solution.py:49
  7.8 2.9 %collective-permute-start.2 = (bf16[32,4096]{1,0:T(8,128)(2,1)S(1)}, bf16[32,4096]{1,0:T(8,128)(2,1)S(1)}, u32[]{:S(2)}, u32[]{:S(2)}) collective-permute-start(bf16[32,4096]{1,0:T(8,128)(2,1)S(1)} %get-tuple-element.40), channel_id=1, source_target_pairs={{0,6},{2,0},{4,2},{6,4},{1,7},{3,1},{5,3},{7,5},{8,14},{10,8},{12,... | collective-permute-start | bytes 786440 | tf_op jit(solution)/shard_map/ppermute | solution.py:51
  10.6 1.7 %copy-done = bf16[320,4096]{1,0:T(8,128)(2,1)S(1)} copy-done((bf16[320,4096]{1,0:T(8,128)(2,1)S(1)}, bf16[320,4096]{1,0:T(8,128)(2,1)}, u32[]{:S(2)}) %copy-start) | copy-done | bytes 2621464
  14.6 3.2 %collective-permute-start.8 = (bf16[32,4096]{1,0:T(8,128)(2,1)S(1)}, bf16[32,4096]{1,0:T(8,128)(2,1)S(1)}, u32[]{:S(2)}, u32[]{:S(2)}) collective-permute-start(bf16[32,4096]{1,0:T(8,128)(2,1)S(1)} %get-tuple-element.50.refs_5_), channel_id=1, source_target_pairs={{0,6},{2,0},{4,2},{6,4},{1,7},{3,1},{5,3},{7,5},{8,14},{10,8},{12,... | collective-permute-start | bytes 786440 | tf_op jit(solution)/shard_map/ppermute | solution.py:64
  17.8 1.5 %collective-permute-done.refs_1_ = bf16[64,4096]{1,0:T(8,128)(2,1)S(1)} collective-permute-done((bf16[64,4096]{1,0:T(8,128)(2,1)}, bf16[64,4096]{1,0:T(8,128)(2,1)S(1)}, u32[]{:S(2)}, u32[]{:S(2)}) %collective-permute-start) | collective-permute-done | bytes 524320 | tf_op jit(solution)/shard_map/ppermute | solution.py:49
  19.3 1.7 %collective-permute-start.4 = (bf16[64,4096]{1,0:T(8,128)(2,1)S(1)}, bf16[64,4096]{1,0:T(8,128)(2,1)S(1)}, u32[]{:S(2)}, u32[]{:S(2)}) collective-permute-start(bf16[64,4096]{1,0:T(8,128)(2,1)S(1)} %collective-permute-done.refs_1_), channel_id=1, source_target_pairs={{0,6},{2,0},{4,2},{6,4},{1,7},{3,1},{5,3},{7,5},{8,14},{10,8},{12,... | collective-permute-start | bytes 1572872 | tf_op jit(solution)/shard_map/ppermute | solution.py:67
  22.6 2.1 %collective-permute-start.9 = (bf16[32,4096]{1,0:T(8,128)(2,1)S(1)}, bf16[32,4096]{1,0:T(8,128)(2,1)S(1)}, u32[]{:S(2)}, u32[]{:S(2)}) collective-permute-start(bf16[32,4096]{1,0:T(8,128)(2,1)S(1)} %collective-permute-done.7.refs_2_), channel_id=1, source_target_pairs={{0,1},{1,0},{2,3},{3,2},{4,5},{5,4},{6,7},{7,6},{8,9},{9,8},{10,11... | collective-permute-start | bytes 786440 | tf_op jit(solution)/shard_map/ppermute | solution.py:68
  26.1 2.6 %near.1.refs_9_ = f32[32,256]{1,0:T(8,128)S(1)} custom-call(bf16[64,4096]{1,0:T(8,128)(2,1)} %bitcast.whole.refs_0_, bf16[64,4096]{1,0:T(8,128)(2,1)S(1)} %collective-permute-done.refs_1_, bf16[32,4096]{1,0:T(8,128)(2,1)S(1)} %get-tuple-element.49.refs_2_, bf16[32,4096]{1,0:T(8,128)(2,1)S(1)} %collective-permute-done.1.refs_3_, ...), custom_call_target="tpu_custom_call" | custom-call | flops 805306368 | bytes 5242880 | tf_op jit(solution)/shard_map/near/pallas_call | solution.py:308
  28.7 3.0 %collective-permute-start.15 = (bf16[320,1024]{1,0:T(8,128)(2,1)S(1)}, bf16[320,1024]{1,0:T(8,128)(2,1)S(1)}, u32[]{:S(2)}, u32[]{:S(2)}) collective-permute-start(bf16[320,1024]{1,0:T(8,128)(2,1)S(1)} %get-tuple-element.58), channel_id=1, source_target_pairs={{0,6},{2,0},{4,2},{6,4},{1,7},{3,1},{5,3},{7,5},{8,14},{10,8},{12,... | collective-permute-start | bytes 1966088 | tf_op jit(solution)/shard_map/ppermute | solution.py:321
  31.7 1.5 %collective-permute-done.9.refs_4_ = bf16[32,4096]{1,0:T(8,128)(2,1)S(1)} collective-permute-done((bf16[32,4096]{1,0:T(8,128)(2,1)S(1)}, bf16[32,4096]{1,0:T(8,128)(2,1)S(1)}, u32[]{:S(2)}, u32[]{:S(2)}) %collective-permute-start.9) | collective-permute-done | bytes 262176 | tf_op jit(solution)/shard_map/ppermute | solution.py:68
  33.2 2.8 %collective-permute-done.10.refs_5_ = bf16[32,4096]{1,0:T(8,128)(2,1)S(1)} collective-permute-done((bf16[32,4096]{1,0:T(8,128)(2,1)S(1)}, bf16[32,4096]{1,0:T(8,128)(2,1)S(1)}, u32[]{:S(2)}, u32[]{:S(2)}) %collective-permute-start.10) | collective-permute-done | bytes 262176 | tf_op jit(solution)/shard_map/ppermute | solution.py:69
  36.0 1.6 %away.1 = f32[64,256]{1,0:T(8,128)S(1)} custom-call(bf16[64,4096]{1,0:T(8,128)(2,1)S(1)} %collective-permute-done.3.refs_0_, bf16[64,4096]{1,0:T(8,128)(2,1)S(1)} %collective-permute-done.4.refs_1_, bf16[32,4096]{1,0:T(8,128)(2,1)S(1)} %collective-permute-done.7.refs_2_, bf16[32,4096]{1,0:T(8,128)(2,1)S(1)} %collective-permute-done.8.refs_3_, ...), custom_call_target="tpu_custom_call" | custom-call | flops 805306368 | bytes 5242880 | tf_op jit(solution)/shard_map/away/pallas_call | solution.py:323
  38.9 1.7 %collective-permute-start.14 = (f32[64,256]{1,0:T(8,128)S(1)}, f32[64,256]{1,0:T(8,128)S(1)}, u32[]{:S(2)}, u32[]{:S(2)}) collective-permute-start(f32[64,256]{1,0:T(8,128)S(1)} %add.21), channel_id=1, source_target_pairs={{0,48},{16,32},{32,16},{48,0},{64,112},{80,96},{96,80},{112,64},{1... | collective-permute-start | bytes 196616 | tf_op jit(solution)/shard_map/ppermute | solution.py:270
  40.6 1.9 %collective-permute-start.13 = (f32[64,256]{1,0:T(8,128)S(1)}, f32[64,256]{1,0:T(8,128)S(1)}, u32[]{:S(2)}, u32[]{:S(2)}) collective-permute-start(f32[64,256]{1,0:T(8,128)S(1)} %add.21), channel_id=1, source_target_pairs={{0,32},{32,0},{64,96},{96,64},{128,160},{160,128},{192,224},{224,1... | collective-permute-start | bytes 196616 | tf_op jit(solution)/shard_map/ppermute | solution.py:270
  42.5 2.2 %collective-permute-done.14 = f32[64,256]{1,0:T(8,128)S(1)} collective-permute-done((f32[64,256]{1,0:T(8,128)S(1)}, f32[64,256]{1,0:T(8,128)S(1)}, u32[]{:S(2)}, u32[]{:S(2)}) %collective-permute-start.14) | collective-permute-done | bytes 65568 | tf_op jit(solution)/shard_map/ppermute | solution.py:270
  46.8 5.9 %collective-permute-start.19 = (f32[64,256]{1,0:T(8,128)S(1)}, f32[64,256]{1,0:T(8,128)S(1)}, u32[]{:S(2)}, u32[]{:S(2)}) collective-permute-start(f32[64,256]{1,0:T(8,128)S(1)} %add_add_fusion.1), channel_id=1, source_target_pairs={{0,160},{32,128},{64,224},{96,192},{128,32},{160,0},{192,96},{224,... | collective-permute-start | bytes 196616 | tf_op jit(solution)/shard_map/ppermute | solution.py:271
  52.7 1.5 %collective-permute-start.18 = (f32[64,256]{1,0:T(8,128)S(1)}, f32[64,256]{1,0:T(8,128)S(1)}, u32[]{:S(2)}, u32[]{:S(2)}) collective-permute-start(f32[64,256]{1,0:T(8,128)S(1)} %add_add_fusion.1), channel_id=1, source_target_pairs={{0,192},{32,96},{64,0},{96,160},{128,64},{160,224},{192,128},{224,... | collective-permute-start | bytes 196616 | tf_op jit(solution)/shard_map/ppermute | solution.py:272
  55.5 3.6 %collective-permute-done.18 = f32[64,256]{1,0:T(8,128)S(1)} collective-permute-done((f32[64,256]{1,0:T(8,128)S(1)}, f32[64,256]{1,0:T(8,128)S(1)}, u32[]{:S(2)}, u32[]{:S(2)}) %collective-permute-start.18) | collective-permute-done | bytes 65568 | tf_op jit(solution)/shard_map/ppermute | solution.py:272
  59.5 3.2 %collective-permute-start.20 = (bf16[64,384]{1,0:T(8,128)(2,1)S(1)}, bf16[64,384]{1,0:T(8,128)(2,1)S(1)}, u32[]{:S(2)}, u32[]{:S(2)}) collective-permute-start(bf16[64,384]{1,0:T(8,128)(2,1)S(1)} %weights.1.own), channel_id=1, source_target_pairs={{0,6},{2,0},{4,2},{6,4},{1,7},{3,1},{5,3},{7,5},{8,14},{10,8},{12,... | collective-permute-start | bytes 147464 | tf_op jit(solution)/shard_map/ppermute | solution.py:345
  62.7 1.5 %compose_own.1 = (f32[256,2048]{1,0:T(8,128)S(1)}, f32[256,128]{1,0:T(8,128)S(1)}, bf16[256,256]{1,0:T(8,128)(2,1)S(1)}) custom-call(s32[4]{0:T(128)S(1)} %copy-done.2, bf16[64,384]{1,0:T(8,128)(2,1)S(1)} %weights.1.own, bf16[320,4096]{1,0:T(8,128)(2,1)S(1)} %copy-done.1), custom_call_target="tpu_custom_call" | custom-call | flops 335544320 | bytes 5242880 | tf_op jit(solution)/shard_map/compose_own/pallas_call | solution.py:347
  64.8 1.9 %compose.1 = bf16[256,2176]{1,0:T(8,128)(2,1)S(1)} custom-call(s32[4]{0:T(128)S(1)} %copy-done.2, f32[256,2048]{1,0:T(8,128)S(1)} %get-tuple-element.62.partial, f32[256,128]{1,0:T(8,128)S(1)} %get-tuple-element.63.own_facts, bf16[256,256]{1,0:T(8,128)(2,1)S(1)} %get-tuple-element.64.order, bf16[64,384]{1,0:T(8,128)(2,1)S(1)} %collective-permute-done.20.up, ...), custom_call_target="tpu_custom_call" | custom-call | flops 335544320 | bytes 5242880 | tf_op jit(solution)/shard_map/compose/pallas_call | solution.py:360
  66.7 21.5 %all_to_all.5.parts = bf16[8,32,2176]{2,1,0:T(8,128)(2,1)S(1)} all-to-all(bf16[8,32,2176]{2,1,0:T(8,128)(2,1)S(1)} %bitcast.4), channel_id=1, replica_groups=mesh['z'=8,'xl'=2,'co'=2,'yh'=2,'yl'=2,'xh'=2] {'yh','yl','xh'}, dimensions={0} | all-to-all | bytes 2228224 | tf_op jit(solution)/shard_map/all_to_all | solution.py:371
  (43 shorter events, 13.4 us)
Async XLA Ops:
  1.1 13.4 %collective-permute-start.5 = (bf16[32,4096]{1,0:T(8,128)(2,1)S(1)}, bf16[32,4096]{1,0:T(8,128)(2,1)S(1)}, u32[]{:S(2)}, u32[]{:S(2)}) collective-permute-start(bf16[32,4096]{1,0:T(8,128)(2,1)S(1)} %get-tuple-element.40), channel_id=1, source_target_pairs={{0,2},{2,4},{4,6},{6,0},{1,3},{3,5},{5,7},{7,1},{8,10},{10,12},{12... | collective-permute-start | bytes 786440 | tf_op jit(solution)/shard_map/ppermute | solution.py:46
  2.7 11.8 %collective-permute-start.6 = (bf16[32,4096]{1,0:T(8,128)(2,1)S(1)}, bf16[32,4096]{1,0:T(8,128)(2,1)S(1)}, u32[]{:S(2)}, u32[]{:S(2)}) collective-permute-start(bf16[32,4096]{1,0:T(8,128)(2,1)S(1)} %get-tuple-element.39), channel_id=1, source_target_pairs={{0,6},{2,0},{4,2},{6,4},{1,7},{3,1},{5,3},{7,5},{8,14},{10,8},{12,... | collective-permute-start | bytes 786440 | tf_op jit(solution)/shard_map/ppermute | solution.py:47
  4.4 15.0 %collective-permute-start = (bf16[64,4096]{1,0:T(8,128)(2,1)}, bf16[64,4096]{1,0:T(8,128)(2,1)S(1)}, u32[]{:S(2)}, u32[]{:S(2)}) collective-permute-start(bf16[64,4096]{1,0:T(8,128)(2,1)} %bitcast.whole.refs_0_), channel_id=1, source_target_pairs={{0,1},{1,0},{2,3},{3,2},{4,5},{5,4},{6,7},{7,6},{8,9},{9,8},{10,11... | collective-permute-start | bytes 1572872 | tf_op jit(solution)/shard_map/ppermute | solution.py:49
  7.4 10.4 %collective-permute-start.1 = (bf16[32,4096]{1,0:T(8,128)(2,1)S(1)}, bf16[32,4096]{1,0:T(8,128)(2,1)S(1)}, u32[]{:S(2)}, u32[]{:S(2)}) collective-permute-start(bf16[32,4096]{1,0:T(8,128)(2,1)S(1)} %get-tuple-element.39), channel_id=1, source_target_pairs={{0,2},{2,4},{4,6},{6,0},{1,3},{3,5},{5,7},{7,1},{8,10},{10,12},{12... | collective-permute-start | bytes 786440 | tf_op jit(solution)/shard_map/ppermute | solution.py:50
  7.8 10.1 %collective-permute-start.2 = (bf16[32,4096]{1,0:T(8,128)(2,1)S(1)}, bf16[32,4096]{1,0:T(8,128)(2,1)S(1)}, u32[]{:S(2)}, u32[]{:S(2)}) collective-permute-start(bf16[32,4096]{1,0:T(8,128)(2,1)S(1)} %get-tuple-element.40), channel_id=1, source_target_pairs={{0,6},{2,0},{4,2},{6,4},{1,7},{3,1},{5,3},{7,5},{8,14},{10,8},{12,... | collective-permute-start | bytes 786440 | tf_op jit(solution)/shard_map/ppermute | solution.py:51
  14.5 11.7 %copy-start.1 = (bf16[320,4096]{1,0:T(8,128)(2,1)S(1)}, bf16[320,4096]{1,0:T(8,128)(2,1)}, u32[]{:S(2)}) copy-start(bf16[320,4096]{1,0:T(8,128)(2,1)} %block.1) | copy-start | bytes 7864324
  14.5 8.1 %collective-permute-start.7 = (bf16[32,4096]{1,0:T(8,128)(2,1)S(1)}, bf16[32,4096]{1,0:T(8,128)(2,1)S(1)}, u32[]{:S(2)}, u32[]{:S(2)}) collective-permute-start(bf16[32,4096]{1,0:T(8,128)(2,1)S(1)} %get-tuple-element.49.refs_2_), channel_id=1, source_target_pairs={{0,2},{2,4},{4,6},{6,0},{1,3},{3,5},{5,7},{7,1},{8,10},{10,12},{12... | collective-permute-start | bytes 786440 | tf_op jit(solution)/shard_map/ppermute | solution.py:63
  14.6 10.1 %collective-permute-start.8 = (bf16[32,4096]{1,0:T(8,128)(2,1)S(1)}, bf16[32,4096]{1,0:T(8,128)(2,1)S(1)}, u32[]{:S(2)}, u32[]{:S(2)}) collective-permute-start(bf16[32,4096]{1,0:T(8,128)(2,1)S(1)} %get-tuple-element.50.refs_5_), channel_id=1, source_target_pairs={{0,6},{2,0},{4,2},{6,4},{1,7},{3,1},{5,3},{7,5},{8,14},{10,8},{12,... | collective-permute-start | bytes 786440 | tf_op jit(solution)/shard_map/ppermute | solution.py:64
  19.3 16.7 %collective-permute-start.4 = (bf16[64,4096]{1,0:T(8,128)(2,1)S(1)}, bf16[64,4096]{1,0:T(8,128)(2,1)S(1)}, u32[]{:S(2)}, u32[]{:S(2)}) collective-permute-start(bf16[64,4096]{1,0:T(8,128)(2,1)S(1)} %collective-permute-done.refs_1_), channel_id=1, source_target_pairs={{0,6},{2,0},{4,2},{6,4},{1,7},{3,1},{5,3},{7,5},{8,14},{10,8},{12,... | collective-permute-start | bytes 1572872 | tf_op jit(solution)/shard_map/ppermute | solution.py:67
  21.0 15.0 %collective-permute-start.3 = (bf16[64,4096]{1,0:T(8,128)(2,1)S(1)}, bf16[64,4096]{1,0:T(8,128)(2,1)S(1)}, u32[]{:S(2)}, u32[]{:S(2)}) collective-permute-start(bf16[64,4096]{1,0:T(8,128)(2,1)S(1)} %collective-permute-done.refs_1_), channel_id=1, source_target_pairs={{0,2},{2,4},{4,6},{6,0},{1,3},{3,5},{5,7},{7,1},{8,10},{10,12},{12... | collective-permute-start | bytes 1572872 | tf_op jit(solution)/shard_map/ppermute | solution.py:66
  22.6 10.6 %collective-permute-start.9 = (bf16[32,4096]{1,0:T(8,128)(2,1)S(1)}, bf16[32,4096]{1,0:T(8,128)(2,1)S(1)}, u32[]{:S(2)}, u32[]{:S(2)}) collective-permute-start(bf16[32,4096]{1,0:T(8,128)(2,1)S(1)} %collective-permute-done.7.refs_2_), channel_id=1, source_target_pairs={{0,1},{1,0},{2,3},{3,2},{4,5},{5,4},{6,7},{7,6},{8,9},{9,8},{10,11... | collective-permute-start | bytes 786440 | tf_op jit(solution)/shard_map/ppermute | solution.py:68
  24.7 11.3 %collective-permute-start.10 = (bf16[32,4096]{1,0:T(8,128)(2,1)S(1)}, bf16[32,4096]{1,0:T(8,128)(2,1)S(1)}, u32[]{:S(2)}, u32[]{:S(2)}) collective-permute-start(bf16[32,4096]{1,0:T(8,128)(2,1)S(1)} %collective-permute-done.8.refs_3_), channel_id=1, source_target_pairs={{0,1},{1,0},{2,3},{3,2},{4,5},{5,4},{6,7},{7,6},{8,9},{9,8},{10,11... | collective-permute-start | bytes 786440 | tf_op jit(solution)/shard_map/ppermute | solution.py:69
  28.7 34.0 %copy-start.2 = (s32[4]{0:T(128)S(1)}, s32[4]{0:T(128)}, u32[]{:S(2)}) copy-start(s32[4]{0:T(128)} %leads.3) | copy-start | bytes 52
  28.7 25.4 %collective-permute-start.15 = (bf16[320,1024]{1,0:T(8,128)(2,1)S(1)}, bf16[320,1024]{1,0:T(8,128)(2,1)S(1)}, u32[]{:S(2)}, u32[]{:S(2)}) collective-permute-start(bf16[320,1024]{1,0:T(8,128)(2,1)S(1)} %get-tuple-element.58), channel_id=1, source_target_pairs={{0,6},{2,0},{4,2},{6,4},{1,7},{3,1},{5,3},{7,5},{8,14},{10,8},{12,... | collective-permute-start | bytes 1966088 | tf_op jit(solution)/shard_map/ppermute | solution.py:321
  33.2 21.0 %collective-permute-start.16 = (bf16[320,1024]{1,0:T(8,128)(2,1)S(1)}, bf16[320,1024]{1,0:T(8,128)(2,1)S(1)}, u32[]{:S(2)}, u32[]{:S(2)}) collective-permute-start(bf16[320,1024]{1,0:T(8,128)(2,1)S(1)} %get-tuple-element.59), channel_id=1, source_target_pairs={{0,2},{2,4},{4,6},{6,0},{1,3},{3,5},{5,7},{7,1},{8,10},{10,12},{12... | collective-permute-start | bytes 1966088 | tf_op jit(solution)/shard_map/ppermute | solution.py:320
  37.6 1.3 %collective-permute-start.11 = (f32[64,256]{1,0:T(8,128)S(1)}, f32[64,256]{1,0:T(8,128)S(1)}, u32[]{:S(2)}, u32[]{:S(2)}) collective-permute-start(f32[64,256]{1,0:T(8,128)S(1)} %away.1), channel_id=1, source_target_pairs={{0,8},{8,0},{1,9},{9,1},{2,10},{10,2},{3,11},{11,3},{4,12},{12,4},... | collective-permute-start | bytes 196616 | tf_op jit(solution)/shard_map/ppermute | solution.py:268
  38.9 5.8 %collective-permute-start.14 = (f32[64,256]{1,0:T(8,128)S(1)}, f32[64,256]{1,0:T(8,128)S(1)}, u32[]{:S(2)}, u32[]{:S(2)}) collective-permute-start(f32[64,256]{1,0:T(8,128)S(1)} %add.21), channel_id=1, source_target_pairs={{0,48},{16,32},{32,16},{48,0},{64,112},{80,96},{96,80},{112,64},{1... | collective-permute-start | bytes 196616 | tf_op jit(solution)/shard_map/ppermute | solution.py:270
  40.6 5.5 %collective-permute-start.13 = (f32[64,256]{1,0:T(8,128)S(1)}, f32[64,256]{1,0:T(8,128)S(1)}, u32[]{:S(2)}, u32[]{:S(2)}) collective-permute-start(f32[64,256]{1,0:T(8,128)S(1)} %add.21), channel_id=1, source_target_pairs={{0,32},{32,0},{64,96},{96,64},{128,160},{160,128},{192,224},{224,1... | collective-permute-start | bytes 196616 | tf_op jit(solution)/shard_map/ppermute | solution.py:270
  42.5 4.3 %collective-permute-start.12 = (f32[64,256]{1,0:T(8,128)S(1)}, f32[64,256]{1,0:T(8,128)S(1)}, u32[]{:S(2)}, u32[]{:S(2)}) collective-permute-start(f32[64,256]{1,0:T(8,128)S(1)} %add.21), channel_id=1, source_target_pairs={{0,16},{16,0},{1,17},{17,1},{2,18},{18,2},{3,19},{19,3},{4,20},{20... | collective-permute-start | bytes 196616 | tf_op jit(solution)/shard_map/ppermute | solution.py:270
  46.8 8.7 %collective-permute-start.19 = (f32[64,256]{1,0:T(8,128)S(1)}, f32[64,256]{1,0:T(8,128)S(1)}, u32[]{:S(2)}, u32[]{:S(2)}) collective-permute-start(f32[64,256]{1,0:T(8,128)S(1)} %add_add_fusion.1), channel_id=1, source_target_pairs={{0,160},{32,128},{64,224},{96,192},{128,32},{160,0},{192,96},{224,... | collective-permute-start | bytes 196616 | tf_op jit(solution)/shard_map/ppermute | solution.py:271
  52.7 6.4 %collective-permute-start.18 = (f32[64,256]{1,0:T(8,128)S(1)}, f32[64,256]{1,0:T(8,128)S(1)}, u32[]{:S(2)}, u32[]{:S(2)}) collective-permute-start(f32[64,256]{1,0:T(8,128)S(1)} %add_add_fusion.1), channel_id=1, source_target_pairs={{0,192},{32,96},{64,0},{96,160},{128,64},{160,224},{192,128},{224,... | collective-permute-start | bytes 196616 | tf_op jit(solution)/shard_map/ppermute | solution.py:272
  54.2 4.9 %collective-permute-start.17 = (f32[64,256]{1,0:T(8,128)S(1)}, f32[64,256]{1,0:T(8,128)S(1)}, u32[]{:S(2)}, u32[]{:S(2)}) collective-permute-start(f32[64,256]{1,0:T(8,128)S(1)} %add_add_fusion.1), channel_id=1, source_target_pairs={{0,224},{32,64},{64,32},{96,128},{128,96},{160,192},{192,160},{224... | collective-permute-start | bytes 196616 | tf_op jit(solution)/shard_map/ppermute | solution.py:274
  59.4 5.4 %collective-permute-start.21 = (bf16[64,384]{1,0:T(8,128)(2,1)S(1)}, bf16[64,384]{1,0:T(8,128)(2,1)S(1)}, u32[]{:S(2)}, u32[]{:S(2)}) collective-permute-start(bf16[64,384]{1,0:T(8,128)(2,1)S(1)} %weights.1.own), channel_id=1, source_target_pairs={{0,2},{2,4},{4,6},{6,0},{1,3},{3,5},{5,7},{7,1},{8,10},{10,12},{12... | collective-permute-start | bytes 147464 | tf_op jit(solution)/shard_map/ppermute | solution.py:344
  59.5 5.3 %collective-permute-start.20 = (bf16[64,384]{1,0:T(8,128)(2,1)S(1)}, bf16[64,384]{1,0:T(8,128)(2,1)S(1)}, u32[]{:S(2)}, u32[]{:S(2)}) collective-permute-start(bf16[64,384]{1,0:T(8,128)(2,1)S(1)} %weights.1.own), channel_id=1, source_target_pairs={{0,6},{2,0},{4,2},{6,4},{1,7},{3,1},{5,3},{7,5},{8,14},{10,8},{12,... | collective-permute-start | bytes 147464 | tf_op jit(solution)/shard_map/ppermute | solution.py:345
  (3 other events, 3.1 us)

commit v11 on v10

--- a/solution.py
+++ b/solution.py
@@ -16,7 +16,6 @@
 VM = pl.BlockSpec(memory_space=pltpu.VMEM)
 SM = pl.BlockSpec(memory_space=pltpu.SMEM)
 HB = pl.BlockSpec(memory_space=pltpu.HBM)
-ANY = pl.BlockSpec(memory_space=pl.ANY)
 PARAMS = pltpu.CompilerParams(vmem_limit_bytes=16 * 1024 * 1024)
 NEAR = ((0, 0), (0, 1), (3, 0), (1, 0))
 AWAY = ((3, 1), (1, 1), (2, 0), (2, 1))
@@ -50,16 +49,6 @@
     below_b = lax.ppermute(late, Y, turn(4, 1))
     above_a = lax.ppermute(early, Y, turn(4, -1))
     below_a, above_b, ready = lax.optimization_barrier((below_a, above_b, ready))
-    below_a, above_b = pl.pallas_call(
-        stay_kernel,
-        out_shape=(jax.ShapeDtypeStruct(below_a.shape, BF16),) * 2,
-        in_specs=[ANY] * 2,
-        out_specs=(ANY,) * 2,
-        input_output_aliases={0: 0, 1: 1},
-        compiler_params=PARAMS,
-        cost_estimate=pl.CostEstimate(flops=1 << 30, bytes_accessed=1 << 20, transcendentals=0),
-        name="stay",
-    )(below_a, above_b)
     far_a = lax.ppermute(below_a, Y, turn(4, 1))
     far_b = lax.ppermute(above_b, Y, turn(4, -1))
     across, below_b, above_a = lax.optimization_barrier((across, below_b, above_a))
@@ -68,10 +57,6 @@
     far_xa = lax.ppermute(far_a, "xh", flip(2, 1))
     far_xb = lax.ppermute(far_b, "xh", flip(2, 1))
     return (own, across, below_a, below_b, above_a, above_b), (below_x, above_x, far_a, far_b, far_xa, far_xb), ready
-
-
-def stay_kernel(*refs):
-    pass
 
 
 def split_kernel(whole, early, late, sems):

time: 89.6 us -> 89.9 us (level)
  waiting for transfers between devices: 17 us -> 18.7 us
  blocking collectives: 21.5 us -> 20.4 us
    ppermute x1, starting transfers between devices: 2.13 us -> 0.01 us  [gather_targets(): far_xa = lax.ppermute(far_a, 'xh', flip(2, 1))]
    ppermute x1, waiting for transfers between devices: 0.01 us -> 1.99 us  [gather_targets(): below_b = lax.ppermute(late, Y, turn(4, 1))]
    ppermute x1, starting transfers between devices: 3.22 us -> 1.66 us  [gather_targets(): far_b = lax.ppermute(above_b, Y, turn(4, -1))]
    ppermute x1, waiting for transfers between devices: 1.52 us -> 0.01 us  [gather_targets(): across = lax.ppermute(sent, 'xh', flip(2, 1))]
    ppermute x1, starting transfers between devices: 0.08 us -> 1.58 us  [gather_targets(): far_a = lax.ppermute(below_a, Y, turn(4, 1))]
    ppermute x1, starting transfers between devices: 1.69 us -> 0.22 us  [total_over_space(): lax.ppermute(value, ('z', 'xl'), both)]
    ppermute x1, starting transfers between devices: 0.01 us -> 1.43 us  [total_over_space(): lax.ppermute(value, 'xl', flip(2, 1))]
    ppermute x1, waiting for transfers between devices: 1.3 us -> 0.01 us  [total_over_space(): lax.ppermute(value, 'z', flip(8, 1))]
  transfers between devices with their start and end apart: 22 -> 22, of which waited for: 11 -> 14; matrix products, arithmetic and copies ran while one was open for 0% -> 0% of each run, Pallas kernels for 7% -> 7%
where the time goes in v11:
time: 89.9 us; the launch traced here: 89.4 us
  starting transfers between devices  36.2 us (40%)
  blocking collectives  20.4 us (23%)
  waiting for transfers between devices  18.7 us (21%)
  Pallas kernels  10.9 us (12%)
  local copies, waits for them, and re-layouts  3.08 us (3%)
    all_to_all x1, blocking collectives, per_device(): parts = lax.all_to_all(parts, LIB, 0, 0, tiled=True)  20.4 us
    ppermute x1, starting transfers between devices, total_over_space(): lax.ppermute(value, 'z', [(z, (z - 3) % 8 if z % 2 == 0 else (z + 3) % 8)...  5.92 us
    ppermute x1, waiting for transfers between devices, total_over_space(): lax.ppermute(value, 'z', [(z, (z - 2) % 8 if z % 2 == 0 else (z + 2) % 8)...  3.33 us
    ppermute x1, starting transfers between devices, gather_targets(): across = lax.ppermute(sent, 'xh', flip(2, 1))  3.11 us
    unnamed x10, local copies, waits for them, and re-layouts  3.08 us
    ppermute x1, starting transfers between devices, gather_targets(): above_a = lax.ppermute(early, Y, turn(4, -1))  2.87 us
    ppermute x1, starting transfers between devices, gather_targets(): above_x = lax.ppermute(across, Y, turn(4, -1))  2.87 us
    ppermute x1, starting transfers between devices, per_device(): up = lax.ppermute(own, Y, turn(4, -1))  2.69 us
  transfers between devices with their start and end apart: 22, of which 14 were waited for; matrix products, arithmetic and copies ran while one was open for 0% of the time, Pallas kernels for 7%

profile of v11, /device:TPU:32, one launch (start us, length us, event | category | flops | bytes accessed | tf_op | source)
XLA Modules:
  0.0 89.4 jit_solution(16988350652257221480)
XLA Ops:
  1.1 3.1 %collective-permute-start = (bf16[64,4096]{1,0:T(8,128)(2,1)}, bf16[64,4096]{1,0:T(8,128)(2,1)S(1)}, u32[]{:S(2)}, u32[]{:S(2)}) collective-permute-start(bf16[64,4096]{1,0:T(8,128)(2,1)} %bitcast.whole.refs_0_), channel_id=1, source_target_pairs={{0,1},{1,0},{2,3},{3,2},{4,5},{5,4},{6,7},{7,6},{8,9},{9,8},{10,11... | collective-permute-start | bytes 1572872 | tf_op jit(solution)/shard_map/ppermute | solution.py:48
  4.2 1.6 %collective-permute-start.5 = (bf16[32,4096]{1,0:T(8,128)(2,1)S(1)}, bf16[32,4096]{1,0:T(8,128)(2,1)S(1)}, u32[]{:S(2)}, u32[]{:S(2)}) collective-permute-start(bf16[32,4096]{1,0:T(8,128)(2,1)S(1)} %get-tuple-element.38), channel_id=1, source_target_pairs={{0,2},{2,4},{4,6},{6,0},{1,3},{3,5},{5,7},{7,1},{8,10},{10,12},{12... | collective-permute-start | bytes 786440 | tf_op jit(solution)/shard_map/ppermute | solution.py:45
  5.7 1.7 %collective-permute-start.6 = (bf16[32,4096]{1,0:T(8,128)(2,1)S(1)}, bf16[32,4096]{1,0:T(8,128)(2,1)S(1)}, u32[]{:S(2)}, u32[]{:S(2)}) collective-permute-start(bf16[32,4096]{1,0:T(8,128)(2,1)S(1)} %get-tuple-element.37), channel_id=1, source_target_pairs={{0,6},{2,0},{4,2},{6,4},{1,7},{3,1},{5,3},{7,5},{8,14},{10,8},{12,... | collective-permute-start | bytes 786440 | tf_op jit(solution)/shard_map/ppermute | solution.py:46
  7.8 2.9 %collective-permute-start.2 = (bf16[32,4096]{1,0:T(8,128)(2,1)S(1)}, bf16[32,4096]{1,0:T(8,128)(2,1)S(1)}, u32[]{:S(2)}, u32[]{:S(2)}) collective-permute-start(bf16[32,4096]{1,0:T(8,128)(2,1)S(1)} %get-tuple-element.38), channel_id=1, source_target_pairs={{0,6},{2,0},{4,2},{6,4},{1,7},{3,1},{5,3},{7,5},{8,14},{10,8},{12,... | collective-permute-start | bytes 786440 | tf_op jit(solution)/shard_map/ppermute | solution.py:50
  10.6 1.7 %copy-done = bf16[320,4096]{1,0:T(8,128)(2,1)S(1)} copy-done((bf16[320,4096]{1,0:T(8,128)(2,1)S(1)}, bf16[320,4096]{1,0:T(8,128)(2,1)}, u32[]{:S(2)}) %copy-start) | copy-done | bytes 2621464
  15.0 1.6 %collective-permute-start.7 = (bf16[32,4096]{1,0:T(8,128)(2,1)S(1)}, bf16[32,4096]{1,0:T(8,128)(2,1)S(1)}, u32[]{:S(2)}, u32[]{:S(2)}) collective-permute-start(bf16[32,4096]{1,0:T(8,128)(2,1)S(1)} %collective-permute-done.5.refs_2_), channel_id=1, source_target_pairs={{0,2},{2,4},{4,6},{6,0},{1,3},{3,5},{5,7},{7,1},{8,10},{10,12},{12... | collective-permute-start | bytes 786440 | tf_op jit(solution)/shard_map/ppermute | solution.py:52
  16.6 1.7 %collective-permute-start.8 = (bf16[32,4096]{1,0:T(8,128)(2,1)S(1)}, bf16[32,4096]{1,0:T(8,128)(2,1)S(1)}, u32[]{:S(2)}, u32[]{:S(2)}) collective-permute-start(bf16[32,4096]{1,0:T(8,128)(2,1)S(1)} %collective-permute-done.6.refs_5_), channel_id=1, source_target_pairs={{0,6},{2,0},{4,2},{6,4},{1,7},{3,1},{5,3},{7,5},{8,14},{10,8},{12,... | collective-permute-start | bytes 786440 | tf_op jit(solution)/shard_map/ppermute | solution.py:53
  18.2 2.0 %collective-permute-done.1.refs_3_ = bf16[32,4096]{1,0:T(8,128)(2,1)S(1)} collective-permute-done((bf16[32,4096]{1,0:T(8,128)(2,1)S(1)}, bf16[32,4096]{1,0:T(8,128)(2,1)S(1)}, u32[]{:S(2)}, u32[]{:S(2)}) %collective-permute-start.1) | collective-permute-done | bytes 262176 | tf_op jit(solution)/shard_map/ppermute | solution.py:49
  20.6 2.9 %collective-permute-start.4 = (bf16[64,4096]{1,0:T(8,128)(2,1)S(1)}, bf16[64,4096]{1,0:T(8,128)(2,1)S(1)}, u32[]{:S(2)}, u32[]{:S(2)}) collective-permute-start(bf16[64,4096]{1,0:T(8,128)(2,1)S(1)} %collective-permute-done.refs_1_), channel_id=1, source_target_pairs={{0,6},{2,0},{4,2},{6,4},{1,7},{3,1},{5,3},{7,5},{8,14},{10,8},{12,... | collective-permute-start | bytes 1572872 | tf_op jit(solution)/shard_map/ppermute | solution.py:56
  23.5 1.6 %collective-permute-done.7.refs_2_ = bf16[32,4096]{1,0:T(8,128)(2,1)S(1)} collective-permute-done((bf16[32,4096]{1,0:T(8,128)(2,1)S(1)}, bf16[32,4096]{1,0:T(8,128)(2,1)S(1)}, u32[]{:S(2)}, u32[]{:S(2)}) %collective-permute-start.7) | collective-permute-done | bytes 262176 | tf_op jit(solution)/shard_map/ppermute | solution.py:52
  26.2 2.4 %collective-permute-start.10 = (bf16[32,4096]{1,0:T(8,128)(2,1)S(1)}, bf16[32,4096]{1,0:T(8,128)(2,1)S(1)}, u32[]{:S(2)}, u32[]{:S(2)}) collective-permute-start(bf16[32,4096]{1,0:T(8,128)(2,1)S(1)} %collective-permute-done.8.refs_3_), channel_id=1, source_target_pairs={{0,1},{1,0},{2,3},{3,2},{4,5},{5,4},{6,7},{7,6},{8,9},{9,8},{10,11... | collective-permute-start | bytes 786440 | tf_op jit(solution)/shard_map/ppermute | solution.py:58
  28.6 2.6 %near.1.refs_9_ = f32[32,256]{1,0:T(8,128)S(1)} custom-call(bf16[64,4096]{1,0:T(8,128)(2,1)} %bitcast.whole.refs_0_, bf16[64,4096]{1,0:T(8,128)(2,1)S(1)} %collective-permute-done.refs_1_, bf16[32,4096]{1,0:T(8,128)(2,1)S(1)} %collective-permute-done.5.refs_2_, bf16[32,4096]{1,0:T(8,128)(2,1)S(1)} %collective-permute-done.1.refs_3_, ...), custom_call_target="tpu_custom_call" | custom-call | flops 805306368 | bytes 5242880 | tf_op jit(solution)/shard_map/near/pallas_call | solution.py:293
  31.2 2.6 %collective-permute-start.15 = (bf16[320,1024]{1,0:T(8,128)(2,1)S(1)}, bf16[320,1024]{1,0:T(8,128)(2,1)S(1)}, u32[]{:S(2)}, u32[]{:S(2)}) collective-permute-start(bf16[320,1024]{1,0:T(8,128)(2,1)S(1)} %get-tuple-element.54), channel_id=1, source_target_pairs={{0,6},{2,0},{4,2},{6,4},{1,7},{3,1},{5,3},{7,5},{8,14},{10,8},{12,... | collective-permute-start | bytes 1966088 | tf_op jit(solution)/shard_map/ppermute | solution.py:306
  33.8 1.8 %collective-permute-done.9.refs_4_ = bf16[32,4096]{1,0:T(8,128)(2,1)S(1)} collective-permute-done((bf16[32,4096]{1,0:T(8,128)(2,1)S(1)}, bf16[32,4096]{1,0:T(8,128)(2,1)S(1)}, u32[]{:S(2)}, u32[]{:S(2)}) %collective-permute-start.9) | collective-permute-done | bytes 262176 | tf_op jit(solution)/shard_map/ppermute | solution.py:57
  35.9 2.6 %collective-permute-done.10.refs_5_ = bf16[32,4096]{1,0:T(8,128)(2,1)S(1)} collective-permute-done((bf16[32,4096]{1,0:T(8,128)(2,1)S(1)}, bf16[32,4096]{1,0:T(8,128)(2,1)S(1)}, u32[]{:S(2)}, u32[]{:S(2)}) %collective-permute-start.10) | collective-permute-done | bytes 262176 | tf_op jit(solution)/shard_map/ppermute | solution.py:58
  38.5 1.6 %away.1 = f32[64,256]{1,0:T(8,128)S(1)} custom-call(bf16[64,4096]{1,0:T(8,128)(2,1)S(1)} %collective-permute-done.3.refs_0_, bf16[64,4096]{1,0:T(8,128)(2,1)S(1)} %collective-permute-done.4.refs_1_, bf16[32,4096]{1,0:T(8,128)(2,1)S(1)} %collective-permute-done.7.refs_2_, bf16[32,4096]{1,0:T(8,128)(2,1)S(1)} %collective-permute-done.8.refs_3_, ...), custom_call_target="tpu_custom_call" | custom-call | flops 805306368 | bytes 5242880 | tf_op jit(solution)/shard_map/away/pallas_call | solution.py:308
  41.6 1.9 %collective-permute-start.13 = (f32[64,256]{1,0:T(8,128)S(1)}, f32[64,256]{1,0:T(8,128)S(1)}, u32[]{:S(2)}, u32[]{:S(2)}) collective-permute-start(f32[64,256]{1,0:T(8,128)S(1)} %add.21), channel_id=1, source_target_pairs={{0,32},{32,0},{64,96},{96,64},{128,160},{160,128},{192,224},{224,1... | collective-permute-start | bytes 196616 | tf_op jit(solution)/shard_map/ppermute | solution.py:255
  44.9 2.3 %collective-permute-done.14 = f32[64,256]{1,0:T(8,128)S(1)} collective-permute-done((f32[64,256]{1,0:T(8,128)S(1)}, f32[64,256]{1,0:T(8,128)S(1)}, u32[]{:S(2)}, u32[]{:S(2)}) %collective-permute-start.14) | collective-permute-done | bytes 65568 | tf_op jit(solution)/shard_map/ppermute | solution.py:255
  47.9 5.9 %collective-permute-start.19 = (f32[64,256]{1,0:T(8,128)S(1)}, f32[64,256]{1,0:T(8,128)S(1)}, u32[]{:S(2)}, u32[]{:S(2)}) collective-permute-start(f32[64,256]{1,0:T(8,128)S(1)} %add_add_fusion.1), channel_id=1, source_target_pairs={{0,160},{32,128},{64,224},{96,192},{128,32},{160,0},{192,96},{224,... | collective-permute-start | bytes 196616 | tf_op jit(solution)/shard_map/ppermute | solution.py:256
  56.9 3.3 %collective-permute-done.18 = f32[64,256]{1,0:T(8,128)S(1)} collective-permute-done((f32[64,256]{1,0:T(8,128)S(1)}, f32[64,256]{1,0:T(8,128)S(1)}, u32[]{:S(2)}, u32[]{:S(2)}) %collective-permute-start.18) | collective-permute-done | bytes 65568 | tf_op jit(solution)/shard_map/ppermute | solution.py:257
  61.2 2.7 %collective-permute-start.20 = (bf16[64,384]{1,0:T(8,128)(2,1)S(1)}, bf16[64,384]{1,0:T(8,128)(2,1)S(1)}, u32[]{:S(2)}, u32[]{:S(2)}) collective-permute-start(bf16[64,384]{1,0:T(8,128)(2,1)S(1)} %weights.1.own), channel_id=1, source_target_pairs={{0,6},{2,0},{4,2},{6,4},{1,7},{3,1},{5,3},{7,5},{8,14},{10,8},{12,... | collective-permute-start | bytes 147464 | tf_op jit(solution)/shard_map/ppermute | solution.py:330
  63.9 1.5 %compose_own.1 = (f32[256,2048]{1,0:T(8,128)S(1)}, f32[256,128]{1,0:T(8,128)S(1)}, bf16[256,256]{1,0:T(8,128)(2,1)S(1)}) custom-call(s32[4]{0:T(128)S(1)} %copy-done.2, bf16[64,384]{1,0:T(8,128)(2,1)S(1)} %weights.1.own, bf16[320,4096]{1,0:T(8,128)(2,1)S(1)} %copy-done.1), custom_call_target="tpu_custom_call" | custom-call | flops 335544320 | bytes 5242880 | tf_op jit(solution)/shard_map/compose_own/pallas_call | solution.py:332
  65.9 1.9 %compose.1 = bf16[256,2176]{1,0:T(8,128)(2,1)S(1)} custom-call(s32[4]{0:T(128)S(1)} %copy-done.2, f32[256,2048]{1,0:T(8,128)S(1)} %get-tuple-element.58.partial, f32[256,128]{1,0:T(8,128)S(1)} %get-tuple-element.59.own_facts, bf16[256,256]{1,0:T(8,128)(2,1)S(1)} %get-tuple-element.60.order, bf16[64,384]{1,0:T(8,128)(2,1)S(1)} %collective-permute-done.20.up, ...), custom_call_target="tpu_custom_call" | custom-call | flops 335544320 | bytes 5242880 | tf_op jit(solution)/shard_map/compose/pallas_call | solution.py:345
  67.8 20.4 %all_to_all.5.parts = bf16[8,32,2176]{2,1,0:T(8,128)(2,1)S(1)} all-to-all(bf16[8,32,2176]{2,1,0:T(8,128)(2,1)S(1)} %bitcast.4), channel_id=1, replica_groups=mesh['z'=8,'xl'=2,'co'=2,'yh'=2,'yl'=2,'xh'=2] {'yh','yl','xh'}, dimensions={0} | all-to-all | bytes 2228224 | tf_op jit(solution)/shard_map/all_to_all | solution.py:356
  (42 shorter events, 15.2 us)
Async XLA Ops:
  1.1 19.6 %collective-permute-start = (bf16[64,4096]{1,0:T(8,128)(2,1)}, bf16[64,4096]{1,0:T(8,128)(2,1)S(1)}, u32[]{:S(2)}, u32[]{:S(2)}) collective-permute-start(bf16[64,4096]{1,0:T(8,128)(2,1)} %bitcast.whole.refs_0_), channel_id=1, source_target_pairs={{0,1},{1,0},{2,3},{3,2},{4,5},{5,4},{6,7},{7,6},{8,9},{9,8},{10,11... | collective-permute-start | bytes 1572872 | tf_op jit(solution)/shard_map/ppermute | solution.py:48
  4.2 10.4 %collective-permute-start.5 = (bf16[32,4096]{1,0:T(8,128)(2,1)S(1)}, bf16[32,4096]{1,0:T(8,128)(2,1)S(1)}, u32[]{:S(2)}, u32[]{:S(2)}) collective-permute-start(bf16[32,4096]{1,0:T(8,128)(2,1)S(1)} %get-tuple-element.38), channel_id=1, source_target_pairs={{0,2},{2,4},{4,6},{6,0},{1,3},{3,5},{5,7},{7,1},{8,10},{10,12},{12... | collective-permute-start | bytes 786440 | tf_op jit(solution)/shard_map/ppermute | solution.py:45
  5.7 9.2 %collective-permute-start.6 = (bf16[32,4096]{1,0:T(8,128)(2,1)S(1)}, bf16[32,4096]{1,0:T(8,128)(2,1)S(1)}, u32[]{:S(2)}, u32[]{:S(2)}) collective-permute-start(bf16[32,4096]{1,0:T(8,128)(2,1)S(1)} %get-tuple-element.37), channel_id=1, source_target_pairs={{0,6},{2,0},{4,2},{6,4},{1,7},{3,1},{5,3},{7,5},{8,14},{10,8},{12,... | collective-permute-start | bytes 786440 | tf_op jit(solution)/shard_map/ppermute | solution.py:46
  7.4 12.8 %collective-permute-start.1 = (bf16[32,4096]{1,0:T(8,128)(2,1)S(1)}, bf16[32,4096]{1,0:T(8,128)(2,1)S(1)}, u32[]{:S(2)}, u32[]{:S(2)}) collective-permute-start(bf16[32,4096]{1,0:T(8,128)(2,1)S(1)} %get-tuple-element.37), channel_id=1, source_target_pairs={{0,2},{2,4},{4,6},{6,0},{1,3},{3,5},{5,7},{7,1},{8,10},{10,12},{12... | collective-permute-start | bytes 786440 | tf_op jit(solution)/shard_map/ppermute | solution.py:49
  7.8 12.8 %collective-permute-start.2 = (bf16[32,4096]{1,0:T(8,128)(2,1)S(1)}, bf16[32,4096]{1,0:T(8,128)(2,1)S(1)}, u32[]{:S(2)}, u32[]{:S(2)}) collective-permute-start(bf16[32,4096]{1,0:T(8,128)(2,1)S(1)} %get-tuple-element.38), channel_id=1, source_target_pairs={{0,6},{2,0},{4,2},{6,4},{1,7},{3,1},{5,3},{7,5},{8,14},{10,8},{12,... | collective-permute-start | bytes 786440 | tf_op jit(solution)/shard_map/ppermute | solution.py:50
  13.7 14.9 %copy-start.1 = (bf16[320,4096]{1,0:T(8,128)(2,1)S(1)}, bf16[320,4096]{1,0:T(8,128)(2,1)}, u32[]{:S(2)}) copy-start(bf16[320,4096]{1,0:T(8,128)(2,1)} %block.1) | copy-start | bytes 7864324
  15.0 10.1 %collective-permute-start.7 = (bf16[32,4096]{1,0:T(8,128)(2,1)S(1)}, bf16[32,4096]{1,0:T(8,128)(2,1)S(1)}, u32[]{:S(2)}, u32[]{:S(2)}) collective-permute-start(bf16[32,4096]{1,0:T(8,128)(2,1)S(1)} %collective-permute-done.5.refs_2_), channel_id=1, source_target_pairs={{0,2},{2,4},{4,6},{6,0},{1,3},{3,5},{5,7},{7,1},{8,10},{10,12},{12... | collective-permute-start | bytes 786440 | tf_op jit(solution)/shard_map/ppermute | solution.py:52
  16.6 9.7 %collective-permute-start.8 = (bf16[32,4096]{1,0:T(8,128)(2,1)S(1)}, bf16[32,4096]{1,0:T(8,128)(2,1)S(1)}, u32[]{:S(2)}, u32[]{:S(2)}) collective-permute-start(bf16[32,4096]{1,0:T(8,128)(2,1)S(1)} %collective-permute-done.6.refs_5_), channel_id=1, source_target_pairs={{0,6},{2,0},{4,2},{6,4},{1,7},{3,1},{5,3},{7,5},{8,14},{10,8},{12,... | collective-permute-start | bytes 786440 | tf_op jit(solution)/shard_map/ppermute | solution.py:53
  20.6 17.9 %collective-permute-start.4 = (bf16[64,4096]{1,0:T(8,128)(2,1)S(1)}, bf16[64,4096]{1,0:T(8,128)(2,1)S(1)}, u32[]{:S(2)}, u32[]{:S(2)}) collective-permute-start(bf16[64,4096]{1,0:T(8,128)(2,1)S(1)} %collective-permute-done.refs_1_), channel_id=1, source_target_pairs={{0,6},{2,0},{4,2},{6,4},{1,7},{3,1},{5,3},{7,5},{8,14},{10,8},{12,... | collective-permute-start | bytes 1572872 | tf_op jit(solution)/shard_map/ppermute | solution.py:56
  23.5 15.0 %collective-permute-start.3 = (bf16[64,4096]{1,0:T(8,128)(2,1)S(1)}, bf16[64,4096]{1,0:T(8,128)(2,1)S(1)}, u32[]{:S(2)}, u32[]{:S(2)}) collective-permute-start(bf16[64,4096]{1,0:T(8,128)(2,1)S(1)} %collective-permute-done.refs_1_), channel_id=1, source_target_pairs={{0,2},{2,4},{4,6},{6,0},{1,3},{3,5},{5,7},{7,1},{8,10},{10,12},{12... | collective-permute-start | bytes 1572872 | tf_op jit(solution)/shard_map/ppermute | solution.py:55
  25.1 10.6 %collective-permute-start.9 = (bf16[32,4096]{1,0:T(8,128)(2,1)S(1)}, bf16[32,4096]{1,0:T(8,128)(2,1)S(1)}, u32[]{:S(2)}, u32[]{:S(2)}) collective-permute-start(bf16[32,4096]{1,0:T(8,128)(2,1)S(1)} %collective-permute-done.7.refs_2_), channel_id=1, source_target_pairs={{0,1},{1,0},{2,3},{3,2},{4,5},{5,4},{6,7},{7,6},{8,9},{9,8},{10,11... | collective-permute-start | bytes 786440 | tf_op jit(solution)/shard_map/ppermute | solution.py:57
  26.2 12.3 %collective-permute-start.10 = (bf16[32,4096]{1,0:T(8,128)(2,1)S(1)}, bf16[32,4096]{1,0:T(8,128)(2,1)S(1)}, u32[]{:S(2)}, u32[]{:S(2)}) collective-permute-start(bf16[32,4096]{1,0:T(8,128)(2,1)S(1)} %collective-permute-done.8.refs_3_), channel_id=1, source_target_pairs={{0,1},{1,0},{2,3},{3,2},{4,5},{5,4},{6,7},{7,6},{8,9},{9,8},{10,11... | collective-permute-start | bytes 786440 | tf_op jit(solution)/shard_map/ppermute | solution.py:58
  31.2 32.6 %copy-start.2 = (s32[4]{0:T(128)S(1)}, s32[4]{0:T(128)}, u32[]{:S(2)}) copy-start(s32[4]{0:T(128)} %leads.3) | copy-start | bytes 52
  31.2 24.1 %collective-permute-start.15 = (bf16[320,1024]{1,0:T(8,128)(2,1)S(1)}, bf16[320,1024]{1,0:T(8,128)(2,1)S(1)}, u32[]{:S(2)}, u32[]{:S(2)}) collective-permute-start(bf16[320,1024]{1,0:T(8,128)(2,1)S(1)} %get-tuple-element.54), channel_id=1, source_target_pairs={{0,6},{2,0},{4,2},{6,4},{1,7},{3,1},{5,3},{7,5},{8,14},{10,8},{12,... | collective-permute-start | bytes 1966088 | tf_op jit(solution)/shard_map/ppermute | solution.py:306
  35.7 19.7 %collective-permute-start.16 = (bf16[320,1024]{1,0:T(8,128)(2,1)S(1)}, bf16[320,1024]{1,0:T(8,128)(2,1)S(1)}, u32[]{:S(2)}, u32[]{:S(2)}) collective-permute-start(bf16[320,1024]{1,0:T(8,128)(2,1)S(1)} %get-tuple-element.55), channel_id=1, source_target_pairs={{0,2},{2,4},{4,6},{6,0},{1,3},{3,5},{5,7},{7,1},{8,10},{10,12},{12... | collective-permute-start | bytes 1966088 | tf_op jit(solution)/shard_map/ppermute | solution.py:305
  40.1 1.3 %collective-permute-start.11 = (f32[64,256]{1,0:T(8,128)S(1)}, f32[64,256]{1,0:T(8,128)S(1)}, u32[]{:S(2)}, u32[]{:S(2)}) collective-permute-start(f32[64,256]{1,0:T(8,128)S(1)} %away.1), channel_id=1, source_target_pairs={{0,8},{8,0},{1,9},{9,1},{2,10},{10,2},{3,11},{11,3},{4,12},{12,4},... | collective-permute-start | bytes 196616 | tf_op jit(solution)/shard_map/ppermute | solution.py:253
  41.4 5.8 %collective-permute-start.14 = (f32[64,256]{1,0:T(8,128)S(1)}, f32[64,256]{1,0:T(8,128)S(1)}, u32[]{:S(2)}, u32[]{:S(2)}) collective-permute-start(f32[64,256]{1,0:T(8,128)S(1)} %add.21), channel_id=1, source_target_pairs={{0,48},{16,32},{32,16},{48,0},{64,112},{80,96},{96,80},{112,64},{1... | collective-permute-start | bytes 196616 | tf_op jit(solution)/shard_map/ppermute | solution.py:255
  41.6 5.6 %collective-permute-start.13 = (f32[64,256]{1,0:T(8,128)S(1)}, f32[64,256]{1,0:T(8,128)S(1)}, u32[]{:S(2)}, u32[]{:S(2)}) collective-permute-start(f32[64,256]{1,0:T(8,128)S(1)} %add.21), channel_id=1, source_target_pairs={{0,32},{32,0},{64,96},{96,64},{128,160},{160,128},{192,224},{224,1... | collective-permute-start | bytes 196616 | tf_op jit(solution)/shard_map/ppermute | solution.py:255
  43.5 4.4 %collective-permute-start.12 = (f32[64,256]{1,0:T(8,128)S(1)}, f32[64,256]{1,0:T(8,128)S(1)}, u32[]{:S(2)}, u32[]{:S(2)}) collective-permute-start(f32[64,256]{1,0:T(8,128)S(1)} %add.21), channel_id=1, source_target_pairs={{0,16},{16,0},{1,17},{17,1},{2,18},{18,2},{3,19},{19,3},{4,20},{20... | collective-permute-start | bytes 196616 | tf_op jit(solution)/shard_map/ppermute | solution.py:255
  47.9 9.0 %collective-permute-start.19 = (f32[64,256]{1,0:T(8,128)S(1)}, f32[64,256]{1,0:T(8,128)S(1)}, u32[]{:S(2)}, u32[]{:S(2)}) collective-permute-start(f32[64,256]{1,0:T(8,128)S(1)} %add_add_fusion.1), channel_id=1, source_target_pairs={{0,160},{32,128},{64,224},{96,192},{128,32},{160,0},{192,96},{224,... | collective-permute-start | bytes 196616 | tf_op jit(solution)/shard_map/ppermute | solution.py:256
  53.9 6.4 %collective-permute-start.18 = (f32[64,256]{1,0:T(8,128)S(1)}, f32[64,256]{1,0:T(8,128)S(1)}, u32[]{:S(2)}, u32[]{:S(2)}) collective-permute-start(f32[64,256]{1,0:T(8,128)S(1)} %add_add_fusion.1), channel_id=1, source_target_pairs={{0,192},{32,96},{64,0},{96,160},{128,64},{160,224},{192,128},{224,... | collective-permute-start | bytes 196616 | tf_op jit(solution)/shard_map/ppermute | solution.py:257
  55.3 4.9 %collective-permute-start.17 = (f32[64,256]{1,0:T(8,128)S(1)}, f32[64,256]{1,0:T(8,128)S(1)}, u32[]{:S(2)}, u32[]{:S(2)}) collective-permute-start(f32[64,256]{1,0:T(8,128)S(1)} %add_add_fusion.1), channel_id=1, source_target_pairs={{0,224},{32,64},{64,32},{96,128},{128,96},{160,192},{192,160},{224... | collective-permute-start | bytes 196616 | tf_op jit(solution)/shard_map/ppermute | solution.py:259
  60.6 5.4 %collective-permute-start.21 = (bf16[64,384]{1,0:T(8,128)(2,1)S(1)}, bf16[64,384]{1,0:T(8,128)(2,1)S(1)}, u32[]{:S(2)}, u32[]{:S(2)}) collective-permute-start(bf16[64,384]{1,0:T(8,128)(2,1)S(1)} %weights.1.own), channel_id=1, source_target_pairs={{0,2},{2,4},{4,6},{6,0},{1,3},{3,5},{5,7},{7,1},{8,10},{10,12},{12... | collective-permute-start | bytes 147464 | tf_op jit(solution)/shard_map/ppermute | solution.py:329
  61.2 4.8 %collective-permute-start.20 = (bf16[64,384]{1,0:T(8,128)(2,1)S(1)}, bf16[64,384]{1,0:T(8,128)(2,1)S(1)}, u32[]{:S(2)}, u32[]{:S(2)}) collective-permute-start(bf16[64,384]{1,0:T(8,128)(2,1)S(1)} %weights.1.own), channel_id=1, source_target_pairs={{0,6},{2,0},{4,2},{6,4},{1,7},{3,1},{5,3},{7,5},{8,14},{10,8},{12,... | collective-permute-start | bytes 147464 | tf_op jit(solution)/shard_map/ppermute | solution.py:330
  (3 other events, 3.1 us)

commit v12 on v11

--- a/solution.py
+++ b/solution.py
@@ -48,10 +48,9 @@
     across = lax.ppermute(sent, "xh", flip(2, 1))
     below_b = lax.ppermute(late, Y, turn(4, 1))
     above_a = lax.ppermute(early, Y, turn(4, -1))
-    below_a, above_b, ready = lax.optimization_barrier((below_a, above_b, ready))
     far_a = lax.ppermute(below_a, Y, turn(4, 1))
     far_b = lax.ppermute(above_b, Y, turn(4, -1))
-    across, below_b, above_a = lax.optimization_barrier((across, below_b, above_a))
+    across, below_b, above_a, ready = lax.optimization_barrier((across, below_b, above_a, ready))
     below_x = lax.ppermute(across, Y, turn(4, 1))
     above_x = lax.ppermute(across, Y, turn(4, -1))
     far_xa = lax.ppermute(far_a, "xh", flip(2, 1))

time: 89.9 us -> 89.9 us (level)
    ppermute x1, waiting for transfers between devices: 0.14 us -> 3.96 us  [gather_targets(): below_a = lax.ppermute(early, Y, turn(4, 1))]
    ppermute x1, waiting for transfers between devices: 1.99 us -> 0.01 us  [gather_targets(): below_b = lax.ppermute(late, Y, turn(4, 1))]
    ppermute x1, starting transfers between devices: 1.66 us -> 2.87 us  [gather_targets(): far_b = lax.ppermute(above_b, Y, turn(4, -1))]
    ppermute x1, starting transfers between devices: 1.58 us -> 0.37 us  [gather_targets(): far_a = lax.ppermute(below_a, Y, turn(4, 1))]
    ppermute x1, starting transfers between devices: 2.87 us -> 1.77 us  [gather_targets(): above_x = lax.ppermute(across, Y, turn(4, -1))]
  transfers between devices with their start and end apart: 22 -> 22, of which waited for: 14 -> 11; matrix products, arithmetic and copies ran while one was open for 0% -> 0% of each run, Pallas kernels for 7% -> 7%
where the time goes in v12:
time: 89.9 us; the launch traced here: 89.4 us
  starting transfers between devices  35.5 us (39%)
  blocking collectives  20.4 us (23%)
  waiting for transfers between devices  19.5 us (22%)
  Pallas kernels  10.9 us (12%)
  local copies, waits for them, and re-layouts  3.08 us (3%)
    all_to_all x1, blocking collectives, per_device(): parts = lax.all_to_all(parts, LIB, 0, 0, tiled=True)  20.4 us
    ppermute x1, starting transfers between devices, total_over_space(): lax.ppermute(value, 'z', [(z, (z - 3) % 8 if z % 2 == 0 else (z + 3) % 8)...  5.92 us
    ppermute x1, waiting for transfers between devices, gather_targets(): below_a = lax.ppermute(early, Y, turn(4, 1))  3.96 us
    ppermute x1, waiting for transfers between devices, total_over_space(): lax.ppermute(value, 'z', [(z, (z - 2) % 8 if z % 2 == 0 else (z + 2) % 8)...  3.32 us
    ppermute x1, starting transfers between devices, gather_targets(): across = lax.ppermute(sent, 'xh', flip(2, 1))  3.11 us
    unnamed x10, local copies, waits for them, and re-layouts  3.08 us
    ppermute x1, starting transfers between devices, gather_targets(): above_a = lax.ppermute(early, Y, turn(4, -1))  2.87 us
    ppermute x1, starting transfers between devices, gather_targets(): far_b = lax.ppermute(above_b, Y, turn(4, -1))  2.87 us
  transfers between devices with their start and end apart: 22, of which 11 were waited for; matrix products, arithmetic and copies ran while one was open for 0% of the time, Pallas kernels for 7%

profile of v12, /device:TPU:32, one launch (start us, length us, event | category | flops | bytes accessed | tf_op | source)
XLA Modules:
  0.0 89.4 jit_solution(11661127603870945103)
XLA Ops:
  1.1 3.1 %collective-permute-start = (bf16[64,4096]{1,0:T(8,128)(2,1)}, bf16[64,4096]{1,0:T(8,128)(2,1)S(1)}, u32[]{:S(2)}, u32[]{:S(2)}) collective-permute-start(bf16[64,4096]{1,0:T(8,128)(2,1)} %bitcast.whole.refs_0_), channel_id=1, source_target_pairs={{0,1},{1,0},{2,3},{3,2},{4,5},{5,4},{6,7},{7,6},{8,9},{9,8},{10,11... | collective-permute-start | bytes 1572872 | tf_op jit(solution)/shard_map/ppermute | solution.py:48
  4.2 1.6 %collective-permute-start.5 = (bf16[32,4096]{1,0:T(8,128)(2,1)S(1)}, bf16[32,4096]{1,0:T(8,128)(2,1)S(1)}, u32[]{:S(2)}, u32[]{:S(2)}) collective-permute-start(bf16[32,4096]{1,0:T(8,128)(2,1)S(1)} %get-tuple-element.36), channel_id=1, source_target_pairs={{0,2},{2,4},{4,6},{6,0},{1,3},{3,5},{5,7},{7,1},{8,10},{10,12},{12... | collective-permute-start | bytes 786440 | tf_op jit(solution)/shard_map/ppermute | solution.py:45
  5.7 1.7 %collective-permute-start.7 = (bf16[32,4096]{1,0:T(8,128)(2,1)S(1)}, bf16[32,4096]{1,0:T(8,128)(2,1)S(1)}, u32[]{:S(2)}, u32[]{:S(2)}) collective-permute-start(bf16[32,4096]{1,0:T(8,128)(2,1)S(1)} %get-tuple-element.35), channel_id=1, source_target_pairs={{0,6},{2,0},{4,2},{6,4},{1,7},{3,1},{5,3},{7,5},{8,14},{10,8},{12,... | collective-permute-start | bytes 786440 | tf_op jit(solution)/shard_map/ppermute | solution.py:46
  7.8 2.9 %collective-permute-start.2 = (bf16[32,4096]{1,0:T(8,128)(2,1)S(1)}, bf16[32,4096]{1,0:T(8,128)(2,1)S(1)}, u32[]{:S(2)}, u32[]{:S(2)}) collective-permute-start(bf16[32,4096]{1,0:T(8,128)(2,1)S(1)} %get-tuple-element.36), channel_id=1, source_target_pairs={{0,6},{2,0},{4,2},{6,4},{1,7},{3,1},{5,3},{7,5},{8,14},{10,8},{12,... | collective-permute-start | bytes 786440 | tf_op jit(solution)/shard_map/ppermute | solution.py:50
  10.6 4.0 %collective-permute-done.5.refs_2_ = bf16[32,4096]{1,0:T(8,128)(2,1)S(1)} collective-permute-done((bf16[32,4096]{1,0:T(8,128)(2,1)S(1)}, bf16[32,4096]{1,0:T(8,128)(2,1)S(1)}, u32[]{:S(2)}, u32[]{:S(2)}) %collective-permute-start.5) | collective-permute-done | bytes 262176 | tf_op jit(solution)/shard_map/ppermute | solution.py:45
  15.0 2.9 %collective-permute-start.8 = (bf16[32,4096]{1,0:T(8,128)(2,1)S(1)}, bf16[32,4096]{1,0:T(8,128)(2,1)S(1)}, u32[]{:S(2)}, u32[]{:S(2)}) collective-permute-start(bf16[32,4096]{1,0:T(8,128)(2,1)S(1)} %collective-permute-done.7.refs_5_), channel_id=1, source_target_pairs={{0,6},{2,0},{4,2},{6,4},{1,7},{3,1},{5,3},{7,5},{8,14},{10,8},{12,... | collective-permute-start | bytes 786440 | tf_op jit(solution)/shard_map/ppermute | solution.py:52
  17.9 1.7 %copy-done = bf16[320,4096]{1,0:T(8,128)(2,1)S(1)} copy-done((bf16[320,4096]{1,0:T(8,128)(2,1)S(1)}, bf16[320,4096]{1,0:T(8,128)(2,1)}, u32[]{:S(2)}) %copy-start) | copy-done | bytes 2621464
  21.7 1.8 %collective-permute-start.4 = (bf16[64,4096]{1,0:T(8,128)(2,1)S(1)}, bf16[64,4096]{1,0:T(8,128)(2,1)S(1)}, u32[]{:S(2)}, u32[]{:S(2)}) collective-permute-start(bf16[64,4096]{1,0:T(8,128)(2,1)S(1)} %collective-permute-done.refs_1_), channel_id=1, source_target_pairs={{0,6},{2,0},{4,2},{6,4},{1,7},{3,1},{5,3},{7,5},{8,14},{10,8},{12,... | collective-permute-start | bytes 1572872 | tf_op jit(solution)/shard_map/ppermute | solution.py:55
  26.2 2.4 %collective-permute-start.10 = (bf16[32,4096]{1,0:T(8,128)(2,1)S(1)}, bf16[32,4096]{1,0:T(8,128)(2,1)S(1)}, u32[]{:S(2)}, u32[]{:S(2)}) collective-permute-start(bf16[32,4096]{1,0:T(8,128)(2,1)S(1)} %collective-permute-done.8.refs_3_), channel_id=1, source_target_pairs={{0,1},{1,0},{2,3},{3,2},{4,5},{5,4},{6,7},{7,6},{8,9},{9,8},{10,11... | collective-permute-start | bytes 786440 | tf_op jit(solution)/shard_map/ppermute | solution.py:57
  28.6 2.6 %near.1.refs_9_ = f32[32,256]{1,0:T(8,128)S(1)} custom-call(bf16[64,4096]{1,0:T(8,128)(2,1)} %bitcast.whole.refs_0_, bf16[64,4096]{1,0:T(8,128)(2,1)S(1)} %collective-permute-done.refs_1_, bf16[32,4096]{1,0:T(8,128)(2,1)S(1)} %collective-permute-done.5.refs_2_, bf16[32,4096]{1,0:T(8,128)(2,1)S(1)} %collective-permute-done.1.refs_3_, ...), custom_call_target="tpu_custom_call" | custom-call | flops 805306368 | bytes 5242880 | tf_op jit(solution)/shard_map/near/pallas_call | solution.py:292
  31.2 2.6 %collective-permute-start.15 = (bf16[320,1024]{1,0:T(8,128)(2,1)S(1)}, bf16[320,1024]{1,0:T(8,128)(2,1)S(1)}, u32[]{:S(2)}, u32[]{:S(2)}) collective-permute-start(bf16[320,1024]{1,0:T(8,128)(2,1)S(1)} %get-tuple-element.50), channel_id=1, source_target_pairs={{0,6},{2,0},{4,2},{6,4},{1,7},{3,1},{5,3},{7,5},{8,14},{10,8},{12,... | collective-permute-start | bytes 1966088 | tf_op jit(solution)/shard_map/ppermute | solution.py:305
  33.8 1.8 %collective-permute-done.9.refs_4_ = bf16[32,4096]{1,0:T(8,128)(2,1)S(1)} collective-permute-done((bf16[32,4096]{1,0:T(8,128)(2,1)S(1)}, bf16[32,4096]{1,0:T(8,128)(2,1)S(1)}, u32[]{:S(2)}, u32[]{:S(2)}) %collective-permute-start.9) | collective-permute-done | bytes 262176 | tf_op jit(solution)/shard_map/ppermute | solution.py:56
  35.9 2.6 %collective-permute-done.10.refs_5_ = bf16[32,4096]{1,0:T(8,128)(2,1)S(1)} collective-permute-done((bf16[32,4096]{1,0:T(8,128)(2,1)S(1)}, bf16[32,4096]{1,0:T(8,128)(2,1)S(1)}, u32[]{:S(2)}, u32[]{:S(2)}) %collective-permute-start.10) | collective-permute-done | bytes 262176 | tf_op jit(solution)/shard_map/ppermute | solution.py:57
  38.5 1.6 %away.1 = f32[64,256]{1,0:T(8,128)S(1)} custom-call(bf16[64,4096]{1,0:T(8,128)(2,1)S(1)} %collective-permute-done.3.refs_0_, bf16[64,4096]{1,0:T(8,128)(2,1)S(1)} %collective-permute-done.4.refs_1_, bf16[32,4096]{1,0:T(8,128)(2,1)S(1)} %collective-permute-done.6.refs_2_, bf16[32,4096]{1,0:T(8,128)(2,1)S(1)} %collective-permute-done.8.refs_3_, ...), custom_call_target="tpu_custom_call" | custom-call | flops 805306368 | bytes 5242880 | tf_op jit(solution)/shard_map/away/pallas_call | solution.py:307
  41.6 1.9 %collective-permute-start.13 = (f32[64,256]{1,0:T(8,128)S(1)}, f32[64,256]{1,0:T(8,128)S(1)}, u32[]{:S(2)}, u32[]{:S(2)}) collective-permute-start(f32[64,256]{1,0:T(8,128)S(1)} %add.21), channel_id=1, source_target_pairs={{0,32},{32,0},{64,96},{96,64},{128,160},{160,128},{192,224},{224,1... | collective-permute-start | bytes 196616 | tf_op jit(solution)/shard_map/ppermute | solution.py:254
  43.5 1.4 %collective-permute-start.12 = (f32[64,256]{1,0:T(8,128)S(1)}, f32[64,256]{1,0:T(8,128)S(1)}, u32[]{:S(2)}, u32[]{:S(2)}) collective-permute-start(f32[64,256]{1,0:T(8,128)S(1)} %add.21), channel_id=1, source_target_pairs={{0,16},{16,0},{1,17},{17,1},{2,18},{18,2},{3,19},{19,3},{4,20},{20... | collective-permute-start | bytes 196616 | tf_op jit(solution)/shard_map/ppermute | solution.py:254
  44.9 2.3 %collective-permute-done.14 = f32[64,256]{1,0:T(8,128)S(1)} collective-permute-done((f32[64,256]{1,0:T(8,128)S(1)}, f32[64,256]{1,0:T(8,128)S(1)}, u32[]{:S(2)}, u32[]{:S(2)}) %collective-permute-start.14) | collective-permute-done | bytes 65568 | tf_op jit(solution)/shard_map/ppermute | solution.py:254
  47.9 5.9 %collective-permute-start.19 = (f32[64,256]{1,0:T(8,128)S(1)}, f32[64,256]{1,0:T(8,128)S(1)}, u32[]{:S(2)}, u32[]{:S(2)}) collective-permute-start(f32[64,256]{1,0:T(8,128)S(1)} %add_add_fusion.1), channel_id=1, source_target_pairs={{0,160},{32,128},{64,224},{96,192},{128,32},{160,0},{192,96},{224,... | collective-permute-start | bytes 196616 | tf_op jit(solution)/shard_map/ppermute | solution.py:255
  53.9 1.5 %collective-permute-start.18 = (f32[64,256]{1,0:T(8,128)S(1)}, f32[64,256]{1,0:T(8,128)S(1)}, u32[]{:S(2)}, u32[]{:S(2)}) collective-permute-start(f32[64,256]{1,0:T(8,128)S(1)} %add_add_fusion.1), channel_id=1, source_target_pairs={{0,192},{32,96},{64,0},{96,160},{128,64},{160,224},{192,128},{224,... | collective-permute-start | bytes 196616 | tf_op jit(solution)/shard_map/ppermute | solution.py:256
  56.9 3.3 %collective-permute-done.18 = f32[64,256]{1,0:T(8,128)S(1)} collective-permute-done((f32[64,256]{1,0:T(8,128)S(1)}, f32[64,256]{1,0:T(8,128)S(1)}, u32[]{:S(2)}, u32[]{:S(2)}) %collective-permute-start.18) | collective-permute-done | bytes 65568 | tf_op jit(solution)/shard_map/ppermute | solution.py:256
  61.2 2.7 %collective-permute-start.20 = (bf16[64,384]{1,0:T(8,128)(2,1)S(1)}, bf16[64,384]{1,0:T(8,128)(2,1)S(1)}, u32[]{:S(2)}, u32[]{:S(2)}) collective-permute-start(bf16[64,384]{1,0:T(8,128)(2,1)S(1)} %weights.1.own), channel_id=1, source_target_pairs={{0,6},{2,0},{4,2},{6,4},{1,7},{3,1},{5,3},{7,5},{8,14},{10,8},{12,... | collective-permute-start | bytes 147464 | tf_op jit(solution)/shard_map/ppermute | solution.py:329
  63.9 1.5 %compose_own.1 = (f32[256,2048]{1,0:T(8,128)S(1)}, f32[256,128]{1,0:T(8,128)S(1)}, bf16[256,256]{1,0:T(8,128)(2,1)S(1)}) custom-call(s32[4]{0:T(128)S(1)} %copy-done.2, bf16[64,384]{1,0:T(8,128)(2,1)S(1)} %weights.1.own, bf16[320,4096]{1,0:T(8,128)(2,1)S(1)} %copy-done.1), custom_call_target="tpu_custom_call" | custom-call | flops 335544320 | bytes 5242880 | tf_op jit(solution)/shard_map/compose_own/pallas_call | solution.py:331
  65.9 1.9 %compose.1 = bf16[256,2176]{1,0:T(8,128)(2,1)S(1)} custom-call(s32[4]{0:T(128)S(1)} %copy-done.2, f32[256,2048]{1,0:T(8,128)S(1)} %get-tuple-element.54.partial, f32[256,128]{1,0:T(8,128)S(1)} %get-tuple-element.55.own_facts, bf16[256,256]{1,0:T(8,128)(2,1)S(1)} %get-tuple-element.56.order, bf16[64,384]{1,0:T(8,128)(2,1)S(1)} %collective-permute-done.20.up, ...), custom_call_target="tpu_custom_call" | custom-call | flops 335544320 | bytes 5242880 | tf_op jit(solution)/shard_map/compose/pallas_call | solution.py:344
  67.8 20.4 %all_to_all.5.parts = bf16[8,32,2176]{2,1,0:T(8,128)(2,1)S(1)} all-to-all(bf16[8,32,2176]{2,1,0:T(8,128)(2,1)S(1)} %bitcast.4), channel_id=1, replica_groups=mesh['z'=8,'xl'=2,'co'=2,'yh'=2,'yl'=2,'xh'=2] {'yh','yl','xh'}, dimensions={0} | all-to-all | bytes 2228224 | tf_op jit(solution)/shard_map/all_to_all | solution.py:355
  (42 shorter events, 13.4 us)
Async XLA Ops:
  1.1 20.6 %collective-permute-start = (bf16[64,4096]{1,0:T(8,128)(2,1)}, bf16[64,4096]{1,0:T(8,128)(2,1)S(1)}, u32[]{:S(2)}, u32[]{:S(2)}) collective-permute-start(bf16[64,4096]{1,0:T(8,128)(2,1)} %bitcast.whole.refs_0_), channel_id=1, source_target_pairs={{0,1},{1,0},{2,3},{3,2},{4,5},{5,4},{6,7},{7,6},{8,9},{9,8},{10,11... | collective-permute-start | bytes 1572872 | tf_op jit(solution)/shard_map/ppermute | solution.py:48
  4.2 10.4 %collective-permute-start.5 = (bf16[32,4096]{1,0:T(8,128)(2,1)S(1)}, bf16[32,4096]{1,0:T(8,128)(2,1)S(1)}, u32[]{:S(2)}, u32[]{:S(2)}) collective-permute-start(bf16[32,4096]{1,0:T(8,128)(2,1)S(1)} %get-tuple-element.36), channel_id=1, source_target_pairs={{0,2},{2,4},{4,6},{6,0},{1,3},{3,5},{5,7},{7,1},{8,10},{10,12},{12... | collective-permute-start | bytes 786440 | tf_op jit(solution)/shard_map/ppermute | solution.py:45
  5.7 9.2 %collective-permute-start.7 = (bf16[32,4096]{1,0:T(8,128)(2,1)S(1)}, bf16[32,4096]{1,0:T(8,128)(2,1)S(1)}, u32[]{:S(2)}, u32[]{:S(2)}) collective-permute-start(bf16[32,4096]{1,0:T(8,128)(2,1)S(1)} %get-tuple-element.35), channel_id=1, source_target_pairs={{0,6},{2,0},{4,2},{6,4},{1,7},{3,1},{5,3},{7,5},{8,14},{10,8},{12,... | collective-permute-start | bytes 786440 | tf_op jit(solution)/shard_map/ppermute | solution.py:46
  7.4 14.3 %collective-permute-start.1 = (bf16[32,4096]{1,0:T(8,128)(2,1)S(1)}, bf16[32,4096]{1,0:T(8,128)(2,1)S(1)}, u32[]{:S(2)}, u32[]{:S(2)}) collective-permute-start(bf16[32,4096]{1,0:T(8,128)(2,1)S(1)} %get-tuple-element.35), channel_id=1, source_target_pairs={{0,2},{2,4},{4,6},{6,0},{1,3},{3,5},{5,7},{7,1},{8,10},{10,12},{12... | collective-permute-start | bytes 786440 | tf_op jit(solution)/shard_map/ppermute | solution.py:49
  7.8 13.9 %collective-permute-start.2 = (bf16[32,4096]{1,0:T(8,128)(2,1)S(1)}, bf16[32,4096]{1,0:T(8,128)(2,1)S(1)}, u32[]{:S(2)}, u32[]{:S(2)}) collective-permute-start(bf16[32,4096]{1,0:T(8,128)(2,1)S(1)} %get-tuple-element.36), channel_id=1, source_target_pairs={{0,6},{2,0},{4,2},{6,4},{1,7},{3,1},{5,3},{7,5},{8,14},{10,8},{12,... | collective-permute-start | bytes 786440 | tf_op jit(solution)/shard_map/ppermute | solution.py:50
  14.6 10.5 %collective-permute-start.6 = (bf16[32,4096]{1,0:T(8,128)(2,1)S(1)}, bf16[32,4096]{1,0:T(8,128)(2,1)S(1)}, u32[]{:S(2)}, u32[]{:S(2)}) collective-permute-start(bf16[32,4096]{1,0:T(8,128)(2,1)S(1)} %collective-permute-done.5.refs_2_), channel_id=1, source_target_pairs={{0,2},{2,4},{4,6},{6,0},{1,3},{3,5},{5,7},{7,1},{8,10},{10,12},{12... | collective-permute-start | bytes 786440 | tf_op jit(solution)/shard_map/ppermute | solution.py:51
  15.0 11.2 %collective-permute-start.8 = (bf16[32,4096]{1,0:T(8,128)(2,1)S(1)}, bf16[32,4096]{1,0:T(8,128)(2,1)S(1)}, u32[]{:S(2)}, u32[]{:S(2)}) collective-permute-start(bf16[32,4096]{1,0:T(8,128)(2,1)S(1)} %collective-permute-done.7.refs_5_), channel_id=1, source_target_pairs={{0,6},{2,0},{4,2},{6,4},{1,7},{3,1},{5,3},{7,5},{8,14},{10,8},{12,... | collective-permute-start | bytes 786440 | tf_op jit(solution)/shard_map/ppermute | solution.py:52
  20.9 7.7 %copy-start.1 = (bf16[320,4096]{1,0:T(8,128)(2,1)S(1)}, bf16[320,4096]{1,0:T(8,128)(2,1)}, u32[]{:S(2)}) copy-start(bf16[320,4096]{1,0:T(8,128)(2,1)} %block.1) | copy-start | bytes 7864324
  21.7 16.8 %collective-permute-start.4 = (bf16[64,4096]{1,0:T(8,128)(2,1)S(1)}, bf16[64,4096]{1,0:T(8,128)(2,1)S(1)}, u32[]{:S(2)}, u32[]{:S(2)}) collective-permute-start(bf16[64,4096]{1,0:T(8,128)(2,1)S(1)} %collective-permute-done.refs_1_), channel_id=1, source_target_pairs={{0,6},{2,0},{4,2},{6,4},{1,7},{3,1},{5,3},{7,5},{8,14},{10,8},{12,... | collective-permute-start | bytes 1572872 | tf_op jit(solution)/shard_map/ppermute | solution.py:55
  23.5 15.0 %collective-permute-start.3 = (bf16[64,4096]{1,0:T(8,128)(2,1)S(1)}, bf16[64,4096]{1,0:T(8,128)(2,1)S(1)}, u32[]{:S(2)}, u32[]{:S(2)}) collective-permute-start(bf16[64,4096]{1,0:T(8,128)(2,1)S(1)} %collective-permute-done.refs_1_), channel_id=1, source_target_pairs={{0,2},{2,4},{4,6},{6,0},{1,3},{3,5},{5,7},{7,1},{8,10},{10,12},{12... | collective-permute-start | bytes 1572872 | tf_op jit(solution)/shard_map/ppermute | solution.py:54
  25.1 10.6 %collective-permute-start.9 = (bf16[32,4096]{1,0:T(8,128)(2,1)S(1)}, bf16[32,4096]{1,0:T(8,128)(2,1)S(1)}, u32[]{:S(2)}, u32[]{:S(2)}) collective-permute-start(bf16[32,4096]{1,0:T(8,128)(2,1)S(1)} %collective-permute-done.6.refs_2_), channel_id=1, source_target_pairs={{0,1},{1,0},{2,3},{3,2},{4,5},{5,4},{6,7},{7,6},{8,9},{9,8},{10,11... | collective-permute-start | bytes 786440 | tf_op jit(solution)/shard_map/ppermute | solution.py:56
  26.2 12.3 %collective-permute-start.10 = (bf16[32,4096]{1,0:T(8,128)(2,1)S(1)}, bf16[32,4096]{1,0:T(8,128)(2,1)S(1)}, u32[]{:S(2)}, u32[]{:S(2)}) collective-permute-start(bf16[32,4096]{1,0:T(8,128)(2,1)S(1)} %collective-permute-done.8.refs_3_), channel_id=1, source_target_pairs={{0,1},{1,0},{2,3},{3,2},{4,5},{5,4},{6,7},{7,6},{8,9},{9,8},{10,11... | collective-permute-start | bytes 786440 | tf_op jit(solution)/shard_map/ppermute | solution.py:57
  31.2 32.6 %copy-start.2 = (s32[4]{0:T(128)S(1)}, s32[4]{0:T(128)}, u32[]{:S(2)}) copy-start(s32[4]{0:T(128)} %leads.3) | copy-start | bytes 52
  31.2 24.1 %collective-permute-start.15 = (bf16[320,1024]{1,0:T(8,128)(2,1)S(1)}, bf16[320,1024]{1,0:T(8,128)(2,1)S(1)}, u32[]{:S(2)}, u32[]{:S(2)}) collective-permute-start(bf16[320,1024]{1,0:T(8,128)(2,1)S(1)} %get-tuple-element.50), channel_id=1, source_target_pairs={{0,6},{2,0},{4,2},{6,4},{1,7},{3,1},{5,3},{7,5},{8,14},{10,8},{12,... | collective-permute-start | bytes 1966088 | tf_op jit(solution)/shard_map/ppermute | solution.py:305
  35.7 19.7 %collective-permute-start.16 = (bf16[320,1024]{1,0:T(8,128)(2,1)S(1)}, bf16[320,1024]{1,0:T(8,128)(2,1)S(1)}, u32[]{:S(2)}, u32[]{:S(2)}) collective-permute-start(bf16[320,1024]{1,0:T(8,128)(2,1)S(1)} %get-tuple-element.51), channel_id=1, source_target_pairs={{0,2},{2,4},{4,6},{6,0},{1,3},{3,5},{5,7},{7,1},{8,10},{10,12},{12... | collective-permute-start | bytes 1966088 | tf_op jit(solution)/shard_map/ppermute | solution.py:304
  40.1 1.3 %collective-permute-start.11 = (f32[64,256]{1,0:T(8,128)S(1)}, f32[64,256]{1,0:T(8,128)S(1)}, u32[]{:S(2)}, u32[]{:S(2)}) collective-permute-start(f32[64,256]{1,0:T(8,128)S(1)} %away.1), channel_id=1, source_target_pairs={{0,8},{8,0},{1,9},{9,1},{2,10},{10,2},{3,11},{11,3},{4,12},{12,4},... | collective-permute-start | bytes 196616 | tf_op jit(solution)/shard_map/ppermute | solution.py:252
  41.4 5.8 %collective-permute-start.14 = (f32[64,256]{1,0:T(8,128)S(1)}, f32[64,256]{1,0:T(8,128)S(1)}, u32[]{:S(2)}, u32[]{:S(2)}) collective-permute-start(f32[64,256]{1,0:T(8,128)S(1)} %add.21), channel_id=1, source_target_pairs={{0,48},{16,32},{32,16},{48,0},{64,112},{80,96},{96,80},{112,64},{1... | collective-permute-start | bytes 196616 | tf_op jit(solution)/shard_map/ppermute | solution.py:254
  41.6 5.6 %collective-permute-start.13 = (f32[64,256]{1,0:T(8,128)S(1)}, f32[64,256]{1,0:T(8,128)S(1)}, u32[]{:S(2)}, u32[]{:S(2)}) collective-permute-start(f32[64,256]{1,0:T(8,128)S(1)} %add.21), channel_id=1, source_target_pairs={{0,32},{32,0},{64,96},{96,64},{128,160},{160,128},{192,224},{224,1... | collective-permute-start | bytes 196616 | tf_op jit(solution)/shard_map/ppermute | solution.py:254
  43.5 4.4 %collective-permute-start.12 = (f32[64,256]{1,0:T(8,128)S(1)}, f32[64,256]{1,0:T(8,128)S(1)}, u32[]{:S(2)}, u32[]{:S(2)}) collective-permute-start(f32[64,256]{1,0:T(8,128)S(1)} %add.21), channel_id=1, source_target_pairs={{0,16},{16,0},{1,17},{17,1},{2,18},{18,2},{3,19},{19,3},{4,20},{20... | collective-permute-start | bytes 196616 | tf_op jit(solution)/shard_map/ppermute | solution.py:254
  47.9 9.0 %collective-permute-start.19 = (f32[64,256]{1,0:T(8,128)S(1)}, f32[64,256]{1,0:T(8,128)S(1)}, u32[]{:S(2)}, u32[]{:S(2)}) collective-permute-start(f32[64,256]{1,0:T(8,128)S(1)} %add_add_fusion.1), channel_id=1, source_target_pairs={{0,160},{32,128},{64,224},{96,192},{128,32},{160,0},{192,96},{224,... | collective-permute-start | bytes 196616 | tf_op jit(solution)/shard_map/ppermute | solution.py:255
  53.9 6.4 %collective-permute-start.18 = (f32[64,256]{1,0:T(8,128)S(1)}, f32[64,256]{1,0:T(8,128)S(1)}, u32[]{:S(2)}, u32[]{:S(2)}) collective-permute-start(f32[64,256]{1,0:T(8,128)S(1)} %add_add_fusion.1), channel_id=1, source_target_pairs={{0,192},{32,96},{64,0},{96,160},{128,64},{160,224},{192,128},{224,... | collective-permute-start | bytes 196616 | tf_op jit(solution)/shard_map/ppermute | solution.py:256
  55.3 4.9 %collective-permute-start.17 = (f32[64,256]{1,0:T(8,128)S(1)}, f32[64,256]{1,0:T(8,128)S(1)}, u32[]{:S(2)}, u32[]{:S(2)}) collective-permute-start(f32[64,256]{1,0:T(8,128)S(1)} %add_add_fusion.1), channel_id=1, source_target_pairs={{0,224},{32,64},{64,32},{96,128},{128,96},{160,192},{192,160},{224... | collective-permute-start | bytes 196616 | tf_op jit(solution)/shard_map/ppermute | solution.py:258
  60.6 5.4 %collective-permute-start.21 = (bf16[64,384]{1,0:T(8,128)(2,1)S(1)}, bf16[64,384]{1,0:T(8,128)(2,1)S(1)}, u32[]{:S(2)}, u32[]{:S(2)}) collective-permute-start(bf16[64,384]{1,0:T(8,128)(2,1)S(1)} %weights.1.own), channel_id=1, source_target_pairs={{0,2},{2,4},{4,6},{6,0},{1,3},{3,5},{5,7},{7,1},{8,10},{10,12},{12... | collective-permute-start | bytes 147464 | tf_op jit(solution)/shard_map/ppermute | solution.py:328
  61.2 4.8 %collective-permute-start.20 = (bf16[64,384]{1,0:T(8,128)(2,1)S(1)}, bf16[64,384]{1,0:T(8,128)(2,1)S(1)}, u32[]{:S(2)}, u32[]{:S(2)}) collective-permute-start(bf16[64,384]{1,0:T(8,128)(2,1)S(1)} %weights.1.own), channel_id=1, source_target_pairs={{0,6},{2,0},{4,2},{6,4},{1,7},{3,1},{5,3},{7,5},{8,14},{10,8},{12,... | collective-permute-start | bytes 147464 | tf_op jit(solution)/shard_map/ppermute | solution.py:329
  (3 other events, 3.1 us)
